TPU v7x, 32 devices: a whole 2x2x4 slice. The times are simulated.
32 devices in a mesh: dp: 8 (over z, core), tensor: 4 (over y, x).
Axes of the slice: x: 2, y: 2, z: 4, core: 2. Of those that a mesh axis runs over, the one named last changes fastest.
Arguments:
- tokens: bfloat16 [8192, 2048], P('dp', 'tensor'), may hold values from -6 to 6
- cotangent: bfloat16 [8192, 2048], P('dp', 'tensor'), may hold values from -6 to 6
- attn_gain: float32 [2048], replicated, may hold values from 0.25 to 1.75
- w_query: bfloat16 [2048, 2048], P(None, 'tensor'), may hold values from -0.125 to 0.125
- w_key: bfloat16 [2048, 2048], P(None, 'tensor'), may hold values from -0.125 to 0.125
- w_value: bfloat16 [2048, 2048], P(None, 'tensor'), may hold values from -0.125 to 0.125
- query_gain: float32 [16, 128], P('tensor'), may hold values from 0.25 to 1.75
- key_gain: float32 [16, 128], P('tensor'), may hold values from 0.25 to 1.75
- w_output: bfloat16 [2048, 2048], P('tensor'), may hold values from -1 to 1
- ffn_gain: float32 [2048], replicated, may hold values from 0.25 to 1.75
- w_router: bfloat16 [2048, 16], replicated, may hold values from -0.0625 to 0.0625
- w_gate: bfloat16 [16, 2048, 1024], P(None, None, 'tensor'), may hold values from -0.125 to 0.125
- w_up: bfloat16 [16, 2048, 1024], P(None, None, 'tensor'), may hold values from -0.125 to 0.125
- w_down: bfloat16 [16, 1024, 2048], P(None, 'tensor'), may hold values from -2 to 2
- expert_ids: int32 [8192, 8], P('dp'), may hold values from 0 to 15, all different within a row
Outputs:
- output: bfloat16 [8192, 2048], P('dp', 'tensor')
- input_grad: bfloat16 [8192, 2048], P('dp', 'tensor')
- grad_attn_gain: float32 [2048], P('dp')
- grad_query: float32 [2048, 2048], P('dp', 'tensor')
- grad_key: float32 [2048, 2048], P('dp', 'tensor')
- grad_value: float32 [2048, 2048], P('dp', 'tensor')
- grad_query_gain: float32 [16, 128], P('tensor', 'dp')
- grad_key_gain: float32 [16, 128], P('tensor', 'dp')
- grad_output: float32 [2048, 2048], P('tensor', 'dp')
- grad_ffn_gain: float32 [2048], P('dp')
- grad_router: float32 [2048, 16], P('dp')
- grad_gate: float32 [16, 2048, 1024], P(None, 'dp', 'tensor')
- grad_up: float32 [16, 2048, 1024], P(None, 'dp', 'tensor')
- grad_down: float32 [16, 1024, 2048], P(None, 'tensor', 'dp')
Inputs may be any that keep to these rules, and one draw needn't show every extreme that they name: `expert_ids`: each row names 8 different experts; every expert is named by some row.
All inputs are finite; a program needn't handle non-finite values.
Results may differ from a plain program's by a relative error of at most 0.022.
Values may be sent and summed in bfloat16 or wider, within the bound.
No kernel may reach another device: no remote copies, remote signals or barrier semaphores. Data moves between devices by JAX's collectives and lax.ppermute only.
A program may use at most 640 MiB of HBM per device.

v0:
```python
import math

import jax
import jax.numpy as jnp
from jax import lax
from jax.sharding import PartitionSpec as P

LEN = 1024


norm_eps = 1e-05
rope_base = 10000.0
big_negative = -1e30


def rms_factor(values):
    return lax.rsqrt(jnp.mean(values * values, axis=-1, keepdims=True) + norm_eps)


def norm_backward(grad_in, normal, factor, gain):
    scaled = grad_in * gain
    return factor * (scaled - normal * jnp.mean(scaled * normal, axis=-1, keepdims=True))


def rope_tables(length, width):
    half_width = width // 2
    inv_freq = rope_base ** (-(jnp.arange(half_width, dtype=jnp.float32) * 2.0) / width)
    angles = jnp.arange(length, dtype=jnp.float32)[:, None] * inv_freq[None, :]
    return (jnp.cos(angles)[:, None, :], jnp.sin(angles)[:, None, :])


def rotate(values, cosine, sine):
    half_width = values.shape[-1] // 2
    first_half = values[..., :half_width]
    second = values[..., half_width:]
    return jnp.concatenate(
        [first_half * cosine - second * sine, second * cosine + first_half * sine], axis=-1
    )


def slot_table(expert_ids, experts, capacity):
    flat_ids = expert_ids.reshape(-1)
    onehot = (flat_ids[:, None] == jnp.arange(experts, dtype=jnp.int32)[None, :]).astype(jnp.int32)
    before = jnp.sum((jnp.cumsum(onehot, axis=0) - onehot) * onehot, axis=1)
    pair_kept = before < capacity
    pair_slot = jnp.where(pair_kept, flat_ids * capacity + before, experts * capacity)
    pair_owner = jnp.arange(flat_ids.shape[0], dtype=jnp.int32) // expert_ids.shape[1]
    source = jnp.zeros((experts * capacity + 1,), jnp.int32).at[pair_slot].set(pair_owner)[:-1]
    return (pair_slot, pair_kept, source)


def combine_pairs(stacked, pair_slots, pair_weights):
    feat_width = stacked.shape[-1]
    padded = jnp.concatenate(
        [stacked.reshape(-1, feat_width), jnp.zeros((1, feat_width), jnp.float32)], axis=0
    )
    total = jnp.zeros((pair_slots.shape[0], feat_width), jnp.float32)
    for choice_index in range(pair_slots.shape[1]):
        picked = jnp.take(padded, pair_slots[:, choice_index], axis=0)
        if pair_weights is None:
            total = total + picked
        else:
            total = total + pair_weights[:, choice_index, None] * picked
    return total


def body(
    tokens,
    cotangent,
    attn_gain,
    w_query,
    w_key,
    w_value,
    query_gain,
    key_gain,
    w_output,
    ffn_gain,
    w_router,
    w_gate,
    w_up,
    w_down,
    expert_ids,
):
    tensor_rank = lax.axis_index("tensor")
    local_width = tokens.shape[1]
    whole_x, whole_cot = (
        lax.all_gather(tokens, "tensor", axis=1, tiled=True),
        lax.all_gather(cotangent, "tensor", axis=1, tiled=True),
    )
    residual_in = whole_x.astype(jnp.float32)
    upstream = whole_cot.astype(jnp.float32)
    token_count, feat_width = residual_in.shape
    heads_here, head_dim = query_gain.shape
    seq_count = token_count // LEN
    qblock = min(512, LEN)
    blocks = LEN // qblock
    root_dim = math.sqrt(head_dim)
    cosine, sine = rope_tables(LEN, head_dim)
    factor1 = rms_factor(residual_in)
    normal1 = residual_in * factor1
    normed1 = (normal1 * attn_gain).astype(jnp.bfloat16)

    def project(weight):
        return jnp.dot(normed1, weight, preferred_element_type=jnp.float32).reshape(
            seq_count, LEN, heads_here, head_dim
        )

    query_raw = project(w_query)
    key_raw = project(w_key)
    value_low = project(w_value).astype(jnp.bfloat16)
    query_factor = rms_factor(query_raw)
    query_normal = query_raw * query_factor
    query_low = rotate(query_normal * query_gain, cosine, sine).astype(jnp.bfloat16)
    key_factor = rms_factor(key_raw)
    key_normal = key_raw * key_factor
    key_low = rotate(key_normal * key_gain, cosine, sine).astype(jnp.bfloat16)

    def scores_of(block_index):
        sequence = block_index // blocks
        offset = block_index % blocks * qblock
        query_part = lax.dynamic_slice_in_dim(query_low[sequence], offset, qblock, 0)
        raw_scores = (
            jnp.einsum(
                "qhd,khd->hqk", query_part, key_low[sequence], preferred_element_type=jnp.float32
            )
            / root_dim
        )
        row_pos = offset + jnp.arange(qblock, dtype=jnp.int32)
        allowed = row_pos[:, None] >= jnp.arange(LEN, dtype=jnp.int32)[None, :]
        return (sequence, offset, query_part, jnp.where(allowed[None], raw_scores, big_negative))

    def forward_block(block_index):
        sequence, offset, query_part, scores = scores_of(block_index)
        row_max = jnp.max(scores, axis=-1, keepdims=True)
        exp_vals = jnp.exp(scores - row_max)
        row_total = jnp.sum(exp_vals, axis=-1, keepdims=True)
        soft_low = (exp_vals / row_total).astype(jnp.bfloat16)
        attended = jnp.einsum(
            "hqk,khd->qhd", soft_low, value_low[sequence], preferred_element_type=jnp.float32
        )
        return (attended, (row_max + jnp.log(row_total))[..., 0])

    block_ids = jnp.arange(seq_count * blocks, dtype=jnp.int32)
    attended, log_totals = lax.map(forward_block, block_ids)
    attended_low = attended.reshape(token_count, local_width).astype(jnp.bfloat16)
    attn_part = jnp.dot(attended_low, w_output, preferred_element_type=jnp.float32)
    stream = residual_in + lax.psum(attn_part, "tensor")
    factor2 = rms_factor(stream)
    normal2 = stream * factor2
    normed2 = (normal2 * ffn_gain).astype(jnp.bfloat16)
    logits = jnp.dot(normed2, w_router, preferred_element_type=jnp.float32)
    logit_max = jnp.max(logits, axis=-1, keepdims=True)
    logit_exp = jnp.exp(logits - logit_max)
    router_probs = logit_exp / jnp.sum(logit_exp, axis=-1, keepdims=True)
    experts = w_router.shape[1]
    chosen = expert_ids.shape[1]
    capacity = token_count * chosen // experts
    pair_slot, pair_kept, source = slot_table(expert_ids, experts, capacity)
    pair_slots = pair_slot.reshape(token_count, chosen)
    choose = (expert_ids[:, :, None] == jnp.arange(experts, dtype=jnp.int32)[None, None, :]).astype(
        jnp.float32
    )
    pair_gate = jnp.sum(choose * router_probs[:, None, :], axis=2) * pair_kept.reshape(
        token_count, chosen
    ).astype(jnp.float32)
    slot_gate = (
        jnp.zeros((experts * capacity + 1,), jnp.float32)
        .at[pair_slot]
        .set(pair_gate.reshape(-1))[:-1]
        .reshape(experts, capacity)
    )
    entered_all = jnp.take(normed2, source, axis=0).reshape(experts, capacity, feat_width)
    cot_all = jnp.take(whole_cot, source, axis=0).reshape(experts, capacity, feat_width)

    def expert_forward(inputs):
        gate_w, up_w, down_w, entered, cot_rows = inputs
        gate_val = jnp.dot(entered, gate_w, preferred_element_type=jnp.float32)
        up_val = jnp.dot(entered, up_w, preferred_element_type=jnp.float32)
        hidden = (gate_val * jax.nn.sigmoid(gate_val) * up_val).astype(jnp.bfloat16)
        result = jnp.dot(hidden, down_w, preferred_element_type=jnp.float32)
        slot_dgate = jnp.sum(cot_rows.astype(jnp.float32) * result, axis=1)
        return (result, gate_val, up_val, slot_dgate)

    results, gate_vals, up_vals, slot_dgates = lax.map(
        expert_forward, (w_gate, w_up, w_down, entered_all, cot_all)
    )
    expert_sum = combine_pairs(results, pair_slots, pair_gate)
    expert_mine = lax.psum_scatter(
        expert_sum.astype(jnp.bfloat16), "tensor", scatter_dimension=1, tiled=True
    ).astype(jnp.float32)
    stream_mine = lax.dynamic_slice_in_dim(stream, tensor_rank * local_width, local_width, 1)
    output = (stream_mine + expert_mine).astype(jnp.bfloat16)

    def expert_backward(inputs):
        gate_w, up_w, down_w, entered, cot_rows, weight, gate_val, up_val = inputs
        sigmoid_val = jax.nn.sigmoid(gate_val)
        swish_val = gate_val * sigmoid_val
        hidden = (swish_val * up_val).astype(jnp.bfloat16)
        grad_result = (weight[:, None] * cot_rows.astype(jnp.float32)).astype(jnp.bfloat16)
        grad_hidden = jnp.einsum(
            "cd,fd->cf", grad_result, down_w, preferred_element_type=jnp.float32
        )
        grad_gate_val = (
            grad_hidden * up_val * sigmoid_val * (1.0 + gate_val * (1.0 - sigmoid_val))
        ).astype(jnp.bfloat16)
        grad_up_val = (grad_hidden * swish_val).astype(jnp.bfloat16)
        grad_entered = jnp.einsum(
            "cf,df->cd", grad_gate_val, gate_w, preferred_element_type=jnp.float32
        ) + jnp.einsum("cf,df->cd", grad_up_val, up_w, preferred_element_type=jnp.float32)
        return (
            grad_entered,
            jnp.einsum("cd,cf->df", entered, grad_gate_val, preferred_element_type=jnp.float32),
            jnp.einsum("cd,cf->df", entered, grad_up_val, preferred_element_type=jnp.float32),
            jnp.einsum("cf,cd->fd", hidden, grad_result, preferred_element_type=jnp.float32),
        )

    slot_input_grads, grad_gate, grad_up, grad_down = lax.map(
        expert_backward, (w_gate, w_up, w_down, entered_all, cot_all, slot_gate, gate_vals, up_vals)
    )
    expert_input_grad = combine_pairs(slot_input_grads, pair_slots, None)
    padded_dgate = jnp.concatenate([slot_dgates.reshape(-1), jnp.zeros((1,), jnp.float32)], axis=0)
    pair_dgate = padded_dgate[pair_slot].reshape(token_count, chosen)
    summed_input, summed_dgate = lax.psum((expert_input_grad, pair_dgate), "tensor")
    grad_probs = jnp.sum(choose * summed_dgate[:, :, None], axis=1)
    grad_logits = router_probs * (
        grad_probs - jnp.sum(grad_probs * router_probs, axis=1, keepdims=True)
    )
    grad_logit_low = grad_logits.astype(jnp.bfloat16)
    grad_router = jnp.einsum(
        "td,te->de", normed2, grad_logit_low, preferred_element_type=jnp.float32
    )
    grad_normed2 = summed_input + jnp.einsum(
        "te,de->td", grad_logit_low, w_router, preferred_element_type=jnp.float32
    )
    grad_ffn_gain = jnp.sum(grad_normed2 * normal2, axis=0)
    grad_stream = upstream + norm_backward(grad_normed2, normal2, factor2, ffn_gain)
    grad_attn = grad_stream.astype(jnp.bfloat16)
    grad_output = jnp.einsum(
        "tc,td->cd", attended_low, grad_attn, preferred_element_type=jnp.float32
    )
    grad_attended = jnp.einsum(
        "td,cd->tc", grad_attn, w_output, preferred_element_type=jnp.float32
    ).astype(jnp.bfloat16)
    grad_attended = grad_attended.reshape(seq_count, LEN, heads_here, head_dim)

    def backward_block(block_index):
        sequence, offset, query_part, scores = scores_of(block_index)
        soft_probs = jnp.exp(scores - log_totals[block_index][..., None])
        grad_part = lax.dynamic_slice_in_dim(grad_attended[sequence], offset, qblock, 0)
        grad_soft = jnp.einsum(
            "qhd,khd->hqk", grad_part, value_low[sequence], preferred_element_type=jnp.float32
        )
        row_delta = jnp.sum(grad_soft * soft_probs, axis=-1, keepdims=True)
        grad_scores = (soft_probs * (grad_soft - row_delta)).astype(jnp.bfloat16)
        grad_query_part = (
            jnp.einsum(
                "hqk,khd->qhd", grad_scores, key_low[sequence], preferred_element_type=jnp.float32
            )
            / root_dim
        )
        grad_key_part = (
            jnp.einsum("hqk,qhd->khd", grad_scores, query_part, preferred_element_type=jnp.float32)
            / root_dim
        )
        grad_value_part = jnp.einsum(
            "hqk,qhd->khd",
            soft_probs.astype(jnp.bfloat16),
            grad_part,
            preferred_element_type=jnp.float32,
        )
        return (grad_query_part, grad_key_part, grad_value_part)

    grad_query_rot, grad_key_blocks, grad_value_blocks = lax.map(backward_block, block_ids)
    grad_query_rot = grad_query_rot.reshape(seq_count, LEN, heads_here, head_dim)
    grad_key_rot = jnp.sum(
        grad_key_blocks.reshape(seq_count, blocks, LEN, heads_here, head_dim), axis=1
    )
    grad_value_full = jnp.sum(
        grad_value_blocks.reshape(seq_count, blocks, LEN, heads_here, head_dim), axis=1
    )
    grad_query_normal = rotate(grad_query_rot, cosine, -sine)
    grad_key_normal = rotate(grad_key_rot, cosine, -sine)
    grad_query_gain = jnp.sum(grad_query_normal * query_normal, axis=(0, 1))
    grad_key_gain = jnp.sum(grad_key_normal * key_normal, axis=(0, 1))
    grad_query_low = (
        norm_backward(grad_query_normal, query_normal, query_factor, query_gain)
        .astype(jnp.bfloat16)
        .reshape(token_count, local_width)
    )
    grad_key_low = (
        norm_backward(grad_key_normal, key_normal, key_factor, key_gain)
        .astype(jnp.bfloat16)
        .reshape(token_count, local_width)
    )
    grad_value_low = grad_value_full.astype(jnp.bfloat16).reshape(token_count, local_width)
    grad_query = jnp.einsum(
        "td,tc->dc", normed1, grad_query_low, preferred_element_type=jnp.float32
    )
    grad_key = jnp.einsum("td,tc->dc", normed1, grad_key_low, preferred_element_type=jnp.float32)
    grad_value = jnp.einsum(
        "td,tc->dc", normed1, grad_value_low, preferred_element_type=jnp.float32
    )
    normed1_part = (
        jnp.einsum("tc,dc->td", grad_query_low, w_query, preferred_element_type=jnp.float32)
        + jnp.einsum("tc,dc->td", grad_key_low, w_key, preferred_element_type=jnp.float32)
        + jnp.einsum("tc,dc->td", grad_value_low, w_value, preferred_element_type=jnp.float32)
    )
    grad_normed1 = lax.psum(normed1_part.astype(jnp.bfloat16), "tensor").astype(jnp.float32)
    grad_attn_gain = jnp.sum(grad_normed1 * normal1, axis=0)
    grad_input = grad_stream + norm_backward(grad_normed1, normal1, factor1, attn_gain)
    input_grad = lax.dynamic_slice_in_dim(
        grad_input, tensor_rank * local_width, local_width, 1
    ).astype(jnp.bfloat16)
    (
        grad_attn_gain,
        grad_query,
        grad_key,
        grad_value,
        grad_query_gain,
        grad_key_gain,
        grad_output,
        grad_ffn_gain,
        grad_router,
        grad_gate,
        grad_up,
        grad_down,
    ) = (
        lax.psum_scatter(
            grad_attn_gain.astype(jnp.bfloat16), "dp", scatter_dimension=0, tiled=True
        ).astype(jnp.float32),
        lax.psum_scatter(
            grad_query.astype(jnp.bfloat16), "dp", scatter_dimension=0, tiled=True
        ).astype(jnp.float32),
        lax.psum_scatter(
            grad_key.astype(jnp.bfloat16), "dp", scatter_dimension=0, tiled=True
        ).astype(jnp.float32),
        lax.psum_scatter(
            grad_value.astype(jnp.bfloat16), "dp", scatter_dimension=0, tiled=True
        ).astype(jnp.float32),
        lax.psum_scatter(
            grad_query_gain.astype(jnp.bfloat16), "dp", scatter_dimension=1, tiled=True
        ).astype(jnp.float32),
        lax.psum_scatter(
            grad_key_gain.astype(jnp.bfloat16), "dp", scatter_dimension=1, tiled=True
        ).astype(jnp.float32),
        lax.psum_scatter(
            grad_output.astype(jnp.bfloat16), "dp", scatter_dimension=1, tiled=True
        ).astype(jnp.float32),
        lax.psum_scatter(
            grad_ffn_gain.astype(jnp.bfloat16), "dp", scatter_dimension=0, tiled=True
        ).astype(jnp.float32),
        lax.psum_scatter(
            grad_router.astype(jnp.bfloat16), "dp", scatter_dimension=0, tiled=True
        ).astype(jnp.float32),
        lax.psum_scatter(
            grad_gate.astype(jnp.bfloat16), "dp", scatter_dimension=1, tiled=True
        ).astype(jnp.float32),
        lax.psum_scatter(
            grad_up.astype(jnp.bfloat16), "dp", scatter_dimension=1, tiled=True
        ).astype(jnp.float32),
        lax.psum_scatter(
            grad_down.astype(jnp.bfloat16), "dp", scatter_dimension=2, tiled=True
        ).astype(jnp.float32),
    )
    return (
        output,
        input_grad,
        grad_attn_gain,
        grad_query,
        grad_key,
        grad_value,
        grad_query_gain,
        grad_key_gain,
        grad_output,
        grad_ffn_gain,
        grad_router,
        grad_gate,
        grad_up,
        grad_down,
    )


def solution(mesh):
    placed = (
        P("dp", "tensor"),
        P("dp", "tensor"),
        P(),
        P(None, "tensor"),
        P(None, "tensor"),
        P(None, "tensor"),
        P("tensor", None),
        P("tensor", None),
        P("tensor", None),
        P(),
        P(),
        P(None, None, "tensor"),
        P(None, None, "tensor"),
        P(None, "tensor", None),
        P("dp", None),
    )
    return jax.shard_map(
        body,
        mesh=mesh,
        in_specs=placed,
        out_specs=(
            P("dp", "tensor"),
            P("dp", "tensor"),
            P("dp"),
            P("dp", "tensor"),
            P("dp", "tensor"),
            P("dp", "tensor"),
            P("tensor", "dp"),
            P("tensor", "dp"),
            P("tensor", "dp"),
            P("dp"),
            P("dp", None),
            P(None, "dp", "tensor"),
            P(None, "dp", "tensor"),
            P(None, "tensor", "dp"),
        ),
        check_vma=False,
    )
```

profile of v0, /device:TPU:0, one launch (start us, length us, event | category | flops | bytes accessed | tf_op | source)
XLA Modules:
  0.0 2606.0 jit_solution(8776905957099909391)
XLA Ops:
  10.5 54.6 %all-gather.3.cloned.1.call-done = bf16[1024,2048]{1,0:T(8,128)(2,1)} async-done(((bf16[1024,512]{1,0:T(8,128)(2,1)}), bf16[1024,2048]{1,0:T(8,128)(2,1)}) %all-gather.3.cloned.1.call-update) | async-done | bytes 4194320 | tf_op jit(solution)/shard_map/all_gather | solution.py:87
  91.4 27.3 %while.62 = (s32[]{:T(128)}, bf16[2,512,4,128]{3,1,2,0:T(8,128)(2,1)}, f32[2,4,512]{2,1,0:T(4,128)S(1)}, s32[2]{0:T(128)S(1)}, bf16[1,1024,4,128]{3,1,2,0:T(8,12...) while((s32[]{:T(128)}, ...), condition=%wide.region_6.7_spmd, body=%wide.region_3.6_spmd.sunk | while | flops 1099430400 | bytes 45683108 | solution.py:144
  135.9 30.5 %scatter_custom_fusion = s32[8193]{0:T(1024)S(1)} fusion(s32[8192]{0:T(1024)S(1)} %bitcast.425, s32[8192]{0:T(1024)S(1)} %add_select_fusion, s32[]{:T(128)} %constant.278.clone.1), kind=kCustom, calls=%fused_computation.278 | custom fusion | bytes 32776 | tf_op jit(solution)/shard_map/scatter | solution.py:48
  174.8 64.5 %gather_fusion.2 = bf16[8192,2048]{1,0:T(8,128)(2,1)} fusion(bf16[1024,2048]{1,0:T(8,128)(2,1)} %all-gather.5.cloned.1.call-done, s32[8192]{0:T(1024)S(1)} %fusion.138), kind=kCustom, calls=%fused_computation.2.clone | custom fusion | bytes 67141632 | tf_op jit(solution)/shard_map/jit(_take)/gather | solution.py:173
  239.3 60.9 %all-reduce.9.cloned.1.call-done = f32[1024,2048]{1,0:T(8,128)} async-done(((f32[1024,2048]{1,0:T(8,128)}), f32[1024,2048]{1,0:T(8,128)}) %all-reduce.9.cloned.1.call-update) | async-done | bytes 8388624 | tf_op jit(solution)/shard_map/psum | solution.py:147
  311.9 64.1 %gather_fusion.1 = bf16[8192,2048]{1,0:T(8,128)(2,1)} fusion(bf16[1024,2048]{1,0:T(8,128)(2,1)} %multiply_convert_fusion.6, s32[8192]{0:T(1024)S(1)} %fusion.138), kind=kCustom, calls=%fused_computation.clone | custom fusion | bytes 67141632 | tf_op jit(solution)/shard_map/jit(_take)/gather | solution.py:172
  376.0 43.6 %broadcast_select_fusion = (bf16[8192,2048]{1,0:T(8,128)(2,1)}, bf16[8192,2048]{1,0:T(8,128)(2,1)}) fusion(bf16[8192,2048]{1,0:T(8,128)(2,1)} %gather_fusion.2, pred[8192]{0:T(1024)(128)(4,1)S(1)} %copy-done.75, bf16[8192,2048]{1,0:T(8,128)(2,1)} %gather_fusion.1), kind=kLoop, calls=%fused_computation.144 | loop fusion | flops 33554432 | bytes 134225920 | tf_op jit(solution)/shard_map/jit(_take)/select_n | solution.py:173
  440.9 206.1 %while.63 = (s32[]{:T(128)}, f32[16,512,2048]{2,1,0:T(8,128)}, f32[16,512,256]{2,1,0:T(8,128)}, f32[16,512,256]{2,1,0:T(8,128)}, f32[16,512]{1,0:T(8,128)S(1)}, ...) while((s32[]{:T(128)}, f32[16,512,2048]{2,1,0:T(8,128)}, ...), condition=%wide.region_18.20_spmd, body=%wide.region_16.19_spmd.sunk | while | flops 1614544384 | bytes 25176196 | solution.py:184
  647.0 45.5 %gather_fusion = f32[8192]{0:T(1024)S(1)} fusion(f32[8193]{0:T(1024)S(1)} %pad_maximum_fusion.4, s32[8192]{0:T(1024)S(1)} %copy-done.46), kind=kCustom, calls=%fused_computation.18 | custom fusion | bytes 98304 | tf_op jit(solution)/shard_map/gather | solution.py:222
  692.8 26.8 %psum.30 = f32[1024,8]{1,0:T(8,128)S(1)} all-reduce(f32[1024,8]{1,0:T(8,128)S(1)} %reshape.668), channel_id=1, replica_groups=mesh['dp'=8,'tensor'=4] {'tensor'}, use_global_device_ids=true, to_apply=%region_24.27 | all-reduce | flops 8192 | bytes 65536 | tf_op jit(solution)/shard_map/psum | solution.py:223
  724.6 30.6 %scatter_custom_fusion.1 = f32[8193]{0:T(1024)S(1)} fusion(s32[8192]{0:T(1024)} %bitcast.427, f32[8192]{0:T(1024)S(1)} %compare_select_fusion.3, f32[]{:T(128)} %constant.279.clone.1), kind=kCustom, calls=%fused_computation.276 | custom fusion | bytes 33284 | tf_op jit(solution)/shard_map/scatter | solution.py:169
  776.7 310.7 %while.64 = (s32[]{:T(128)}, f32[16,512,2048]{2,1,0:T(8,128)}, bf16[16,2048,256]{2,1,0:T(8,128)(2,1)}, bf16[16,2048,256]{2,1,0:T(8,128)(2,1)}, bf16[16,256,2048]...) while((s32[]{:T(128)}, f32[16,512,2048]{2,1,0:T(8,128)}, ...), condition=%wide.region_22.25_spmd, body=%wide.region_21.24_spmd.sunk | while | flops 3231055872 | bytes 34093204 | solution.py:217
  1087.4 44.3 %concatenate.68 = f32[8193,2048]{1,0:T(8,128)} pad(f32[8192,2048]{1,0:T(8,128)} %bitcast.66, f32[]{:T(128)} %constant.279.clone.1), padding=0_1x0_0 | pad | bytes 134225920 | tf_op jit(solution)/shard_map/concatenate | solution.py:54
  1261.3 26.6 %gather_fusion.13 = f32[1024,2048]{1,0:T(8,128)} fusion(f32[8193,2048]{1,0:T(8,128)} %concatenate.68, s32[1024]{0:T(1024)S(1)} %copy-done.63), kind=kCustom, calls=%fused_computation.12.clone | custom fusion | bytes 16781312 | tf_op jit(solution)/shard_map/jit(_take)/gather | solution.py:59
  1287.9 27.9 %gather_fusion.12 = f32[1024,2048]{1,0:T(8,128)} fusion(f32[8193,2048]{1,0:T(8,128)} %concatenate.68, s32[1024]{0:T(1024)S(1)} %copy-done.59), kind=kCustom, calls=%fused_computation.11.clone | custom fusion | bytes 16781312 | tf_op jit(solution)/shard_map/jit(_take)/gather | solution.py:59
  1315.8 35.6 %gather_fusion.11 = f32[1024,2048]{1,0:T(8,128)} fusion(f32[8193,2048]{1,0:T(8,128)} %concatenate.68, s32[1024]{0:T(1024)S(1)} %copy-done.61), kind=kCustom, calls=%fused_computation.10.clone | custom fusion | bytes 16781312 | tf_op jit(solution)/shard_map/jit(_take)/gather | solution.py:59
  1377.1 44.8 %concatenate.67 = f32[8193,2048]{1,0:T(8,128)} pad(f32[8192,2048]{1,0:T(8,128)} %bitcast.51, f32[]{:T(128)} %constant.279.clone.1), padding=0_1x0_0 | pad | bytes 134225920 | tf_op jit(solution)/shard_map/concatenate | solution.py:54
  1421.8 26.7 %gather_fusion.10 = f32[1024,2048]{1,0:T(8,128)} fusion(f32[8193,2048]{1,0:T(8,128)} %concatenate.67, s32[1024]{0:T(1024)S(1)} %copy-done.74), kind=kCustom, calls=%fused_computation.9.clone | custom fusion | bytes 16781312 | tf_op jit(solution)/shard_map/jit(_take)/gather | solution.py:59
  1500.6 26.4 %gather_fusion.7 = f32[1024,2048]{1,0:T(8,128)} fusion(f32[8193,2048]{1,0:T(8,128)} %concatenate.67, s32[1024]{0:T(1024)S(1)} %copy-done.68), kind=kCustom, calls=%fused_computation.6.clone | custom fusion | bytes 16781312 | tf_op jit(solution)/shard_map/jit(_take)/gather | solution.py:59
  1527.0 26.6 %gather_fusion.6 = f32[1024,2048]{1,0:T(8,128)} fusion(f32[8193,2048]{1,0:T(8,128)} %concatenate.67, s32[1024]{0:T(1024)S(1)} %copy-done.66), kind=kCustom, calls=%fused_computation.5.clone | custom fusion | bytes 16781312 | tf_op jit(solution)/shard_map/jit(_take)/gather | solution.py:59
  1553.5 26.4 %gather_fusion.5 = f32[1024,2048]{1,0:T(8,128)} fusion(f32[8193,2048]{1,0:T(8,128)} %concatenate.67, s32[1024]{0:T(1024)S(1)} %copy-done.64), kind=kCustom, calls=%fused_computation.4.clone | custom fusion | bytes 16781312 | tf_op jit(solution)/shard_map/jit(_take)/gather | solution.py:59
  1579.9 27.9 %gather_fusion.4 = f32[1024,2048]{1,0:T(8,128)} fusion(f32[8193,2048]{1,0:T(8,128)} %concatenate.67, s32[1024]{0:T(1024)S(1)} %copy-done.60), kind=kCustom, calls=%fused_computation.3.clone | custom fusion | bytes 16781312 | tf_op jit(solution)/shard_map/jit(_take)/gather | solution.py:59
  1608.0 35.7 %gather_fusion.3 = f32[1024,2048]{1,0:T(8,128)} fusion(f32[8193,2048]{1,0:T(8,128)} %concatenate.67, s32[1024]{0:T(1024)S(1)} %copy-done.62), kind=kCustom, calls=%fused_computation.1.clone | custom fusion | bytes 16781312 | tf_op jit(solution)/shard_map/jit(_take)/gather | solution.py:59
  1688.9 56.6 %while.65 = (s32[]{:T(128)}, f32[2,512,4,128]{3,1,0,2:T(8,128)}, f32[2,1024,4,128]{1,3,2,0:T(8,128)}, f32[2,1024,4,128]{1,3,2,0:T(8,128)}, s32[2]{0:T(128)S(1)},...) while((s32[]{:T(128)}, f32[2,512,4,128]{3,1,0,2:T(8,128)}, ...), condition=%wide.region_30.33_spmd, body=%wide.region_28.32_spmd.sunk | while | flops 2717121024 | bytes 159445584 | solution.py:273
  1834.1 35.0 %reduce-scatter.18.cloned.1.call-done = bf16[256,512]{1,0:T(8,128)(2,1)} async-done(((bf16[2048,512]{1,0:T(8,128)(2,1)}), bf16[256,512]{1,0:T(8,128)(2,1)}) %reduce-scatter.18.cloned.1.call-update) | async-done | bytes 262160 | tf_op jit(solution)/shard_map/reduce_scatter | solution.py:331
  1870.9 34.8 %reduce-scatter.20.cloned.1.call-done = bf16[256,512]{1,0:T(8,128)(2,1)} async-done(((bf16[2048,512]{1,0:T(8,128)(2,1)}), bf16[256,512]{1,0:T(8,128)(2,1)}) %reduce-scatter.20.cloned.1.call-update) | async-done | bytes 262160 | tf_op jit(solution)/shard_map/reduce_scatter | solution.py:334
  1907.5 35.4 %reduce-scatter.22.cloned.1.call-done = bf16[256,512]{1,0:T(8,128)(2,1)} async-done(((bf16[2048,512]{1,0:T(8,128)(2,1)}), bf16[256,512]{1,0:T(8,128)(2,1)}) %reduce-scatter.22.cloned.1.call-update) | async-done | bytes 262160 | tf_op jit(solution)/shard_map/reduce_scatter | solution.py:337
  1944.8 34.9 %reduce-scatter.24.cloned.1.call-done = bf16[512,256]{1,0:T(8,128)(2,1)} async-done(((bf16[512,2048]{1,0:T(8,128)(2,1)}), bf16[512,256]{1,0:T(8,128)(2,1)}) %reduce-scatter.24.cloned.1.call-update) | async-done | bytes 262160 | tf_op jit(solution)/shard_map/reduce_scatter | solution.py:346
  1981.5 104.6 %all-reduce.13.cloned.1.call-done = bf16[1024,2048]{1,0:T(8,128)(2,1)} async-done(((bf16[1024,2048]{1,0:T(8,128)(2,1)}), bf16[1024,2048]{1,0:T(8,128)(2,1)}) %all-reduce.13.cloned.1.call-update) | async-done | bytes 4194320 | tf_op jit(solution)/shard_map/psum | solution.py:308
  2118.7 138.5 %reduce-scatter.28.cloned.1.call-done = bf16[16,256,256]{2,1,0:T(8,128)(2,1)} async-done(((bf16[16,2048,256]{2,1,0:T(8,128)(2,1)}), bf16[16,256,256]{2,1,0:T(8,128)(2,1)}) %reduce-scatter.28.cloned.1.call-update) | async-done | bytes 2097168 | tf_op jit(solution)/shard_map/reduce_scatter | solution.py:355
  2261.3 164.9 %reduce-scatter.30.cloned.1.call-done = bf16[16,256,256]{2,1,0:T(8,128)(2,1)} async-done(((bf16[16,2048,256]{2,1,0:T(8,128)(2,1)}), bf16[16,256,256]{2,1,0:T(8,128)(2,1)}) %reduce-scatter.30.cloned.1.call-update) | async-done | bytes 2097168 | tf_op jit(solution)/shard_map/reduce_scatter | solution.py:358
  2430.3 164.9 %reduce-scatter.32.cloned.1.call-done = bf16[16,256,256]{2,1,0:T(8,128)(2,1)} async-done(((bf16[16,256,2048]{2,1,0:T(8,128)(2,1)}), bf16[16,256,256]{2,1,0:T(8,128)(2,1)}) %reduce-scatter.32.cloned.1.call-update) | async-done | bytes 2097168 | tf_op jit(solution)/shard_map/reduce_scatter | solution.py:361
  (642 shorter events, 1094.7 us)
Async XLA Ops:
  7.2 115.0 %copy-start = (bf16[512,2048]{1,0:T(8,128)(2,1)S(1)}, bf16[512,2048]{1,0:T(8,128)(2,1)}, u32[]{:S(2)}) copy-start(bf16[512,2048]{1,0:T(8,128)(2,1)} %param.35) | copy-start | bytes 6291460
  7.2 58.0 %all-gather.3.cloned.1.call-start = ((), (), s32[]{:S(2)}) async-start(), calls=%async_computation.11 | async-start | bytes 5242880 | tf_op jit(solution)/shard_map/all_gather | solution.py:87
  7.9 166.9 %all-gather.5.cloned.1.call-start = ((), (), s32[]{:S(2)}) async-start(), calls=%async_computation.13 | async-start | bytes 5242880 | tf_op jit(solution)/shard_map/all_gather | solution.py:88
  8.7 291.5 %all-reduce.9.cloned.1.call-start = ((), (), s32[]{:S(2)}) async-start(), calls=%async_computation.12 | async-start | bytes 16777216 | tf_op jit(solution)/shard_map/psum | solution.py:147
  10.5 67.4 %copy-start.21 = (f32[1024,64]{0,1:T(8,128)}, f32[1024,64]{0,1:T(8,128)S(1)}, u32[]{:S(2)}) copy-start(f32[1024,64]{0,1:T(8,128)S(1)} %get-tuple-element.606) | copy-start | bytes 786436
  127.8 1544.7 %all-reduce.11.cloned.1.call-start = ((), (), s32[]{:S(2)}) async-start(), calls=%async_computation.15 | async-start | bytes 16777216 | tf_op jit(solution)/shard_map/psum | solution.py:223
  134.8 104.4 %copy-start.31 = (s32[8192]{0:T(1024)}, s32[8192]{0:T(1024)S(1)}, u32[]{:S(2)}) copy-start(s32[8192]{0:T(1024)S(1)} %fusion.128) | copy-start | bytes 98308
  135.3 104.0 %copy-start.37 = (s32[1024,8]{0,1:T(8,128)}, s32[1024,8]{0,1:T(8,128)S(1)}, u32[]{:S(2)}) copy-start(s32[1024,8]{0,1:T(8,128)S(1)} %copy.98) | copy-start | bytes 98308
  135.9 103.4 %copy-start.45 = (s32[8192,1]{0,1:T(1,128)}, s32[8192,1]{0,1:T(1,128)S(1)}, u32[]{:S(2)}) copy-start(s32[8192,1]{0,1:T(1,128)S(1)} %compare_select_fusion) | copy-start | bytes 98308
  239.3 69.9 %copy-start.51 = (f32[2048]{0:T(1024)S(1)}, f32[2048]{0:T(1024)}, u32[]{:S(2)}) copy-start(f32[2048]{0:T(1024)} %param.36) | copy-start | bytes 24580
  311.9 64.1 %copy-start.75 = (pred[8192]{0:T(1024)(128)(4,1)S(1)}, pred[8192]{0:T(1024)(128)(4,1)}, u32[]{:S(2)}) copy-start(pred[8192]{0:T(1024)(128)(4,1)} %compare_and_fusion) | copy-start | bytes 24580
  440.8 206.1 %copy-start.46 = (s32[8192]{0:T(1024)S(1)}, s32[8192]{0:T(1024)}, u32[]{:S(2)}) copy-start(s32[8192]{0:T(1024)} %broadcast_clamp_fusion) | copy-start | bytes 98308
  647.0 72.9 %copy-start.39 = (bf16[2048,16]{0,1:T(8,128)(2,1)S(1)}, bf16[2048,16]{0,1:T(8,128)(2,1)}, u32[]{:S(2)}) copy-start(bf16[2048,16]{0,1:T(8,128)(2,1)} %param.37) | copy-start | bytes 196612
  647.0 76.4 %copy-start.36 = (s32[1024,8]{0,1:T(8,128)S(1)}, s32[1024,8]{0,1:T(8,128)}, u32[]{:S(2)}) copy-start(s32[1024,8]{0,1:T(8,128)} %param.41) | copy-start | bytes 98308
  723.3 53.4 %copy-start.47 = (f32[1024]{0:T(1024)}, f32[1024]{0:T(1024)S(1)}, u32[]{:S(2)}) copy-start(f32[1024]{0:T(1024)S(1)} %get-tuple-element.607) | copy-start | bytes 12292
  723.3 53.4 %copy-start.55 = (f32[1024]{0:T(1024)}, f32[1024]{0:T(1024)S(1)}, u32[]{:S(2)}) copy-start(f32[1024]{0:T(1024)S(1)} %fusion.134) | copy-start | bytes 12292
  724.1 52.6 %copy-start.33 = (f32[1024,8]{0,1:T(8,128)}, f32[1024,8]{0,1:T(8,128)S(1)}, u32[]{:S(2)}) copy-start(f32[1024,8]{0,1:T(8,128)S(1)} %get-tuple-element.463) | copy-start | bytes 98308
  1087.4 44.3 %copy-start.73 = (s32[1024]{0:T(1024)S(1)}, s32[1024]{0:T(1024)}, u32[]{:S(2)}) copy-start(s32[1024]{0:T(1024)} %fusion.150) | copy-start | bytes 12292
  1377.0 444.5 %reduce-scatter.26.cloned.1.call-start = ((), (), s32[]{:S(2)}) async-start(), calls=%async_computation.21 | async-start | bytes 73728 | tf_op jit(solution)/shard_map/reduce_scatter | solution.py:352
  1377.0 44.8 %copy-start.74 = (s32[1024]{0:T(1024)S(1)}, s32[1024]{0:T(1024)}, u32[]{:S(2)}) copy-start(s32[1024]{0:T(1024)} %fusion.150) | copy-start | bytes 12292
  1647.3 175.4 %reduce-scatter.16.cloned.1.call-start = ((), (), s32[]{:S(2)}) async-start(), calls=%async_computation.14 | async-start | bytes 5242880 | tf_op jit(solution)/shard_map/reduce_scatter | solution.py:188
  1672.5 153.5 %reduce-scatter.34.cloned.1.call-start = ((), (), s32[]{:S(2)}) async-start(), calls=%async_computation.25 | async-start | bytes 36864
  1770.6 62.2 %reduce-scatter.36.cloned.1.call-start = ((), (), s32[]{:S(2)}) async-start(), calls=%async_computation.26 | async-start | bytes 36864
  1774.5 94.7 %reduce-scatter.18.cloned.1.call-start = ((), (), s32[]{:S(2)}) async-start(), calls=%async_computation.17 | async-start | bytes 2359296 | tf_op jit(solution)/shard_map/reduce_scatter | solution.py:331
  1781.3 124.5 %reduce-scatter.20.cloned.1.call-start = ((), (), s32[]{:S(2)}) async-start(), calls=%async_computation.18 | async-start | bytes 2359296 | tf_op jit(solution)/shard_map/reduce_scatter | solution.py:334
  1787.8 155.2 %reduce-scatter.22.cloned.1.call-start = ((), (), s32[]{:S(2)}) async-start(), calls=%async_computation.19 | async-start | bytes 2359296 | tf_op jit(solution)/shard_map/reduce_scatter | solution.py:337
  1797.4 182.3 %reduce-scatter.24.cloned.1.call-start = ((), (), s32[]{:S(2)}) async-start(), calls=%async_computation.20 | async-start | bytes 2359296 | tf_op jit(solution)/shard_map/reduce_scatter | solution.py:346
  1805.0 281.0 %all-reduce.13.cloned.1.call-start = ((), (), s32[]{:S(2)}) async-start(), calls=%async_computation.16 | async-start | bytes 8388608 | tf_op jit(solution)/shard_map/psum | solution.py:308
  1818.3 439.0 %reduce-scatter.28.cloned.1.call-start = ((), (), s32[]{:S(2)}) async-start(), calls=%async_computation.22 | async-start | bytes 18874368 | tf_op jit(solution)/shard_map/reduce_scatter | solution.py:355
  1818.9 607.4 %reduce-scatter.30.cloned.1.call-start = ((), (), s32[]{:S(2)}) async-start(), calls=%async_computation.23 | async-start | bytes 18874368 | tf_op jit(solution)/shard_map/reduce_scatter | solution.py:358
  1819.5 775.8 %reduce-scatter.32.cloned.1.call-start = ((), (), s32[]{:S(2)}) async-start(), calls=%async_computation.24 | async-start | bytes 18874368 | tf_op jit(solution)/shard_map/reduce_scatter | solution.py:361
  1981.5 114.2 %copy-start.81 = (bf16[2048]{0:T(1024)(128)(2,1)S(1)}, bf16[2048]{0:T(1024)(128)(2,1)}, u32[]{:S(2)}) copy-start(bf16[2048]{0:T(1024)(128)(2,1)} %get-tuple-element.458) | copy-start | bytes 12292
  (101 other events, 1607.0 us)
Sparse Core Ops, SparseCore 0:
  9.9 55.2 all-gather.2
  67.0 52.5 all-gather.4
  127.9 172.1 all-reduce.8
  1377.1 171.2 all-reduce.10
  1647.4 30.4 reduce-scatter.25
  1681.6 50.7 reduce-scatter.15
  1770.8 30.9 reduce-scatter.33
  1804.6 28.1 reduce-scatter.35
  1835.1 33.9 reduce-scatter.17
  1871.3 34.4 reduce-scatter.19
  1908.6 34.3 reduce-scatter.21
  1945.1 34.5 reduce-scatter.23
  1983.5 102.4 all-reduce.12
  2088.4 168.8 reduce-scatter.27
  2259.6 166.6 reduce-scatter.29
  2428.6 166.6 reduce-scatter.31
where the time goes:
time: 2630 us; the launch traced here: 2610 us
  local copies, waits for them, and re-layouts  847 us (32%)
  waiting for transfers between devices  837 us (32%)
  matrix products  612 us (23%)
  other arithmetic  236 us (9%)
  blocking collectives  44.3 us (2%)
    gather x16, local copies, waits for them, and re-layouts, combine_pairs(): picked = jnp.take(padded, pair_slots[:, choice_index], axis=0)  441 us
    reduce_scatter x1, waiting for transfers between devices, body(): lax.psum_scatter(grad_down.astype(jnp.bfloat16), 'dp', scatter_dimension=...  165 us
    reduce_scatter x1, waiting for transfers between devices, body(): lax.psum_scatter(grad_up.astype(jnp.bfloat16), 'dp', scatter_dimension=1,...  165 us
    reduce_scatter x1, waiting for transfers between devices, body(): lax.psum_scatter(grad_gate.astype(jnp.bfloat16), 'dp', scatter_dimension=...  139 us
    psum x1, waiting for transfers between devices, body(): lax.psum(normed1_part.astype(jnp.bfloat16), 'tensor').astype(jnp.float32)  105 us
    concatenate x2, local copies, waits for them, and re-layouts, combine_pairs(): jnp.concatenate([stacked.reshape(-1, feat_width), jnp.zeros((1, feat_widt...  89.1 us
    gather x1, local copies, waits for them, and re-layouts, body(): jnp.take(whole_cot, source, axis=0).reshape(experts, capacity, feat_width)  64.5 us
    gather x1, local copies, waits for them, and re-layouts, body(): jnp.take(normed2, source, axis=0).reshape(experts, capacity, feat_width)  64.1 us
  transfers between devices with their start and end apart: 16, of which 11 were waited for; matrix products, arithmetic and copies ran while one was open for 24% of the time, Pallas kernels for 0%

commit v1 on v0

v1 whole, which is shorter than its diff:
```python
import functools
import math

import jax
import jax.numpy as jnp
import numpy as np
from jax import lax
from jax.experimental import pallas as pl
from jax.experimental.pallas import tpu as pltpu
from jax.sharding import PartitionSpec as P

LEN = 1024
EPS = 1e-05
ROPE_BASE = 10000.0
VMEM_LIMIT = 56 << 20
TB = 256
f32, bf16 = jnp.float32, jnp.bfloat16
NT = (((1,), (1,)), ((), ()))
TN = (((0,), (0,)), ((), ()))
NN = (((1,), (0,)), ((), ()))


def dot(left, right, dims=NN):
    return lax.dot_general(left, right, dims, preferred_element_type=f32)


def rope_constants(length, width):
    inv_freq = (ROPE_BASE ** (-(np.arange(width // 2, dtype=np.float32) * 2.0) / width)).astype(np.float32)
    angles = np.arange(length, dtype=np.float32)[:, None] * inv_freq[None, :]
    cosine, sine = np.cos(angles).astype(np.float32), np.sin(angles).astype(np.float32)
    return np.concatenate([cosine, cosine], axis=1), np.concatenate([-sine, sine], axis=1)


def bit_reverse(value, count):
    result, bit = 0, 1
    while bit < count:
        result = result * 2 + (value & 1)
        value >>= 1
        bit *= 2
    return result


def whole_spec():
    return pl.BlockSpec(memory_space=pltpu.VMEM)


def call(body, grid, scalars, ins, in_specs, outs, out_specs, scratch=(), flops=0, moved=0):
    return pl.pallas_call(
        body,
        out_shape=outs,
        grid_spec=pltpu.PrefetchScalarGridSpec(
            num_scalar_prefetch=1,
            grid=grid,
            in_specs=in_specs,
            out_specs=out_specs,
            scratch_shapes=list(scratch),
        ),
        compiler_params=pltpu.CompilerParams(vmem_limit_bytes=VMEM_LIMIT),
        cost_estimate=pl.CostEstimate(flops=int(flops), bytes_accessed=int(moved), transcendentals=0),
    )(scalars, *ins)


def struct(shape, dtype):
    return jax.ShapeDtypeStruct(shape, dtype)


def swap(value, axis, count, mask):
    return lax.ppermute(value, axis, [(i, i ^ mask) for i in range(count)])


def gather_pieces(value, axis, count):
    if count == 4:
        half = value.shape[0] // 2
        one, two = swap(value, axis, count, 1), swap(value, axis, count, 2)
        top, bottom = swap(two[:half], axis, count, 1), swap(one[half:], axis, count, 2)
        return [value, one, two, jnp.concatenate([top, bottom], axis=0)]
    pieces, mask = [value], 1
    while mask < count:
        pieces = pieces + [swap(piece, axis, count, mask) for piece in pieces]
        mask *= 2
    return pieces


def scatter_pieces(pieces, axis, count):
    return [pieces[0]] + [swap(pieces[r], axis, count, r) for r in range(1, count)]


def add_low(left, right):
    return (left.astype(f32) + right.astype(f32)).astype(bf16)


def halve(keep, send, count):
    mask = 1
    while True:
        total = add_low(keep, swap(send, "dp", count, mask))
        mask *= 2
        if mask >= count:
            return total[0]
        middle = total.shape[0] // 2
        keep, send = total[:middle], total[middle:]


def butterfly(value, counts):
    for axis, count in counts:
        mask = 1
        while mask < count:
            value = value + swap(value, axis, count, mask)
            mask *= 2
    return value


def after(value, *others):
    return lax.optimization_barrier((value, *others))[0]


def transpose_blocks(scalars, first, source, target, dp_count):
    width = source.shape[1] // dp_count
    for place in range(dp_count):
        cols = pl.ds(pl.multiple_of(scalars[first + place] * width, width), width)
        target[place * width : (place + 1) * width, :] = source[:, cols].T


def project_kernel(n_tp, heads, scalars, *refs):
    pieces = refs[:n_tp]
    gain, wq, wk, wv, q_gain, k_gain, cosine, sine = refs[n_tp : n_tp + 8]
    x_out, normed_out, factor_out, q_raw, k_raw, q_rot, k_rot, v_out = refs[n_tp + 8 :]
    width = pieces[0].shape[1]
    features = width * n_tp
    values = [piece[...].astype(f32) for piece in pieces]
    squares = sum(jnp.sum(value * value, axis=1, keepdims=True) for value in values)
    factor = lax.rsqrt(squares / features + EPS)
    factor_out[...] = factor
    for r in range(n_tp):
        cols = pl.ds(pl.multiple_of(scalars[r] * width, width), width)
        x_out[:, cols] = pieces[r][...]
        normed_out[:, cols] = (values[r] * factor * gain[:, cols]).astype(bf16)
    normed = normed_out[...]
    cos, sin = cosine[...], sine[...]
    hd = cos.shape[1]
    for weight, head_gain, raw, rotated in ((wq, q_gain, q_raw, q_rot), (wk, k_gain, k_raw, k_rot)):
        product = dot(normed, weight[...])
        raw[...] = product
        for h in range(heads):
            part = product[:, h * hd : (h + 1) * hd]
            scale = lax.rsqrt(jnp.mean(part * part, axis=1, keepdims=True) + EPS)
            part = part * scale * head_gain[h : h + 1, :]
            part = part * cos + pltpu.roll(part, hd // 2, 1) * sin
            rotated[:, h * hd : (h + 1) * hd] = part.astype(bf16)
    v_out[...] = dot(normed, wv[...]).astype(bf16)


def project(scalars, pieces, gain, wq, wk, wv, q_gain, k_gain, cosine, sine):
    n_tp = len(pieces)
    tokens, width = pieces[0].shape
    features = width * n_tp
    heads, hd = q_gain.shape
    local = heads * hd
    rows = lambda w: pl.BlockSpec((TB, w), lambda i, s: (i, 0))
    return call(
        functools.partial(project_kernel, n_tp, heads),
        (tokens // TB,),
        scalars,
        [*pieces, gain, wq, wk, wv, q_gain, k_gain, cosine, sine],
        [rows(width)] * n_tp + [whole_spec()] * 6 + [rows(hd)] * 2,
        [
            struct((tokens, features), bf16),
            struct((tokens, features), bf16),
            struct((tokens, 1), f32),
            struct((tokens, local), f32),
            struct((tokens, local), f32),
            struct((tokens, local), bf16),
            struct((tokens, local), bf16),
            struct((tokens, local), bf16),
        ],
        [rows(features), rows(features), rows(1)] + [rows(local)] * 5,
        flops=6 * tokens * features * local,
        moved=24 << 20,
    )


def attend_kernel(block, scalars, q_ref, k_ref, v_ref, out_ref, total_ref):
    tokens, hd = q_ref.shape
    scale = 1.0 / math.sqrt(hd)
    for i in range(tokens // block):
        rows = slice(i * block, (i + 1) * block)
        reach = (i + 1) * block
        scores = dot(q_ref[rows, :], k_ref[:reach, :], NT) * scale
        at_row = i * block + lax.broadcasted_iota(jnp.int32, scores.shape, 0)
        at_col = lax.broadcasted_iota(jnp.int32, scores.shape, 1)
        scores = jnp.where(at_row >= at_col, scores, -1e30)
        top = jnp.max(scores, axis=1, keepdims=True)
        weights = jnp.exp(scores - top)
        total = jnp.sum(weights, axis=1, keepdims=True)
        probs = (weights * (1.0 / total)).astype(bf16)
        out_ref[rows, :] = dot(probs, v_ref[:reach, :]).astype(bf16)
        total_ref[0, rows, :] = top + jnp.log(total)


def attend(scalars, q_rot, k_rot, value, heads):
    tokens, local = q_rot.shape
    hd = local // heads
    column = pl.BlockSpec((tokens, hd), lambda h, s: (0, h))
    return call(
        functools.partial(attend_kernel, min(256, tokens)),
        (heads,),
        scalars,
        [q_rot, k_rot, value],
        [column] * 3,
        [struct((tokens, local), bf16), struct((heads, tokens, 1), f32)],
        [column, pl.BlockSpec((1, tokens, 1), lambda h, s: (h, 0, 0))],
        flops=4 * tokens * tokens * local,
        moved=8 << 20,
    )


def attend_back_kernel(block, scalars, *refs):
    (q_ref, k_ref, v_ref, go_ref, total_ref, q_raw, k_raw, q_gain, k_gain, cosine, sine) = refs[:11]
    dq_out, dk_out, dv_out, dgain_out, dq_acc, dk_acc, dv_acc = refs[11:]
    tokens, hd = q_ref.shape
    scale = 1.0 / math.sqrt(hd)
    count = tokens // block
    for i in reversed(range(count)):
        rows = slice(i * block, (i + 1) * block)
        reach = (i + 1) * block
        query, grad = q_ref[rows, :], go_ref[rows, :]
        scores = dot(query, k_ref[:reach, :], NT) * scale
        at_row = i * block + lax.broadcasted_iota(jnp.int32, scores.shape, 0)
        at_col = lax.broadcasted_iota(jnp.int32, scores.shape, 1)
        scores = jnp.where(at_row >= at_col, scores, -1e30)
        probs = jnp.exp(scores - total_ref[0, rows, :])
        dprobs = dot(grad, v_ref[:reach, :], NT)
        delta = jnp.sum(dprobs * probs, axis=1, keepdims=True)
        dscores = (probs * (dprobs - delta)).astype(bf16)
        dq_acc[rows, :] = dot(dscores, k_ref[:reach, :]) * scale
        dk = dot(dscores, query, TN) * scale
        dv = dot(probs.astype(bf16), grad, TN)
        if i == count - 1:
            dk_acc[...] = dk
            dv_acc[...] = dv
        else:
            dk_acc[:reach, :] += dk
            dv_acc[:reach, :] += dv
    dv_out[...] = dv_acc[...].astype(bf16)
    cos, sin = cosine[...], sine[...]
    dgains = []
    for acc, raw_ref, gain_ref, out in ((dq_acc, q_raw, q_gain, dq_out), (dk_acc, k_raw, k_gain, dk_out)):
        grad = acc[...]
        grad = grad * cos - pltpu.roll(grad, hd // 2, 1) * sin
        raw = raw_ref[...]
        factor = lax.rsqrt(jnp.mean(raw * raw, axis=1, keepdims=True) + EPS)
        normal = raw * factor
        dgains.append(jnp.sum(grad * normal, axis=0, keepdims=True))
        scaled = grad * gain_ref[0]
        mean = jnp.mean(scaled * normal, axis=1, keepdims=True)
        out[...] = (factor * (scaled - normal * mean)).astype(bf16)
    dgain_out[0] = jnp.concatenate(dgains, axis=0)


def attend_back(scalars, q_rot, k_rot, value, grad, totals, q_raw, k_raw, q_gain, k_gain, cosine, sine):
    tokens, local = q_rot.shape
    heads, hd = q_gain.shape
    column = pl.BlockSpec((tokens, hd), lambda h, s: (0, h))
    gain_spec = pl.BlockSpec((1, 1, hd), lambda h, s: (h, 0, 0))
    table = pl.BlockSpec((tokens, hd), lambda h, s: (0, 0))
    return call(
        functools.partial(attend_back_kernel, min(256, tokens)),
        (heads,),
        scalars,
        [q_rot, k_rot, value, grad, totals, q_raw, k_raw, q_gain[:, None, :], k_gain[:, None, :], cosine, sine],
        [column] * 4
        + [pl.BlockSpec((1, tokens, 1), lambda h, s: (h, 0, 0))]
        + [column] * 2
        + [gain_spec] * 2
        + [table] * 2,
        [struct((tokens, local), bf16)] * 3 + [struct((heads, 2, hd), f32)],
        [column] * 3 + [pl.BlockSpec((1, 2, hd), lambda h, s: (h, 0, 0))],
        [pltpu.VMEM((tokens, hd), f32)] * 3,
        flops=10 * tokens * tokens * local,
        moved=16 << 20,
    )


def whole_grad_kernel(n_tp, dp_count, scalars, *refs):
    pieces = refs[:n_tp]
    whole_out, turned_out = refs[n_tp:]
    width = pieces[0].shape[1]
    for r in range(n_tp):
        cols = pl.ds(pl.multiple_of(scalars[r] * width, width), width)
        whole_out[:, cols] = pieces[r][...]
    transpose_blocks(scalars, n_tp, whole_out, turned_out, dp_count)


def whole_grad(scalars, pieces, dp_count):
    n_tp = len(pieces)
    tokens, width = pieces[0].shape
    features = width * n_tp
    return call(
        functools.partial(whole_grad_kernel, n_tp, dp_count),
        (tokens // TB,),
        scalars,
        pieces,
        [pl.BlockSpec((TB, width), lambda i, s: (i, 0))] * n_tp,
        [struct((tokens, features), bf16), struct((features, tokens), bf16)],
        [
            pl.BlockSpec((TB, features), lambda i, s: (i, 0)),
            pl.BlockSpec((features, TB), lambda i, s: (0, i)),
        ],
        moved=12 << 20,
    )


def stream_kernel(n_tp, dp_count, scalars, *refs):
    pieces = refs[:n_tp]
    x_ref, w_ref, gain, router, kept = refs[n_tp : n_tp + 5]
    stream_out, normed_out, turned_out, factor_out, probs_out, gates_out = refs[n_tp + 5 :]
    width = pieces[0].shape[1]
    total = x_ref[...].astype(f32)
    for r in range(n_tp):
        weight = w_ref[:, pl.ds(scalars[r], 1)]
        total += dot(pieces[r][...], weight.reshape(width, weight.shape[-1]))
    stream_out[...] = total
    factor = lax.rsqrt(jnp.mean(total * total, axis=1, keepdims=True) + EPS)
    factor_out[...] = factor
    normed = (total * factor * gain[...]).astype(bf16)
    normed_out[...] = normed
    logits = dot(normed, router[...])
    power = jnp.exp(logits - jnp.max(logits, axis=1, keepdims=True))
    probs = power / jnp.sum(power, axis=1, keepdims=True)
    probs_out[...] = probs
    gates_out[...] = probs * kept[...]
    transpose_blocks(scalars, n_tp, normed_out, turned_out, dp_count)


def stream_of(scalars, pieces, x, w_all, gain, router, kept, dp_count):
    n_tp = len(pieces)
    tokens, features = x.shape
    experts = router.shape[1]
    rows = lambda w: pl.BlockSpec((TB, w), lambda i, s: (i, 0))
    return call(
        functools.partial(stream_kernel, n_tp, dp_count),
        (tokens // TB,),
        scalars,
        [*pieces, x, w_all, gain, router, kept],
        [rows(pieces[0].shape[1])] * n_tp + [rows(features)] + [whole_spec()] * 3 + [rows(experts)],
        [
            struct((tokens, features), f32),
            struct((tokens, features), bf16),
            struct((features, tokens), bf16),
            struct((tokens, 1), f32),
            struct((tokens, experts), f32),
            struct((tokens, experts), f32),
        ],
        [
            rows(features),
            rows(features),
            pl.BlockSpec((features, TB), lambda i, s: (0, i)),
            rows(1),
            rows(experts),
            rows(experts),
        ],
        flops=2 * tokens * features * features,
        moved=32 << 20,
    )


def expert_kernel(first, scalars, n_ref, g_ref, gates_ref, wg, wu, wd, hidden_out, pair_out, dgate_out):
    step = pl.program_id(0)
    expert = first + step
    width = wg.shape[-1]

    @pl.when(step == 0)
    def _():
        dgate_out[...] = jnp.zeros_like(dgate_out)

    gate_val, up_val = dot(n_ref[...], wg[0]), dot(n_ref[...], wu[0])
    back = dot(g_ref[...], wd[0], NT)
    gates = gates_ref[...]
    here = lax.broadcasted_iota(jnp.int32, gates.shape, 1) == expert
    gate = jnp.sum(jnp.where(here, gates, 0.0), axis=1, keepdims=True)
    sigmoid = 1.0 / (1.0 + jnp.exp(-gate_val))
    swish = gate_val * sigmoid
    hidden = (swish * up_val).astype(bf16).astype(f32)
    hidden_out[0] = (hidden * gate).astype(bf16)
    dgate = jnp.sum(back * hidden, axis=1, keepdims=True)
    dgate_out[...] = jnp.where(here, dgate, dgate_out[...])
    dhidden = back * gate
    pair_out[0, :, :width] = (dhidden * up_val * sigmoid * (1.0 + gate_val * (1.0 - sigmoid))).astype(bf16)
    pair_out[0, :, width:] = (dhidden * swish).astype(bf16)


def run_experts(scalars, normed, grad, gates, wg, wu, wd, first, count):
    tokens, features = normed.shape
    experts, _, width = wg.shape
    weight = lambda shape: pl.BlockSpec((1, *shape), lambda i, s: (first + i, 0, 0))
    given = lambda shape: pl.BlockSpec((1, *shape), lambda i, s: (i, 0, 0))
    return call(
        functools.partial(expert_kernel, first),
        (count,),
        scalars,
        [normed, grad, gates, wg, wu, wd],
        [whole_spec()] * 3 + [weight((features, width))] * 2 + [weight((width, features))],
        [
            struct((count, tokens, width), bf16),
            struct((count, tokens, 2 * width), bf16),
            struct((tokens, experts), f32),
        ],
        [
            given((tokens, width)),
            given((tokens, 2 * width)),
            pl.BlockSpec((tokens, experts), lambda i, s: (0, 0)),
        ],
        flops=6 * count * tokens * features * width,
        moved=count * 5 << 20,
    )


def weight_grads_kernel(scalars, turned, g_turned, hidden, pair, keep_out, send_out):
    half, _, rows, _ = keep_out.shape
    width = hidden.shape[-1]
    first = dot(turned[...], pair[0]).astype(bf16).reshape(2 * half, rows, 2 * width)
    keep_out[:, 0, :, : 2 * width] = first[:half]
    send_out[:, 0, :, : 2 * width] = first[half:]
    second = dot(g_turned[...], hidden[0]).astype(bf16).reshape(2 * half, rows, width)
    keep_out[:, 0, :, 2 * width :] = second[:half]
    send_out[:, 0, :, 2 * width :] = second[half:]


def weight_grads(scalars, turned, g_turned, hidden, pair, offset, count, dp_count):
    features, tokens = turned.shape
    width = hidden.shape[-1]
    half, rows = dp_count // 2, features // dp_count
    out = struct((half, count, rows, 3 * width), bf16)
    out_spec = pl.BlockSpec((half, 1, rows, 3 * width), lambda i, s: (0, i, 0, 0))
    return call(
        weight_grads_kernel,
        (count,),
        scalars,
        [turned, g_turned, hidden, pair],
        [
            whole_spec(),
            whole_spec(),
            pl.BlockSpec((1, tokens, width), lambda i, s: (offset + i, 0, 0)),
            pl.BlockSpec((1, tokens, 2 * width), lambda i, s: (offset + i, 0, 0)),
        ],
        [out, out],
        [out_spec, out_spec],
        flops=6 * count * tokens * features * width,
        moved=count * 5 << 20,
    )


def chunk_specs(chunks, shape):
    specs, first = [], 0
    for chunk in chunks:
        count = chunk.shape[0]
        specs.append(
            pl.BlockSpec(
                (1, *shape), lambda i, s, first=first, count=count: (jnp.clip(i - first, 0, count - 1), 0, 0)
            )
        )
        first += count
    return specs


def input_grad_kernel(sizes, n_tp, scalars, *refs):
    pairs, (wg, wu) = refs[: len(sizes)], refs[len(sizes) : len(sizes) + 2]
    outs, acc = refs[len(sizes) + 2 : -1], refs[-1]
    step = pl.program_id(0)
    width = wg.shape[-1]
    first = 0
    for pair, size in zip(pairs, sizes):

        @pl.when((step >= first) & (step < first + size))
        def _(pair=pair, first=first):
            part = dot(pair[0, :, :width], wg[0], NT) + dot(pair[0, :, width:], wu[0], NT)
            if first == 0:

                @pl.when(step == 0)
                def _():
                    acc[...] = part

                @pl.when(step > 0)
                def _():
                    acc[...] += part

            else:
                acc[...] += part

        first += size

    @pl.when(step == pl.num_programs(0) - 1)
    def _():
        rows = acc.shape[0] // n_tp
        for r in range(n_tp):
            outs[r][...] = acc[pl.ds(pl.multiple_of(scalars[r] * rows, rows), rows), :].astype(bf16)


def input_grads(scalars, pairs, wg, wu, n_tp):
    experts, features, width = wg.shape
    tokens = pairs[0].shape[1]
    rows = tokens // n_tp
    weight = pl.BlockSpec((1, features, width), lambda i, s: (i, 0, 0))
    return call(
        functools.partial(input_grad_kernel, [pair.shape[0] for pair in pairs], n_tp),
        (experts,),
        scalars,
        [*pairs, wg, wu],
        chunk_specs(pairs, (tokens, 2 * width)) + [weight] * 2,
        [struct((rows, features), bf16)] * n_tp,
        [pl.BlockSpec((rows, features), lambda i, s: (0, 0))] * n_tp,
        [pltpu.VMEM((tokens, features), f32)],
        flops=4 * experts * tokens * features * width,
        moved=experts * 3 << 20,
    )


def result_kernel(sizes, n_tp, scalars, *refs):
    hiddens, wd = refs[: len(sizes)], refs[len(sizes)]
    outs, acc = refs[len(sizes) + 1 : -1], refs[-1]
    step = pl.program_id(0)
    first = 0
    for hidden, size in zip(hiddens, sizes):

        @pl.when((step >= first) & (step < first + size))
        def _(hidden=hidden, first=first):
            part = dot(hidden[0], wd[0])
            if first == 0:

                @pl.when(step == 0)
                def _():
                    acc[...] = part

                @pl.when(step > 0)
                def _():
                    acc[...] += part

            else:
                acc[...] += part

        first += size

    @pl.when(step == pl.num_programs(0) - 1)
    def _():
        cols = acc.shape[1] // n_tp
        for r in range(n_tp):
            outs[r][...] = acc[:, pl.ds(pl.multiple_of(scalars[r] * cols, cols), cols)].astype(bf16)


def results(scalars, hiddens, wd, n_tp):
    experts, width, features = wd.shape
    tokens = hiddens[0].shape[1]
    cols = features // n_tp
    return call(
        functools.partial(result_kernel, [hidden.shape[0] for hidden in hiddens], n_tp),
        (experts,),
        scalars,
        [*hiddens, wd],
        chunk_specs(hiddens, (tokens, width)) + [pl.BlockSpec((1, width, features), lambda i, s: (i, 0, 0))],
        [struct((tokens, cols), bf16)] * n_tp,
        [pl.BlockSpec((tokens, cols), lambda i, s: (0, 0))] * n_tp,
        [pltpu.VMEM((tokens, features), f32)],
        flops=2 * experts * tokens * features * width,
        moved=experts * 2 << 20,
    )


def rows_kernel(n_tp, scalars, *refs):
    parts, dgates = refs[:n_tp], refs[n_tp : 2 * n_tp]
    probs, kept, stream, normed, factor, upstream, gain, router = refs[2 * n_tp : 2 * n_tp + 8]
    grad_out, dgain_out, drouter_out = refs[2 * n_tp + 8 :]
    total = sum(part[...].astype(f32) for part in parts)
    dprobs = sum(part[...] for part in dgates) * kept[...]
    soft = probs[...]
    dlogits = soft * (dprobs - jnp.sum(dprobs * soft, axis=1, keepdims=True))
    dlogits = dlogits.astype(bf16)
    drouter_out[...] = dot(normed[...], dlogits, TN)
    total += dot(dlogits, router[...], NT)
    scale = factor[...]
    normal = stream[...] * scale
    dgain_out[...] = jnp.sum(total * normal, axis=0, keepdims=True)
    scaled = total * gain[...]
    mean = jnp.mean(scaled * normal, axis=1, keepdims=True)
    grad_out[...] = (upstream[...].astype(f32) + scale * (scaled - normal * mean)).astype(bf16)


def stream_grad_rows(scalars, parts, dgates, probs, kept, stream, normed, factor, upstream, gain, router):
    n_tp = len(parts)
    rows, features = parts[0].shape
    experts = router.shape[1]
    mine = lambda w: pl.BlockSpec((rows, w), lambda i, s: (s[0], 0))
    plain = lambda h, w: pl.BlockSpec((h, w), lambda i, s: (0, 0))
    return call(
        functools.partial(rows_kernel, n_tp),
        (1,),
        scalars,
        [*parts, *dgates, probs, kept, stream, normed, factor, upstream, gain, router],
        [plain(rows, features)] * n_tp
        + [plain(rows, experts)] * n_tp
        + [mine(experts), mine(experts), mine(features), mine(features), mine(1), mine(features)]
        + [plain(1, features), plain(features, experts)],
        [struct((rows, features), bf16), struct((1, features), f32), struct((features, experts), f32)],
        [plain(rows, features), plain(1, features), plain(features, experts)],
        flops=1 << 24,
        moved=10 << 20,
    )


def attended_grad_kernel(n_tp, scalars, *refs):
    pieces, w_ref = refs[:n_tp], refs[n_tp]
    whole_out, grad_out = refs[n_tp + 1 :]
    rows = pieces[0].shape[0]
    for r in range(n_tp):
        place = pl.ds(pl.multiple_of(scalars[r] * rows, rows), rows)
        whole_out[place, :] = pieces[r][...]
    grad_out[...] = dot(whole_out[...], w_ref[...], NT).astype(bf16)


def attended_grad(scalars, pieces, w_output):
    n_tp = len(pieces)
    rows, features = pieces[0].shape
    local = w_output.shape[0]
    tokens = rows * n_tp
    plain = lambda h, w: pl.BlockSpec((h, w), lambda i, s: (0, 0))
    return call(
        functools.partial(attended_grad_kernel, n_tp),
        (1,),
        scalars,
        [*pieces, w_output],
        [plain(rows, features)] * n_tp + [plain(local, features)],
        [struct((tokens, features), bf16), struct((tokens, local), bf16)],
        [plain(tokens, features), plain(tokens, local)],
        flops=2 * tokens * features * local,
        moved=11 << 20,
    )


def normed_grad_kernel(scalars, dq, dk, dv, wq, wk, wv, x_ref, factor, gain, out, dot_out, dgain_out):
    total = dot(dq[...], wq[...], NT) + dot(dk[...], wk[...], NT) + dot(dv[...], wv[...], NT)
    out[...] = total.astype(bf16)
    normal = x_ref[...].astype(f32) * factor[...]
    product = total * normal
    dgain_out[...] = jnp.sum(product, axis=0, keepdims=True)
    dot_out[...] = jnp.sum(product * gain[...], axis=1, keepdims=True)


def normed_grad(scalars, r, dq, dk, dv, wq, wk, wv, x, factor, gain, n_tp):
    tokens, local = dq.shape
    features = wq.shape[0]
    width = features // n_tp
    plain = lambda h, w: pl.BlockSpec((h, w), lambda i, s: (0, 0))
    weight = pl.BlockSpec((width, local), lambda i, s: (s[r], 0))
    return call(
        normed_grad_kernel,
        (1,),
        scalars,
        [dq, dk, dv, wq, wk, wv, x, factor, gain],
        [plain(tokens, local)] * 3
        + [weight] * 3
        + [
            pl.BlockSpec((tokens, width), lambda i, s: (0, s[r])),
            plain(tokens, 1),
            pl.BlockSpec((1, width), lambda i, s: (0, s[r])),
        ],
        [struct((tokens, width), bf16), struct((tokens, 1), f32), struct((1, width), f32)],
        [plain(tokens, width), plain(tokens, 1), plain(1, width)],
        flops=6 * tokens * local * width,
        moved=7 << 20,
    )


def kept_pairs(expert_ids, experts, capacity):
    tokens = expert_ids.shape[0]
    named = jnp.any(expert_ids[:, :, None] == jnp.arange(experts, dtype=jnp.int32), axis=1)
    earlier = jnp.arange(tokens)[:, None] > jnp.arange(tokens)[None, :]
    rank = dot(earlier.astype(bf16), named.astype(bf16))
    return (named & (rank < capacity)).astype(f32)


def body(n_dp, n_tp, cosine, sine, tokens, cotangent, attn_gain, w_query, w_key, w_value, query_gain, key_gain,
         w_output, ffn_gain, w_router, w_gate, w_up, w_down, expert_ids):
    tp, dp = lax.axis_index("tensor"), lax.axis_index("dp")
    scalars = jnp.stack(
        [tp ^ r for r in range(n_tp)] + [dp ^ bit_reverse(place, n_dp) for place in range(n_dp)]
    ).astype(jnp.int32)
    token_count, width = tokens.shape
    features = width * n_tp
    heads, hd = query_gain.shape
    local = heads * hd
    experts = w_router.shape[1]
    capacity = token_count * expert_ids.shape[1] // experts
    gain1, gain2 = attn_gain[None, :], ffn_gain[None, :]

    share = local // n_dp
    w_share = lax.dynamic_slice_in_dim(w_output, dp * share, share, 0)
    w_all = lax.all_gather(lax.all_gather(w_share, "tensor"), "dp")

    x_pieces = gather_pieces(tokens, "tensor", n_tp)
    x, normed1, factor1, q_raw, k_raw, q_rot, k_rot, value = project(
        scalars, x_pieces, gain1, w_query, w_key, w_value, query_gain, key_gain, cosine, sine
    )
    g_pieces = gather_pieces(after(cotangent, x_pieces[-1]), "tensor", n_tp)
    upstream, g_turned = whole_grad(scalars, g_pieces, n_dp)
    kept = kept_pairs(expert_ids, experts, capacity)
    attended, totals = attend(scalars, q_rot, k_rot, value, heads)
    stream, normed2, turned, factor2, probs, gates = stream_of(
        scalars, gather_pieces(attended, "tensor", n_tp), x, w_all, gain2, w_router, kept, n_dp
    )

    blocks = [(0, 2), (2, 4), (6, experts - 6)]
    hiddens, pairs, dgates, sums = [], [], [], []
    start = normed2
    for index, (first, count) in enumerate(blocks):
        hidden, pair, dgate = run_experts(scalars, start, upstream, gates, w_gate, w_up, w_down, first, count)
        hiddens.append(hidden)
        pairs.append(pair)
        dgates.append(dgate)
        if index < len(blocks) - 1:
            keep, send = weight_grads(scalars, turned, g_turned, hidden, pair, 0, count, n_dp)
            sums.append((first, count, keep, send))
            start = after(normed2, keep)
    dgate = sum(dgates)
    input_parts = input_grads(scalars, pairs, w_gate, w_up, n_tp)
    rows = token_count // n_tp
    dgate_rows = [lax.dynamic_slice_in_dim(dgate, (tp ^ r) * rows, rows, 0) for r in range(n_tp)]
    dgate_parts = scatter_pieces(dgate_rows, "tensor", n_tp)
    arrived = scatter_pieces(input_parts, "tensor", n_tp)

    first, count = blocks[-1]
    ready = input_parts[0]
    for offset in range(0, count, 4):
        size = min(4, count - offset)
        keep, send = weight_grads(
            scalars, after(turned, ready), g_turned, hiddens[-1], pairs[-1], offset, size, n_dp
        )
        ready = keep
        sums.append((first + offset, size, keep, send))
        if offset == 0:
            result_parts = results(scalars, hiddens, after(w_down, ready), n_tp)
            ready = result_parts[0]
    reduced = [halve(keep, send, n_dp) for _, _, keep, send in sums]

    dattn_rows, dgain2, drouter = stream_grad_rows(
        scalars, arrived, dgate_parts, probs, kept, stream, normed2, factor2, upstream, gain2, w_router
    )
    dattn, dattended = attended_grad(scalars, gather_pieces(dattn_rows, "tensor", n_tp), w_output)
    dq, dk, dv, dhead_gains = attend_back(
        scalars, q_rot, k_rot, value, dattended, totals, q_raw, k_raw, query_gain, key_gain, cosine, sine
    )
    slices, row_dots, dgain1 = [None] * n_tp, [None] * n_tp, [None] * n_tp
    for r in reversed(range(n_tp)):
        slices[r], row_dots[r], dgain1[r] = normed_grad(
            scalars, r, dq, dk, dv, w_query, w_key, w_value, x, factor1, gain1, n_tp
        )
    row_dot = butterfly(sum(row_dots).reshape(8, token_count // 8), [("tensor", n_tp)])
    arrived1 = scatter_pieces(slices, "tensor", n_tp)
    dnormed1 = sum(part.astype(f32) for part in arrived1)
    my_cols = lambda array: lax.dynamic_slice_in_dim(array, tp * width, width, 1)
    normal1 = tokens.astype(f32) * factor1
    input_grad = my_cols(dattn).astype(f32) + factor1 * (
        dnormed1 * my_cols(gain1) - normal1 * (row_dot.reshape(token_count, 1) / features)
    )
    arrived_y = scatter_pieces(result_parts, "tensor", n_tp)
    output = my_cols(stream) + sum(part.astype(f32) for part in arrived_y)

    def spread(value, dimension):
        return lax.psum_scatter(value.astype(bf16), "dp", scatter_dimension=dimension, tiled=True).astype(f32)

    grad_output = spread(dot(attended, dattn, TN), 1)
    dqkv = jnp.concatenate([dq, dk, dv], axis=1)
    grad_qkv = spread(dot(normed1, dqkv, TN), 0)

    everywhere = [("dp", n_dp), ("tensor", n_tp)]
    early = butterfly(jnp.concatenate([drouter.T, dgain2], axis=0), everywhere)
    gain_row = jnp.zeros((1, features), f32)
    for r in range(n_tp):
        gain_row = lax.dynamic_update_slice(gain_row, dgain1[r], (0, (tp ^ r) * width))
    gain_row = butterfly(gain_row, everywhere)
    head_gains = butterfly(dhead_gains, [("dp", n_dp)])
    mine = lambda array, dimension: lax.dynamic_slice_in_dim(
        array, dp * (array.shape[dimension] // n_dp), array.shape[dimension] // n_dp, dimension
    )
    early = mine(early, 1)
    head_gains = mine(head_gains, 2)

    expert_width = w_gate.shape[-1]
    stacked = jnp.concatenate(reduced, axis=0)
    grad_gate = stacked[:, :, :expert_width].astype(f32)
    grad_up = stacked[:, :, expert_width : 2 * expert_width].astype(f32)
    grad_down = jnp.swapaxes(stacked[:, :, 2 * expert_width :], 1, 2).astype(f32)
    return (
        output.astype(bf16),
        input_grad.astype(bf16),
        mine(gain_row, 1)[0],
        grad_qkv[:, :local],
        grad_qkv[:, local : 2 * local],
        grad_qkv[:, 2 * local :],
        head_gains[:, 0],
        head_gains[:, 1],
        grad_output,
        early[experts],
        early[:experts].T,
        grad_gate,
        grad_up,
        grad_down,
    )


def solution(mesh):
    placed = (
        P("dp", "tensor"),
        P("dp", "tensor"),
        P(),
        P(None, "tensor"),
        P(None, "tensor"),
        P(None, "tensor"),
        P("tensor", None),
        P("tensor", None),
        P("tensor", None),
        P(),
        P(),
        P(None, None, "tensor"),
        P(None, None, "tensor"),
        P(None, "tensor", None),
        P("dp", None),
    )
    n_dp, n_tp = mesh.shape["dp"], mesh.shape["tensor"]

    def layer(*args):
        cosine, sine = rope_constants(LEN, args[6].shape[1])
        return body(n_dp, n_tp, jnp.asarray(cosine), jnp.asarray(sine), *args)

    return jax.shard_map(
        layer,
        mesh=mesh,
        in_specs=placed,
        out_specs=(
            P("dp", "tensor"),
            P("dp", "tensor"),
            P("dp"),
            P("dp", "tensor"),
            P("dp", "tensor"),
            P("dp", "tensor"),
            P("tensor", "dp"),
            P("tensor", "dp"),
            P("tensor", "dp"),
            P("dp"),
            P("dp", None),
            P(None, "dp", "tensor"),
            P(None, "dp", "tensor"),
            P(None, "tensor", "dp"),
        ),
        check_vma=False,
    )
```

time: 2630 us -> 1230 us (0.47)
  local copies, waits for them, and re-layouts: 847 us -> 42.4 us
  matrix products: 612 us -> 18.3 us
  Pallas kernels: 0 us -> 359 us
  waiting for transfers between devices: 837 us -> 635 us
  other arithmetic: 236 us -> 82.4 us
  starting transfers between devices: 0.82 us -> 64.2 us
  blocking collectives: 44.3 us -> 0 us
    gather x19 -> x0, local copies, waits for them, and re-layouts: 615 us -> none  [the longest x16 441 us: combine_pairs(): picked = jnp.take(padded, pair_slots[:, choice_index], axis=0)]
    reduce_scatter x9 -> x2, waiting for transfers between devices: 609 us -> 0.01 us  [spread(): lax.psum_scatter(value.astype(bf16), 'dp', scatter_dimension=dimension, t...]
    ppermute x0 -> x58, waiting for transfers between devices: none -> 604 us  [swap(): return lax.ppermute(value, axis, [(i, i ^ mask) for i in range(count)])]
    dot_general x173 -> x3, matrix products: 612 us -> 18.3 us  [dot(): return lax.dot_general(left, right, dims, preferred_element_type=f32)]
    pallas_call x0 -> x21, Pallas kernels: none -> 359 us  [call(): pl.pallas_call(body, out_shape=outs, grid_spec=pltpu.PrefetchScalarGridSp...]
    psum x3 -> x0, waiting for transfers between devices: 165 us -> none  [the longest x1 105 us: body(): lax.psum(normed1_part.astype(jnp.bfloat16), 'tensor').astype(jnp.float32)]
    concatenate x2 -> x1, local copies, waits for them, and re-layouts: 89.1 us -> 0.03 us  [gather_pieces(): return [value, one, two, jnp.concatenate([top, bottom], axis=0)]]
    reduce_sum x33 -> x0, other arithmetic: 73.5 us -> none  [the longest x16 33.2 us: expert_forward(): slot_dgate = jnp.sum(cot_rows.astype(jnp.float32) * result, axis=1)]
  transfers between devices with their start and end apart: 16 -> 62, of which waited for: 11 -> 29; matrix products, arithmetic and copies ran while one was open for 24% -> 11% of each run, Pallas kernels for 0% -> 14%
where the time goes in v1:
time: 1230 us; the launch traced here: 1220 us
  waiting for transfers between devices  635 us (52%)
  Pallas kernels  359 us (29%)
  other arithmetic  82.4 us (7%)
  starting transfers between devices  64.2 us (5%)
  local copies, waits for them, and re-layouts  42.4 us (3%)
  matrix products  18.3 us (1%)
  between operations  14.7 us (1%)
    ppermute x58, waiting for transfers between devices, swap(): return lax.ppermute(value, axis, [(i, i ^ mask) for i in range(count)])  604 us
    pallas_call x21, Pallas kernels, call(): pl.pallas_call(body, out_shape=outs, grid_spec=pltpu.PrefetchScalarGridSp...  359 us
    ppermute x58, starting transfers between devices, swap(): return lax.ppermute(value, axis, [(i, i ^ mask) for i in range(count)])  64 us
    convert_element_type x10, other arithmetic, add_low(): return (left.astype(f32) + right.astype(f32)).astype(bf16)  42.7 us
    all_gather x2, waiting for transfers between devices, body(): w_all = lax.all_gather(lax.all_gather(w_share, 'tensor'), 'dp')  30.7 us
  transfers between devices with their start and end apart: 62, of which 29 were waited for; matrix products, arithmetic and copies ran while one was open for 11% of the time, Pallas kernels for 14%

profile of v1, /device:TPU:0, one launch (start us, length us, event | category | flops | bytes accessed | tf_op | source)
XLA Modules:
  0.0 1216.0 jit_solution(10338277636341577333)
XLA Ops:
  9.1 30.7 %all-gather.5.cloned.1.call-done = bf16[256,2048]{1,0:T(8,128)(2,1)} async-done(((bf16[64,2048]{1,0:T(8,128)(2,1)}), bf16[256,2048]{1,0:T(8,128)(2,1)}) %all-gather.5.cloned.1.call-update) | async-done | bytes 1048592 | tf_op jit(solution)/shard_map/all_gather | solution.py:695
  42.0 23.1 %collective-permute-done.1.refs_2_ = bf16[1024,512]{1,0:T(8,128)(2,1)S(1)} collective-permute-done((bf16[1024,512]{1,0:T(8,128)(2,1)}, bf16[1024,512]{1,0:T(8,128)(2,1)S(1)}, u32[]{:S(2)}, u32[]{:S(2)}) %collective-permute-start.1) | collective-permute-done | bytes 1048608 | tf_op jit(solution)/shard_map/ppermute | solution.py:68
  69.1 8.9 collective-permute-done.2
  82.5 15.2 %shard_map.272 = (bf16[1024,2048]{1,0:T(8,128)(2,1)}, bf16[1024,2048]{1,0:T(8,128)(2,1)}, f32[1024,1]{1,0:T(8,128)}, f32[1024,512]{1,0:T(8,128)}, f32[1024,512]{...) custom-call(s32[12]{0:T(128)} %stack.51.scalars, ...), custom_call_target="tpu_custom_call" | custom-call | flops 6442450944 | bytes 25165824 | tf_op jit(solution)/shard_map/pallas_call | solution.py:48
  97.7 11.7 shard_map.273
  115.3 20.5 %collective-permute-done.5.refs_2_ = bf16[1024,512]{1,0:T(8,128)(2,1)S(1)} collective-permute-done((bf16[1024,512]{1,0:T(8,128)(2,1)}, bf16[1024,512]{1,0:T(8,128)(2,1)S(1)}, u32[]{:S(2)}, u32[]{:S(2)}) %collective-permute-start.5) | collective-permute-done | bytes 1048608 | tf_op jit(solution)/shard_map/ppermute | solution.py:68
  159.5 20.2 %shard_map.274 = (f32[1024,2048]{1,0:T(8,128)}, bf16[1024,2048]{1,0:T(8,128)(2,1)}, bf16[2048,1024]{1,0:T(8,128)(2,1)}, f32[1024,1]{1,0:T(8,128)}, f32[1024,16]{1,0:T(8,128)}, /*index=5*/f32[1024,16]{1,0:T(8,128)}) custom-call(s32[12]{0:T(128)} %stack.51.scalars, bf16[1024,512]{1,0:T(8,128)(2,1)} %get-tuple-element.90.refs_0_, bf16[1024,512]{1,0:T(8,128)(2,1)} %copy-done.32, ...), custom_call_target="tpu_custom_call" | custom-call | flops 8589934592 | bytes 33554432 | tf_op jit(solution)/shard_map/pallas_call | solution.py:48
  179.7 14.1 %shard_map.276 = (bf16[2,1024,256]{2,1,0:T(8,128)(2,1)}, bf16[2,1024,512]{2,1,0:T(8,128)(2,1)}, f32[1024,16]{1,0:T(8,128)}) custom-call(s32[12]{0:T(128)} %stack.51.scalars, bf16[1024,2048]{1,0:T(8,128)(2,1)} %get-tuple-element.106.n_ref.refs_11_, bf16[1024,2048]{1,0:T(8,128)(2,1)} %get-tuple-element.95.g_ref.refs_13_, ...), custom_call_target="tpu_custom_call" | custom-call | flops 6442450944 | bytes 10485760 | tf_op jit(solution)/shard_map/pallas_call | solution.py:48
  193.8 13.4 %shard_map.277 = (bf16[4,2,256,768]{3,2,1,0:T(8,128)(2,1)}, bf16[4,2,256,768]{3,2,1,0:T(8,128)(2,1)}) custom-call(s32[12]{0:T(128)} %stack.51.scalars, bf16[2048,1024]{1,0:T(8,128)(2,1)} %get-tuple-element.157.turned, bf16[2048,1024]{1,0:T(8,128)(2,1)} %get-tuple-element.99.g_turned, bf16[2,1024,256]{2,1,0:T(8,128)(2,1)} %get-tuple-element.97.hidden.refs_0_, ...), custom_call_target="tpu_custom_call" | custom-call | flops 6442450944 | bytes 10485760 | tf_op jit(solution)/shard_map/pallas_call | solution.py:48
  207.2 21.9 %shard_map.278 = (bf16[4,1024,256]{2,1,0:T(8,128)(2,1)}, bf16[4,1024,512]{2,1,0:T(8,128)(2,1)}, f32[1024,16]{1,0:T(8,128)}) custom-call(s32[12]{0:T(128)} %stack.51.scalars, bf16[1024,2048]{1,0:T(8,128)(2,1)} %get-tuple-element.106.n_ref.refs_11_, bf16[1024,2048]{1,0:T(8,128)(2,1)} %get-tuple-element.95.g_ref.refs_13_, ...), custom_call_target="tpu_custom_call" | custom-call | flops 12884901888 | bytes 20971520 | tf_op jit(solution)/shard_map/pallas_call | solution.py:48
  229.1 20.2 %shard_map.279 = (bf16[4,4,256,768]{3,2,1,0:T(8,128)(2,1)}, bf16[4,4,256,768]{3,2,1,0:T(8,128)(2,1)}) custom-call(s32[12]{0:T(128)} %stack.51.scalars, bf16[2048,1024]{1,0:T(8,128)(2,1)} %get-tuple-element.157.turned, bf16[2048,1024]{1,0:T(8,128)(2,1)} %get-tuple-element.99.g_turned, bf16[4,1024,256]{2,1,0:T(8,128)(2,1)} %get-tuple-element.103.hidden.refs_1_, ...), custom_call_target="tpu_custom_call" | custom-call | flops 12884901888 | bytes 20971520 | tf_op jit(solution)/shard_map/pallas_call | solution.py:48
  249.3 44.2 %shard_map.280 = (bf16[10,1024,256]{2,1,0:T(8,128)(2,1)}, bf16[10,1024,512]{2,1,0:T(8,128)(2,1)}, f32[1024,16]{1,0:T(8,128)}) custom-call(s32[12]{0:T(128)} %stack.51.scalars, bf16[1024,2048]{1,0:T(8,128)(2,1)} %get-tuple-element.106.n_ref.refs_11_, bf16[1024,2048]{1,0:T(8,128)(2,1)} %get-tuple-element.95.g_ref.refs_13_, ...), custom_call_target="tpu_custom_call" | custom-call | flops 32212254720 | bytes 52428800 | tf_op jit(solution)/shard_map/pallas_call | solution.py:48
  293.6 46.6 %shard_map.281 = (bf16[256,2048]{1,0:T(8,128)(2,1)}, bf16[256,2048]{1,0:T(8,128)(2,1)}, bf16[256,2048]{1,0:T(8,128)(2,1)}, bf16[256,2048]{1,0:T(8,128)(2,1)}) custom-call(s32[12]{0:T(128)} %stack.51.scalars, bf16[2,1024,512]{2,1,0:T(8,128)(2,1)} %get-tuple-element.100.pair.refs_0_, bf16[4,1024,512]{2,1,0:T(8,128)(2,1)} %get-tuple-element.104.pair.refs_1_, ...), custom_call_target="tpu_custom_call" | custom-call | flops 34359738368 | bytes 50331648 | tf_op jit(solution)/shard_map/pallas_call | solution.py:48
  348.2 39.0 %collective-permute-done.20.refs_7_ = f32[256,16]{1,0:T(8,128)S(1)} collective-permute-done((f32[256,16]{1,0:T(8,128)S(1)}, f32[256,16]{1,0:T(8,128)S(1)}, u32[]{:S(2)}, u32[]{:S(2)}) %collective-permute-start.20) | collective-permute-done | bytes 16416 | tf_op jit(solution)/shard_map/ppermute | solution.py:68
  403.2 20.3 %collective-permute-done.22.refs_2_ = bf16[256,2048]{1,0:T(8,128)(2,1)S(1)} collective-permute-done((bf16[256,2048]{1,0:T(8,128)(2,1)}, bf16[256,2048]{1,0:T(8,128)(2,1)S(1)}, u32[]{:S(2)}, u32[]{:S(2)}) %collective-permute-start.22) | collective-permute-done | bytes 1048608 | tf_op jit(solution)/shard_map/ppermute | solution.py:68
  426.5 20.2 %shard_map.282 = (bf16[4,4,256,768]{3,2,1,0:T(8,128)(2,1)}, bf16[4,4,256,768]{3,2,1,0:T(8,128)(2,1)}) custom-call(s32[12]{0:T(128)} %stack.51.scalars, bf16[2048,1024]{1,0:T(8,128)(2,1)} %get-tuple-element.157.turned, bf16[2048,1024]{1,0:T(8,128)(2,1)} %get-tuple-element.99.g_turned, bf16[10,1024,256]{2,1,0:T(8,128)(2,1)} %get-tuple-element.107.hidden.refs_2_, ...), custom_call_target="tpu_custom_call" | custom-call | flops 12884901888 | bytes 20971520 | tf_op jit(solution)/shard_map/pallas_call | solution.py:48
  461.1 27.7 %shard_map.283 = (bf16[1024,512]{1,0:T(8,128)(2,1)}, bf16[1024,512]{1,0:T(8,128)(2,1)}, bf16[1024,512]{1,0:T(8,128)(2,1)}, bf16[1024,512]{1,0:T(8,128)(2,1)}) custom-call(s32[12]{0:T(128)} %stack.51.scalars, bf16[2,1024,256]{2,1,0:T(8,128)(2,1)} %get-tuple-element.97.hidden.refs_0_, bf16[4,1024,256]{2,1,0:T(8,128)(2,1)} %get-tuple-element.103.hidden.refs_1_, ...), custom_call_target="tpu_custom_call" | custom-call | flops 17179869184 | bytes 33554432 | tf_op jit(solution)/shard_map/pallas_call | solution.py:48
  488.8 20.4 %shard_map.291 = (bf16[4,4,256,768]{3,2,1,0:T(8,128)(2,1)}, bf16[4,4,256,768]{3,2,1,0:T(8,128)(2,1)}) custom-call(s32[12]{0:T(128)} %stack.51.scalars, bf16[2048,1024]{1,0:T(8,128)(2,1)} %get-tuple-element.157.turned, bf16[2048,1024]{1,0:T(8,128)(2,1)} %get-tuple-element.99.g_turned, bf16[10,1024,256]{2,1,0:T(8,128)(2,1)} %get-tuple-element.107.hidden.refs_2_, ...), custom_call_target="tpu_custom_call" | custom-call | flops 12884901888 | bytes 20971520 | tf_op jit(solution)/shard_map/pallas_call | solution.py:48
  509.7 22.2 %shard_map.286 = (bf16[1024,512]{1,0:T(8,128)(2,1)}, bf16[1024,512]{1,0:T(8,128)(2,1)}, bf16[1024,512]{1,0:T(8,128)(2,1)}, f32[4,2,128]{2,1,0:T(2,128)}) custom-call(s32[12]{0:T(128)} %stack.51.scalars, bf16[1024,512]{1,0:T(8,128)(2,1)} %get-tuple-element.87.q_ref.refs_0_, bf16[1024,512]{1,0:T(8,128)(2,1)} %get-tuple-element.88.k_ref.refs_1_, ...), custom_call_target="tpu_custom_call" | custom-call | flops 5368709120 | bytes 16777216 | tf_op jit(solution)/shard_map/pallas_call | solution.py:48
  531.9 10.9 convolution_convert_fusion
  557.9 16.5 %collective-permute-done.40 = f32[17,2048]{1,0:T(8,128)S(1)} collective-permute-done((f32[17,2048]{1,0:T(8,128)S(1)}, f32[17,2048]{1,0:T(8,128)S(1)}, u32[]{:S(2)}, u32[]{:S(2)}) %collective-permute-start.40) | collective-permute-done | bytes 139296 | tf_op jit(solution)/shard_map/ppermute | solution.py:68
  631.9 13.4 %shard_map.292 = (bf16[4,2,256,768]{3,2,1,0:T(8,128)(2,1)}, bf16[4,2,256,768]{3,2,1,0:T(8,128)(2,1)}) custom-call(s32[12]{0:T(128)} %stack.51.scalars, bf16[2048,1024]{1,0:T(8,128)(2,1)} %get-tuple-element.157.turned, bf16[2048,1024]{1,0:T(8,128)(2,1)} %get-tuple-element.99.g_turned, bf16[10,1024,256]{2,1,0:T(8,128)(2,1)} %get-tuple-element.107.hidden.refs_2_, ...), custom_call_target="tpu_custom_call" | custom-call | flops 6442450944 | bytes 10485760 | tf_op jit(solution)/shard_map/pallas_call | solution.py:48
  654.9 9.1 add_convert_fusion.1
  674.3 9.2 add_convert_fusion
  704.8 205.9 %collective-permute-done.44 = bf16[2,2,256,768]{3,2,1,0:T(8,128)(2,1)S(1)} collective-permute-done((bf16[2,2,256,768]{3,2,1,0:T(8,128)(2,1)S(1)}, bf16[2,2,256,768]{3,2,1,0:T(8,128)(2,1)S(1)}, u32[]{:S(2)}, u32[]{:S(2)}) %collective-permute-start.44) | collective-permute-done | bytes 1572896 | tf_op jit(solution)/shard_map/ppermute | solution.py:68
  926.1 8.9 collective-permute-done.26
  948.2 27.6 %collective-permute-done.56 = bf16[2,2,256,768]{3,2,1,0:T(8,128)(2,1)} collective-permute-done((bf16[2,2,256,768]{3,2,1,0:T(8,128)(2,1)S(1)}, bf16[2,2,256,768]{3,2,1,0:T(8,128)(2,1)}, u32[]{:S(2)}, u32[]{:S(2)}) %collective-permute-start.56) | collective-permute-done | bytes 1572896 | tf_op jit(solution)/shard_map/ppermute | solution.py:68
  982.3 127.7 %collective-permute-done.45 = bf16[1,2,256,768]{3,2,1,0:T(8,128)(2,1)S(1)} collective-permute-done((bf16[1,2,256,768]{3,2,1,0:T(8,128)(2,1)S(1)}, bf16[1,2,256,768]{3,2,1,0:T(8,128)(2,1)S(1)}, u32[]{:S(2)}, u32[]{:S(2)}) %collective-permute-start.45) | collective-permute-done | bytes 786464 | tf_op jit(solution)/shard_map/ppermute | solution.py:68
  1116.0 27.9 %collective-permute-done.51 = bf16[1,4,256,768]{3,2,1,0:T(8,128)(2,1)} collective-permute-done((bf16[1,4,256,768]{3,2,1,0:T(8,128)(2,1)}, bf16[1,4,256,768]{3,2,1,0:T(8,128)(2,1)}, u32[]{:S(2)}, u32[]{:S(2)}) %collective-permute-start.51) | collective-permute-done | bytes 1572896 | tf_op jit(solution)/shard_map/ppermute | solution.py:68
  1146.8 30.7 %collective-permute-done.54 = bf16[1,4,256,768]{3,2,1,0:T(8,128)(2,1)} collective-permute-done((bf16[1,4,256,768]{3,2,1,0:T(8,128)(2,1)}, bf16[1,4,256,768]{3,2,1,0:T(8,128)(2,1)}, u32[]{:S(2)}, u32[]{:S(2)}) %collective-permute-start.54) | collective-permute-done | bytes 1572896 | tf_op jit(solution)/shard_map/ppermute | solution.py:68
  1180.5 10.8 collective-permute-done.57
  1193.6 8.0 convert_bitcast_fusion
  (307 shorter events, 254.2 us)
Async XLA Ops:
  7.2 32.6 %all-gather.5.cloned.1.call-start = ((), (), s32[]{:S(2)}) async-start(), calls=%async_computation.4 | async-start | bytes 1310720 | tf_op jit(solution)/shard_map/all_gather | solution.py:695
  9.0 150.5 %all-gather.7.cloned.1.call-start = ((), (), s32[]{:S(2)}) async-start(), calls=%async_computation.5 | async-start | bytes 9437184 | tf_op jit(solution)/shard_map/all_gather | solution.py:695
  39.8 1071.3 %reduce-scatter.5.cloned.1.call-start = ((), (), s32[]{:S(2)}) async-start(), calls=%async_computation.3 | async-start | bytes 2359296 | tf_op jit(solution)/shard_map/reduce_scatter | solution.py:766
  80.4 31.1 %collective-permute-start.9 = (bf16[1024,512]{1,0:T(8,128)(2,1)S(1)}, bf16[1024,512]{1,0:T(8,128)(2,1)S(1)}, u32[]{:S(2)}, u32[]{:S(2)}) collective-permute-start(bf16[1024,512]{1,0:T(8,128)(2,1)S(1)} %copy-done.14), channel_id=1, source_target_pairs={{0,2},{1,3},{2,0},{3,1},{4,6},{5,7},{6,4},{7,5},{8,10},{9,11},{10,... | collective-permute-start | bytes 3145736 | tf_op jit(solution)/shard_map/ppermute | solution.py:68
  81.6 31.9 %collective-permute-start.8 = (bf16[1024,512]{1,0:T(8,128)(2,1)S(1)}, bf16[1024,512]{1,0:T(8,128)(2,1)S(1)}, u32[]{:S(2)}, u32[]{:S(2)}) collective-permute-start(bf16[1024,512]{1,0:T(8,128)(2,1)S(1)} %copy-done.14), channel_id=1, source_target_pairs={{0,1},{1,0},{2,3},{3,2},{4,5},{5,4},{6,7},{7,6},{8,9},{9,8},{10,11... | collective-permute-start | bytes 3145736 | tf_op jit(solution)/shard_map/ppermute | solution.py:68
  112.3 35.9 %collective-permute-start.10 = (bf16[512,512]{1,0:T(8,128)(2,1)}, bf16[512,512]{1,0:T(8,128)(2,1)}, u32[]{:S(2)}, u32[]{:S(2)}) collective-permute-start(bf16[512,512]{1,0:T(8,128)(2,1)} %slice.156), channel_id=1, source_target_pairs={{0,1},{1,0},{2,3},{3,2},{4,5},{5,4},{6,7},{7,6},{8,9},{9,8},{10,11... | collective-permute-start | bytes 1572872 | tf_op jit(solution)/shard_map/ppermute | solution.py:68
  114.4 33.8 %collective-permute-start.11 = (bf16[512,512]{1,0:T(8,128)(2,1)}, bf16[512,512]{1,0:T(8,128)(2,1)}, u32[]{:S(2)}, u32[]{:S(2)}) collective-permute-start(bf16[512,512]{1,0:T(8,128)(2,1)} %slice.157), channel_id=1, source_target_pairs={{0,2},{1,3},{2,0},{3,1},{4,6},{5,7},{6,4},{7,5},{8,10},{9,11},{10,... | collective-permute-start | bytes 1572872 | tf_op jit(solution)/shard_map/ppermute | solution.py:68
  340.1 52.0 %collective-permute-start.15 = (bf16[256,2048]{1,0:T(8,128)(2,1)}, bf16[256,2048]{1,0:T(8,128)(2,1)S(1)}, u32[]{:S(2)}, u32[]{:S(2)}) collective-permute-start(bf16[256,2048]{1,0:T(8,128)(2,1)} %get-tuple-element.117), channel_id=1, source_target_pairs={{0,1},{1,0},{2,3},{3,2},{4,5},{5,4},{6,7},{7,6},{8,9},{9,8},{10,11... | collective-permute-start | bytes 3145736 | tf_op jit(solution)/shard_map/ppermute | solution.py:68
  341.1 51.0 %collective-permute-start.16 = (bf16[256,2048]{1,0:T(8,128)(2,1)}, bf16[256,2048]{1,0:T(8,128)(2,1)S(1)}, u32[]{:S(2)}, u32[]{:S(2)}) collective-permute-start(bf16[256,2048]{1,0:T(8,128)(2,1)} %get-tuple-element.118), channel_id=1, source_target_pairs={{0,2},{1,3},{2,0},{3,1},{4,6},{5,7},{6,4},{7,5},{8,10},{9,11},{10,... | collective-permute-start | bytes 3145736 | tf_op jit(solution)/shard_map/ppermute | solution.py:68
  342.2 49.9 %collective-permute-start.17 = (bf16[256,2048]{1,0:T(8,128)(2,1)}, bf16[256,2048]{1,0:T(8,128)(2,1)S(1)}, u32[]{:S(2)}, u32[]{:S(2)}) collective-permute-start(bf16[256,2048]{1,0:T(8,128)(2,1)} %get-tuple-element.119), channel_id=1, source_target_pairs={{0,3},{1,2},{2,1},{3,0},{4,7},{5,6},{6,5},{7,4},{8,11},{9,10},{10,... | collective-permute-start | bytes 3145736 | tf_op jit(solution)/shard_map/ppermute | solution.py:68
  345.8 41.3 %collective-permute-start.20 = (f32[256,16]{1,0:T(8,128)S(1)}, f32[256,16]{1,0:T(8,128)S(1)}, u32[]{:S(2)}, u32[]{:S(2)}) collective-permute-start(f32[256,16]{1,0:T(8,128)S(1)} %get-tuple-element.236), channel_id=1, source_target_pairs={{0,3},{1,2},{2,1},{3,0},{4,7},{5,6},{6,5},{7,4},{8,11},{9,10},{10,... | collective-permute-start | bytes 49160 | tf_op jit(solution)/shard_map/ppermute | solution.py:68
  347.3 41.4 %collective-permute-start.19 = (f32[256,16]{1,0:T(8,128)S(1)}, f32[256,16]{1,0:T(8,128)S(1)}, u32[]{:S(2)}, u32[]{:S(2)}) collective-permute-start(f32[256,16]{1,0:T(8,128)S(1)} %get-tuple-element.237), channel_id=1, source_target_pairs={{0,2},{1,3},{2,0},{3,1},{4,6},{5,7},{6,4},{7,5},{8,10},{9,11},{10,... | collective-permute-start | bytes 49160 | tf_op jit(solution)/shard_map/ppermute | solution.py:68
  403.2 242.1 %collective-permute-start.46 = (bf16[4,4,256,768]{3,2,1,0:T(8,128)(2,1)}, bf16[4,4,256,768]{3,2,1,0:T(8,128)(2,1)}, u32[]{:S(2)}, u32[]{:S(2)}) collective-permute-start(bf16[4,4,256,768]{3,2,1,0:T(8,128)(2,1)} %get-tuple-element.152), channel_id=1, source_target_pairs={{0,4},{4,0},{8,12},{12,8},{16,20},{20,16},{24,28},{28,24},{1,5},{5... | collective-permute-start | bytes 18874376 | tf_op jit(solution)/shard_map/ppermute | solution.py:68
  461.0 745.9 %reduce-scatter.3.cloned.1.call-start = ((), (), s32[]{:S(2)}) async-start(), calls=%async_computation.2 | async-start | bytes 7077888 | tf_op jit(solution)/shard_map/reduce_scatter | solution.py:766
  488.8 164.5 %collective-permute-start.49 = (bf16[4,4,256,768]{3,2,1,0:T(8,128)(2,1)}, bf16[4,4,256,768]{3,2,1,0:T(8,128)(2,1)}, u32[]{:S(2)}, u32[]{:S(2)}) collective-permute-start(bf16[4,4,256,768]{3,2,1,0:T(8,128)(2,1)} %get-tuple-element.153), channel_id=1, source_target_pairs={{0,4},{4,0},{8,12},{12,8},{16,20},{20,16},{24,28},{28,24},{1,5},{5... | collective-permute-start | bytes 18874376 | tf_op jit(solution)/shard_map/ppermute | solution.py:68
  509.3 164.8 %collective-permute-start.52 = (bf16[4,4,256,768]{3,2,1,0:T(8,128)(2,1)}, bf16[4,4,256,768]{3,2,1,0:T(8,128)(2,1)}, u32[]{:S(2)}, u32[]{:S(2)}) collective-permute-start(bf16[4,4,256,768]{3,2,1,0:T(8,128)(2,1)} %get-tuple-element.156), channel_id=1, source_target_pairs={{0,4},{4,0},{8,12},{12,8},{16,20},{20,16},{24,28},{28,24},{1,5},{5... | collective-permute-start | bytes 18874376 | tf_op jit(solution)/shard_map/ppermute | solution.py:68
  547.3 57.7 %collective-permute-start.12 = (bf16[1024,512]{1,0:T(8,128)(2,1)}, bf16[1024,512]{1,0:T(8,128)(2,1)S(1)}, u32[]{:S(2)}, u32[]{:S(2)}) collective-permute-start(bf16[1024,512]{1,0:T(8,128)(2,1)} %get-tuple-element.114), channel_id=1, source_target_pairs={{0,1},{1,0},{2,3},{3,2},{4,5},{5,4},{6,7},{7,6},{8,9},{9,8},{10,11... | collective-permute-start | bytes 3145736 | tf_op jit(solution)/shard_map/ppermute | solution.py:68
  574.3 31.7 %collective-permute-start.13 = (bf16[1024,512]{1,0:T(8,128)(2,1)S(1)}, bf16[1024,512]{1,0:T(8,128)(2,1)}, u32[]{:S(2)}, u32[]{:S(2)}) collective-permute-start(bf16[1024,512]{1,0:T(8,128)(2,1)S(1)} %copy-done.47), channel_id=1, source_target_pairs={{0,2},{1,3},{2,0},{3,1},{4,6},{5,7},{6,4},{7,5},{8,10},{9,11},{10,... | collective-permute-start | bytes 3145736 | tf_op jit(solution)/shard_map/ppermute | solution.py:68
  610.7 77.3 %collective-permute-start.43 = (bf16[4,2,256,768]{3,2,1,0:T(8,128)(2,1)}, bf16[4,2,256,768]{3,2,1,0:T(8,128)(2,1)}, u32[]{:S(2)}, u32[]{:S(2)}) collective-permute-start(bf16[4,2,256,768]{3,2,1,0:T(8,128)(2,1)} %get-tuple-element.151), channel_id=1, source_target_pairs={{0,4},{4,0},{8,12},{12,8},{16,20},{20,16},{24,28},{28,24},{1,5},{5... | collective-permute-start | bytes 9437192 | tf_op jit(solution)/shard_map/ppermute | solution.py:68
  645.4 53.9 %collective-permute-start.55 = (bf16[4,2,256,768]{3,2,1,0:T(8,128)(2,1)}, bf16[4,2,256,768]{3,2,1,0:T(8,128)(2,1)}, u32[]{:S(2)}, u32[]{:S(2)}) collective-permute-start(bf16[4,2,256,768]{3,2,1,0:T(8,128)(2,1)} %get-tuple-element.159), channel_id=1, source_target_pairs={{0,4},{4,0},{8,12},{12,8},{16,20},{20,16},{24,28},{28,24},{1,5},{5... | collective-permute-start | bytes 9437192 | tf_op jit(solution)/shard_map/ppermute | solution.py:68
  672.2 241.8 %collective-permute-start.47 = (bf16[2,4,256,768]{3,2,1,0:T(8,128)(2,1)}, bf16[2,4,256,768]{3,2,1,0:T(8,128)(2,1)}, u32[]{:S(2)}, u32[]{:S(2)}) collective-permute-start(bf16[2,4,256,768]{3,2,1,0:T(8,128)(2,1)} %slice.172), channel_id=1, source_target_pairs={{0,8},{4,12},{8,0},{12,4},{16,24},{20,28},{24,16},{28,20},{1,9},{5... | collective-permute-start | bytes 9437192 | tf_op jit(solution)/shard_map/ppermute | solution.py:68
  674.1 245.8 %collective-permute-start.50 = (bf16[2,4,256,768]{3,2,1,0:T(8,128)(2,1)}, bf16[2,4,256,768]{3,2,1,0:T(8,128)(2,1)}, u32[]{:S(2)}, u32[]{:S(2)}) collective-permute-start(bf16[2,4,256,768]{3,2,1,0:T(8,128)(2,1)} %slice.176), channel_id=1, source_target_pairs={{0,8},{4,12},{8,0},{12,4},{16,24},{20,28},{24,16},{28,20},{1,9},{5... | collective-permute-start | bytes 9437192 | tf_op jit(solution)/shard_map/ppermute | solution.py:68
  688.0 247.2 %collective-permute-start.53 = (bf16[2,4,256,768]{3,2,1,0:T(8,128)(2,1)}, bf16[2,4,256,768]{3,2,1,0:T(8,128)(2,1)}, u32[]{:S(2)}, u32[]{:S(2)}) collective-permute-start(bf16[2,4,256,768]{3,2,1,0:T(8,128)(2,1)} %slice.180), channel_id=1, source_target_pairs={{0,8},{4,12},{8,0},{12,4},{16,24},{20,28},{24,16},{28,20},{1,9},{5... | collective-permute-start | bytes 9437192 | tf_op jit(solution)/shard_map/ppermute | solution.py:68
  692.5 218.3 %collective-permute-start.44 = (bf16[2,2,256,768]{3,2,1,0:T(8,128)(2,1)S(1)}, bf16[2,2,256,768]{3,2,1,0:T(8,128)(2,1)S(1)}, u32[]{:S(2)}, u32[]{:S(2)}) collective-permute-start(bf16[2,2,256,768]{3,2,1,0:T(8,128)(2,1)S(1)} %slice.168), channel_id=1, source_target_pairs={{0,8},{4,12},{8,0},{12,4},{16,24},{20,28},{24,16},{28,20},{1,9},{5... | collective-permute-start | bytes 4718600 | tf_op jit(solution)/shard_map/ppermute | solution.py:68
  699.3 213.2 %collective-permute-start.27 = (bf16[1024,512]{1,0:T(8,128)(2,1)S(1)}, bf16[1024,512]{1,0:T(8,128)(2,1)S(1)}, u32[]{:S(2)}, u32[]{:S(2)}) collective-permute-start(bf16[1024,512]{1,0:T(8,128)(2,1)S(1)} %copy-done.45), channel_id=1, source_target_pairs={{0,3},{1,2},{2,1},{3,0},{4,7},{5,6},{6,5},{7,4},{8,11},{9,10},{10,... | collective-permute-start | bytes 3145736 | tf_op jit(solution)/shard_map/ppermute | solution.py:68
  912.6 29.5 %collective-permute-start.25 = (bf16[1024,512]{1,0:T(8,128)(2,1)}, bf16[1024,512]{1,0:T(8,128)(2,1)}, u32[]{:S(2)}, u32[]{:S(2)}) collective-permute-start(bf16[1024,512]{1,0:T(8,128)(2,1)} %get-tuple-element.136), channel_id=1, source_target_pairs={{0,1},{1,0},{2,3},{3,2},{4,5},{5,4},{6,7},{7,6},{8,9},{9,8},{10,11... | collective-permute-start | bytes 3145736 | tf_op jit(solution)/shard_map/ppermute | solution.py:68
  914.1 61.8 %collective-permute-start.56 = (bf16[2,2,256,768]{3,2,1,0:T(8,128)(2,1)S(1)}, bf16[2,2,256,768]{3,2,1,0:T(8,128)(2,1)}, u32[]{:S(2)}, u32[]{:S(2)}) collective-permute-start(bf16[2,2,256,768]{3,2,1,0:T(8,128)(2,1)S(1)} %slice.184), channel_id=1, source_target_pairs={{0,8},{4,12},{8,0},{12,4},{16,24},{20,28},{24,16},{28,20},{1,9},{5... | collective-permute-start | bytes 4718600 | tf_op jit(solution)/shard_map/ppermute | solution.py:68
  919.9 193.1 %collective-permute-start.48 = (bf16[1,4,256,768]{3,2,1,0:T(8,128)(2,1)}, bf16[1,4,256,768]{3,2,1,0:T(8,128)(2,1)}, u32[]{:S(2)}, u32[]{:S(2)}) collective-permute-start(bf16[1,4,256,768]{3,2,1,0:T(8,128)(2,1)} %slice.174), channel_id=1, source_target_pairs={{0,16},{4,20},{8,24},{12,28},{16,0},{20,4},{24,8},{28,12},{1,17},{... | collective-permute-start | bytes 4718600 | tf_op jit(solution)/shard_map/ppermute | solution.py:68
  935.0 175.0 %collective-permute-start.45 = (bf16[1,2,256,768]{3,2,1,0:T(8,128)(2,1)S(1)}, bf16[1,2,256,768]{3,2,1,0:T(8,128)(2,1)S(1)}, u32[]{:S(2)}, u32[]{:S(2)}) collective-permute-start(bf16[1,2,256,768]{3,2,1,0:T(8,128)(2,1)S(1)} %copy-done.26), channel_id=1, source_target_pairs={{0,16},{4,20},{8,24},{12,28},{16,0},{20,4},{24,8},{28,12},{1,17},{... | collective-permute-start | bytes 2359304 | tf_op jit(solution)/shard_map/ppermute | solution.py:68
  935.3 208.5 %collective-permute-start.51 = (bf16[1,4,256,768]{3,2,1,0:T(8,128)(2,1)}, bf16[1,4,256,768]{3,2,1,0:T(8,128)(2,1)}, u32[]{:S(2)}, u32[]{:S(2)}) collective-permute-start(bf16[1,4,256,768]{3,2,1,0:T(8,128)(2,1)} %slice.178), channel_id=1, source_target_pairs={{0,16},{4,20},{8,24},{12,28},{16,0},{20,4},{24,8},{28,12},{1,17},{... | collective-permute-start | bytes 4718600 | tf_op jit(solution)/shard_map/ppermute | solution.py:68
  942.1 235.5 %collective-permute-start.54 = (bf16[1,4,256,768]{3,2,1,0:T(8,128)(2,1)}, bf16[1,4,256,768]{3,2,1,0:T(8,128)(2,1)}, u32[]{:S(2)}, u32[]{:S(2)}) collective-permute-start(bf16[1,4,256,768]{3,2,1,0:T(8,128)(2,1)} %slice.182), channel_id=1, source_target_pairs={{0,16},{4,20},{8,24},{12,28},{16,0},{20,4},{24,8},{28,12},{1,17},{... | collective-permute-start | bytes 4718600 | tf_op jit(solution)/shard_map/ppermute | solution.py:68
  979.8 211.5 %collective-permute-start.57 = (bf16[1,2,256,768]{3,2,1,0:T(8,128)(2,1)}, bf16[1,2,256,768]{3,2,1,0:T(8,128)(2,1)}, u32[]{:S(2)}, u32[]{:S(2)}) collective-permute-start(bf16[1,2,256,768]{3,2,1,0:T(8,128)(2,1)} %slice.186), channel_id=1, source_target_pairs={{0,16},{4,20},{8,24},{12,28},{16,0},{20,4},{24,8},{28,12},{1,17},{... | collective-permute-start | bytes 2359304 | tf_op jit(solution)/shard_map/ppermute | solution.py:68
  (83 other events, 1296.6 us)
Sparse Core Ops, SparseCore 0:
  10.4 29.3 all-gather.4
  41.4 82.0 all-gather.6
  461.2 39.3 reduce-scatter.4
  543.0 76.5 reduce-scatter.2

commit v2 on v1

--- a/solution.py
+++ b/solution.py
@@ -89,15 +89,9 @@
     return (left.astype(f32) + right.astype(f32)).astype(bf16)
 
 
-def halve(keep, send, count):
-    mask = 1
-    while True:
-        total = add_low(keep, swap(send, "dp", count, mask))
-        mask *= 2
-        if mask >= count:
-            return total[0]
-        middle = total.shape[0] // 2
-        keep, send = total[:middle], total[middle:]
+def add_halves(keep, arrived):
+    middle = keep.shape[0] // 2
+    return add_low(keep[:middle], arrived[:middle]), add_low(keep[middle:], arrived[middle:])
 
 
 def butterfly(value, counts):
@@ -312,7 +306,7 @@
 def stream_kernel(n_tp, dp_count, scalars, *refs):
     pieces = refs[:n_tp]
     x_ref, w_ref, gain, router, kept = refs[n_tp : n_tp + 5]
-    stream_out, normed_out, turned_out, factor_out, probs_out, gates_out = refs[n_tp + 5 :]
+    stream_out, normed_out, mine_out, turned_out, factor_out, probs_out, gates_out = refs[n_tp + 5 :]
     width = pieces[0].shape[1]
     total = x_ref[...].astype(f32)
     for r in range(n_tp):
@@ -323,6 +317,7 @@
     factor_out[...] = factor
     normed = (total * factor * gain[...]).astype(bf16)
     normed_out[...] = normed
+    mine_out[...] = normed_out[:, pl.ds(pl.multiple_of(scalars[0] * width, width), width)]
     logits = dot(normed, router[...])
     power = jnp.exp(logits - jnp.max(logits, axis=1, keepdims=True))
     probs = power / jnp.sum(power, axis=1, keepdims=True)
@@ -345,6 +340,7 @@
         [
             struct((tokens, features), f32),
             struct((tokens, features), bf16),
+            struct((tokens, features // n_tp), bf16),
             struct((features, tokens), bf16),
             struct((tokens, 1), f32),
             struct((tokens, experts), f32),
@@ -353,6 +349,7 @@
         [
             rows(features),
             rows(features),
+            rows(features // n_tp),
             pl.BlockSpec((features, TB), lambda i, s: (0, i)),
             rows(1),
             rows(experts),
@@ -363,9 +360,9 @@
     )
 
 
-def expert_kernel(first, scalars, n_ref, g_ref, gates_ref, wg, wu, wd, hidden_out, pair_out, dgate_out):
+def expert_kernel(first, shift, scalars, n_ref, g_ref, gates_ref, wg, wu, wd, hidden_out, pair_out, dgate_out):
     step = pl.program_id(0)
-    expert = first + step
+    expert = first + step + (0 if shift is None else scalars[shift])
     width = wg.shape[-1]
 
     @pl.when(step == 0)
@@ -388,13 +385,14 @@
     pair_out[0, :, width:] = (dhidden * swish).astype(bf16)
 
 
-def run_experts(scalars, normed, grad, gates, wg, wu, wd, first, count):
+def run_experts(scalars, normed, grad, gates, wg, wu, wd, first, count, shift=None):
     tokens, features = normed.shape
     experts, _, width = wg.shape
-    weight = lambda shape: pl.BlockSpec((1, *shape), lambda i, s: (first + i, 0, 0))
+    place = lambda i, s: first + i + (0 if shift is None else s[shift])
+    weight = lambda shape: pl.BlockSpec((1, *shape), lambda i, s: (place(i, s), 0, 0))
     given = lambda shape: pl.BlockSpec((1, *shape), lambda i, s: (i, 0, 0))
     return call(
-        functools.partial(expert_kernel, first),
+        functools.partial(expert_kernel, first, shift),
         (count,),
         scalars,
         [normed, grad, gates, wg, wu, wd],
@@ -447,6 +445,79 @@
         flops=6 * count * tokens * features * width,
         moved=count * 5 << 20,
     )
+
+
+def inner_swap(index):
+    return (index & ~3) | ((index & 1) << 1) | ((index >> 1) & 1)
+
+
+def shared_grads_kernel(scalars, *refs):
+    turned, turned2, g_turned, g_turned2, hidden, hidden2, pair, pair2, keep_out, send_out = refs
+    half, _, rows, _ = keep_out.shape
+    width = hidden.shape[-1]
+    first = dot(turned[...], pair[0]) + dot(turned2[...], pair2[0])
+    first = first.astype(bf16).reshape(2 * half, rows, 2 * width)
+    second = dot(g_turned[...], hidden[0]) + dot(g_turned2[...], hidden2[0])
+    second = second.astype(bf16).reshape(2 * half, rows, width)
+    for out, base in ((keep_out, 0), (send_out, half)):
+        for place in range(half):
+            out[inner_swap(place), 0, :, : 2 * width] = first[base + place]
+            out[inner_swap(place), 0, :, 2 * width :] = second[base + place]
+
+
+def shared_grads(scalars, turned, turned2, g_turned, g_turned2, hidden, hidden2, pair, pair2, shift, offset, count,
+                 dp_count):
+    features, tokens = turned.shape
+    width = hidden.shape[-1]
+    half, rows = dp_count // 2, features // dp_count
+    out = struct((half, count, rows, 3 * width), bf16)
+    out_spec = pl.BlockSpec((half, 1, rows, 3 * width), lambda i, s: (0, i, 0, 0))
+    mine = lambda w: pl.BlockSpec((1, tokens, w), lambda i, s: (s[shift] + offset + i, 0, 0))
+    other = lambda w: pl.BlockSpec((1, tokens, w), lambda i, s: (offset + i, 0, 0))
+    return call(
+        shared_grads_kernel,
+        (count,),
+        scalars,
+        [turned, turned2, g_turned, g_turned2, hidden, hidden2, pair, pair2],
+        [whole_spec()] * 4 + [mine(width), other(width), mine(2 * width), other(2 * width)],
+        [out, out],
+        [out_spec, out_spec],
+        flops=12 * count * tokens * features * width,
+        moved=(16 + count * 6) << 20,
+    )
+
+
+def finish_kernel(n_parts, n_old, scalars, *refs):
+    parts = refs[:n_parts]
+    gate_out, up_out, down_out = refs[n_parts + n_old :]
+    width = gate_out.shape[-1]
+    total = sum(part[0].astype(f32) for part in parts)
+    gate_out[0] = total[:, :width]
+    up_out[0] = total[:, width : 2 * width]
+    down_out[0] = total[:, 2 * width :].T
+
+
+def finish(scalars, parts, old, first, shift, experts):
+    count, rows, wide = parts[0].shape
+    width = wide // 3
+    place = lambda i, s: (first + i + (0 if shift is None else s[shift]), 0, 0)
+    spec = pl.BlockSpec((1, rows, width), place)
+    down_spec = pl.BlockSpec((1, width, rows), place)
+    shapes = [struct((experts, rows, width), f32)] * 2 + [struct((experts, width, rows), f32)]
+    return pl.pallas_call(
+        functools.partial(finish_kernel, len(parts), len(old)),
+        out_shape=shapes,
+        grid_spec=pltpu.PrefetchScalarGridSpec(
+            num_scalar_prefetch=1,
+            grid=(count,),
+            in_specs=[pl.BlockSpec((1, rows, wide), lambda i, s: (i, 0, 0))] * len(parts)
+            + [pl.BlockSpec(memory_space=pl.ANY)] * len(old),
+            out_specs=[spec, spec, down_spec],
+        ),
+        input_output_aliases={1 + len(parts) + k: k for k in range(len(old))},
+        compiler_params=pltpu.CompilerParams(vmem_limit_bytes=VMEM_LIMIT),
+        cost_estimate=pl.CostEstimate(flops=0, bytes_accessed=count << 20, transcendentals=0),
+    )(scalars, *parts, *old)
 
 
 def chunk_specs(chunks, shape):
@@ -679,9 +750,8 @@
 def body(n_dp, n_tp, cosine, sine, tokens, cotangent, attn_gain, w_query, w_key, w_value, query_gain, key_gain,
          w_output, ffn_gain, w_router, w_gate, w_up, w_down, expert_ids):
     tp, dp = lax.axis_index("tensor"), lax.axis_index("dp")
-    scalars = jnp.stack(
-        [tp ^ r for r in range(n_tp)] + [dp ^ bit_reverse(place, n_dp) for place in range(n_dp)]
-    ).astype(jnp.int32)
+    far, near = n_dp // 2, n_dp // 4
+    side = (dp // near) % 2
     token_count, width = tokens.shape
     features = width * n_tp
     heads, hd = query_gain.shape
@@ -689,88 +759,163 @@
     experts = w_router.shape[1]
     capacity = token_count * expert_ids.shape[1] // experts
     gain1, gain2 = attn_gain[None, :], ffn_gain[None, :]
+    lead = 6
+    shared = (experts - lead) // 2
+    first_block, second_block = 2, lead - 2
+    shift, other_shift = n_tp + n_dp, n_tp + n_dp + 1
+    scalars = jnp.stack(
+        [tp ^ r for r in range(n_tp)]
+        + [dp ^ bit_reverse(place, n_dp) for place in range(n_dp)]
+        + [side * shared, (1 - side) * shared]
+    ).astype(jnp.int32)
 
     share = local // n_dp
     w_share = lax.dynamic_slice_in_dim(w_output, dp * share, share, 0)
-    w_all = lax.all_gather(lax.all_gather(w_share, "tensor"), "dp")
+    w_all = lax.all_gather(w_share, ("dp", "tensor")).reshape(n_dp, n_tp, share, features)
 
     x_pieces = gather_pieces(tokens, "tensor", n_tp)
+    kept = kept_pairs(expert_ids, experts, capacity)
+    x_pieces[0] = after(x_pieces[0], kept)
     x, normed1, factor1, q_raw, k_raw, q_rot, k_rot, value = project(
         scalars, x_pieces, gain1, w_query, w_key, w_value, query_gain, key_gain, cosine, sine
     )
     g_pieces = gather_pieces(after(cotangent, x_pieces[-1]), "tensor", n_tp)
+    attended, totals = attend(scalars, q_rot, k_rot, value, heads)
+    attended_pieces = gather_pieces(attended, "tensor", n_tp)
+    g_pieces[0] = after(g_pieces[0], attended)
     upstream, g_turned = whole_grad(scalars, g_pieces, n_dp)
-    kept = kept_pairs(expert_ids, experts, capacity)
-    attended, totals = attend(scalars, q_rot, k_rot, value, heads)
-    stream, normed2, turned, factor2, probs, gates = stream_of(
-        scalars, gather_pieces(attended, "tensor", n_tp), x, w_all, gain2, w_router, kept, n_dp
-    )
-
-    blocks = [(0, 2), (2, 4), (6, experts - 6)]
-    hiddens, pairs, dgates, sums = [], [], [], []
-    start = normed2
-    for index, (first, count) in enumerate(blocks):
-        hidden, pair, dgate = run_experts(scalars, start, upstream, gates, w_gate, w_up, w_down, first, count)
-        hiddens.append(hidden)
-        pairs.append(pair)
-        dgates.append(dgate)
-        if index < len(blocks) - 1:
-            keep, send = weight_grads(scalars, turned, g_turned, hidden, pair, 0, count, n_dp)
-            sums.append((first, count, keep, send))
-            start = after(normed2, keep)
-    dgate = sum(dgates)
-    input_parts = input_grads(scalars, pairs, w_gate, w_up, n_tp)
+    stream, normed2, normed2_mine, turned, factor2, probs, gates = stream_of(
+        scalars, attended_pieces, after(x, upstream), w_all, gain2, w_router, kept, n_dp
+    )
+    g_near = swap(after(cotangent, g_pieces[-1]), "dp", n_dp, near)
+    normed_near = swap(normed2_mine, "dp", n_dp, near)
+    gates_near = swap(gates, "dp", n_dp, near)
+    g_near_pieces = gather_pieces(after(g_near, attended_pieces[-1]), "tensor", n_tp)
+    normed_near_pieces = gather_pieces(normed_near, "tensor", n_tp)
+
+    run = lambda normed, first, count: run_experts(
+        scalars, normed, upstream, gates, w_gate, w_up, w_down, first, count
+    )
+    hidden0, pair0, dgate0 = run(normed2, 0, first_block)
+    keep0, send0 = weight_grads(scalars, turned, g_turned, hidden0, pair0, 0, first_block, n_dp)
+    hidden1, pair1, dgate1 = run(after(normed2, send0), first_block, second_block)
+    arrived0 = swap(send0, "dp", n_dp, 1)
+    keep0, send0 = add_halves(after(keep0, pair1), arrived0)
+    keep1, send1 = weight_grads(scalars, after(turned, send0), g_turned, hidden1, pair1, 0, second_block, n_dp)
+    hidden2, pair2, dgate2 = run(after(normed2, send1), lead, experts - lead)
+    arrived1 = swap(send1, "dp", n_dp, 1)
+    keep1, send1 = add_halves(after(keep1, pair2), arrived1)
+    masks, mask = [], 2
+    while mask < n_dp:
+        masks.append(mask)
+        mask *= 2
+    last = send1
+    for mask in masks[:-1]:
+        arrived0 = swap(send0, "dp", n_dp, mask)
+        keep0, send0 = add_halves(after(keep0, last), arrived0)
+    last = send0
+
+    hiddens, pairs = [hidden0, hidden1, hidden2], [pair0, pair1, pair2]
+    dgate = dgate0 + dgate1 + dgate2
+    input_parts = input_grads(scalars, [*pairs[:-1], after(pair2, last)], w_gate, w_up, n_tp)
     rows = token_count // n_tp
     dgate_rows = [lax.dynamic_slice_in_dim(dgate, (tp ^ r) * rows, rows, 0) for r in range(n_tp)]
     dgate_parts = scatter_pieces(dgate_rows, "tensor", n_tp)
-    arrived = scatter_pieces(input_parts, "tensor", n_tp)
-
-    first, count = blocks[-1]
-    ready = input_parts[0]
-    for offset in range(0, count, 4):
-        size = min(4, count - offset)
-        keep, send = weight_grads(
-            scalars, after(turned, ready), g_turned, hiddens[-1], pairs[-1], offset, size, n_dp
+    input_arrived = scatter_pieces(input_parts, "tensor", n_tp)
+
+    g_near_pieces[0] = after(g_near_pieces[0], input_parts[0])
+    upstream_near, g_turned_near = whole_grad(scalars, g_near_pieces, n_dp)
+    normed_near_pieces[0] = after(normed_near_pieces[0], g_turned_near)
+    normed2_near, turned_near = whole_grad(scalars, normed_near_pieces, n_dp)
+    hidden_near, pair_near, _ = run_experts(
+        scalars, normed2_near, upstream_near, gates_near, w_gate, w_up, w_down, lead, shared, shift
+    )
+    last = pair_near
+    for mask in masks[:-1]:
+        arrived1 = swap(send1, "dp", n_dp, mask)
+        keep1, send1 = add_halves(after(keep1, last), arrived1)
+        last = send1
+    chunk = (shared + 1) // 2
+    shares = []
+    for offset in range(0, shared, chunk):
+        size = min(chunk, shared - offset)
+        shares.append(
+            shared_grads(
+                scalars, after(turned, last), turned_near, g_turned, g_turned_near, hidden2, hidden_near, pair2,
+                pair_near, shift, offset, size, n_dp,
+            )
         )
-        ready = keep
-        sums.append((first + offset, size, keep, send))
+        last = shares[-1][1]
         if offset == 0:
-            result_parts = results(scalars, hiddens, after(w_down, ready), n_tp)
-            ready = result_parts[0]
-    reduced = [halve(keep, send, n_dp) for _, _, keep, send in sums]
-
-    dattn_rows, dgain2, drouter = stream_grad_rows(
-        scalars, arrived, dgate_parts, probs, kept, stream, normed2, factor2, upstream, gain2, w_router
-    )
-    dattn, dattended = attended_grad(scalars, gather_pieces(dattn_rows, "tensor", n_tp), w_output)
+            input_arrived[0] = after(input_arrived[0], last)
+            dattn_rows, dgain2, drouter = stream_grad_rows(
+                scalars, input_arrived, dgate_parts, probs, kept, stream, normed2, factor2, upstream, gain2, w_router
+            )
+            dattn_pieces = gather_pieces(dattn_rows, "tensor", n_tp)
+            last = dattn_rows
+            keep, send = shares[0]
+            for mask in [1] + [m for m in masks if m not in (near, far)]:
+                keep, send = add_halves(after(keep, last), swap(send, "dp", n_dp, mask))
+                last = send
+            shares[0] = keep, send
+    result_parts = results(scalars, hiddens, after(w_down, last), n_tp)
+    last = result_parts[0]
+    keep, send = shares[1]
+    for mask in [1] + [m for m in masks if m not in (near, far)]:
+        keep, send = add_halves(after(keep, last), swap(send, "dp", n_dp, mask))
+        last = send
+    shares[1] = keep, send
+    result_arrived = scatter_pieces(result_parts, "tensor", n_tp)
+
+    dattn_pieces[0] = after(dattn_pieces[0], last)
+    dattn, dattended = attended_grad(scalars, dattn_pieces, w_output)
     dq, dk, dv, dhead_gains = attend_back(
         scalars, q_rot, k_rot, value, dattended, totals, q_raw, k_raw, query_gain, key_gain, cosine, sine
     )
     slices, row_dots, dgain1 = [None] * n_tp, [None] * n_tp, [None] * n_tp
+    last = dq
     for r in reversed(range(n_tp)):
         slices[r], row_dots[r], dgain1[r] = normed_grad(
-            scalars, r, dq, dk, dv, w_query, w_key, w_value, x, factor1, gain1, n_tp
+            scalars, r, after(dq, last), dk, dv, w_query, w_key, w_value, x, factor1, gain1, n_tp
         )
+        last = slices[r]
+
+    def spread(value, dimension):
+        return lax.psum_scatter(value.astype(bf16), "dp", scatter_dimension=dimension, tiled=True).astype(f32)
+
+    grad_output = spread(dot(attended, after(dattn, dq), TN), 1)
+    dqkv = jnp.concatenate([dq, dk, after(dv, last)], axis=1)
+    grad_qkv = spread(dot(normed1, dqkv, TN), 0)
+
     row_dot = butterfly(sum(row_dots).reshape(8, token_count // 8), [("tensor", n_tp)])
-    arrived1 = scatter_pieces(slices, "tensor", n_tp)
-    dnormed1 = sum(part.astype(f32) for part in arrived1)
+    arrived1n = scatter_pieces(slices, "tensor", n_tp)
+    dnormed1 = sum(part.astype(f32) for part in arrived1n)
     my_cols = lambda array: lax.dynamic_slice_in_dim(array, tp * width, width, 1)
     normal1 = tokens.astype(f32) * factor1
     input_grad = my_cols(dattn).astype(f32) + factor1 * (
         dnormed1 * my_cols(gain1) - normal1 * (row_dot.reshape(token_count, 1) / features)
     )
-    arrived_y = scatter_pieces(result_parts, "tensor", n_tp)
-    output = my_cols(stream) + sum(part.astype(f32) for part in arrived_y)
-
-    def spread(value, dimension):
-        return lax.psum_scatter(value.astype(bf16), "dp", scatter_dimension=dimension, tiled=True).astype(f32)
-
-    grad_output = spread(dot(attended, dattn, TN), 1)
-    dqkv = jnp.concatenate([dq, dk, dv], axis=1)
-    grad_qkv = spread(dot(normed1, dqkv, TN), 0)
+    output = my_cols(stream) + sum(part.astype(f32) for part in result_arrived)
+
+    old = []
+    arrived0 = swap(send0, "dp", n_dp, far)
+    old = finish(scalars, [after(keep0, last)[0], arrived0[0]], old, 0, None, experts)
+    arrived1 = swap(send1, "dp", n_dp, far)
+    old = finish(scalars, [keep1[0], arrived1[0]], old, first_block, None, experts)
+    offset = lead
+    for keep, send in shares:
+        size = keep.shape[1]
+        keep, send = add_halves(keep, swap(send, "dp", n_dp, far))
+        given = swap(send, "dp", n_dp, near)
+        old = finish(scalars, [keep[0]], old, offset, shift, experts)
+        old = finish(scalars, [given[0]], old, offset, other_shift, experts)
+        offset += size
+    grad_gate, grad_up, grad_down = old
 
     everywhere = [("dp", n_dp), ("tensor", n_tp)]
-    early = butterfly(jnp.concatenate([drouter.T, dgain2], axis=0), everywhere)
+    early = jnp.concatenate([drouter.T, dgain2], axis=0)
+    early = lax.psum_scatter(early, "dp", scatter_dimension=1, tiled=True)
+    early = jnp.sum(lax.all_gather(early, "tensor"), axis=0)
     gain_row = jnp.zeros((1, features), f32)
     for r in range(n_tp):
         gain_row = lax.dynamic_update_slice(gain_row, dgain1[r], (0, (tp ^ r) * width))
@@ -779,14 +924,7 @@
     mine = lambda array, dimension: lax.dynamic_slice_in_dim(
         array, dp * (array.shape[dimension] // n_dp), array.shape[dimension] // n_dp, dimension
     )
-    early = mine(early, 1)
     head_gains = mine(head_gains, 2)
-
-    expert_width = w_gate.shape[-1]
-    stacked = jnp.concatenate(reduced, axis=0)
-    grad_gate = stacked[:, :, :expert_width].astype(f32)
-    grad_up = stacked[:, :, expert_width : 2 * expert_width].astype(f32)
-    grad_down = jnp.swapaxes(stacked[:, :, 2 * expert_width :], 1, 2).astype(f32)
     return (
         output.astype(bf16),
         input_grad.astype(bf16),

time: 1230 us -> 1200 us (0.976)
  waiting for transfers between devices: 635 us -> 549 us
  Pallas kernels: 359 us -> 430 us
  other arithmetic: 82.4 us -> 48 us
  starting transfers between devices: 64.2 us -> 95.6 us
    ppermute x58 -> x61, waiting for transfers between devices: 604 us -> 549 us  [swap(): return lax.ppermute(value, axis, [(i, i ^ mask) for i in range(count)])]
    pallas_call x21 -> x23, Pallas kernels: 359 us -> 408 us  [call(): pl.pallas_call(body, out_shape=outs, grid_spec=pltpu.PrefetchScalarGridSp...]
    ppermute x58 -> x61, starting transfers between devices: 64 us -> 95.5 us  [swap(): return lax.ppermute(value, axis, [(i, i ^ mask) for i in range(count)])]
    all_gather x2 -> x1, waiting for transfers between devices: 30.7 us -> 0.02 us  [body(): lax.all_gather(w_share, ('dp', 'tensor'))]
    convert_element_type x10 -> x5, other arithmetic: 42.7 us -> 18.6 us  [add_low(): return (left.astype(f32) + right.astype(f32)).astype(bf16)]
    pallas_call x0 -> x6, Pallas kernels: none -> 21.9 us  [finish(): pl.pallas_call(functools.partial(finish_kernel, len(parts), len(old)), ou...]
    slice x10 -> x0, local copies, waits for them, and re-layouts: 13.6 us -> none  [halve(): keep, send = (total[:middle], total[middle:])]
  transfers between devices with their start and end apart: 62 -> 65, of which waited for: 29 -> 26; matrix products, arithmetic and copies ran while one was open for 11% -> 6% of each run, Pallas kernels for 14% -> 28%
where the time goes in v2:
time: 1200 us; the launch traced here: 1190 us
  waiting for transfers between devices  549 us (46%)
  Pallas kernels  430 us (36%)
  starting transfers between devices  95.6 us (8%)
  other arithmetic  48 us (4%)
  local copies, waits for them, and re-layouts  30.5 us (3%)
  matrix products  16.8 us (1%)
  between operations  14.9 us (1%)
    ppermute x61, waiting for transfers between devices, swap(): return lax.ppermute(value, axis, [(i, i ^ mask) for i in range(count)])  549 us
    pallas_call x23, Pallas kernels, call(): pl.pallas_call(body, out_shape=outs, grid_spec=pltpu.PrefetchScalarGridSp...  408 us
    ppermute x61, starting transfers between devices, swap(): return lax.ppermute(value, axis, [(i, i ^ mask) for i in range(count)])  95.5 us
  transfers between devices with their start and end apart: 65, of which 26 were waited for; matrix products, arithmetic and copies ran while one was open for 6% of the time, Pallas kernels for 28%

profile of v2, /device:TPU:0, one launch (start us, length us, event | category | flops | bytes accessed | tf_op | source)
XLA Modules:
  0.0 1193.5 jit_solution(6066403275276333981)
XLA Ops:
  13.5 23.7 %collective-permute-done.1.refs_2_ = bf16[1024,512]{1,0:T(8,128)(2,1)S(1)} collective-permute-done((bf16[1024,512]{1,0:T(8,128)(2,1)}, bf16[1024,512]{1,0:T(8,128)(2,1)S(1)}, u32[]{:S(2)}, u32[]{:S(2)}) %collective-permute-start.1) | collective-permute-done | bytes 1048608 | tf_op jit(solution)/shard_map/ppermute | solution.py:68
  44.9 13.2 %collective-permute-done.2 = bf16[512,512]{1,0:T(8,128)(2,1)S(1)} collective-permute-done((bf16[512,512]{1,0:T(8,128)(2,1)S(1)}, bf16[512,512]{1,0:T(8,128)(2,1)S(1)}, u32[]{:S(2)}, u32[]{:S(2)}) %collective-permute-start.2) | collective-permute-done | bytes 524320 | tf_op jit(solution)/shard_map/ppermute | solution.py:68
  61.5 15.1 %shard_map.272 = (bf16[1024,2048]{1,0:T(8,128)(2,1)}, bf16[1024,2048]{1,0:T(8,128)(2,1)}, f32[1024,1]{1,0:T(8,128)}, f32[1024,512]{1,0:T(8,128)}, f32[1024,512]{...) custom-call(s32[14]{0:T(128)} %stack.59.scalars, ...), custom_call_target="tpu_custom_call" | custom-call | flops 6442450944 | bytes 25165824 | tf_op jit(solution)/shard_map/pallas_call | solution.py:48
  76.6 11.7 shard_map.273
  100.9 18.9 %collective-permute-done.5.refs_2_ = bf16[1024,512]{1,0:T(8,128)(2,1)S(1)} collective-permute-done((bf16[1024,512]{1,0:T(8,128)(2,1)}, bf16[1024,512]{1,0:T(8,128)(2,1)S(1)}, u32[]{:S(2)}, u32[]{:S(2)}) %collective-permute-start.5) | collective-permute-done | bytes 1048608 | tf_op jit(solution)/shard_map/ppermute | solution.py:68
  126.0 7.4 collective-permute-done.10
  145.5 20.5 %shard_map.275 = (f32[1024,2048]{1,0:T(8,128)}, bf16[1024,2048]{1,0:T(8,128)(2,1)}, bf16[1024,512]{1,0:T(8,128)(2,1)}, bf16[2048,1024]{1,0:T(8,128)(2,1)}, f32[1...) custom-call(s32[14]{0:T(128)} %stack.59.scalars, bf16[1024,512]{1,0:T(8,128)(2,1)} %get-tuple-element.137.refs_0_, ...), custom_call_target="tpu_custom_call" | custom-call | flops 8589934592 | bytes 33554432 | tf_op jit(solution)/shard_map/pallas_call | solution.py:48
  166.0 14.1 %shard_map.276 = (bf16[2,1024,256]{2,1,0:T(8,128)(2,1)}, bf16[2,1024,512]{2,1,0:T(8,128)(2,1)}, f32[1024,16]{1,0:T(8,128)}) custom-call(s32[14]{0:T(128)} %stack.59.scalars, bf16[1024,2048]{1,0:T(8,128)(2,1)} %get-tuple-element.158.n_ref.refs_11_, bf16[1024,2048]{1,0:T(8,128)(2,1)} %get-tuple-element.141.g_ref.refs_13_, ...), custom_call_target="tpu_custom_call" | custom-call | flops 6442450944 | bytes 10485760 | tf_op jit(solution)/shard_map/pallas_call | solution.py:48
  180.1 13.5 %shard_map.277 = (bf16[4,2,256,768]{3,2,1,0:T(8,128)(2,1)}, bf16[4,2,256,768]{3,2,1,0:T(8,128)(2,1)}) custom-call(s32[14]{0:T(128)} %stack.59.scalars, bf16[2048,1024]{1,0:T(8,128)(2,1)} %get-tuple-element.192.turned.refs_0_, bf16[2048,1024]{1,0:T(8,128)(2,1)} %get-tuple-element.148.g_turned.refs_2_, ...), custom_call_target="tpu_custom_call" | custom-call | flops 6442450944 | bytes 10485760 | tf_op jit(solution)/shard_map/pallas_call | solution.py:48
  193.6 21.8 %shard_map.278 = (bf16[4,1024,256]{2,1,0:T(8,128)(2,1)}, bf16[4,1024,512]{2,1,0:T(8,128)(2,1)}, f32[1024,16]{1,0:T(8,128)}) custom-call(s32[14]{0:T(128)} %stack.59.scalars, bf16[1024,2048]{1,0:T(8,128)(2,1)} %get-tuple-element.158.n_ref.refs_11_, bf16[1024,2048]{1,0:T(8,128)(2,1)} %get-tuple-element.141.g_ref.refs_13_, ...), custom_call_target="tpu_custom_call" | custom-call | flops 12884901888 | bytes 20971520 | tf_op jit(solution)/shard_map/pallas_call | solution.py:48
  217.4 20.4 %shard_map.279 = (bf16[4,4,256,768]{3,2,1,0:T(8,128)(2,1)}, bf16[4,4,256,768]{3,2,1,0:T(8,128)(2,1)}) custom-call(s32[14]{0:T(128)} %stack.59.scalars, bf16[2048,1024]{1,0:T(8,128)(2,1)} %get-tuple-element.192.turned.refs_0_, bf16[2048,1024]{1,0:T(8,128)(2,1)} %get-tuple-element.148.g_turned.refs_2_, ...), custom_call_target="tpu_custom_call" | custom-call | flops 12884901888 | bytes 20971520 | tf_op jit(solution)/shard_map/pallas_call | solution.py:48
  240.1 24.0 %collective-permute-done.15.refs_0_ = bf16[1024,512]{1,0:T(8,128)(2,1)S(1)} collective-permute-done((bf16[1024,512]{1,0:T(8,128)(2,1)S(1)}, bf16[1024,512]{1,0:T(8,128)(2,1)S(1)}, u32[]{:S(2)}, u32[]{:S(2)}) %collective-permute-start.15) | collective-permute-done | bytes 1048608 | tf_op jit(solution)/shard_map/ppermute | solution.py:68
  265.3 20.5 %collective-permute-done.14.refs_0_ = bf16[1024,512]{1,0:T(8,128)(2,1)S(1)} collective-permute-done((bf16[1024,512]{1,0:T(8,128)(2,1)S(1)}, bf16[1024,512]{1,0:T(8,128)(2,1)S(1)}, u32[]{:S(2)}, u32[]{:S(2)}) %collective-permute-start.14) | collective-permute-done | bytes 1048608 | tf_op jit(solution)/shard_map/ppermute | solution.py:68
  292.1 19.8 %collective-permute-done.22.refs_2_ = bf16[1024,512]{1,0:T(8,128)(2,1)S(1)} collective-permute-done((bf16[1024,512]{1,0:T(8,128)(2,1)S(1)}, bf16[1024,512]{1,0:T(8,128)(2,1)S(1)}, u32[]{:S(2)}, u32[]{:S(2)}) %collective-permute-start.22) | collective-permute-done | bytes 1048608 | tf_op jit(solution)/shard_map/ppermute | solution.py:68
  315.3 7.9 collective-permute-done.19
  335.2 53.9 %shard_map.280 = (bf16[10,1024,256]{2,1,0:T(8,128)(2,1)}, bf16[10,1024,512]{2,1,0:T(8,128)(2,1)}, f32[1024,16]{1,0:T(8,128)}) custom-call(s32[14]{0:T(128)} %stack.59.scalars, bf16[1024,2048]{1,0:T(8,128)(2,1)} %get-tuple-element.158.n_ref.refs_11_, bf16[1024,2048]{1,0:T(8,128)(2,1)} %get-tuple-element.141.g_ref.refs_13_, ...), custom_call_target="tpu_custom_call" | custom-call | flops 32212254720 | bytes 52428800 | tf_op jit(solution)/shard_map/pallas_call | solution.py:48
  398.1 46.2 %shard_map.281 = (bf16[256,2048]{1,0:T(8,128)(2,1)}, bf16[256,2048]{1,0:T(8,128)(2,1)}, bf16[256,2048]{1,0:T(8,128)(2,1)}, bf16[256,2048]{1,0:T(8,128)(2,1)}) custom-call(s32[14]{0:T(128)} %stack.59.scalars, bf16[2,1024,512]{2,1,0:T(8,128)(2,1)} %get-tuple-element.149.pair.refs_0_, bf16[4,1024,512]{2,1,0:T(8,128)(2,1)} %get-tuple-element.154.pair.refs_1_, ...), custom_call_target="tpu_custom_call" | custom-call | flops 34359738368 | bytes 50331648 | tf_op jit(solution)/shard_map/pallas_call | solution.py:48
  457.8 25.7 %shard_map.284 = (bf16[5,1024,256]{2,1,0:T(8,128)(2,1)}, bf16[5,1024,512]{2,1,0:T(8,128)(2,1)}, f32[1024,16]{1,0:T(8,128)}) custom-call(s32[14]{0:T(128)} %stack.59.scalars, bf16[1024,2048]{1,0:T(8,128)(2,1)} %get-tuple-element.172.n_ref, bf16[1024,2048]{1,0:T(8,128)(2,1)} %get-tuple-element.173.g_ref, f32[1024,16]{1,0:T(8,128)} %collective-permute-done.25.gates_ref, ...), custom_call_target="tpu_custom_call" | custom-call | flops 16106127360 | bytes 26214400 | tf_op jit(solution)/shard_map/pallas_call | solution.py:48
  487.8 30.0 %shard_map.285 = (bf16[4,3,256,768]{3,2,1,0:T(8,128)(2,1)}, bf16[4,3,256,768]{3,2,1,0:T(8,128)(2,1)}) custom-call(s32[14]{0:T(128)} %stack.59.scalars, bf16[2048,1024]{1,0:T(8,128)(2,1)} %get-tuple-element.192.turned.refs_0_, bf16[2048,1024]{1,0:T(8,128)(2,1)} %get-tuple-element.177.refs_1_, bf16[2048,1024]{1,0:T(8,128)(2,1)} %get-tuple-element.148.g_turned.refs_2_, ...), custom_call_target="tpu_custom_call" | custom-call | flops 19327352832 | bytes 35651584 | tf_op jit(solution)/shard_map/pallas_call | solution.py:48
  524.5 44.5 %collective-permute-done.30.refs_5_ = f32[256,16]{1,0:T(8,128)S(1)} collective-permute-done((f32[256,16]{1,0:T(8,128)S(1)}, f32[256,16]{1,0:T(8,128)S(1)}, u32[]{:S(2)}, u32[]{:S(2)}) %collective-permute-start.30) | collective-permute-done | bytes 16416 | tf_op jit(solution)/shard_map/ppermute | solution.py:68
  581.7 7.7 shard_map.286
  595.9 23.0 %shard_map.287 = (bf16[4,2,256,768]{3,2,1,0:T(8,128)(2,1)}, bf16[4,2,256,768]{3,2,1,0:T(8,128)(2,1)}) custom-call(s32[14]{0:T(128)} %stack.59.scalars, bf16[2048,1024]{1,0:T(8,128)(2,1)} %get-tuple-element.192.turned.refs_0_, bf16[2048,1024]{1,0:T(8,128)(2,1)} %get-tuple-element.177.refs_1_, bf16[2048,1024]{1,0:T(8,128)(2,1)} %get-tuple-element.148.g_turned.refs_2_, ...), custom_call_target="tpu_custom_call" | custom-call | flops 12884901888 | bytes 29360128 | tf_op jit(solution)/shard_map/pallas_call | solution.py:48
  625.4 10.1 collective-permute-done.40
  640.6 27.8 %shard_map.288 = (bf16[1024,512]{1,0:T(8,128)(2,1)}, bf16[1024,512]{1,0:T(8,128)(2,1)}, bf16[1024,512]{1,0:T(8,128)(2,1)}, bf16[1024,512]{1,0:T(8,128)(2,1)}) custom-call(s32[14]{0:T(128)} %stack.59.scalars, bf16[2,1024,256]{2,1,0:T(8,128)(2,1)} %get-tuple-element.146.hidden.refs_0_, bf16[4,1024,256]{2,1,0:T(8,128)(2,1)} %get-tuple-element.152.hidden.refs_1_, ...), custom_call_target="tpu_custom_call" | custom-call | flops 17179869184 | bytes 33554432 | tf_op jit(solution)/shard_map/pallas_call | solution.py:48
  680.0 22.3 %shard_map.290 = (bf16[1024,512]{1,0:T(8,128)(2,1)}, bf16[1024,512]{1,0:T(8,128)(2,1)}, bf16[1024,512]{1,0:T(8,128)(2,1)}, f32[4,2,128]{2,1,0:T(2,128)}) custom-call(s32[14]{0:T(128)} %stack.59.scalars, bf16[1024,512]{1,0:T(8,128)(2,1)} %get-tuple-element.134.q_ref.refs_0_, bf16[1024,512]{1,0:T(8,128)(2,1)} %get-tuple-element.135.k_ref.refs_1_, ...), custom_call_target="tpu_custom_call" | custom-call | flops 5368709120 | bytes 16777216 | tf_op jit(solution)/shard_map/pallas_call | solution.py:48
  732.7 11.7 convolution_convert_fusion
  752.0 256.9 %collective-permute-done.60 = bf16[1,2,256,768]{3,2,1,0:T(8,128)(2,1)} collective-permute-done((bf16[1,2,256,768]{3,2,1,0:T(8,128)(2,1)}, bf16[1,2,256,768]{3,2,1,0:T(8,128)(2,1)}, u32[]{:S(2)}, u32[]{:S(2)}) %collective-permute-start.60) | collective-permute-done | bytes 786464 | tf_op jit(solution)/shard_map/ppermute | solution.py:68
  1013.5 21.3 %collective-permute-done.45 = f32[8,128]{1,0:T(8,128)S(1)} collective-permute-done((f32[8,128]{1,0:T(8,128)S(1)}, f32[8,128]{1,0:T(8,128)S(1)}, u32[]{:S(2)}, u32[]{:S(2)}) %collective-permute-start.45) | collective-permute-done | bytes 4128 | tf_op jit(solution)/shard_map/ppermute | solution.py:68
  1049.7 8.6 all-gather.2
  1065.8 30.6 %collective-permute-start.58 = (bf16[1,3,256,768]{3,2,1,0:T(8,128)(2,1)S(1)}, bf16[1,3,256,768]{3,2,1,0:T(8,128)(2,1)S(1)}, u32[]{:S(2)}, u32[]{:S(2)}) collective-permute-start(bf16[1,3,256,768]{3,2,1,0:T(8,128)(2,1)S(1)} %get-tuple-element.305), channel_id=1, source_target_pairs={{0,8},{4,12},{8,0},{12,4},{16,24},{20,28},{24,16},{28,20},{1,9},{5... | collective-permute-start | bytes 3538952 | tf_op jit(solution)/shard_map/ppermute | solution.py:68
  1097.7 16.8 %collective-permute-done.54 = f32[4,2,128]{2,1,0:T(2,128)S(1)} collective-permute-done((f32[4,2,128]{2,1,0:T(2,128)S(1)}, f32[4,2,128]{2,1,0:T(2,128)S(1)}, u32[]{:S(2)}, u32[]{:S(2)}) %collective-permute-start.54) | collective-permute-done | bytes 4128 | tf_op jit(solution)/shard_map/ppermute | solution.py:68
  1138.2 23.5 %collective-permute-done.51 = f32[1,2048]{1,0:T(1,128)S(1)} collective-permute-done((f32[1,2048]{1,0:T(1,128)S(1)}, f32[1,2048]{1,0:T(1,128)S(1)}, u32[]{:S(2)}, u32[]{:S(2)}) %collective-permute-start.51) | collective-permute-done | bytes 8224 | tf_op jit(solution)/shard_map/ppermute | solution.py:68
  (296 shorter events, 265.6 us)
Async XLA Ops:
  7.2 137.3 %all-gather.5.cloned.1.call-start = ((), (), s32[]{:S(2)}) async-start(), calls=%async_computation.6 | async-start | bytes 8650752 | tf_op jit(solution)/shard_map/all_gather | solution.py:774
  8.9 1040.7 %reduce-scatter.8.cloned.1.call-start = ((), (), s32[]{:S(2)}) async-start(), calls=%async_computation.5 | async-start | bytes 221184 | tf_op jit(solution)/shard_map/reduce_scatter | solution.py:917
  58.2 37.9 %collective-permute-start.9 = (bf16[1024,512]{1,0:T(8,128)(2,1)S(1)}, bf16[1024,512]{1,0:T(8,128)(2,1)S(1)}, u32[]{:S(2)}, u32[]{:S(2)}) collective-permute-start(bf16[1024,512]{1,0:T(8,128)(2,1)S(1)} %copy-done.15), channel_id=1, source_target_pairs={{0,2},{1,3},{2,0},{3,1},{4,6},{5,7},{6,4},{7,5},{8,10},{9,11},{10,... | collective-permute-start | bytes 3145736 | tf_op jit(solution)/shard_map/ppermute | solution.py:68
  59.7 39.1 %collective-permute-start.8 = (bf16[1024,512]{1,0:T(8,128)(2,1)S(1)}, bf16[1024,512]{1,0:T(8,128)(2,1)S(1)}, u32[]{:S(2)}, u32[]{:S(2)}) collective-permute-start(bf16[1024,512]{1,0:T(8,128)(2,1)S(1)} %copy-done.15), channel_id=1, source_target_pairs={{0,1},{1,0},{2,3},{3,2},{4,5},{5,4},{6,7},{7,6},{8,9},{9,8},{10,11... | collective-permute-start | bytes 3145736 | tf_op jit(solution)/shard_map/ppermute | solution.py:68
  97.0 36.4 %collective-permute-start.10 = (bf16[512,512]{1,0:T(8,128)(2,1)}, bf16[512,512]{1,0:T(8,128)(2,1)}, u32[]{:S(2)}, u32[]{:S(2)}) collective-permute-start(bf16[512,512]{1,0:T(8,128)(2,1)} %slice.208), channel_id=1, source_target_pairs={{0,1},{1,0},{2,3},{3,2},{4,5},{5,4},{6,7},{7,6},{8,9},{9,8},{10,11... | collective-permute-start | bytes 1572872 | tf_op jit(solution)/shard_map/ppermute | solution.py:68
  237.7 151.4 %collective-permute-start.13 = (bf16[4,4,256,768]{3,2,1,0:T(8,128)(2,1)}, bf16[4,4,256,768]{3,2,1,0:T(8,128)(2,1)}, u32[]{:S(2)}, u32[]{:S(2)}) collective-permute-start(bf16[4,4,256,768]{3,2,1,0:T(8,128)(2,1)} %get-tuple-element.157), channel_id=1, source_target_pairs={{0,4},{4,0},{8,12},{12,8},{16,20},{20,16},{24,28},{28,24},{1,5},{5... | collective-permute-start | bytes 18874376 | tf_op jit(solution)/shard_map/ppermute | solution.py:68
  239.5 46.2 %collective-permute-start.14 = (bf16[1024,512]{1,0:T(8,128)(2,1)S(1)}, bf16[1024,512]{1,0:T(8,128)(2,1)S(1)}, u32[]{:S(2)}, u32[]{:S(2)}) collective-permute-start(bf16[1024,512]{1,0:T(8,128)(2,1)S(1)} %copy-done.45), channel_id=1, source_target_pairs={{0,8},{4,12},{8,0},{12,4},{16,24},{20,28},{24,16},{28,20},{1,9},{5... | collective-permute-start | bytes 3145736 | tf_op jit(solution)/shard_map/ppermute | solution.py:68
  324.2 133.7 %collective-permute-start.25 = (f32[1024,16]{1,0:T(8,128)}, f32[1024,16]{1,0:T(8,128)}, u32[]{:S(2)}, u32[]{:S(2)}) collective-permute-start(f32[1024,16]{1,0:T(8,128)} %get-tuple-element.145.gates_ref), channel_id=1, source_target_pairs={{0,8},{4,12},{8,0},{12,4},{16,24},{20,28},{24,16},{28,20},{1,9},{5... | collective-permute-start | bytes 196616 | tf_op jit(solution)/shard_map/ppermute | solution.py:68
  333.7 61.5 %collective-permute-start.16 = (bf16[2,2,256,768]{3,2,1,0:T(8,128)(2,1)}, bf16[2,2,256,768]{3,2,1,0:T(8,128)(2,1)}, u32[]{:S(2)}, u32[]{:S(2)}) collective-permute-start(bf16[2,2,256,768]{3,2,1,0:T(8,128)(2,1)} %get-tuple-element.303), channel_id=1, source_target_pairs={{0,8},{4,12},{8,0},{12,4},{16,24},{20,28},{24,16},{28,20},{1,9},{5... | collective-permute-start | bytes 4718600 | tf_op jit(solution)/shard_map/ppermute | solution.py:68
  394.6 88.9 %collective-permute-start.26 = (bf16[2,4,256,768]{3,2,1,0:T(8,128)(2,1)S(1)}, bf16[2,4,256,768]{3,2,1,0:T(8,128)(2,1)}, u32[]{:S(2)}, u32[]{:S(2)}) collective-permute-start(bf16[2,4,256,768]{3,2,1,0:T(8,128)(2,1)S(1)} %get-tuple-element.295), channel_id=1, source_target_pairs={{0,8},{4,12},{8,0},{12,4},{16,24},{20,28},{24,16},{28,20},{1,9},{5... | collective-permute-start | bytes 9437192 | tf_op jit(solution)/shard_map/ppermute | solution.py:68
  517.8 74.1 %collective-permute-start.33 = (bf16[4,3,256,768]{3,2,1,0:T(8,128)(2,1)}, bf16[4,3,256,768]{3,2,1,0:T(8,128)(2,1)}, u32[]{:S(2)}, u32[]{:S(2)}) collective-permute-start(bf16[4,3,256,768]{3,2,1,0:T(8,128)(2,1)} %get-tuple-element.180), channel_id=1, source_target_pairs={{0,4},{4,0},{8,12},{12,8},{16,20},{20,16},{24,28},{28,24},{1,5},{5... | collective-permute-start | bytes 14155784 | tf_op jit(solution)/shard_map/ppermute | solution.py:68
  517.9 62.0 %collective-permute-start.27 = (bf16[256,2048]{1,0:T(8,128)(2,1)}, bf16[256,2048]{1,0:T(8,128)(2,1)S(1)}, u32[]{:S(2)}, u32[]{:S(2)}) collective-permute-start(bf16[256,2048]{1,0:T(8,128)(2,1)} %get-tuple-element.182), channel_id=1, source_target_pairs={{0,1},{1,0},{2,3},{3,2},{4,5},{5,4},{6,7},{7,6},{8,9},{9,8},{10,11... | collective-permute-start | bytes 3145736 | tf_op jit(solution)/shard_map/ppermute | solution.py:68
  518.9 61.1 %collective-permute-start.28 = (bf16[256,2048]{1,0:T(8,128)(2,1)}, bf16[256,2048]{1,0:T(8,128)(2,1)S(1)}, u32[]{:S(2)}, u32[]{:S(2)}) collective-permute-start(bf16[256,2048]{1,0:T(8,128)(2,1)} %get-tuple-element.183), channel_id=1, source_target_pairs={{0,2},{1,3},{2,0},{3,1},{4,6},{5,7},{6,4},{7,5},{8,10},{9,11},{10,... | collective-permute-start | bytes 3145736 | tf_op jit(solution)/shard_map/ppermute | solution.py:68
  520.6 59.4 %collective-permute-start.29 = (bf16[256,2048]{1,0:T(8,128)(2,1)}, bf16[256,2048]{1,0:T(8,128)(2,1)S(1)}, u32[]{:S(2)}, u32[]{:S(2)}) collective-permute-start(bf16[256,2048]{1,0:T(8,128)(2,1)} %get-tuple-element.184), channel_id=1, source_target_pairs={{0,3},{1,2},{2,1},{3,0},{4,7},{5,6},{6,5},{7,4},{8,11},{9,10},{10,... | collective-permute-start | bytes 3145736 | tf_op jit(solution)/shard_map/ppermute | solution.py:68
  523.6 45.4 %collective-permute-start.30 = (f32[256,16]{1,0:T(8,128)S(1)}, f32[256,16]{1,0:T(8,128)S(1)}, u32[]{:S(2)}, u32[]{:S(2)}) collective-permute-start(f32[256,16]{1,0:T(8,128)S(1)} %get-tuple-element.315), channel_id=1, source_target_pairs={{0,1},{1,0},{2,3},{3,2},{4,5},{5,4},{6,7},{7,6},{8,9},{9,8},{10,11... | collective-permute-start | bytes 49160 | tf_op jit(solution)/shard_map/ppermute | solution.py:68
  618.9 49.6 %collective-permute-start.37 = (bf16[4,2,256,768]{3,2,1,0:T(8,128)(2,1)}, bf16[4,2,256,768]{3,2,1,0:T(8,128)(2,1)}, u32[]{:S(2)}, u32[]{:S(2)}) collective-permute-start(bf16[4,2,256,768]{3,2,1,0:T(8,128)(2,1)} %get-tuple-element.193), channel_id=1, source_target_pairs={{0,4},{4,0},{8,12},{12,8},{16,20},{20,16},{24,28},{28,24},{1,5},{5... | collective-permute-start | bytes 9437192 | tf_op jit(solution)/shard_map/ppermute | solution.py:68
  625.3 557.1 %reduce-scatter.6.cloned.1.call-start = ((), (), s32[]{:S(2)}) async-start(), calls=%async_computation.4 | async-start | bytes 2359296 | tf_op jit(solution)/shard_map/reduce_scatter | solution.py:884
  706.0 478.2 %reduce-scatter.4.cloned.1.call-start = ((), (), s32[]{:S(2)}) async-start(), calls=%async_computation.3 | async-start | bytes 7077888 | tf_op jit(solution)/shard_map/reduce_scatter | solution.py:884
  744.4 264.5 %collective-permute-start.59 = (bf16[1,4,256,768]{3,2,1,0:T(8,128)(2,1)}, bf16[1,4,256,768]{3,2,1,0:T(8,128)(2,1)}, u32[]{:S(2)}, u32[]{:S(2)}) collective-permute-start(bf16[1,4,256,768]{3,2,1,0:T(8,128)(2,1)} %get-tuple-element.299), channel_id=1, source_target_pairs={{0,16},{4,20},{8,24},{12,28},{16,0},{20,4},{24,8},{28,12},{1,17},{... | collective-permute-start | bytes 4718600 | tf_op jit(solution)/shard_map/ppermute | solution.py:68
  747.1 314.7 %collective-permute-start.57 = (bf16[2,3,256,768]{3,2,1,0:T(8,128)(2,1)}, bf16[2,3,256,768]{3,2,1,0:T(8,128)(2,1)}, u32[]{:S(2)}, u32[]{:S(2)}) collective-permute-start(bf16[2,3,256,768]{3,2,1,0:T(8,128)(2,1)} %get-tuple-element.297), channel_id=1, source_target_pairs={{0,16},{4,20},{8,24},{12,28},{16,0},{20,4},{24,8},{28,12},{1,17},{... | collective-permute-start | bytes 7077896 | tf_op jit(solution)/shard_map/ppermute | solution.py:68
  747.4 261.5 %collective-permute-start.60 = (bf16[1,2,256,768]{3,2,1,0:T(8,128)(2,1)}, bf16[1,2,256,768]{3,2,1,0:T(8,128)(2,1)}, u32[]{:S(2)}, u32[]{:S(2)}) collective-permute-start(bf16[1,2,256,768]{3,2,1,0:T(8,128)(2,1)} %get-tuple-element.307), channel_id=1, source_target_pairs={{0,16},{4,20},{8,24},{12,28},{16,0},{20,4},{24,8},{28,12},{1,17},{... | collective-permute-start | bytes 2359304 | tf_op jit(solution)/shard_map/ppermute | solution.py:68
  750.0 309.4 %collective-permute-start.34 = (bf16[1024,512]{1,0:T(8,128)(2,1)}, bf16[1024,512]{1,0:T(8,128)(2,1)}, u32[]{:S(2)}, u32[]{:S(2)}) collective-permute-start(bf16[1024,512]{1,0:T(8,128)(2,1)} %get-tuple-element.196), channel_id=1, source_target_pairs={{0,1},{1,0},{2,3},{3,2},{4,5},{5,4},{6,7},{7,6},{8,9},{9,8},{10,11... | collective-permute-start | bytes 3145736 | tf_op jit(solution)/shard_map/ppermute | solution.py:68
  751.7 309.2 %collective-permute-start.35 = (bf16[1024,512]{1,0:T(8,128)(2,1)}, bf16[1024,512]{1,0:T(8,128)(2,1)}, u32[]{:S(2)}, u32[]{:S(2)}) collective-permute-start(bf16[1024,512]{1,0:T(8,128)(2,1)} %get-tuple-element.197), channel_id=1, source_target_pairs={{0,2},{1,3},{2,0},{3,1},{4,6},{5,7},{6,4},{7,5},{8,10},{9,11},{10,... | collective-permute-start | bytes 3145736 | tf_op jit(solution)/shard_map/ppermute | solution.py:68
  1009.0 56.8 %collective-permute-start.36 = (bf16[1024,512]{1,0:T(8,128)(2,1)}, bf16[1024,512]{1,0:T(8,128)(2,1)}, u32[]{:S(2)}, u32[]{:S(2)}) collective-permute-start(bf16[1024,512]{1,0:T(8,128)(2,1)} %get-tuple-element.198), channel_id=1, source_target_pairs={{0,3},{1,2},{2,1},{3,0},{4,7},{5,6},{6,5},{7,4},{8,11},{9,10},{10,... | collective-permute-start | bytes 3145736 | tf_op jit(solution)/shard_map/ppermute | solution.py:68
  1046.6 87.4 %collective-permute-start.55 = (bf16[2,2,256,768]{3,2,1,0:T(8,128)(2,1)}, bf16[2,2,256,768]{3,2,1,0:T(8,128)(2,1)}, u32[]{:S(2)}, u32[]{:S(2)}) collective-permute-start(bf16[2,2,256,768]{3,2,1,0:T(8,128)(2,1)} %get-tuple-element.301), channel_id=1, source_target_pairs={{0,16},{4,20},{8,24},{12,28},{16,0},{20,4},{24,8},{28,12},{1,17},{... | collective-permute-start | bytes 4718600 | tf_op jit(solution)/shard_map/ppermute | solution.py:68
  1059.4 37.0 %collective-permute-start.46 = (f32[8,128]{1,0:T(8,128)S(1)}, f32[8,128]{1,0:T(8,128)S(1)}, u32[]{:S(2)}, u32[]{:S(2)}) collective-permute-start(f32[8,128]{1,0:T(8,128)S(1)} %bitcast_add_fusion), channel_id=1, source_target_pairs={{0,2},{1,3},{2,0},{3,1},{4,6},{5,7},{6,4},{7,5},{8,10},{9,11},{10,... | collective-permute-start | bytes 12296 | tf_op jit(solution)/shard_map/ppermute | solution.py:68
  1060.9 53.6 %collective-permute-start.54 = (f32[4,2,128]{2,1,0:T(2,128)S(1)}, f32[4,2,128]{2,1,0:T(2,128)S(1)}, u32[]{:S(2)}, u32[]{:S(2)}) collective-permute-start(f32[4,2,128]{2,1,0:T(2,128)S(1)} %add.204), channel_id=1, source_target_pairs={{0,16},{4,20},{8,24},{12,28},{16,0},{20,4},{24,8},{28,12},{1,17},{... | collective-permute-start | bytes 12296 | tf_op jit(solution)/shard_map/ppermute | solution.py:68
  1061.8 54.3 %collective-permute-start.50 = (f32[1,2048]{1,0:T(1,128)S(1)}, f32[1,2048]{1,0:T(1,128)S(1)}, u32[]{:S(2)}, u32[]{:S(2)}) collective-permute-start(f32[1,2048]{1,0:T(1,128)S(1)} %add.199), channel_id=1, source_target_pairs={{0,1},{1,0},{2,3},{3,2},{4,5},{5,4},{6,7},{7,6},{8,9},{9,8},{10,11... | collective-permute-start | bytes 24584 | tf_op jit(solution)/shard_map/ppermute | solution.py:68
  1065.8 97.1 %collective-permute-start.58 = (bf16[1,3,256,768]{3,2,1,0:T(8,128)(2,1)S(1)}, bf16[1,3,256,768]{3,2,1,0:T(8,128)(2,1)S(1)}, u32[]{:S(2)}, u32[]{:S(2)}) collective-permute-start(bf16[1,3,256,768]{3,2,1,0:T(8,128)(2,1)S(1)} %get-tuple-element.305), channel_id=1, source_target_pairs={{0,8},{4,12},{8,0},{12,4},{16,24},{20,28},{24,16},{28,20},{1,9},{5... | collective-permute-start | bytes 3538952 | tf_op jit(solution)/shard_map/ppermute | solution.py:68
  1096.4 71.7 %collective-permute-start.42 = (bf16[1024,512]{1,0:T(8,128)(2,1)}, bf16[1024,512]{1,0:T(8,128)(2,1)S(1)}, u32[]{:S(2)}, u32[]{:S(2)}) collective-permute-start(bf16[1024,512]{1,0:T(8,128)(2,1)} %get-tuple-element.216), channel_id=1, source_target_pairs={{0,1},{1,0},{2,3},{3,2},{4,5},{5,4},{6,7},{7,6},{8,9},{9,8},{10,11... | collective-permute-start | bytes 3145736 | tf_op jit(solution)/shard_map/ppermute | solution.py:68
  1114.5 53.6 %collective-permute-start.43 = (bf16[1024,512]{1,0:T(8,128)(2,1)}, bf16[1024,512]{1,0:T(8,128)(2,1)S(1)}, u32[]{:S(2)}, u32[]{:S(2)}) collective-permute-start(bf16[1024,512]{1,0:T(8,128)(2,1)} %get-tuple-element.214), channel_id=1, source_target_pairs={{0,2},{1,3},{2,0},{3,1},{4,6},{5,7},{6,4},{7,5},{8,10},{9,11},{10,... | collective-permute-start | bytes 3145736 | tf_op jit(solution)/shard_map/ppermute | solution.py:68
  1116.1 52.1 %collective-permute-start.44 = (bf16[1024,512]{1,0:T(8,128)(2,1)}, bf16[1024,512]{1,0:T(8,128)(2,1)S(1)}, u32[]{:S(2)}, u32[]{:S(2)}) collective-permute-start(bf16[1024,512]{1,0:T(8,128)(2,1)} %get-tuple-element.212), channel_id=1, source_target_pairs={{0,3},{1,2},{2,1},{3,0},{4,7},{5,6},{6,5},{7,4},{8,11},{9,10},{10,... | collective-permute-start | bytes 3145736 | tf_op jit(solution)/shard_map/ppermute | solution.py:68
  (81 other events, 2362.7 us)
Sparse Core Ops, SparseCore 0:
  10.9 102.5 all-gather.4
  625.4 31.6 reduce-scatter.7
  706.1 36.0 reduce-scatter.5
  744.5 194.2 reduce-scatter.3

commit v3 on v1

v3 whole, which is shorter than its diff:
```python
import functools
import math

import jax
import jax.numpy as jnp
import numpy as np
from jax import lax
from jax.experimental import pallas as pl
from jax.experimental.pallas import tpu as pltpu
from jax.sharding import PartitionSpec as P

LEN = 1024
EPS = 1e-05
ROPE_BASE = 10000.0
VMEM_LIMIT = 56 << 20
TB = 256
MARKS = 4
HEAVY = 10**12
f32, bf16 = jnp.float32, jnp.bfloat16
NT = (((1,), (1,)), ((), ()))
TN = (((0,), (0,)), ((), ()))
NN = (((1,), (0,)), ((), ()))


def dot(left, right, dims=NN):
    return lax.dot_general(left, right, dims, preferred_element_type=f32)


def rope_constants(length, width):
    inv_freq = (ROPE_BASE ** (-(np.arange(width // 2, dtype=np.float32) * 2.0) / width)).astype(np.float32)
    angles = np.arange(length, dtype=np.float32)[:, None] * inv_freq[None, :]
    cosine, sine = np.cos(angles).astype(np.float32), np.sin(angles).astype(np.float32)
    return np.concatenate([cosine, cosine], axis=1), np.concatenate([-sine, sine], axis=1)


def bit_reverse(value, count):
    result, bit = 0, 1
    while bit < count:
        result = result * 2 + (value & 1)
        value >>= 1
        bit *= 2
    return result


def whole_spec():
    return pl.BlockSpec(memory_space=pltpu.VMEM)


class Line:
    def __init__(self):
        self.last = []

    def tick(self, axis, count):
        self.sent = swap(self.last[0], axis, count, 1)

    def take(self):
        self.last = [*self.last, self.sent]

    def pin(self, value):
        return lax.optimization_barrier((value, *self.last))[0]


line = Line()


def call(body, grid, scalars, ins, in_specs, outs, out_specs, scratch=(), aliases=None):
    deps, n_in, n_out = line.last, len(ins), len(outs)

    def without_deps(scalars, *refs):
        ins_outs = refs[len(deps) : n_in + n_out + len(deps)]
        body(scalars, *ins_outs, *refs[n_in + n_out + len(deps) + MARKS :])

    outs, out_specs = list(outs), list(out_specs)
    any_place = pl.BlockSpec(memory_space=pl.ANY)

    result = pl.pallas_call(
        without_deps,
        out_shape=outs + [struct((8, 128), f32)] * MARKS,
        grid_spec=pltpu.PrefetchScalarGridSpec(
            num_scalar_prefetch=1,
            grid=grid,
            in_specs=[any_place] * len(deps) + list(in_specs),
            out_specs=out_specs + [any_place] * MARKS,
            scratch_shapes=list(scratch),
        ),
        input_output_aliases={1 + len(deps) + k: v for k, v in (aliases or {}).items()},
        compiler_params=pltpu.CompilerParams(vmem_limit_bytes=VMEM_LIMIT),
        cost_estimate=pl.CostEstimate(flops=HEAVY, bytes_accessed=1, transcendentals=0),
    )(scalars, *deps, *ins)
    line.last = result[len(outs) :]
    return result[: len(outs)]


def struct(shape, dtype):
    return jax.ShapeDtypeStruct(shape, dtype)


def swap(value, axis, count, mask):
    return lax.ppermute(value, axis, [(i, i ^ mask) for i in range(count)])


def gather_pieces(value, axis, count, pin=lambda v: v):
    if count == 4:
        half = value.shape[0] // 2
        one, two = swap(value, axis, count, 1), swap(value, axis, count, 2)
        one, two = pin((one, two))
        top, bottom = swap(two[:half], axis, count, 1), swap(one[half:], axis, count, 2)
        return [value, one, two, (top, bottom)]
    pieces, mask = [value], 1
    while mask < count:
        pieces = pieces + [swap(piece, axis, count, mask) for piece in pieces]
        mask *= 2
    return pieces


def direct_pieces(value, axis, count):
    return [value] + [swap(value, axis, count, r) for r in range(1, count)]


def flat(pieces):
    return [part for piece in pieces for part in (piece if isinstance(piece, tuple) else (piece,))]


def piece_specs(pieces, block, width):
    specs = []
    for piece in pieces:
        if isinstance(piece, tuple):
            count = piece[0].shape[0] // block
            specs.append(pl.BlockSpec((block, width), lambda i, s, n=count: (jnp.minimum(i, n - 1), 0)))
            specs.append(pl.BlockSpec((block, width), lambda i, s, n=count: (jnp.maximum(i - n, 0), 0)))
        else:
            specs.append(pl.BlockSpec((block, width), lambda i, s: (i, 0)))
    return specs


def read_pieces(refs, n_tp):
    values = [ref[...] for ref in refs]
    if len(refs) == n_tp:
        return values
    early = pl.program_id(0) < pl.num_programs(0) // 2
    return values[: n_tp - 1] + [jnp.where(early, values[n_tp - 1], values[n_tp])]


def trade(pieces, axis):
    return lax.all_to_all(pieces, axis, 0, 0, tiled=True)


def halves_kernel(scalars, keep, keep2, arrived, arrived2, keep_out, send_out):
    keep_out[...] = (keep[...].astype(f32) + arrived[...].astype(f32)).astype(bf16)
    send_out[...] = (keep2[...].astype(f32) + arrived2[...].astype(f32)).astype(bf16)


def add_halves(scalars, keep, arrived):
    blocks, count, rows, width = keep.shape
    half = blocks // 2
    low = pl.BlockSpec((half, 1, rows, width), lambda i, s: (0, i, 0, 0))
    high = pl.BlockSpec((half, 1, rows, width), lambda i, s: (1, i, 0, 0))
    out = struct((half, count, rows, width), bf16)
    return call(halves_kernel, (count,), scalars, [keep, keep, arrived, arrived], [low, high] * 2, [out] * 2, [low] * 2)


def sum_kernel(scalars, left, right, out):
    out[...] = left[...] + right[...]


def add_to(scalars, left, right):
    whole = pl.BlockSpec(left.shape, lambda i, s: (0, 0))
    return call(sum_kernel, (1,), scalars, [left, right], [whole] * 2, [struct(left.shape, f32)], [whole])[0]


def two_terms(value, width):
    high = value.astype(bf16)
    low = (value - high.astype(f32)).astype(bf16)
    rest = jnp.zeros((value.shape[0], width - 2 * value.shape[1]), bf16)
    return jnp.concatenate([high, low, rest], axis=1)


def transpose_blocks(scalars, first, source, target, dp_count):
    width = source.shape[1] // dp_count
    for place in range(dp_count):
        cols = pl.ds(pl.multiple_of(scalars[first + place] * width, width), width)
        target[place * width : (place + 1) * width, :] = source[:, cols].T


def project_kernel(n_tp, n_in, heads, scalars, *refs):
    pieces = read_pieces(refs[:n_in], n_tp)
    gain, wq, wk, wv, q_gain, k_gain, cosine, sine = refs[n_in : n_in + 8]
    x_out, normed_out, factor_out, q_raw, k_raw, q_rot, k_rot, v_out = refs[n_in + 8 :]
    width = pieces[0].shape[1]
    features = width * n_tp
    values = [piece.astype(f32) for piece in pieces]
    squares = sum(jnp.sum(value * value, axis=1, keepdims=True) for value in values)
    factor = lax.rsqrt(squares / features + EPS)
    factor_out[...] = factor
    for r in range(n_tp):
        cols = pl.ds(pl.multiple_of(scalars[r] * width, width), width)
        x_out[:, cols] = pieces[r]
        normed_out[:, cols] = (values[r] * factor * gain[:, cols]).astype(bf16)
    normed = normed_out[...]
    cos, sin = cosine[...], sine[...]
    hd = cos.shape[1]
    for weight, head_gain, raw, rotated in ((wq, q_gain, q_raw, q_rot), (wk, k_gain, k_raw, k_rot)):
        product = dot(normed, weight[...])
        raw[...] = product
        for h in range(heads):
            part = product[:, h * hd : (h + 1) * hd]
            scale = lax.rsqrt(jnp.mean(part * part, axis=1, keepdims=True) + EPS)
            part = part * scale * head_gain[h : h + 1, :]
            part = part * cos + pltpu.roll(part, hd // 2, 1) * sin
            rotated[:, h * hd : (h + 1) * hd] = part.astype(bf16)
    v_out[...] = dot(normed, wv[...]).astype(bf16)


def project(scalars, pieces, gain, wq, wk, wv, q_gain, k_gain, cosine, sine):
    n_tp = len(pieces)
    tokens, width = pieces[0].shape
    features = width * n_tp
    heads, hd = q_gain.shape
    local = heads * hd
    rows = lambda w: pl.BlockSpec((TB, w), lambda i, s: (i, 0))
    return call(
        functools.partial(project_kernel, n_tp, len(flat(pieces)), heads),
        (tokens // TB,),
        scalars,
        [*flat(pieces), gain, wq, wk, wv, q_gain, k_gain, cosine, sine],
        piece_specs(pieces, TB, width) + [whole_spec()] * 6 + [rows(hd)] * 2,
        [
            struct((tokens, features), bf16),
            struct((tokens, features), bf16),
            struct((tokens, 1), f32),
            struct((tokens, local), f32),
            struct((tokens, local), f32),
            struct((tokens, local), bf16),
            struct((tokens, local), bf16),
            struct((tokens, local), bf16),
        ],
        [rows(features), rows(features), rows(1)] + [rows(local)] * 5,
    )


def attend_kernel(block, scalars, q_ref, k_ref, v_ref, out_ref, total_ref):
    tokens, hd = q_ref.shape
    scale = 1.0 / math.sqrt(hd)
    for i in range(tokens // block):
        rows = slice(i * block, (i + 1) * block)
        reach = (i + 1) * block
        scores = dot(q_ref[rows, :], k_ref[:reach, :], NT) * scale
        at_row = i * block + lax.broadcasted_iota(jnp.int32, scores.shape, 0)
        at_col = lax.broadcasted_iota(jnp.int32, scores.shape, 1)
        scores = jnp.where(at_row >= at_col, scores, -1e30)
        top = jnp.max(scores, axis=1, keepdims=True)
        weights = jnp.exp(scores - top)
        total = jnp.sum(weights, axis=1, keepdims=True)
        probs = (weights * (1.0 / total)).astype(bf16)
        out_ref[rows, :] = dot(probs, v_ref[:reach, :]).astype(bf16)
        total_ref[0, rows, :] = top + jnp.log(total)


def attend(scalars, q_rot, k_rot, value, heads):
    tokens, local = q_rot.shape
    hd = local // heads
    column = pl.BlockSpec((tokens, hd), lambda h, s: (0, h))
    return call(
        functools.partial(attend_kernel, min(256, tokens)),
        (heads,),
        scalars,
        [q_rot, k_rot, value],
        [column] * 3,
        [struct((tokens, local), bf16), struct((heads, tokens, 1), f32)],
        [column, pl.BlockSpec((1, tokens, 1), lambda h, s: (h, 0, 0))],
    )


def attend_back_kernel(block, scalars, *refs):
    (q_ref, k_ref, v_ref, go_ref, total_ref, q_raw, k_raw, q_gain, k_gain, cosine, sine) = refs[:11]
    grads_out, dgain_out, dq_acc, dk_acc, dv_acc = refs[11:]
    tokens, hd = q_ref.shape
    scale = 1.0 / math.sqrt(hd)
    count = tokens // block
    for i in reversed(range(count)):
        rows = slice(i * block, (i + 1) * block)
        reach = (i + 1) * block
        query, grad = q_ref[rows, :], go_ref[rows, :]
        scores = dot(query, k_ref[:reach, :], NT) * scale
        at_row = i * block + lax.broadcasted_iota(jnp.int32, scores.shape, 0)
        at_col = lax.broadcasted_iota(jnp.int32, scores.shape, 1)
        scores = jnp.where(at_row >= at_col, scores, -1e30)
        probs = jnp.exp(scores - total_ref[0, rows, :])
        dprobs = dot(grad, v_ref[:reach, :], NT)
        delta = jnp.sum(dprobs * probs, axis=1, keepdims=True)
        dscores = (probs * (dprobs - delta)).astype(bf16)
        dq_acc[rows, :] = dot(dscores, k_ref[:reach, :]) * scale
        dk = dot(dscores, query, TN) * scale
        dv = dot(probs.astype(bf16), grad, TN)
        if i == count - 1:
            dk_acc[...] = dk
            dv_acc[...] = dv
        else:
            dk_acc[:reach, :] += dk
            dv_acc[:reach, :] += dv
    grads_out[2] = dv_acc[...].astype(bf16)
    cos, sin = cosine[...], sine[...]
    dgains = []
    for j, acc, raw_ref, gain_ref in ((0, dq_acc, q_raw, q_gain), (1, dk_acc, k_raw, k_gain)):
        grad = acc[...]
        grad = grad * cos - pltpu.roll(grad, hd // 2, 1) * sin
        raw = raw_ref[...]
        factor = lax.rsqrt(jnp.mean(raw * raw, axis=1, keepdims=True) + EPS)
        normal = raw * factor
        dgains.append(jnp.sum(grad * normal, axis=0, keepdims=True))
        scaled = grad * gain_ref[0]
        mean = jnp.mean(scaled * normal, axis=1, keepdims=True)
        grads_out[j] = (factor * (scaled - normal * mean)).astype(bf16)
    dgain_out[0] = jnp.concatenate(dgains, axis=0)


def attend_back(scalars, q_rot, k_rot, value, grad, totals, q_raw, k_raw, q_gain, k_gain, cosine, sine):
    tokens, local = q_rot.shape
    heads, hd = q_gain.shape
    column = pl.BlockSpec((tokens, hd), lambda h, s: (0, h))
    gain_spec = pl.BlockSpec((1, 1, hd), lambda h, s: (h, 0, 0))
    table = pl.BlockSpec((tokens, hd), lambda h, s: (0, 0))
    return call(
        functools.partial(attend_back_kernel, min(256, tokens)),
        (heads,),
        scalars,
        [q_rot, k_rot, value, grad, totals, q_raw, k_raw, q_gain[:, None, :], k_gain[:, None, :], cosine, sine],
        [column] * 4
        + [pl.BlockSpec((1, tokens, 1), lambda h, s: (h, 0, 0))]
        + [column] * 2
        + [gain_spec] * 2
        + [table] * 2,
        [struct((3, tokens, local), bf16), struct((heads, 2, hd), f32)],
        [
            pl.BlockSpec((3, tokens, hd), lambda h, s: (0, 0, h)),
            pl.BlockSpec((1, 2, hd), lambda h, s: (h, 0, 0)),
        ],
        [pltpu.VMEM((tokens, hd), f32)] * 3,
    )


def whole_grad_kernel(n_tp, n_in, dp_count, scalars, *refs):
    pieces = read_pieces(refs[:n_in], n_tp)
    whole_out, turned_out = refs[n_in:]
    width = pieces[0].shape[1]
    for r in range(n_tp):
        cols = pl.ds(pl.multiple_of(scalars[r] * width, width), width)
        whole_out[:, cols] = pieces[r]
    transpose_blocks(scalars, n_tp, whole_out, turned_out, dp_count)


def whole_grad(scalars, pieces, dp_count):
    n_tp = len(pieces)
    tokens, width = pieces[0].shape
    features = width * n_tp
    return call(
        functools.partial(whole_grad_kernel, n_tp, len(flat(pieces)), dp_count),
        (tokens // TB,),
        scalars,
        flat(pieces),
        piece_specs(pieces, TB, width),
        [struct((tokens, features), bf16), struct((features, tokens), bf16)],
        [
            pl.BlockSpec((TB, features), lambda i, s: (i, 0)),
            pl.BlockSpec((features, TB), lambda i, s: (0, i)),
        ],
    )


def stream_kernel(n_tp, n_in, dp_count, scalars, *refs):
    pieces = read_pieces(refs[:n_in], n_tp)
    x_ref, w_ref, gain, router, kept = refs[n_in : n_in + 5]
    stream_out, normed_out, mine_out, turned_out, factor_out, probs_out, gates_out = refs[n_in + 5 :]
    width = pieces[0].shape[1]
    total = x_ref[...].astype(f32)
    for r in range(n_tp):
        weight = w_ref[:, pl.ds(scalars[r], 1)]
        total += dot(pieces[r], weight.reshape(width, weight.shape[-1]))
    stream_out[...] = total
    factor = lax.rsqrt(jnp.mean(total * total, axis=1, keepdims=True) + EPS)
    factor_out[...] = factor
    normed = (total * factor * gain[...]).astype(bf16)
    normed_out[...] = normed
    mine_out[:, :width] = normed_out[:, pl.ds(pl.multiple_of(scalars[0] * width, width), width)]
    logits = dot(normed, router[...])
    power = jnp.exp(logits - jnp.max(logits, axis=1, keepdims=True))
    probs = power / jnp.sum(power, axis=1, keepdims=True)
    probs_out[...] = probs
    gates = probs * kept[...]
    gates_out[...] = gates
    mine_out[:, width:] = two_terms(gates, mine_out.shape[1] - width)
    transpose_blocks(scalars, n_tp, normed_out, turned_out, dp_count)


def stream_of(scalars, pieces, x, w_all, gain, router, kept, dp_count):
    n_tp = len(pieces)
    tokens, features = x.shape
    experts = router.shape[1]
    rows = lambda w: pl.BlockSpec((TB, w), lambda i, s: (i, 0))
    return call(
        functools.partial(stream_kernel, n_tp, len(flat(pieces)), dp_count),
        (tokens // TB,),
        scalars,
        [*flat(pieces), x, w_all, gain, router, kept],
        piece_specs(pieces, TB, pieces[0].shape[1]) + [rows(features)] + [whole_spec()] * 3 + [rows(experts)],
        [
            struct((tokens, features), f32),
            struct((tokens, features), bf16),
            struct((tokens, features // n_tp + 128), bf16),
            struct((features, tokens), bf16),
            struct((tokens, 1), f32),
            struct((tokens, experts), f32),
            struct((tokens, experts), f32),
        ],
        [
            rows(features),
            rows(features),
            rows(features // n_tp + 128),
            pl.BlockSpec((features, TB), lambda i, s: (0, i)),
            rows(1),
            rows(experts),
            rows(experts),
        ],
    )


def expert_kernel(first, shift, scalars, n_ref, g_ref, gates_ref, wg, wu, wd, hidden_out, pair_out, dgate_out):
    step = pl.program_id(0)
    expert = first + step + (0 if shift is None else scalars[shift])
    width = wg.shape[-1]

    @pl.when(step == 0)
    def _():
        dgate_out[...] = jnp.zeros_like(dgate_out)

    gate_val, up_val = dot(n_ref[...], wg[0]), dot(n_ref[...], wu[0])
    back = dot(g_ref[...], wd[0], NT)
    gates = gates_ref[...]
    here = lax.broadcasted_iota(jnp.int32, gates.shape, 1) == expert
    gate = jnp.sum(jnp.where(here, gates, 0.0), axis=1, keepdims=True)
    sigmoid = 1.0 / (1.0 + jnp.exp(-gate_val))
    swish = gate_val * sigmoid
    hidden = (swish * up_val).astype(bf16).astype(f32)
    hidden_out[0] = (hidden * gate).astype(bf16)
    dgate = jnp.sum(back * hidden, axis=1, keepdims=True)
    dgate_out[...] = jnp.where(here, dgate, dgate_out[...])
    dhidden = back * gate
    pair_out[0, :, :width] = (dhidden * up_val * sigmoid * (1.0 + gate_val * (1.0 - sigmoid))).astype(bf16)
    pair_out[0, :, width:] = (dhidden * swish).astype(bf16)


def run_experts(scalars, normed, grad, gates, wg, wu, wd, first, count, shift=None):
    tokens, features = normed.shape
    experts, _, width = wg.shape
    place = lambda i, s: first + i + (0 if shift is None else s[shift])
    weight = lambda shape: pl.BlockSpec((1, *shape), lambda i, s: (place(i, s), 0, 0))
    given = lambda shape: pl.BlockSpec((1, *shape), lambda i, s: (i, 0, 0))
    return call(
        functools.partial(expert_kernel, first, shift),
        (count,),
        scalars,
        [normed, grad, gates, wg, wu, wd],
        [whole_spec()] * 3 + [weight((features, width))] * 2 + [weight((width, features))],
        [
            struct((count, tokens, width), bf16),
            struct((count, tokens, 2 * width), bf16),
            struct((tokens, experts), f32),
        ],
        [
            given((tokens, width)),
            given((tokens, 2 * width)),
            pl.BlockSpec((tokens, experts), lambda i, s: (0, 0)),
        ],
    )


def weight_grads_kernel(scalars, turned, g_turned, hidden, pair, keep_out, send_out):
    half, _, rows, _ = keep_out.shape
    width = hidden.shape[-1]
    first = dot(turned[...], pair[0]).astype(bf16).reshape(2 * half, rows, 2 * width)
    keep_out[:, 0, :, : 2 * width] = first[:half]
    send_out[:, 0, :, : 2 * width] = first[half:]
    second = dot(g_turned[...], hidden[0]).astype(bf16).reshape(2 * half, rows, width)
    keep_out[:, 0, :, 2 * width :] = second[:half]
    send_out[:, 0, :, 2 * width :] = second[half:]


def weight_grads(scalars, turned, g_turned, hidden, pair, offset, count, dp_count):
    features, tokens = turned.shape
    width = hidden.shape[-1]
    half, rows = dp_count // 2, features // dp_count
    out = struct((half, count, rows, 3 * width), bf16)
    out_spec = pl.BlockSpec((half, 1, rows, 3 * width), lambda i, s: (0, i, 0, 0))
    return call(
        weight_grads_kernel,
        (count,),
        scalars,
        [turned, g_turned, hidden, pair],
        [
            whole_spec(),
            whole_spec(),
            pl.BlockSpec((1, tokens, width), lambda i, s: (offset + i, 0, 0)),
            pl.BlockSpec((1, tokens, 2 * width), lambda i, s: (offset + i, 0, 0)),
        ],
        [out, out],
        [out_spec, out_spec],
    )


def inner_swap(index):
    return (index & ~3) | ((index & 1) << 1) | ((index >> 1) & 1)


def shared_grads_kernel(shift, scalars, *refs):
    turned, turned2, g_turned, g_turned2, hidden_a, hidden_b, hidden2, pair_a, pair_b, pair2 = refs[:10]
    keep_out, send_out = refs[10:]
    here = scalars[shift] == 0
    hidden = jnp.where(here, hidden_a[0], hidden_b[0])
    pair = jnp.where(here, pair_a[0], pair_b[0])
    half, _, rows, _ = keep_out.shape
    width = hidden.shape[-1]
    first = dot(turned[...], pair) + dot(turned2[...], pair2[0])
    first = first.astype(bf16).reshape(2 * half, rows, 2 * width)
    second = dot(g_turned[...], hidden) + dot(g_turned2[...], hidden2[0])
    second = second.astype(bf16).reshape(2 * half, rows, width)
    for out, base in ((keep_out, 0), (send_out, half)):
        for place in range(half):
            out[inner_swap(place), 0, :, : 2 * width] = first[base + place]
            out[inner_swap(place), 0, :, 2 * width :] = second[base + place]


def shared_grads(scalars, turned, turned2, g_turned, g_turned2, hidden, hidden2, pair, pair2, shift, offset, count,
                 dp_count):
    features, tokens = turned.shape
    width = hidden2.shape[-1]
    half, rows = dp_count // 2, features // dp_count
    out = struct((half, count, rows, 3 * width), bf16)
    out_spec = pl.BlockSpec((half, 1, rows, 3 * width), lambda i, s: (0, i, 0, 0))
    block = lambda w: pl.BlockSpec((1, tokens, w), lambda i, s: (offset + i, 0, 0))
    return call(
        functools.partial(shared_grads_kernel, shift),
        (count,),
        scalars,
        [turned, turned2, g_turned, g_turned2, *hidden, hidden2, *pair, pair2],
        [whole_spec()] * 4 + [block(width)] * 3 + [block(2 * width)] * 3,
        [out, out],
        [out_spec, out_spec],
    )


def finish_kernel(n_parts, n_old, scalars, *refs):
    parts = refs[:n_parts]
    gate_out, up_out, down_out = refs[n_parts + n_old :]
    width = gate_out.shape[-1]
    total = sum(part[0].astype(f32) for part in parts)
    gate_out[0] = total[:, :width]
    up_out[0] = total[:, width : 2 * width]
    down_out[0] = total[:, 2 * width :].T


def finish(scalars, parts, old, first, shift, experts):
    count, rows, wide = parts[0].shape
    width = wide // 3
    place = lambda i, s: (first + i + (0 if shift is None else s[shift]), 0, 0)
    spec = pl.BlockSpec((1, rows, width), place)
    down_spec = pl.BlockSpec((1, width, rows), place)
    return call(
        functools.partial(finish_kernel, len(parts), len(old)),
        (count,),
        scalars,
        [*parts, *old],
        [pl.BlockSpec((1, rows, wide), lambda i, s: (i, 0, 0))] * len(parts)
        + [pl.BlockSpec(memory_space=pl.ANY)] * len(old),
        [struct((experts, rows, width), f32)] * 2 + [struct((experts, width, rows), f32)],
        [spec, spec, down_spec],
        aliases={len(parts) + k: k for k in range(len(old))},
    )


def chunk_specs(chunks, shape):
    specs, first = [], 0
    for chunk in chunks:
        count = chunk.shape[0]
        specs.append(
            pl.BlockSpec(
                (1, *shape), lambda i, s, first=first, count=count: (jnp.clip(i - first, 0, count - 1), 0, 0)
            )
        )
        first += count
    return specs


def input_grad_kernel(sizes, n_tp, scalars, *refs):
    n = len(sizes)
    pairs, (wg, wu), dgates = refs[:n], refs[n : n + 2], refs[n + 2 : 2 * n + 2]
    out, acc = refs[-2:]
    step = pl.program_id(0)
    width = wg.shape[-1]
    first = 0
    for pair, size in zip(pairs, sizes):

        @pl.when((step >= first) & (step < first + size))
        def _(pair=pair, first=first):
            part = dot(pair[0, :, :width], wg[0], NT) + dot(pair[0, :, width:], wu[0], NT)
            if first == 0:

                @pl.when(step == 0)
                def _():
                    acc[...] = part

                @pl.when(step > 0)
                def _():
                    acc[...] += part

            else:
                acc[...] += part

        first += size

    @pl.when(step == pl.num_programs(0) - 1)
    def _():
        rows, features = acc.shape[0] // n_tp, acc.shape[1]
        for k in range(n_tp):
            place = slice(k * rows, (k + 1) * rows)
            out[k, :, :features] = acc[place, :].astype(bf16)
            dgate = sum(ref[place, :] for ref in dgates)
            out[k, :, features:] = two_terms(dgate, out.shape[2] - features)


def input_grads(scalars, pairs, wg, wu, dgates, n_tp):
    experts, features, width = wg.shape
    tokens = pairs[0].shape[1]
    rows = tokens // n_tp
    weight = pl.BlockSpec((1, features, width), lambda i, s: (i, 0, 0))
    return call(
        functools.partial(input_grad_kernel, [pair.shape[0] for pair in pairs], n_tp),
        (experts,),
        scalars,
        [*pairs, wg, wu, *dgates],
        chunk_specs(pairs, (tokens, 2 * width)) + [weight] * 2 + [whole_spec()] * len(dgates),
        [struct((n_tp, rows, features + 128), bf16)],
        [pl.BlockSpec((n_tp, rows, features + 128), lambda i, s: (0, 0, 0))],
        [pltpu.VMEM((tokens, features), f32)],
    )


def result_kernel(sizes, n_tp, scalars, *refs):
    hiddens, wd = refs[: len(sizes)], refs[len(sizes)]
    out, acc = refs[-2:]
    step = pl.program_id(0)
    first = 0
    for hidden, size in zip(hiddens, sizes):

        @pl.when((step >= first) & (step < first + size))
        def _(hidden=hidden, first=first):
            part = dot(hidden[0], wd[0])
            if first == 0:

                @pl.when(step == 0)
                def _():
                    acc[...] = part

                @pl.when(step > 0)
                def _():
                    acc[...] += part

            else:
                acc[...] += part

        first += size

    @pl.when(step == pl.num_programs(0) - 1)
    def _():
        cols = acc.shape[1] // n_tp
        for k in range(n_tp):
            out[k] = acc[:, k * cols : (k + 1) * cols].astype(bf16)


def results(scalars, hiddens, wd, n_tp):
    experts, width, features = wd.shape
    tokens = hiddens[0].shape[1]
    cols = features // n_tp
    return call(
        functools.partial(result_kernel, [hidden.shape[0] for hidden in hiddens], n_tp),
        (experts,),
        scalars,
        [*hiddens, wd],
        chunk_specs(hiddens, (tokens, width)) + [pl.BlockSpec((1, width, features), lambda i, s: (i, 0, 0))],
        [struct((n_tp, tokens, cols), bf16)],
        [pl.BlockSpec((n_tp, tokens, cols), lambda i, s: (0, 0, 0))],
        [pltpu.VMEM((tokens, features), f32)],
    )


def rows_kernel(n_tp, scalars, *refs):
    parts, probs, kept, stream, normed, factor, upstream, gain, router = refs[:9]
    grad_out, dgain_out, drouter_out = refs[9:]
    features, experts = router.shape
    total = sum(parts[k, :, :features].astype(f32) for k in range(n_tp))
    both = sum(parts[k, :, features:].astype(f32) for k in range(n_tp))
    dprobs = (both[:, :experts] + both[:, experts : 2 * experts]) * kept[...]
    soft = probs[...]
    dlogits = soft * (dprobs - jnp.sum(dprobs * soft, axis=1, keepdims=True))
    dlogits = dlogits.astype(bf16)
    drouter_out[...] = dot(normed[...], dlogits, TN)
    total += dot(dlogits, router[...], NT)
    scale = factor[...]
    normal = stream[...] * scale
    dgain_out[...] = jnp.sum(total * normal, axis=0, keepdims=True)
    scaled = total * gain[...]
    mean = jnp.mean(scaled * normal, axis=1, keepdims=True)
    grad_out[...] = (upstream[...].astype(f32) + scale * (scaled - normal * mean)).astype(bf16)


def stream_grad_rows(scalars, parts, probs, kept, stream, normed, factor, upstream, gain, router):
    n_tp, rows, _ = parts.shape
    features, experts = router.shape
    mine = lambda w: pl.BlockSpec((rows, w), lambda i, s: (s[0], 0))
    plain = lambda h, w: pl.BlockSpec((h, w), lambda i, s: (0, 0))
    return call(
        functools.partial(rows_kernel, n_tp),
        (1,),
        scalars,
        [parts, probs, kept, stream, normed, factor, upstream, gain, router],
        [pl.BlockSpec(parts.shape, lambda i, s: (0, 0, 0))]
        + [mine(experts), mine(experts), mine(features), mine(features), mine(1), mine(features)]
        + [plain(1, features), plain(features, experts)],
        [struct((rows, features), bf16), struct((1, features), f32), struct((features, experts), f32)],
        [plain(rows, features), plain(1, features), plain(features, experts)],
    )


def attended_grad_kernel(scalars, grad, w_ref, out):
    out[...] = dot(grad[...], w_ref[...], NT).astype(bf16)


def attended_grad(scalars, grad, w_output):
    tokens, features = grad.shape
    local = w_output.shape[0]
    rows = lambda w: pl.BlockSpec((tokens // 2, w), lambda i, s: (i, 0))
    return call(
        attended_grad_kernel,
        (2,),
        scalars,
        [grad, w_output],
        [rows(features), whole_spec()],
        [struct((tokens, local), bf16)],
        [rows(local)],
    )[0]


def normed_grad_kernel(scalars, grads, wq, wk, wv, x_ref, factor, gain, out, dot_out, dgain_out):
    total = sum(dot(grads[j], weight[...], NT) for j, weight in enumerate((wq, wk, wv)))
    out[0] = total.astype(bf16)
    normal = x_ref[...].astype(f32) * factor[...]
    product = total * normal
    dgain_out[...] = jnp.sum(product, axis=0, keepdims=True)
    part = jnp.sum(product * gain[...], axis=1, keepdims=True)

    @pl.when(pl.program_id(0) == 0)
    def _():
        dot_out[...] = part

    @pl.when(pl.program_id(0) > 0)
    def _():
        dot_out[...] += part


def normed_grad(scalars, grads, wq, wk, wv, x, factor, gain, n_tp):
    _, tokens, local = grads.shape
    features = wq.shape[0]
    width = features // n_tp
    weight = pl.BlockSpec((width, local), lambda i, s: (i, 0))
    column = lambda h: pl.BlockSpec((h, width), lambda i, s: (0, i))
    whole = pl.BlockSpec((tokens, 1), lambda i, s: (0, 0))
    return call(
        normed_grad_kernel,
        (n_tp,),
        scalars,
        [grads, wq, wk, wv, x, factor, gain],
        [pl.BlockSpec(grads.shape, lambda i, s: (0, 0, 0))] + [weight] * 3 + [column(tokens), whole, column(1)],
        [struct((n_tp, tokens, width), bf16), struct((tokens, 1), f32), struct((1, features), f32)],
        [pl.BlockSpec((1, tokens, width), lambda i, s: (i, 0, 0)), whole, column(1)],
    )


def turn_kernel(first, dp_count, scalars, source, target):
    transpose_blocks(scalars, first, source, target, dp_count)


def turn(scalars, value, n_tp, dp_count):
    tokens, features = value.shape
    return call(
        functools.partial(turn_kernel, n_tp, dp_count),
        (tokens // TB,),
        scalars,
        [value],
        [pl.BlockSpec((TB, features), lambda i, s: (i, 0))],
        [struct((features, tokens), bf16)],
        [pl.BlockSpec((features, TB), lambda i, s: (0, i))],
    )[0]


def output_kernel(scalars, stream, parts, out):
    out[...] = (stream[...] + sum(parts[k].astype(f32) for k in range(parts.shape[0]))).astype(bf16)


def output_of(scalars, stream, parts):
    n_tp, tokens, width = parts.shape
    return call(
        output_kernel,
        (tokens // TB,),
        scalars,
        [stream, parts],
        [
            pl.BlockSpec((TB, width), lambda i, s: (i, s[0])),
            pl.BlockSpec((n_tp, TB, width), lambda i, s: (0, i, 0)),
        ],
        [struct((tokens, width), bf16)],
        [pl.BlockSpec((TB, width), lambda i, s: (i, 0))],
    )[0]


def final_kernel(features, scalars, dattn, x_ref, factor, row_dot, gain, parts, out):
    total = sum(parts[k].astype(f32) for k in range(parts.shape[0]))
    scale = factor[...]
    normal = x_ref[...].astype(f32) * scale
    back = scale * (total * gain[...] - normal * (row_dot[...] / features))
    out[...] = (dattn[...].astype(f32) + back).astype(bf16)


def final_grad(scalars, dattn, x, factor, row_dot, gain, parts):
    n_tp, tokens, width = parts.shape
    plain = lambda w: pl.BlockSpec((TB, w), lambda i, s: (i, 0))
    mine = pl.BlockSpec((TB, width), lambda i, s: (i, s[0]))
    return call(
        functools.partial(final_kernel, dattn.shape[1]),
        (tokens // TB,),
        scalars,
        [dattn, x, factor, row_dot, gain, parts],
        [mine, mine, plain(1), plain(1), pl.BlockSpec((1, width), lambda i, s: (0, s[0]))]
        + [pl.BlockSpec((n_tp, TB, width), lambda i, s: (0, i, 0))],
        [struct((tokens, width), bf16)],
        [plain(width)],
    )[0]


def kept_pairs(expert_ids, experts, capacity):
    tokens = expert_ids.shape[0]
    named = jnp.any(expert_ids[:, :, None] == jnp.arange(experts, dtype=jnp.int32), axis=1)
    earlier = jnp.arange(tokens)[:, None] > jnp.arange(tokens)[None, :]
    rank = dot(earlier.astype(bf16), named.astype(bf16))
    return (named & (rank < capacity)).astype(f32)


def body(n_dp, n_tp, cosine, sine, tokens, cotangent, attn_gain, w_query, w_key, w_value, query_gain, key_gain,
         w_output, ffn_gain, w_router, w_gate, w_up, w_down, expert_ids):
    tp, dp = lax.axis_index("tensor"), lax.axis_index("dp")
    far, near = n_dp // 2, n_dp // 4
    side = (dp // near) % 2
    token_count, width = tokens.shape
    features = width * n_tp
    heads, hd = query_gain.shape
    local = heads * hd
    experts = w_router.shape[1]
    capacity = token_count * expert_ids.shape[1] // experts
    gain1, gain2 = attn_gain[None, :], ffn_gain[None, :]
    blocks = (2, 3, 3)
    lead = sum(blocks)
    shared = (experts - lead) // 2
    shift, other_shift = n_tp + n_dp, n_tp + n_dp + 1
    scalars = jnp.stack(
        [tp ^ r for r in range(n_tp)]
        + [dp ^ bit_reverse(place, n_dp) for place in range(n_dp)]
        + [side * shared, (1 - side) * shared]
    ).astype(jnp.int32)

    line.last = []

    share = local // n_dp
    w_share = lax.dynamic_slice_in_dim(w_output, dp * share, share, 0)
    w_all = lax.all_gather(w_share, ("dp", "tensor")).reshape(n_dp, n_tp, share, features)

    x_pieces = gather_pieces(tokens, "tensor", n_tp)
    kept = kept_pairs(expert_ids, experts, capacity)
    x_pieces, g_mine, kept = lax.optimization_barrier((x_pieces, cotangent, kept))
    g_near = swap(g_mine, "dp", n_dp, near)
    g_pieces = [g_mine, swap(g_mine, "tensor", n_tp, 1), swap(g_mine, "tensor", n_tp, 2)]
    x, normed1, factor1, q_raw, k_raw, q_rot, k_rot, value = project(
        scalars, x_pieces, gain1, w_query, w_key, w_value, query_gain, key_gain, cosine, sine
    )
    attended, totals = attend(scalars, q_rot, k_rot, value, heads)
    attended, g_pieces = lax.optimization_barrier((attended, g_pieces))
    attended_pieces = gather_pieces(attended, "tensor", n_tp)
    attended_pieces, g_pieces, g_near = lax.optimization_barrier((attended_pieces, g_pieces, g_near))
    if n_tp == 4:
        half = token_count // 2
        one, two = g_pieces[1], g_pieces[2]
        g_pieces.append((swap(two[:half], "tensor", n_tp, 1), swap(one[half:], "tensor", n_tp, 2)))
    else:
        g_pieces = direct_pieces(g_pieces[0], "tensor", n_tp)
    stream, normed2, normed2_mine, turned, factor2, probs, gates = stream_of(
        scalars, attended_pieces, x, w_all, gain2, w_router, kept, n_dp
    )
    upstream, g_turned = whole_grad(scalars, g_pieces, n_dp)
    normed_near = swap(normed2_mine, "dp", n_dp, near)
    g_near, _ = lax.optimization_barrier((g_near, upstream))
    upstream_near = lax.all_gather(g_near, "tensor", axis=1, tiled=True)
    gates_near = normed_near[:, width : width + experts].astype(f32)
    gates_near += normed_near[:, width + experts : width + 2 * experts].astype(f32)
    normed2_near = lax.all_gather(normed_near[:, :width], "tensor", axis=1, tiled=True)

    hiddens, pairs, dgates = [], [], []

    def run(first, count):
        out = run_experts(scalars, normed2, upstream, gates, w_gate, w_up, w_down, first, count)
        for kind, array in zip((hiddens, pairs, dgates), out):
            kind.append(array)

    def sum_step(keep, send, mask):
        arrived = swap(send, "dp", n_dp, mask)
        return lambda: add_halves(scalars, keep, arrived)

    lower = [mask for mask in (2, 4, 8, 16) if mask < far]

    def own_sums(index):
        first, count = sum(blocks[:index]), blocks[index]
        keep, send = weight_grads(scalars, turned, g_turned, hiddens[index], pairs[index], 0, count, n_dp)
        return sum_step(keep, send, 1)

    def last_step(take):
        keep, send = take()
        for mask in lower[1:]:
            keep, send = sum_step(keep, send, mask)()
        return [keep[0], swap(send, "dp", n_dp, far)[0]]

    run(0, blocks[0])
    take0 = own_sums(0)
    run(blocks[0], blocks[1])
    take0 = sum_step(*take0(), lower[0])
    take1 = own_sums(1)
    run(blocks[0] + blocks[1], blocks[2])
    parts0 = last_step(take0)
    take1 = sum_step(*take1(), lower[0])
    take2 = own_sums(2)
    run(lead, shared)
    take2 = sum_step(*take2(), lower[0])
    parts1 = last_step(take1)
    line.tick("dp", n_dp)
    run(lead + shared, shared)
    old = finish(scalars, parts0, [], 0, None, experts)
    line.take()
    input_parts = input_grads(scalars, pairs, w_gate, w_up, dgates, n_tp)[0]
    input_arrived = trade(input_parts, "tensor")
    parts2 = last_step(take2)
    g_turned_near = turn(scalars, upstream_near, n_tp, n_dp)
    turned_near = turn(scalars, normed2_near, n_tp, n_dp)
    old = finish(scalars, parts1, old, blocks[0], None, experts)
    hidden_near, pair_near, _ = run_experts(
        scalars, normed2_near, upstream_near, gates_near, w_gate, w_up, w_down, lead, shared, shift
    )

    def shared_sums(offset, size):
        keep, send = shared_grads(
            scalars, turned, turned_near, g_turned, g_turned_near, hiddens[3:], hidden_near, pairs[3:], pair_near,
            shift, offset, size, n_dp,
        )
        return sum_step(keep, send, 1)

    def shared_next(take):
        keep, send = take()
        for mask in lower:
            if mask != near:
                keep, send = sum_step(keep, send, mask)()
        return sum_step(keep, send, far)

    first_share = (shared + 1) // 2
    take3 = shared_sums(0, first_share)
    dattn_rows, dgain2, drouter = stream_grad_rows(
        scalars, input_arrived, probs, kept, stream, normed2, factor2, upstream, gain2, w_router
    )
    dattn = lax.all_gather(dattn_rows, "tensor", axis=0, tiled=True)
    take3 = shared_next(take3)
    line.tick("dp", n_dp)
    old = finish(scalars, parts2, old, blocks[0] + blocks[1], None, experts)
    line.take()
    take4 = shared_sums(first_share, shared - first_share)
    result_arrived = trade(results(scalars, hiddens, w_down, n_tp)[0], "tensor")
    take4 = shared_next(take4)

    def spread(value, dimension):
        value = value.astype(bf16)
        line.last = [value]
        return lax.psum_scatter(value, "dp", scatter_dimension=dimension, tiled=True).astype(f32)

    dattended = attended_grad(scalars, dattn, w_output)
    grad_output = spread(dot(attended, line.pin(dattn), TN), 1)
    grads, dhead_gains = attend_back(
        scalars, q_rot, k_rot, value, dattended, totals, q_raw, k_raw, query_gain, key_gain, cosine, sine
    )
    keep3, send3 = take3()
    given3 = swap(send3, "dp", n_dp, near)
    grad_qkv = spread(jnp.einsum("td,jtc->jdc", line.pin(normed1), grads, preferred_element_type=f32), 1)
    slices, row_dot, dgain1 = normed_grad(scalars, grads, w_query, w_key, w_value, x, factor1, gain1, n_tp)
    slices_arrived = trade(slices, "tensor")

    mine = lambda array, dimension: lax.dynamic_slice_in_dim(
        array, dp * (array.shape[dimension] // n_dp), array.shape[dimension] // n_dp, dimension
    )
    flat_heads = dhead_gains.reshape(1, -1)
    flat_heads = jnp.pad(flat_heads, ((0, 0), (0, features - flat_heads.shape[1])))
    small = jnp.concatenate([drouter.T, dgain2, dgain1, flat_heads], axis=0)
    row_dot = row_dot.reshape(8, token_count // 8)

    def chain(value, axis, count):
        mask = 1
        while mask < count:
            arrived = swap(value, axis, count, mask)
            yield
            value = add_to(scalars, value, arrived)
            mask *= 2
        return value

    def small_chain():
        total = yield from chain(small, "dp", n_dp)
        own = yield from chain(mine(total[: experts + 2], 1), "tensor", n_tp)
        return total[experts + 2], own

    done = {}

    def advance(name, steps):
        if name not in done:
            try:
                next(steps)
            except StopIteration as end:
                done[name] = end.value

    rows_chain, small_chain = chain(row_dot, "tensor", n_tp), small_chain()
    advance("rows", rows_chain)
    advance("small", small_chain)
    output = output_of(scalars, stream, result_arrived)
    advance("rows", rows_chain)
    advance("small", small_chain)
    old = finish(scalars, [keep3[0]], old, lead, shift, experts)
    advance("rows", rows_chain)
    keep4, send4 = take4()
    given4 = swap(send4, "dp", n_dp, near)
    advance("small", small_chain)
    old = finish(scalars, [given3[0]], old, lead, other_shift, experts)
    advance("small", small_chain)
    old = finish(scalars, [keep4[0]], old, lead + first_share, shift, experts)
    while "rows" not in done:
        advance("rows", rows_chain)
    advance("small", small_chain)
    row_dot = done["rows"].reshape(token_count, 1)
    input_grad = final_grad(scalars, dattn, x, factor1, row_dot, gain1, slices_arrived)
    while "small" not in done:
        advance("small", small_chain)
    head_gains, small = done["small"]
    head_gains = mine(head_gains[: dhead_gains.size].reshape(dhead_gains.shape), 2)
    grad_gate, grad_up, grad_down = finish(scalars, [given4[0]], old, lead + first_share, other_shift, experts)
    return (
        output,
        input_grad,
        small[experts + 1],
        grad_qkv[0],
        grad_qkv[1],
        grad_qkv[2],
        head_gains[:, 0],
        head_gains[:, 1],
        grad_output,
        small[experts],
        small[:experts].T,
        grad_gate,
        grad_up,
        grad_down,
    )


def solution(mesh):
    placed = (
        P("dp", "tensor"),
        P("dp", "tensor"),
        P(),
        P(None, "tensor"),
        P(None, "tensor"),
        P(None, "tensor"),
        P("tensor", None),
        P("tensor", None),
        P("tensor", None),
        P(),
        P(),
        P(None, None, "tensor"),
        P(None, None, "tensor"),
        P(None, "tensor", None),
        P("dp", None),
    )
    n_dp, n_tp = mesh.shape["dp"], mesh.shape["tensor"]

    def layer(*args):
        cosine, sine = rope_constants(LEN, args[6].shape[1])
        return body(n_dp, n_tp, jnp.asarray(cosine), jnp.asarray(sine), *args)

    return jax.shard_map(
        layer,
        mesh=mesh,
        in_specs=placed,
        out_specs=(
            P("dp", "tensor"),
            P("dp", "tensor"),
            P("dp"),
            P("dp", "tensor"),
            P("dp", "tensor"),
            P("dp", "tensor"),
            P("tensor", "dp"),
            P("tensor", "dp"),
            P("tensor", "dp"),
            P("dp"),
            P("dp", None),
            P(None, "dp", "tensor"),
            P(None, "dp", "tensor"),
            P(None, "tensor", "dp"),
        ),
        check_vma=False,
    )
```

time: 1230 us -> 796 us (0.65)
  waiting for transfers between devices: 635 us -> 164 us
  Pallas kernels: 359 us -> 506 us
  other arithmetic: 82.4 us -> 9.18 us
  local copies, waits for them, and re-layouts: 42.4 us -> 20.4 us
    ppermute x58 -> x38, waiting for transfers between devices: 604 us -> 149 us  [swap(): return lax.ppermute(value, axis, [(i, i ^ mask) for i in range(count)])]
    pallas_call x21 -> x49, Pallas kernels: 359 us -> 506 us  [call(): pl.pallas_call(without_deps, out_shape=outs + [struct((8, 128), f32)] * M...]
    convert_element_type x14 -> x2, other arithmetic: 60.7 us -> 3.12 us  [spread(): lax.psum_scatter(value, 'dp', scatter_dimension=dimension, tiled=True)]
    all_gather x2 -> x4, waiting for transfers between devices: 30.7 us -> 2.87 us  [the longest x1 2.87 us: body(): lax.all_gather(w_share, ('dp', 'tensor'))]
    ppermute x58 -> x38, starting transfers between devices: 64 us -> 40.1 us  [swap(): return lax.ppermute(value, axis, [(i, i ^ mask) for i in range(count)])]
    all_to_all x0 -> x3, starting transfers between devices: none -> 15 us  [trade(): return lax.all_to_all(pieces, axis, 0, 0, tiled=True)]
    unnamed x109 -> x29, local copies, waits for them, and re-layouts: 16.3 us -> 2.03 us
  transfers between devices with their start and end apart: 62 -> 47, of which waited for: 29 -> 16; matrix products, arithmetic and copies ran while one was open for 11% -> 5% of each run, Pallas kernels for 14% -> 64%
where the time goes in v3:
time: 796 us; the launch traced here: 786 us
  Pallas kernels  506 us (64%)
  waiting for transfers between devices  164 us (21%)
  starting transfers between devices  55.5 us (7%)
  local copies, waits for them, and re-layouts  20.4 us (3%)
  matrix products  16.2 us (2%)
  between operations  15 us (2%)
  other arithmetic  9.18 us (1%)
    pallas_call x49, Pallas kernels, call(): pl.pallas_call(without_deps, out_shape=outs + [struct((8, 128), f32)] * M...  506 us
    ppermute x38, waiting for transfers between devices, swap(): return lax.ppermute(value, axis, [(i, i ^ mask) for i in range(count)])  149 us
    ppermute x38, starting transfers between devices, swap(): return lax.ppermute(value, axis, [(i, i ^ mask) for i in range(count)])  40.1 us
  transfers between devices with their start and end apart: 47, of which 16 were waited for; matrix products, arithmetic and copies ran while one was open for 5% of the time, Pallas kernels for 64%

profile of v3, /device:TPU:0, one launch (start us, length us, event | category | flops | bytes accessed | tf_op | source)
XLA Modules:
  0.0 786.3 jit_solution(5678935160888458806)
XLA Ops:
  11.7 21.9 %collective-permute-done.refs_1_ = bf16[1024,512]{1,0:T(8,128)(2,1)S(1)} collective-permute-done((bf16[1024,512]{1,0:T(8,128)(2,1)}, bf16[1024,512]{1,0:T(8,128)(2,1)S(1)}, u32[]{:S(2)}, u32[]{:S(2)}) %collective-permute-start) | collective-permute-done | bytes 1048608 | tf_op jit(solution)/shard_map/ppermute | solution.py:99
  50.2 15.5 %shard_map.272 = (bf16[1024,2048]{1,0:T(8,128)(2,1)}, bf16[1024,2048]{1,0:T(8,128)(2,1)}, f32[1024,1]{1,0:T(8,128)}, f32[1024,512]{1,0:T(8,128)}, f32[1024,512]{...) custom-call(s32[14]{0:T(128)} %stack.59.scalars, ...), custom_call_target="tpu_custom_call" | custom-call | flops 999999995904 | bytes 1 | tf_op jit(solution)/shard_map/pallas_call | solution.py:76
  65.7 11.8 %shard_map.273 = (bf16[1024,512]{1,0:T(8,128)(2,1)}, f32[4,1024,1]{2,1,0:T(8,128)}, f32[8,128]{1,0:T(8,128)}, f32[8,128]{1,0:T(8,128)}, f32[8,128]{1,0:T(8,128)}, /*index=5*/f32[8,128]{1,0:T(8,128)}) custom-call(s32[14]{0:T(128)} %stack.59.scalars, f32[8,128]{1,0:T(8,128)} %get-tuple-element.333.refs_0_, f32[8,128]{1,0:T(8,128)} %get-tuple-element.334.refs_1_, ...), custom_call_target="tpu_custom_call" | custom-call | flops 999999995904 | bytes 1 | tf_op jit(solution)/shard_map/pallas_call | solution.py:76
  86.1 21.8 %collective-permute-done.7.refs_6_ = bf16[1024,512]{1,0:T(8,128)(2,1)S(1)} collective-permute-done((bf16[1024,512]{1,0:T(8,128)(2,1)}, bf16[1024,512]{1,0:T(8,128)(2,1)S(1)}, u32[]{:S(2)}, u32[]{:S(2)}) %collective-permute-start.7) | collective-permute-done | bytes 1048608 | tf_op jit(solution)/shard_map/ppermute | solution.py:99
  111.1 7.8 collective-permute-done.6.refs_5_
  121.9 10.4 %collective-permute-done.8.refs_7_ = bf16[512,512]{1,0:T(8,128)(2,1)} collective-permute-done((bf16[512,512]{1,0:T(8,128)(2,1)S(1)}, bf16[512,512]{1,0:T(8,128)(2,1)}, u32[]{:S(2)}, u32[]{:S(2)}) %collective-permute-start.8) | collective-permute-done | bytes 524320 | tf_op jit(solution)/shard_map/ppermute | solution.py:99
  140.0 21.4 %shard_map.274 = (f32[1024,2048]{1,0:T(8,128)}, bf16[1024,2048]{1,0:T(8,128)(2,1)}, bf16[1024,640]{1,0:T(8,128)(2,1)}, bf16[2048,1024]{1,0:T(8,128)(2,1)}, f32[1...) custom-call(s32[14]{0:T(128)} %stack.59.scalars, ...), custom_call_target="tpu_custom_call" | custom-call | flops 999999995904 | bytes 1 | tf_op jit(solution)/shard_map/pallas_call | solution.py:76
  162.9 6.8 shard_map.275
  170.0 14.2 %shard_map.276 = (bf16[2,1024,256]{2,1,0:T(8,128)(2,1)}, bf16[2,1024,512]{2,1,0:T(8,128)(2,1)}, f32[1024,16]{1,0:T(8,128)}, f32[8,128]{1,0:T(8,128)}, f32[8,128]...) custom-call(s32[14]{0:T(128)} %stack.59.scalars, f32[8,128]{1,0:T(8,128)} %get-tuple-element.364.refs_0_, ...), custom_call_target="tpu_custom_call" | custom-call | flops 999999995904 | bytes 1 | tf_op jit(solution)/shard_map/pallas_call | solution.py:76
  184.3 13.2 %shard_map.277 = (bf16[4,2,256,768]{3,2,1,0:T(8,128)(2,1)}, bf16[4,2,256,768]{3,2,1,0:T(8,128)(2,1)}, f32[8,128]{1,0:T(8,128)}, f32[8,128]{1,0:T(8,128)}, f32[8,128]{1,0:T(8,128)}, /*index=5*/f32[8,128]{1,0:T(8,128)}) custom-call(s32[14]{0:T(128)} %stack.59.scalars, f32[8,128]{1,0:T(8,128)} %get-tuple-element.371.refs_0_, ...), custom_call_target="tpu_custom_call" | custom-call | flops 999999995904 | bytes 1 | tf_op jit(solution)/shard_map/pallas_call | solution.py:76
  197.5 18.2 %shard_map.278 = (bf16[3,1024,256]{2,1,0:T(8,128)(2,1)}, bf16[3,1024,512]{2,1,0:T(8,128)(2,1)}, f32[1024,16]{1,0:T(8,128)}, f32[8,128]{1,0:T(8,128)}, f32[8,128]...) custom-call(s32[14]{0:T(128)} %stack.59.scalars, f32[8,128]{1,0:T(8,128)} %get-tuple-element.379.refs_0_, ...), custom_call_target="tpu_custom_call" | custom-call | flops 999999995904 | bytes 1 | tf_op jit(solution)/shard_map/pallas_call | solution.py:76
  225.6 17.6 %shard_map.280 = (bf16[4,3,256,768]{3,2,1,0:T(8,128)(2,1)}, bf16[4,3,256,768]{3,2,1,0:T(8,128)(2,1)}, f32[8,128]{1,0:T(8,128)}, f32[8,128]{1,0:T(8,128)}, f32[8,128]{1,0:T(8,128)}, /*index=5*/f32[8,128]{1,0:T(8,128)}) custom-call(s32[14]{0:T(128)} %stack.59.scalars, f32[8,128]{1,0:T(8,128)} %get-tuple-element.389.refs_0_, ...), custom_call_target="tpu_custom_call" | custom-call | flops 999999995904 | bytes 1 | tf_op jit(solution)/shard_map/pallas_call | solution.py:76
  243.3 17.8 %shard_map.281 = (bf16[3,1024,256]{2,1,0:T(8,128)(2,1)}, bf16[3,1024,512]{2,1,0:T(8,128)(2,1)}, f32[1024,16]{1,0:T(8,128)}, f32[8,128]{1,0:T(8,128)}, f32[8,128]...) custom-call(s32[14]{0:T(128)} %stack.59.scalars, f32[8,128]{1,0:T(8,128)} %get-tuple-element.395.refs_0_, ...), custom_call_target="tpu_custom_call" | custom-call | flops 999999995904 | bytes 1 | tf_op jit(solution)/shard_map/pallas_call | solution.py:76
  266.7 7.5 shard_map.283
  275.7 16.8 %shard_map.284 = (bf16[4,3,256,768]{3,2,1,0:T(8,128)(2,1)}, bf16[4,3,256,768]{3,2,1,0:T(8,128)(2,1)}, f32[8,128]{1,0:T(8,128)}, f32[8,128]{1,0:T(8,128)}, f32[8,128]{1,0:T(8,128)}, /*index=5*/f32[8,128]{1,0:T(8,128)}) custom-call(s32[14]{0:T(128)} %stack.59.scalars, f32[8,128]{1,0:T(8,128)} %get-tuple-element.411.refs_0_, ...), custom_call_target="tpu_custom_call" | custom-call | flops 999999995904 | bytes 1 | tf_op jit(solution)/shard_map/pallas_call | solution.py:76
  292.5 21.7 %shard_map.285 = (bf16[4,1024,256]{2,1,0:T(8,128)(2,1)}, bf16[4,1024,512]{2,1,0:T(8,128)(2,1)}, f32[1024,16]{1,0:T(8,128)}, f32[8,128]{1,0:T(8,128)}, f32[8,128]...) custom-call(s32[14]{0:T(128)} %stack.59.scalars, f32[8,128]{1,0:T(8,128)} %get-tuple-element.417.refs_0_, ...), custom_call_target="tpu_custom_call" | custom-call | flops 999999995904 | bytes 1 | tf_op jit(solution)/shard_map/pallas_call | solution.py:76
  314.3 7.5 shard_map.286
  321.8 22.0 %collective-permute-done.17.refs_6_.refs_7_ = bf16[2,3,256,768]{3,2,1,0:T(8,128)(2,1)} collective-permute-done((bf16[2,3,256,768]{3,2,1,0:T(8,128)(2,1)}, bf16[2,3,256,768]{3,2,1,0:T(8,128)(2,1)}, u32[]{:S(2)}, u32[]{:S(2)}) %collective-permute-start.17) | collective-permute-done | bytes 2359328 | tf_op jit(solution)/shard_map/ppermute | solution.py:99
  351.6 21.6 %shard_map.288 = (bf16[4,1024,256]{2,1,0:T(8,128)(2,1)}, bf16[4,1024,512]{2,1,0:T(8,128)(2,1)}, f32[1024,16]{1,0:T(8,128)}, f32[8,128]{1,0:T(8,128)}, f32[8,128]...) custom-call(s32[14]{0:T(128)} %stack.59.scalars, f32[8,128]{1,0:T(8,128)} %get-tuple-element.433.refs_0_, ...), custom_call_target="tpu_custom_call" | custom-call | flops 999999995904 | bytes 1 | tf_op jit(solution)/shard_map/pallas_call | solution.py:76
  376.2 49.6 %shard_map.290 = (bf16[4,256,2176]{2,1,0:T(8,128)(2,1)}, f32[8,128]{1,0:T(8,128)}, f32[8,128]{1,0:T(8,128)}, f32[8,128]{1,0:T(8,128)}, f32[8,128]{1,0:T(8,128)}) custom-call(s32[14]{0:T(128)} %stack.59.scalars, f32[8,128]{1,0:T(8,128)} %get-tuple-element.443.refs_0_, f32[8,128]{1,0:T(8,128)} %get-tuple-element.444.refs_1_, ...), custom_call_target="tpu_custom_call" | custom-call | flops 999999995904 | bytes 1 | tf_op jit(solution)/shard_map/pallas_call | solution.py:76
  452.8 21.6 %shard_map.295 = (bf16[4,1024,256]{2,1,0:T(8,128)(2,1)}, bf16[4,1024,512]{2,1,0:T(8,128)(2,1)}, f32[1024,16]{1,0:T(8,128)}, f32[8,128]{1,0:T(8,128)}, f32[8,128]...) custom-call(s32[14]{0:T(128)} %stack.59.scalars, f32[8,128]{1,0:T(8,128)} %get-tuple-element.480.refs_0_, ...), custom_call_target="tpu_custom_call" | custom-call | flops 999999995904 | bytes 1 | tf_op jit(solution)/shard_map/pallas_call | solution.py:76
  474.4 23.7 %shard_map.296 = (bf16[4,2,256,768]{3,2,1,0:T(8,128)(2,1)}, bf16[4,2,256,768]{3,2,1,0:T(8,128)(2,1)}, f32[8,128]{1,0:T(8,128)}, f32[8,128]{1,0:T(8,128)}, f32[8,128]{1,0:T(8,128)}, /*index=5*/f32[8,128]{1,0:T(8,128)}) custom-call(s32[14]{0:T(128)} %stack.59.scalars, f32[8,128]{1,0:T(8,128)} %get-tuple-element.484.refs_0_, ...), custom_call_target="tpu_custom_call" | custom-call | flops 999999995904 | bytes 1 | tf_op jit(solution)/shard_map/pallas_call | solution.py:76
  498.3 7.5 shard_map.297
  520.7 23.7 %shard_map.300 = (bf16[4,2,256,768]{3,2,1,0:T(8,128)(2,1)}, bf16[4,2,256,768]{3,2,1,0:T(8,128)(2,1)}, f32[8,128]{1,0:T(8,128)}, f32[8,128]{1,0:T(8,128)}, f32[8,128]{1,0:T(8,128)}, /*index=5*/f32[8,128]{1,0:T(8,128)}) custom-call(s32[14]{0:T(128)} %stack.59.scalars, f32[8,128]{1,0:T(8,128)} %get-tuple-element.518.refs_0_, ...), custom_call_target="tpu_custom_call" | custom-call | flops 999999995904 | bytes 1 | tf_op jit(solution)/shard_map/pallas_call | solution.py:76
  544.4 28.4 %shard_map.301 = (bf16[4,1024,512]{2,1,0:T(8,128)(2,1)}, f32[8,128]{1,0:T(8,128)}, f32[8,128]{1,0:T(8,128)}, f32[8,128]{1,0:T(8,128)}, f32[8,128]{1,0:T(8,128)}) custom-call(s32[14]{0:T(128)} %stack.59.scalars, f32[8,128]{1,0:T(8,128)} %get-tuple-element.522.refs_0_, f32[8,128]{1,0:T(8,128)} %get-tuple-element.523.refs_1_, ...), custom_call_target="tpu_custom_call" | custom-call | flops 999999995904 | bytes 1 | tf_op jit(solution)/shard_map/pallas_call | solution.py:76
  595.7 21.7 %shard_map.304 = (bf16[3,1024,512]{2,1,0:T(8,128)(2,1)}, f32[4,2,128]{2,1,0:T(2,128)}, f32[8,128]{1,0:T(8,128)}, f32[8,128]{1,0:T(8,128)}, f32[8,128]{1,0:T(8,128)}, /*index=5*/f32[8,128]{1,0:T(8,128)}) custom-call(s32[14]{0:T(128)} %stack.59.scalars, bf16[512,2048]{1,0:T(8,128)(2,1)} %convolution_convert_fusion.refs_0_, ...), custom_call_target="tpu_custom_call" | custom-call | flops 999999995904 | bytes 1 | tf_op jit(solution)/shard_map/pallas_call | solution.py:76
  623.5 8.8 %convert_bitcast_fusion.refs_0_ = bf16[3,2048,512]{2,1,0:T(8,128)(2,1)} fusion(bf16[3,1024,512]{2,1,0:T(8,128)(2,1)S(1)} %copy-done.13, bf16[1024,2048]{1,0:T(8,128)(2,1)S(1)} %copy-done.12), kind=kOutput, calls=%fused_computation | convolution fusion | flops 6445596672 | bytes 13631488 | tf_op jit(solution)/shard_map/td,jtc->jdc/dot_general | solution.py:1003
  632.4 13.6 %shard_map.305 = (bf16[4,1024,512]{2,1,0:T(8,128)(2,1)}, f32[1024,1]{1,0:T(8,128)}, f32[1,2048]{1,0:T(1,128)}, f32[8,128]{1,0:T(8,128)}, f32[8,128]{1,0:T(8,128)}, /*index=5*/f32[8,128]{1,0:T(8,128)}, f32[8,128]{1,0:T(8,128)}) custom-call(s32[14]{0:T(128)} %stack.59.scalars, bf16[3,2048,512]{2,1,0:T(8,128)(2,1)} %convert_bitcast_fusion.refs_0_, ...), custom_call_target="tpu_custom_call" | custom-call | flops 999999995904 | bytes 1 | tf_op jit(solution)/shard_map/pallas_call | solution.py:76
  671.4 33.4 %collective-permute-done.30.refs_5_ = f32[8,128]{1,0:T(8,128)} collective-permute-done((f32[8,128]{1,0:T(8,128)}, f32[8,128]{1,0:T(8,128)}, u32[]{:S(2)}, u32[]{:S(2)}) %collective-permute-start.30) | collective-permute-done | bytes 4128 | tf_op jit(solution)/shard_map/ppermute | solution.py:99
  719.7 12.7 %collective-permute-done.34.refs_5_ = f32[19,2048]{1,0:T(8,128)} collective-permute-done((f32[19,2048]{1,0:T(8,128)}, f32[19,2048]{1,0:T(8,128)}, u32[]{:S(2)}, u32[]{:S(2)}) %collective-permute-start.34) | collective-permute-done | bytes 155680 | tf_op jit(solution)/shard_map/ppermute | solution.py:99
  752.0 6.7 collective-permute-done.37
  764.7 11.8 %reduce-scatter.3.cloned.1.call-done = bf16[3,256,512]{2,1,0:T(8,128)(2,1)} async-done(((bf16[3,2048,512]{2,1,0:T(8,128)(2,1)}), bf16[3,256,512]{2,1,0:T(8,128)(2,1)}) %reduce-scatter.3.cloned.1.call-update) | async-done | bytes 786448 | tf_op jit(solution)/shard_map/reduce_scatter | solution.py:994
  (173 shorter events, 212.8 us)
Async XLA Ops:
  7.2 132.8 %all-gather.12.cloned.1.call-start = ((), (), s32[]{:S(2)}) async-start(), calls=%async_computation.10 | async-start | bytes 8650752 | tf_op jit(solution)/shard_map/all_gather | solution.py:882
  7.2 26.4 %collective-permute-start = (bf16[1024,512]{1,0:T(8,128)(2,1)}, bf16[1024,512]{1,0:T(8,128)(2,1)S(1)}, u32[]{:S(2)}, u32[]{:S(2)}) collective-permute-start(bf16[1024,512]{1,0:T(8,128)(2,1)} %refs_0_), channel_id=1, source_target_pairs={{0,1},{1,0},{2,3},{3,2},{4,5},{5,4},{6,7},{7,6},{8,9},{9,8},{10,11... | collective-permute-start | bytes 3145736 | tf_op jit(solution)/shard_map/ppermute | solution.py:99
  38.8 397.5 %all-gather.6.cloned.1.call-start = ((), (), s32[]{:S(2)}) async-start(), calls=%async_computation.5 | async-start | bytes 5242880 | tf_op jit(solution)/shard_map/all_gather | solution.py:908
  48.2 29.3 %collective-permute-start.5 = (bf16[1024,512]{1,0:T(8,128)(2,1)}, bf16[1024,512]{1,0:T(8,128)(2,1)}, u32[]{:S(2)}, u32[]{:S(2)}) collective-permute-start(bf16[1024,512]{1,0:T(8,128)(2,1)} %refs_4_.1), channel_id=1, source_target_pairs={{0,2},{1,3},{2,0},{3,1},{4,6},{5,7},{6,4},{7,5},{8,10},{9,11},{10,... | collective-permute-start | bytes 3145736 | tf_op jit(solution)/shard_map/ppermute | solution.py:99
  49.3 32.3 %collective-permute-start.4 = (bf16[1024,512]{1,0:T(8,128)(2,1)}, bf16[1024,512]{1,0:T(8,128)(2,1)}, u32[]{:S(2)}, u32[]{:S(2)}) collective-permute-start(bf16[1024,512]{1,0:T(8,128)(2,1)} %refs_4_.1), channel_id=1, source_target_pairs={{0,1},{1,0},{2,3},{3,2},{4,5},{5,4},{6,7},{7,6},{8,9},{9,8},{10,11... | collective-permute-start | bytes 3145736 | tf_op jit(solution)/shard_map/ppermute | solution.py:99
  81.6 26.3 %collective-permute-start.7 = (bf16[1024,512]{1,0:T(8,128)(2,1)}, bf16[1024,512]{1,0:T(8,128)(2,1)S(1)}, u32[]{:S(2)}, u32[]{:S(2)}) collective-permute-start(bf16[1024,512]{1,0:T(8,128)(2,1)} %get-tuple-element.350.refs_4_), channel_id=1, source_target_pairs={{0,2},{1,3},{2,0},{3,1},{4,6},{5,7},{6,4},{7,5},{8,10},{9,11},{10,... | collective-permute-start | bytes 3145736 | tf_op jit(solution)/shard_map/ppermute | solution.py:99
  82.1 36.7 %collective-permute-start.6 = (bf16[1024,512]{1,0:T(8,128)(2,1)}, bf16[1024,512]{1,0:T(8,128)(2,1)S(1)}, u32[]{:S(2)}, u32[]{:S(2)}) collective-permute-start(bf16[1024,512]{1,0:T(8,128)(2,1)} %get-tuple-element.350.refs_4_), channel_id=1, source_target_pairs={{0,1},{1,0},{2,3},{3,2},{4,5},{5,4},{6,7},{7,6},{8,9},{9,8},{10,11... | collective-permute-start | bytes 3145736 | tf_op jit(solution)/shard_map/ppermute | solution.py:99
  84.6 37.3 %collective-permute-start.10 = (bf16[1024,512]{1,0:T(8,128)(2,1)}, bf16[1024,512]{1,0:T(8,128)(2,1)S(1)}, u32[]{:S(2)}, u32[]{:S(2)}) collective-permute-start(bf16[1024,512]{1,0:T(8,128)(2,1)} %refs_4_.1), channel_id=1, source_target_pairs={{0,8},{4,12},{8,0},{12,4},{16,24},{20,28},{24,16},{28,20},{1,9},{5... | collective-permute-start | bytes 3145736 | tf_op jit(solution)/shard_map/ppermute | solution.py:99
  136.1 26.9 %collective-permute-start.11 = (bf16[512,512]{1,0:T(8,128)(2,1)}, bf16[512,512]{1,0:T(8,128)(2,1)}, u32[]{:S(2)}, u32[]{:S(2)}) collective-permute-start(bf16[512,512]{1,0:T(8,128)(2,1)} %slice.64), channel_id=1, source_target_pairs={{0,1},{1,0},{2,3},{3,2},{4,5},{5,4},{6,7},{7,6},{8,9},{9,8},{10,11... | collective-permute-start | bytes 1572872 | tf_op jit(solution)/shard_map/ppermute | solution.py:99
  136.2 26.7 %collective-permute-start.12 = (bf16[512,512]{1,0:T(8,128)(2,1)}, bf16[512,512]{1,0:T(8,128)(2,1)}, u32[]{:S(2)}, u32[]{:S(2)}) collective-permute-start(bf16[512,512]{1,0:T(8,128)(2,1)} %slice.65), channel_id=1, source_target_pairs={{0,2},{1,3},{2,0},{3,1},{4,6},{5,7},{6,4},{7,5},{8,10},{9,11},{10,... | collective-permute-start | bytes 1572872 | tf_op jit(solution)/shard_map/ppermute | solution.py:99
  161.3 54.4 %collective-permute-start.21 = (bf16[1024,640]{1,0:T(8,128)(2,1)}, bf16[1024,640]{1,0:T(8,128)(2,1)}, u32[]{:S(2)}, u32[]{:S(2)}) collective-permute-start(bf16[1024,640]{1,0:T(8,128)(2,1)} %get-tuple-element.470), channel_id=1, source_target_pairs={{0,8},{4,12},{8,0},{12,4},{16,24},{20,28},{24,16},{28,20},{1,9},{5... | collective-permute-start | bytes 3932168 | tf_op jit(solution)/shard_map/ppermute | solution.py:99
  169.7 272.5 %all-gather.8.cloned.1.call-start = ((), (), s32[]{:S(2)}) async-start(), calls=%async_computation.6 | async-start | bytes 5242880 | tf_op jit(solution)/shard_map/all_gather | solution.py:911
  225.0 37.1 %collective-permute-start.14 = (bf16[2,2,256,768]{3,2,1,0:T(8,128)(2,1)}, bf16[2,2,256,768]{3,2,1,0:T(8,128)(2,1)}, u32[]{:S(2)}, u32[]{:S(2)}) collective-permute-start(bf16[2,2,256,768]{3,2,1,0:T(8,128)(2,1)} %get-tuple-element.404), channel_id=1, source_target_pairs={{0,8},{4,12},{8,0},{12,4},{16,24},{20,28},{24,16},{28,20},{1,9},{5... | collective-permute-start | bytes 4718600 | tf_op jit(solution)/shard_map/ppermute | solution.py:99
  265.6 107.6 %collective-permute-start.18 = (bf16[1,2,256,768]{3,2,1,0:T(8,128)(2,1)}, bf16[1,2,256,768]{3,2,1,0:T(8,128)(2,1)}, u32[]{:S(2)}, u32[]{:S(2)}) collective-permute-start(bf16[1,2,256,768]{3,2,1,0:T(8,128)(2,1)} %get-tuple-element.442), channel_id=1, source_target_pairs={{0,16},{4,20},{8,24},{12,28},{16,0},{20,4},{24,8},{28,12},{1,17},{... | collective-permute-start | bytes 2359304 | tf_op jit(solution)/shard_map/ppermute | solution.py:99
  274.2 69.6 %collective-permute-start.17 = (bf16[2,3,256,768]{3,2,1,0:T(8,128)(2,1)}, bf16[2,3,256,768]{3,2,1,0:T(8,128)(2,1)}, u32[]{:S(2)}, u32[]{:S(2)}) collective-permute-start(bf16[2,3,256,768]{3,2,1,0:T(8,128)(2,1)} %get-tuple-element.432), channel_id=1, source_target_pairs={{0,8},{4,12},{8,0},{12,4},{16,24},{20,28},{24,16},{28,20},{1,9},{5... | collective-permute-start | bytes 7077896 | tf_op jit(solution)/shard_map/ppermute | solution.py:99
  348.9 27.3 %collective-permute-start.19 = (f32[8,128]{1,0:T(8,128)}, f32[8,128]{1,0:T(8,128)}, u32[]{:S(2)}, u32[]{:S(2)}) collective-permute-start(f32[8,128]{1,0:T(8,128)} %get-tuple-element.433.refs_0_), channel_id=1, source_target_pairs={{0,4},{4,0},{8,12},{12,8},{16,20},{20,16},{24,28},{28,24},{1,5},{5... | collective-permute-start | bytes 12296 | tf_op jit(solution)/shard_map/ppermute | solution.py:99
  348.9 99.4 %collective-permute-start.22 = (bf16[1,3,256,768]{3,2,1,0:T(8,128)(2,1)}, bf16[1,3,256,768]{3,2,1,0:T(8,128)(2,1)}, u32[]{:S(2)}, u32[]{:S(2)}) collective-permute-start(bf16[1,3,256,768]{3,2,1,0:T(8,128)(2,1)} %get-tuple-element.476), channel_id=1, source_target_pairs={{0,16},{4,20},{8,24},{12,28},{16,0},{20,4},{24,8},{28,12},{1,17},{... | collective-permute-start | bytes 3538952 | tf_op jit(solution)/shard_map/ppermute | solution.py:99
  349.1 81.7 %collective-permute-start.20 = (bf16[2,3,256,768]{3,2,1,0:T(8,128)(2,1)}, bf16[2,3,256,768]{3,2,1,0:T(8,128)(2,1)}, u32[]{:S(2)}, u32[]{:S(2)}) collective-permute-start(bf16[2,3,256,768]{3,2,1,0:T(8,128)(2,1)} %get-tuple-element.459), channel_id=1, source_target_pairs={{0,8},{4,12},{8,0},{12,4},{16,24},{20,28},{24,16},{28,20},{1,9},{5... | collective-permute-start | bytes 7077896 | tf_op jit(solution)/shard_map/ppermute | solution.py:99
  425.8 72.4 %all-to-all-start = ((bf16[4,256,2176]{2,1,0:T(8,128)(2,1)}), bf16[4,256,2176]{2,1,0:T(8,128)(2,1)}, u32[]{:S(2)}, u32[]{:S(2)}) async-start(bf16[4,256,2176]{2,1,0:T(8,128)(2,1)} %get-tuple-element.498), calls=%async_computation | async-start | bytes 8912896 | tf_op jit(solution)/shard_map/all_to_all | solution.py:145
  430.7 152.5 %all-gather.10.cloned.1.call-start = ((), (), s32[]{:S(2)}) async-start(), calls=%async_computation.7 | async-start | bytes 5242880 | tf_op jit(solution)/shard_map/all_gather | solution.py:982
  436.0 80.1 %collective-permute-start.24 = (bf16[1,3,256,768]{3,2,1,0:T(8,128)(2,1)}, bf16[1,3,256,768]{3,2,1,0:T(8,128)(2,1)}, u32[]{:S(2)}, u32[]{:S(2)}) collective-permute-start(bf16[1,3,256,768]{3,2,1,0:T(8,128)(2,1)} %get-tuple-element.514), channel_id=1, source_target_pairs={{0,16},{4,20},{8,24},{12,28},{16,0},{20,4},{24,8},{28,12},{1,17},{... | collective-permute-start | bytes 3538952 | tf_op jit(solution)/shard_map/ppermute | solution.py:99
  513.4 104.0 %collective-permute-start.29 = (bf16[2,2,256,768]{3,2,1,0:T(8,128)(2,1)}, bf16[2,2,256,768]{3,2,1,0:T(8,128)(2,1)}, u32[]{:S(2)}, u32[]{:S(2)}) collective-permute-start(bf16[2,2,256,768]{3,2,1,0:T(8,128)(2,1)} %get-tuple-element.571), channel_id=1, source_target_pairs={{0,16},{4,20},{8,24},{12,28},{16,0},{20,4},{24,8},{28,12},{1,17},{... | collective-permute-start | bytes 4718600 | tf_op jit(solution)/shard_map/ppermute | solution.py:99
  544.4 33.3 %collective-permute-start.26 = (bf16[4,2,256,768]{3,2,1,0:T(8,128)(2,1)}, bf16[4,2,256,768]{3,2,1,0:T(8,128)(2,1)}, u32[]{:S(2)}, u32[]{:S(2)}) collective-permute-start(bf16[4,2,256,768]{3,2,1,0:T(8,128)(2,1)} %get-tuple-element.531), channel_id=1, source_target_pairs={{0,4},{4,0},{8,12},{12,8},{16,20},{20,16},{24,28},{28,24},{1,5},{5... | collective-permute-start | bytes 9437192 | tf_op jit(solution)/shard_map/ppermute | solution.py:99
  572.8 78.4 %all-to-all-start.1 = ((bf16[4,1024,512]{2,1,0:T(8,128)(2,1)}), bf16[4,1024,512]{2,1,0:T(8,128)(2,1)}, u32[]{:S(2)}, u32[]{:S(2)}) async-start(bf16[4,1024,512]{2,1,0:T(8,128)(2,1)} %get-tuple-element.547), calls=%async_computation.1 | async-start | bytes 8388608 | tf_op jit(solution)/shard_map/all_to_all | solution.py:145
  577.7 185.2 %reduce-scatter.5.cloned.1.call-start = ((), (), s32[]{:S(2)}) async-start(), calls=%async_computation.9 | async-start | bytes 2359296 | tf_op jit(solution)/shard_map/reduce_scatter | solution.py:994
  582.9 125.5 %collective-permute-start.31 = (bf16[2,2,256,768]{3,2,1,0:T(8,128)(2,1)}, bf16[2,2,256,768]{3,2,1,0:T(8,128)(2,1)}, u32[]{:S(2)}, u32[]{:S(2)}) collective-permute-start(bf16[2,2,256,768]{3,2,1,0:T(8,128)(2,1)} %get-tuple-element.586), channel_id=1, source_target_pairs={{0,16},{4,20},{8,24},{12,28},{16,0},{20,4},{24,8},{28,12},{1,17},{... | collective-permute-start | bytes 4718600 | tf_op jit(solution)/shard_map/ppermute | solution.py:99
  589.2 187.3 %reduce-scatter.3.cloned.1.call-start = ((), (), s32[]{:S(2)}) async-start(), calls=%async_computation.8 | async-start | bytes 7077888 | tf_op jit(solution)/shard_map/reduce_scatter | solution.py:994
  621.5 95.3 %collective-permute-start.33 = (bf16[1,2,256,768]{3,2,1,0:T(8,128)(2,1)}, bf16[1,2,256,768]{3,2,1,0:T(8,128)(2,1)}, u32[]{:S(2)}, u32[]{:S(2)}) collective-permute-start(bf16[1,2,256,768]{3,2,1,0:T(8,128)(2,1)} %get-tuple-element.596), channel_id=1, source_target_pairs={{0,8},{4,12},{8,0},{12,4},{16,24},{20,28},{24,16},{28,20},{1,9},{5... | collective-permute-start | bytes 2359304 | tf_op jit(solution)/shard_map/ppermute | solution.py:99
  651.2 93.0 %all-to-all-start.2 = ((bf16[4,1024,512]{2,1,0:T(8,128)(2,1)}), bf16[4,1024,512]{2,1,0:T(8,128)(2,1)}, u32[]{:S(2)}, u32[]{:S(2)}) async-start(bf16[4,1024,512]{2,1,0:T(8,128)(2,1)} %get-tuple-element.623), calls=%async_computation.2 | async-start | bytes 8388608 | tf_op jit(solution)/shard_map/all_to_all | solution.py:145
  663.5 41.2 %collective-permute-start.30 = (f32[8,128]{1,0:T(8,128)}, f32[8,128]{1,0:T(8,128)}, u32[]{:S(2)}, u32[]{:S(2)}) collective-permute-start(f32[8,128]{1,0:T(8,128)} %get-tuple-element.580.refs_4_), channel_id=1, source_target_pairs={{0,2},{1,3},{2,0},{3,1},{4,6},{5,7},{6,4},{7,5},{8,10},{9,11},{10,... | collective-permute-start | bytes 12296 | tf_op jit(solution)/shard_map/ppermute | solution.py:99
  667.9 44.0 %collective-permute-start.32 = (f32[19,2048]{1,0:T(8,128)}, f32[19,2048]{1,0:T(8,128)}, u32[]{:S(2)}, u32[]{:S(2)}) collective-permute-start(f32[19,2048]{1,0:T(8,128)} %get-tuple-element.591.refs_4_), channel_id=1, source_target_pairs={{0,8},{4,12},{8,0},{12,4},{16,24},{20,28},{24,16},{28,20},{1,9},{5... | collective-permute-start | bytes 466952 | tf_op jit(solution)/shard_map/ppermute | solution.py:99
  715.5 43.2 %collective-permute-start.37 = (bf16[1,2,256,768]{3,2,1,0:T(8,128)(2,1)}, bf16[1,2,256,768]{3,2,1,0:T(8,128)(2,1)}, u32[]{:S(2)}, u32[]{:S(2)}) collective-permute-start(bf16[1,2,256,768]{3,2,1,0:T(8,128)(2,1)} %get-tuple-element.635), channel_id=1, source_target_pairs={{0,8},{4,12},{8,0},{12,4},{16,24},{20,28},{24,16},{28,20},{1,9},{5... | collective-permute-start | bytes 2359304 | tf_op jit(solution)/shard_map/ppermute | solution.py:99
  (29 other events, 464.5 us)
Sparse Core Ops, SparseCore 0:
  38.9 101.0 all-gather.11
  169.9 51.3 all-gather.5
  223.1 52.5 all-gather.7
  505.9 53.5 all-gather.9
  589.3 91.1 reduce-scatter.4
  682.7 93.7 reduce-scatter.2

commit v4 on v3

--- a/solution.py
+++ b/solution.py
@@ -12,9 +12,10 @@
 LEN = 1024
 EPS = 1e-05
 ROPE_BASE = 10000.0
-VMEM_LIMIT = 56 << 20
+VMEM_MIB = 60
 TB = 256
 MARKS = 4
+PARTS = 1
 HEAVY = 10**12
 f32, bf16 = jnp.float32, jnp.bfloat16
 NT = (((1,), (1,)), ((), ()))
@@ -57,13 +58,14 @@
         self.last = [*self.last, self.sent]
 
     def pin(self, value):
-        return lax.optimization_barrier((value, *self.last))[0]
+        value, *self.last = lax.optimization_barrier((value, *self.last))
+        return value
 
 
 line = Line()
 
 
-def call(body, grid, scalars, ins, in_specs, outs, out_specs, scratch=(), aliases=None):
+def call(body, grid, scalars, ins, in_specs, outs, out_specs, scratch=(), aliases=None, vmem=VMEM_MIB):
     deps, n_in, n_out = line.last, len(ins), len(outs)
 
     def without_deps(scalars, *refs):
@@ -84,7 +86,7 @@
             scratch_shapes=list(scratch),
         ),
         input_output_aliases={1 + len(deps) + k: v for k, v in (aliases or {}).items()},
-        compiler_params=pltpu.CompilerParams(vmem_limit_bytes=VMEM_LIMIT),
+        compiler_params=pltpu.CompilerParams(vmem_limit_bytes=vmem << 20),
         cost_estimate=pl.CostEstimate(flops=HEAVY, bytes_accessed=1, transcendentals=0),
     )(scalars, *deps, *ins)
     line.last = result[len(outs) :]
@@ -100,12 +102,17 @@
 
 
 def gather_pieces(value, axis, count, pin=lambda v: v):
+    if count == 4 and isinstance(value, tuple):
+        one, two = (tuple(swap(half, axis, count, mask) for half in value) for mask in (1, 2))
+        one, two = pin((one, two))
+        return [value, one, two, (swap(two[0], axis, count, 1), swap(one[1], axis, count, 2))]
+    if isinstance(value, tuple):
+        value = jnp.concatenate(value, axis=0)
     if count == 4:
         half = value.shape[0] // 2
         one, two = swap(value, axis, count, 1), swap(value, axis, count, 2)
         one, two = pin((one, two))
-        top, bottom = swap(two[:half], axis, count, 1), swap(one[half:], axis, count, 2)
-        return [value, one, two, (top, bottom)]
+        return [value, one, two, (swap(two[:half], axis, count, 1), swap(one[half:], axis, count, 2))]
     pieces, mask = [value], 1
     while mask < count:
         pieces = pieces + [swap(piece, axis, count, mask) for piece in pieces]
@@ -133,12 +140,17 @@
     return specs
 
 
-def read_pieces(refs, n_tp):
-    values = [ref[...] for ref in refs]
-    if len(refs) == n_tp:
-        return values
+def halved(pieces):
+    return [isinstance(piece, tuple) for piece in pieces]
+
+
+def read_pieces(refs, halves):
+    refs, values = list(refs), []
     early = pl.program_id(0) < pl.num_programs(0) // 2
-    return values[: n_tp - 1] + [jnp.where(early, values[n_tp - 1], values[n_tp])]
+    for in_halves in halves:
+        value = refs.pop(0)[...]
+        values.append(jnp.where(early, value, refs.pop(0)[...]) if in_halves else value)
+    return values
 
 
 def trade(pieces, axis):
@@ -151,12 +163,12 @@
 
 
 def add_halves(scalars, keep, arrived):
-    blocks, count, rows, width = keep.shape
-    half = blocks // 2
-    low = pl.BlockSpec((half, 1, rows, width), lambda i, s: (0, i, 0, 0))
-    high = pl.BlockSpec((half, 1, rows, width), lambda i, s: (1, i, 0, 0))
-    out = struct((half, count, rows, width), bf16)
-    return call(halves_kernel, (count,), scalars, [keep, keep, arrived, arrived], [low, high] * 2, [out] * 2, [low] * 2)
+    keep, arrived = line.pin((keep, arrived))
+    half = keep.shape[0] // 2
+    low = lambda left, right: (left.astype(f32) + right.astype(f32)).astype(bf16)
+    out = low(keep[:half], arrived[:half]), low(keep[half:], arrived[half:])
+    line.last = [*line.last, out[1]]
+    return out
 
 
 def sum_kernel(scalars, left, right, out):
@@ -182,8 +194,51 @@
         target[place * width : (place + 1) * width, :] = source[:, cols].T
 
 
-def project_kernel(n_tp, n_in, heads, scalars, *refs):
-    pieces = read_pieces(refs[:n_in], n_tp)
+def named_kernel(scalars, ids, *refs):
+    *shares, out, shares_out = refs
+    for r, share in enumerate(shares):
+        shares_out[scalars[r]] = share[...]
+    named = jnp.zeros(out.shape, jnp.bool_)
+    lanes = lax.broadcasted_iota(jnp.int32, out.shape, 1)
+    for choice in range(ids.shape[1]):
+        named = named | (ids[:, choice : choice + 1] == lanes)
+    out[...] = named.astype(f32)
+
+
+def kept_kernel(capacity, scalars, named, out):
+    tokens = named.shape[0]
+    earlier = lax.broadcasted_iota(jnp.int32, (tokens, tokens), 0) > lax.broadcasted_iota(
+        jnp.int32, (tokens, tokens), 1
+    )
+    rank = dot(jnp.where(earlier, 1.0, 0.0).astype(bf16), named[...].astype(bf16))
+    out[...] = jnp.where(rank < capacity, named[...], 0.0)
+
+
+def named_pairs(scalars, expert_ids, shares, experts):
+    tokens, chosen = expert_ids.shape
+    plain = lambda h, w: pl.BlockSpec((h, w), lambda i, s: (0, 0))
+    rows, features = shares[0].shape
+    whole = (len(shares), rows, features)
+    return call(
+        named_kernel,
+        (1,),
+        scalars,
+        [expert_ids, *shares],
+        [plain(tokens, chosen)] + [plain(rows, features)] * len(shares),
+        [struct((tokens, experts), f32), struct(whole, shares[0].dtype)],
+        [plain(tokens, experts), pl.BlockSpec(whole, lambda i, s: (0, 0, 0))],
+    )
+
+
+def kept_pairs(scalars, named, capacity):
+    plain = pl.BlockSpec(named.shape, lambda i, s: (0, 0))
+    out = [struct(named.shape, f32)]
+    return call(functools.partial(kept_kernel, capacity), (1,), scalars, [named], [plain], out, [plain])[0]
+
+
+def project_kernel(n_tp, halves, heads, scalars, *refs):
+    n_in = len(halves) + sum(halves)
+    pieces = read_pieces(refs[:n_in], halves)
     gain, wq, wk, wv, q_gain, k_gain, cosine, sine = refs[n_in : n_in + 8]
     x_out, normed_out, factor_out, q_raw, k_raw, q_rot, k_rot, v_out = refs[n_in + 8 :]
     width = pieces[0].shape[1]
@@ -219,7 +274,7 @@
     local = heads * hd
     rows = lambda w: pl.BlockSpec((TB, w), lambda i, s: (i, 0))
     return call(
-        functools.partial(project_kernel, n_tp, len(flat(pieces)), heads),
+        functools.partial(project_kernel, n_tp, halved(pieces), heads),
         (tokens // TB,),
         scalars,
         [*flat(pieces), gain, wq, wk, wv, q_gain, k_gain, cosine, sine],
@@ -238,7 +293,7 @@
     )
 
 
-def attend_kernel(block, scalars, q_ref, k_ref, v_ref, out_ref, total_ref):
+def attend_kernel(block, scalars, q_ref, k_ref, v_ref, top_ref, bottom_ref, total_ref):
     tokens, hd = q_ref.shape
     scale = 1.0 / math.sqrt(hd)
     for i in range(tokens // block):
@@ -252,7 +307,9 @@
         weights = jnp.exp(scores - top)
         total = jnp.sum(weights, axis=1, keepdims=True)
         probs = (weights * (1.0 / total)).astype(bf16)
-        out_ref[rows, :] = dot(probs, v_ref[:reach, :]).astype(bf16)
+        half = tokens // 2
+        out_ref, first = (top_ref, 0) if reach <= half else (bottom_ref, half)
+        out_ref[i * block - first : reach - first, :] = dot(probs, v_ref[:reach, :]).astype(bf16)
         total_ref[0, rows, :] = top + jnp.log(total)
 
 
@@ -261,13 +318,14 @@
     hd = local // heads
     column = pl.BlockSpec((tokens, hd), lambda h, s: (0, h))
     return call(
-        functools.partial(attend_kernel, min(256, tokens)),
+        functools.partial(attend_kernel, min(256, tokens // 2)),
         (heads,),
         scalars,
         [q_rot, k_rot, value],
         [column] * 3,
-        [struct((tokens, local), bf16), struct((heads, tokens, 1), f32)],
-        [column, pl.BlockSpec((1, tokens, 1), lambda h, s: (h, 0, 0))],
+        [struct((tokens // 2, local), bf16)] * 2 + [struct((heads, tokens, 1), f32)],
+        [pl.BlockSpec((tokens // 2, hd), lambda h, s: (0, h))] * 2
+        + [pl.BlockSpec((1, tokens, 1), lambda h, s: (h, 0, 0))],
     )
 
 
@@ -339,26 +397,32 @@
     )
 
 
-def whole_grad_kernel(n_tp, n_in, dp_count, scalars, *refs):
-    pieces = read_pieces(refs[:n_in], n_tp)
-    whole_out, turned_out = refs[n_in:]
+def whole_first_kernel(n_in, each, base, scalars, *refs):
+    pieces, (whole_out, turned_out) = refs[:n_in], refs[n_in:]
     width = pieces[0].shape[1]
-    for r in range(n_tp):
+    part = width // each
+    for r in range(n_in):
         cols = pl.ds(pl.multiple_of(scalars[r] * width, width), width)
-        whole_out[:, cols] = pieces[r]
-    transpose_blocks(scalars, n_tp, whole_out, turned_out, dp_count)
-
-
-def whole_grad(scalars, pieces, dp_count):
-    n_tp = len(pieces)
+        whole_out[:, cols] = pieces[r][...]
+        for q in range(each):
+            rows = pl.ds(pl.multiple_of(scalars[base + r * each + q] * part, part), part)
+            turned_out[rows, :] = pieces[r][:, q * part : (q + 1) * part].T
+
+
+def whole_last_kernel(scalars, piece, old_whole, old_turned, whole_out, turned_out):
+    whole_out[...] = piece[...]
+    turned_out[...] = piece[...].T
+
+
+def whole_first(scalars, pieces, n_tp, dp_count, base):
     tokens, width = pieces[0].shape
     features = width * n_tp
     return call(
-        functools.partial(whole_grad_kernel, n_tp, len(flat(pieces)), dp_count),
+        functools.partial(whole_first_kernel, len(pieces), dp_count // n_tp, base),
         (tokens // TB,),
         scalars,
-        flat(pieces),
-        piece_specs(pieces, TB, width),
+        pieces,
+        [pl.BlockSpec((TB, width), lambda i, s: (i, 0))] * len(pieces),
         [struct((tokens, features), bf16), struct((features, tokens), bf16)],
         [
             pl.BlockSpec((TB, features), lambda i, s: (i, 0)),
@@ -367,15 +431,65 @@
     )
 
 
-def stream_kernel(n_tp, n_in, dp_count, scalars, *refs):
-    pieces = read_pieces(refs[:n_in], n_tp)
-    x_ref, w_ref, gain, router, kept = refs[n_in : n_in + 5]
-    stream_out, normed_out, mine_out, turned_out, factor_out, probs_out, gates_out = refs[n_in + 5 :]
-    width = pieces[0].shape[1]
-    total = x_ref[...].astype(f32)
-    for r in range(n_tp):
-        weight = w_ref[:, pl.ds(scalars[r], 1)]
-        total += dot(pieces[r], weight.reshape(width, weight.shape[-1]))
+def whole_last(scalars, piece, r, whole, turned, dp_count, n_tp, base):
+    tokens, width = piece.shape
+    each = dp_count // n_tp
+    part = width // each
+    place = lambda s, q: s[base + r * each + q]
+    return call(
+        whole_last_kernel,
+        (tokens // TB, each),
+        scalars,
+        [piece, whole, turned],
+        [pl.BlockSpec((TB, part), lambda i, q, s: (i, q))] + [pl.BlockSpec(memory_space=pl.ANY)] * 2,
+        [struct(whole.shape, bf16), struct(turned.shape, bf16)],
+        [
+            pl.BlockSpec((TB, part), lambda i, q, s: (i, s[r] * each + q)),
+            pl.BlockSpec((part, TB), lambda i, q, s: (place(s, q), i)),
+        ],
+        aliases={1: 0, 2: 1},
+    )
+
+
+def add_products(total, pieces, weights):
+    for piece, weight in zip(pieces, weights):
+        total += dot(piece, weight[...].reshape(piece.shape[1], weight.shape[-1]))
+    return total
+
+
+def stream_first_kernel(halves, scalars, x_ref, *refs):
+    n_in = len(halves) + sum(halves)
+    pieces, weights, out = read_pieces(refs[:n_in], halves), refs[n_in:-1], refs[-1]
+    out[...] = add_products(x_ref[...].astype(f32), pieces, weights)
+
+
+def weight_specs(w_all, places):
+    n_dp, _, share, features = w_all.shape
+    return [pl.BlockSpec((n_dp, 1, share, features), lambda i, s, r=r: (0, s[r], 0, 0)) for r in places]
+
+
+def stream_first(scalars, pieces, x, w_all):
+    tokens, features = x.shape
+    rows = pl.BlockSpec((TB, features), lambda i, s: (i, 0))
+    return call(
+        functools.partial(stream_first_kernel, halved(pieces)),
+        (tokens // TB,),
+        scalars,
+        [x, *flat(pieces)] + [w_all] * len(pieces),
+        [rows] + piece_specs(pieces, TB, flat(pieces)[0].shape[1]) + weight_specs(w_all, range(len(pieces))),
+        [struct((tokens, features), f32)],
+        [rows],
+    )[0]
+
+
+def stream_kernel(n_tp, halves, dp_count, scalars, *refs):
+    n_last, n_in = len(halves), len(halves) + sum(halves)
+    pieces = read_pieces(refs[:n_in], halves)
+    weights = refs[n_in : n_in + n_last]
+    first, gain, router, kept = refs[n_in + n_last : n_in + n_last + 4]
+    stream_out, normed_out, mine_out, turned_out, factor_out, probs_out, gates_out = refs[n_in + n_last + 4 :]
+    total = add_products(first[...], pieces, weights)
+    width = total.shape[1] // n_tp
     stream_out[...] = total
     factor = lax.rsqrt(jnp.mean(total * total, axis=1, keepdims=True) + EPS)
     factor_out[...] = factor
@@ -392,21 +506,24 @@
     transpose_blocks(scalars, n_tp, normed_out, turned_out, dp_count)
 
 
-def stream_of(scalars, pieces, x, w_all, gain, router, kept, dp_count):
-    n_tp = len(pieces)
-    tokens, features = x.shape
+def stream_of(scalars, pieces, first, w_all, gain, router, kept, n_tp, dp_count):
+    tokens, features = first.shape
     experts = router.shape[1]
+    width = features // n_tp
     rows = lambda w: pl.BlockSpec((TB, w), lambda i, s: (i, 0))
-    return call(
-        functools.partial(stream_kernel, n_tp, len(flat(pieces)), dp_count),
+    places = range(n_tp - len(pieces), n_tp)
+    return call(
+        functools.partial(stream_kernel, n_tp, halved(pieces), dp_count),
         (tokens // TB,),
         scalars,
-        [*flat(pieces), x, w_all, gain, router, kept],
-        piece_specs(pieces, TB, pieces[0].shape[1]) + [rows(features)] + [whole_spec()] * 3 + [rows(experts)],
+        [*flat(pieces)] + [w_all] * len(pieces) + [first, gain, router, kept],
+        piece_specs(pieces, TB, flat(pieces)[0].shape[1])
+        + weight_specs(w_all, places)
+        + [rows(features), whole_spec(), whole_spec(), rows(experts)],
         [
             struct((tokens, features), f32),
             struct((tokens, features), bf16),
-            struct((tokens, features // n_tp + 128), bf16),
+            struct((tokens, width + 128), bf16),
             struct((features, tokens), bf16),
             struct((tokens, 1), f32),
             struct((tokens, experts), f32),
@@ -415,7 +532,7 @@
         [
             rows(features),
             rows(features),
-            rows(features // n_tp + 128),
+            rows(width + 128),
             pl.BlockSpec((features, TB), lambda i, s: (0, i)),
             rows(1),
             rows(experts),
@@ -511,17 +628,13 @@
     return (index & ~3) | ((index & 1) << 1) | ((index >> 1) & 1)
 
 
-def shared_grads_kernel(shift, scalars, *refs):
-    turned, turned2, g_turned, g_turned2, hidden_a, hidden_b, hidden2, pair_a, pair_b, pair2 = refs[:10]
-    keep_out, send_out = refs[10:]
-    here = scalars[shift] == 0
-    hidden = jnp.where(here, hidden_a[0], hidden_b[0])
-    pair = jnp.where(here, pair_a[0], pair_b[0])
+def shared_grads_kernel(scalars, *refs):
+    turned, turned2, g_turned, g_turned2, hidden, hidden2, pair, pair2, keep_out, send_out = refs
     half, _, rows, _ = keep_out.shape
     width = hidden.shape[-1]
-    first = dot(turned[...], pair) + dot(turned2[...], pair2[0])
+    first = dot(turned[...], pair[0]) + dot(turned2[...], pair2[0])
     first = first.astype(bf16).reshape(2 * half, rows, 2 * width)
-    second = dot(g_turned[...], hidden) + dot(g_turned2[...], hidden2[0])
+    second = dot(g_turned[...], hidden[0]) + dot(g_turned2[...], hidden2[0])
     second = second.astype(bf16).reshape(2 * half, rows, width)
     for out, base in ((keep_out, 0), (send_out, half)):
         for place in range(half):
@@ -529,20 +642,21 @@
             out[inner_swap(place), 0, :, 2 * width :] = second[base + place]
 
 
-def shared_grads(scalars, turned, turned2, g_turned, g_turned2, hidden, hidden2, pair, pair2, shift, offset, count,
+def shared_grads(scalars, turned, turned2, g_turned, g_turned2, hidden, hidden2, pair, pair2, shift, base, offset, count,
                  dp_count):
     features, tokens = turned.shape
     width = hidden2.shape[-1]
     half, rows = dp_count // 2, features // dp_count
     out = struct((half, count, rows, 3 * width), bf16)
     out_spec = pl.BlockSpec((half, 1, rows, 3 * width), lambda i, s: (0, i, 0, 0))
-    block = lambda w: pl.BlockSpec((1, tokens, w), lambda i, s: (offset + i, 0, 0))
-    return call(
-        functools.partial(shared_grads_kernel, shift),
+    mine = lambda w: pl.BlockSpec((1, tokens, w), lambda i, s: (base + s[shift] + offset + i, 0, 0))
+    other = lambda w: pl.BlockSpec((1, tokens, w), lambda i, s: (offset + i, 0, 0))
+    return call(
+        shared_grads_kernel,
         (count,),
         scalars,
-        [turned, turned2, g_turned, g_turned2, *hidden, hidden2, *pair, pair2],
-        [whole_spec()] * 4 + [block(width)] * 3 + [block(2 * width)] * 3,
+        [turned, turned2, g_turned, g_turned2, hidden, hidden2, pair, pair2],
+        [whole_spec()] * 4 + [mine(width), other(width), mine(2 * width), other(2 * width)],
         [out, out],
         [out_spec, out_spec],
     )
@@ -599,21 +713,18 @@
     first = 0
     for pair, size in zip(pairs, sizes):
 
-        @pl.when((step >= first) & (step < first + size))
-        def _(pair=pair, first=first):
-            part = dot(pair[0, :, :width], wg[0], NT) + dot(pair[0, :, width:], wu[0], NT)
-            if first == 0:
-
-                @pl.when(step == 0)
-                def _():
-                    acc[...] = part
-
-                @pl.when(step > 0)
-                def _():
-                    acc[...] += part
-
-            else:
-                acc[...] += part
+        def product(pair=pair):
+            return dot(pair[0, :, :width], wg[0], NT) + dot(pair[0, :, width:], wu[0], NT)
+
+        if first == 0:
+
+            @pl.when(step == 0)
+            def _(product=product):
+                acc[...] = product()
+
+        @pl.when((step >= max(first, 1)) & (step < first + size))
+        def _(product=product):
+            acc[...] += product()
 
         first += size
 
@@ -651,21 +762,15 @@
     first = 0
     for hidden, size in zip(hiddens, sizes):
 
-        @pl.when((step >= first) & (step < first + size))
-        def _(hidden=hidden, first=first):
-            part = dot(hidden[0], wd[0])
-            if first == 0:
-
-                @pl.when(step == 0)
-                def _():
-                    acc[...] = part
-
-                @pl.when(step > 0)
-                def _():
-                    acc[...] += part
-
-            else:
-                acc[...] += part
+        if first == 0:
+
+            @pl.when(step == 0)
+            def _(hidden=hidden):
+                acc[...] = dot(hidden[0], wd[0])
+
+        @pl.when((step >= max(first, 1)) & (step < first + size))
+        def _(hidden=hidden):
+            acc[...] += dot(hidden[0], wd[0])
 
         first += size
 
@@ -784,6 +889,63 @@
     )
 
 
+def flip_kernel(source, target):
+    target[...] = source[...].T
+
+
+def flip(scalars, value):
+    tokens, features = value.shape
+    return call(
+        lambda scalars, source, target: flip_kernel(source, target),
+        (tokens // TB,),
+        scalars,
+        [value],
+        [pl.BlockSpec((TB, features), lambda i, s: (i, 0))],
+        [struct((features, tokens), bf16)],
+        [pl.BlockSpec((features, TB), lambda i, s: (0, i))],
+    )[0]
+
+
+def head_weight_grads(scalars, flipped, grads):
+    features, tokens = flipped.shape
+    count, _, local = grads.shape
+
+    def kernel(scalars, flipped, grad, out):
+        out[0] = dot(flipped[...], grad[0]).astype(bf16)
+
+    return call(
+        kernel,
+        (count,),
+        scalars,
+        [flipped, grads],
+        [whole_spec(), pl.BlockSpec((1, tokens, local), lambda i, s: (i, 0, 0))],
+        [struct((count, features, local), bf16)],
+        [pl.BlockSpec((1, features, local), lambda i, s: (i, 0, 0))],
+    )[0]
+
+
+def output_weight_grads(scalars, top, bottom, grad, first, dp_count):
+    half, local = top.shape
+    width = grad.shape[1] // dp_count
+
+    def kernel(scalars, top, bottom, keep, send, keep_out, send_out):
+        for grad, out in ((keep, keep_out), (send, send_out)):
+            product = dot(top[...], grad[:half, :], TN) + dot(bottom[...], grad[half:, :], TN)
+            out[0, 0] = product.astype(bf16)
+
+    column = lambda base: pl.BlockSpec((2 * half, width), lambda i, s: (0, s[base + i]))
+    block = pl.BlockSpec((1, 1, local, width), lambda i, s: (i, 0, 0, 0))
+    return call(
+        kernel,
+        (dp_count // 2,),
+        scalars,
+        [top, bottom, grad, grad],
+        [whole_spec(), whole_spec(), column(first), column(first + dp_count // 2)],
+        [struct((dp_count // 2, 1, local, width), bf16)] * 2,
+        [block] * 2,
+    )
+
+
 def turn_kernel(first, dp_count, scalars, source, target):
     transpose_blocks(scalars, first, source, target, dp_count)
 
@@ -843,14 +1005,6 @@
         [struct((tokens, width), bf16)],
         [plain(width)],
     )[0]
-
-
-def kept_pairs(expert_ids, experts, capacity):
-    tokens = expert_ids.shape[0]
-    named = jnp.any(expert_ids[:, :, None] == jnp.arange(experts, dtype=jnp.int32), axis=1)
-    earlier = jnp.arange(tokens)[:, None] > jnp.arange(tokens)[None, :]
-    rank = dot(earlier.astype(bf16), named.astype(bf16))
-    return (named & (rank < capacity)).astype(f32)
 
 
 def body(n_dp, n_tp, cosine, sine, tokens, cotangent, attn_gain, w_query, w_key, w_value, query_gain, key_gain,
@@ -869,40 +1023,47 @@
     lead = sum(blocks)
     shared = (experts - lead) // 2
     shift, other_shift = n_tp + n_dp, n_tp + n_dp + 1
+    each = n_dp // n_tp
     scalars = jnp.stack(
         [tp ^ r for r in range(n_tp)]
         + [dp ^ bit_reverse(place, n_dp) for place in range(n_dp)]
         + [side * shared, (1 - side) * shared]
+        + [bit_reverse(((tp ^ r) * each + q) ^ dp, n_dp) for r in range(n_tp) for q in range(each)]
     ).astype(jnp.int32)
+    turned_base = n_tp + n_dp + 2
 
     line.last = []
 
     share = local // n_dp
     w_share = lax.dynamic_slice_in_dim(w_output, dp * share, share, 0)
-    w_all = lax.all_gather(w_share, ("dp", "tensor")).reshape(n_dp, n_tp, share, features)
-
-    x_pieces = gather_pieces(tokens, "tensor", n_tp)
-    kept = kept_pairs(expert_ids, experts, capacity)
-    x_pieces, g_mine, kept = lax.optimization_barrier((x_pieces, cotangent, kept))
-    g_near = swap(g_mine, "dp", n_dp, near)
-    g_pieces = [g_mine, swap(g_mine, "tensor", n_tp, 1), swap(g_mine, "tensor", n_tp, 2)]
+    w_shares = direct_pieces(w_share, "tensor", n_tp)
+
+    named, w_some = named_pairs(scalars, expert_ids, w_shares, experts)
+    w_all = lax.all_gather(w_some, "dp")
+    x_pieces = gather_pieces(tokens, "tensor", n_tp, pin=line.pin)
+    kept = kept_pairs(scalars, named, capacity)
+    x_pieces, g_mine = lax.optimization_barrier((x_pieces, cotangent))
+    early = n_tp - 1 if n_tp == 4 else n_tp // 2
+    g_pieces = [g_mine] + [swap(g_mine, "tensor", n_tp, r) for r in range(1, early)]
     x, normed1, factor1, q_raw, k_raw, q_rot, k_rot, value = project(
         scalars, x_pieces, gain1, w_query, w_key, w_value, query_gain, key_gain, cosine, sine
     )
-    attended, totals = attend(scalars, q_rot, k_rot, value, heads)
-    attended, g_pieces = lax.optimization_barrier((attended, g_pieces))
-    attended_pieces = gather_pieces(attended, "tensor", n_tp)
-    attended_pieces, g_pieces, g_near = lax.optimization_barrier((attended_pieces, g_pieces, g_near))
-    if n_tp == 4:
-        half = token_count // 2
-        one, two = g_pieces[1], g_pieces[2]
-        g_pieces.append((swap(two[:half], "tensor", n_tp, 1), swap(one[half:], "tensor", n_tp, 2)))
-    else:
-        g_pieces = direct_pieces(g_pieces[0], "tensor", n_tp)
+    *attended, totals = attend(scalars, q_rot, k_rot, value, heads)
+    attended, g_pieces = lax.optimization_barrier((tuple(attended), g_pieces))
+    upstream, g_turned = whole_first(scalars, g_pieces, n_tp, n_dp, turned_base)
+    flipped = flip(scalars, normed1)
+    attended_pieces = gather_pieces(attended, "tensor", n_tp, pin=line.pin)
+    stream = stream_first(scalars, attended_pieces[:early], x, w_all)
+    g_mine = line.pin(g_mine)
+    g_last = [swap(g_mine, "tensor", n_tp, r) for r in range(early, n_tp)]
+    g_near = swap(g_mine, "dp", n_dp, near)
     stream, normed2, normed2_mine, turned, factor2, probs, gates = stream_of(
-        scalars, attended_pieces, x, w_all, gain2, w_router, kept, n_dp
-    )
-    upstream, g_turned = whole_grad(scalars, g_pieces, n_dp)
+        scalars, attended_pieces[early:], stream, w_all, gain2, w_router, kept, n_tp, n_dp
+    )
+    for r in range(early, n_tp):
+        upstream, g_turned = whole_last(
+            scalars, g_last[r - early], r, upstream, g_turned, n_dp, n_tp, turned_base
+        )
     normed_near = swap(normed2_mine, "dp", n_dp, near)
     g_near, _ = lax.optimization_barrier((g_near, upstream))
     upstream_near = lax.all_gather(g_near, "tensor", axis=1, tiled=True)
@@ -924,9 +1085,11 @@
     lower = [mask for mask in (2, 4, 8, 16) if mask < far]
 
     def own_sums(index):
-        first, count = sum(blocks[:index]), blocks[index]
-        keep, send = weight_grads(scalars, turned, g_turned, hiddens[index], pairs[index], 0, count, n_dp)
+        keep, send = weight_grads(scalars, turned, g_turned, hiddens[index], pairs[index], 0, blocks[index], n_dp)
         return sum_step(keep, send, 1)
+
+    def next_step(take):
+        return sum_step(*take(), lower[0])
 
     def last_step(take):
         keep, send = take()
@@ -934,36 +1097,43 @@
             keep, send = sum_step(keep, send, mask)()
         return [keep[0], swap(send, "dp", n_dp, far)[0]]
 
+    def complete(parts, old, index):
+        return finish(scalars, parts, old, sum(blocks[:index]), None, experts)
+
     run(0, blocks[0])
     take0 = own_sums(0)
     run(blocks[0], blocks[1])
-    take0 = sum_step(*take0(), lower[0])
+    take0 = next_step(take0)
     take1 = own_sums(1)
     run(blocks[0] + blocks[1], blocks[2])
     parts0 = last_step(take0)
-    take1 = sum_step(*take1(), lower[0])
+    take1 = next_step(take1)
+    line.tick("dp", n_dp)
+    run(sum(blocks[:3]), experts - sum(blocks[:3]))
+    line.take()
     take2 = own_sums(2)
-    run(lead, shared)
-    take2 = sum_step(*take2(), lower[0])
+    g_turned_near = turn(scalars, upstream_near, n_tp, n_dp)
+    old = complete(parts0, [], 0)
+    take2 = next_step(take2)
+    line.tick("dp", n_dp)
     parts1 = last_step(take1)
-    line.tick("dp", n_dp)
-    run(lead + shared, shared)
-    old = finish(scalars, parts0, [], 0, None, experts)
     line.take()
     input_parts = input_grads(scalars, pairs, w_gate, w_up, dgates, n_tp)[0]
     input_arrived = trade(input_parts, "tensor")
+    line.tick("dp", n_dp)
+    turned_near = turn(scalars, normed2_near, n_tp, n_dp)
+    line.take()
     parts2 = last_step(take2)
-    g_turned_near = turn(scalars, upstream_near, n_tp, n_dp)
-    turned_near = turn(scalars, normed2_near, n_tp, n_dp)
-    old = finish(scalars, parts1, old, blocks[0], None, experts)
+    line.tick("dp", n_dp)
     hidden_near, pair_near, _ = run_experts(
         scalars, normed2_near, upstream_near, gates_near, w_gate, w_up, w_down, lead, shared, shift
     )
-
-    def shared_sums(offset, size):
+    line.take()
+
+    def shared_sums(offset, count):
         keep, send = shared_grads(
-            scalars, turned, turned_near, g_turned, g_turned_near, hiddens[3:], hidden_near, pairs[3:], pair_near,
-            shift, offset, size, n_dp,
+            scalars, turned, turned_near, g_turned, g_turned_near, hiddens[3], hidden_near, pairs[3], pair_near,
+            shift, 0, offset, count, n_dp,
         )
         return sum_step(keep, send, 1)
 
@@ -974,33 +1144,40 @@
                 keep, send = sum_step(keep, send, mask)()
         return sum_step(keep, send, far)
 
-    first_share = (shared + 1) // 2
-    take3 = shared_sums(0, first_share)
+    some = (shared + 1) // 2
+    take3 = shared_sums(0, some)
     dattn_rows, dgain2, drouter = stream_grad_rows(
         scalars, input_arrived, probs, kept, stream, normed2, factor2, upstream, gain2, w_router
     )
     dattn = lax.all_gather(dattn_rows, "tensor", axis=0, tiled=True)
     take3 = shared_next(take3)
     line.tick("dp", n_dp)
-    old = finish(scalars, parts2, old, blocks[0] + blocks[1], None, experts)
+    old = complete(parts1, old, 1)
     line.take()
-    take4 = shared_sums(first_share, shared - first_share)
-    result_arrived = trade(results(scalars, hiddens, w_down, n_tp)[0], "tensor")
+    take4 = shared_sums(some, shared - some)
+    result_parts = results(scalars, hiddens, w_down, n_tp)[0]
     take4 = shared_next(take4)
 
     def spread(value, dimension):
-        value = value.astype(bf16)
-        line.last = [value]
         return lax.psum_scatter(value, "dp", scatter_dimension=dimension, tiled=True).astype(f32)
 
+    take5 = sum_step(*output_weight_grads(scalars, *attended, dattn, n_tp, n_dp), 1)
+    line.tick("dp", n_dp)
     dattended = attended_grad(scalars, dattn, w_output)
-    grad_output = spread(dot(attended, line.pin(dattn), TN), 1)
+    result_arrived = trade(line.pin(result_parts), "tensor")
+    line.take()
+    take5 = sum_step(*take5(), lower[0])
     grads, dhead_gains = attend_back(
         scalars, q_rot, k_rot, value, dattended, totals, q_raw, k_raw, query_gain, key_gain, cosine, sine
     )
+    line.tick("dp", n_dp)
     keep3, send3 = take3()
     given3 = swap(send3, "dp", n_dp, near)
-    grad_qkv = spread(jnp.einsum("td,jtc->jdc", line.pin(normed1), grads, preferred_element_type=f32), 1)
+    line.take()
+    grad_qkv = spread(head_weight_grads(scalars, flipped, grads), 1)
+    line.tick("dp", n_dp)
+    old = complete(parts2, old, 2)
+    line.take()
     slices, row_dot, dgain1 = normed_grad(scalars, grads, w_query, w_key, w_value, x, factor1, gain1, n_tp)
     slices_arrived = trade(slices, "tensor")
 
@@ -1041,24 +1218,28 @@
     output = output_of(scalars, stream, result_arrived)
     advance("rows", rows_chain)
     advance("small", small_chain)
-    old = finish(scalars, [keep3[0]], old, lead, shift, experts)
-    advance("rows", rows_chain)
+    keep5, send5 = take5()
+    for mask in lower[1:]:
+        keep5, send5 = sum_step(keep5, send5, mask)()
+    arrived5 = swap(send5, "dp", n_dp, far)
     keep4, send4 = take4()
     given4 = swap(send4, "dp", n_dp, near)
+    old = finish(scalars, [keep3[0]], old, lead, shift, experts)
     advance("small", small_chain)
     old = finish(scalars, [given3[0]], old, lead, other_shift, experts)
     advance("small", small_chain)
-    old = finish(scalars, [keep4[0]], old, lead + first_share, shift, experts)
     while "rows" not in done:
         advance("rows", rows_chain)
-    advance("small", small_chain)
     row_dot = done["rows"].reshape(token_count, 1)
     input_grad = final_grad(scalars, dattn, x, factor1, row_dot, gain1, slices_arrived)
+    advance("small", small_chain)
+    old = finish(scalars, [keep4[0]], old, lead + some, shift, experts)
     while "small" not in done:
         advance("small", small_chain)
+    grad_gate, grad_up, grad_down = finish(scalars, [given4[0]], old, lead + some, other_shift, experts)
     head_gains, small = done["small"]
     head_gains = mine(head_gains[: dhead_gains.size].reshape(dhead_gains.shape), 2)
-    grad_gate, grad_up, grad_down = finish(scalars, [given4[0]], old, lead + first_share, other_shift, experts)
+    grad_output = keep5[0, 0].astype(f32) + line.pin(arrived5)[0, 0].astype(f32)
     return (
         output,
         input_grad,

time: 796 us -> 737 us (0.926)
  waiting for transfers between devices: 164 us -> 87.9 us
  other arithmetic: 9.18 us -> 52.8 us
  Pallas kernels: 506 us -> 488 us
  matrix products: 16.2 us -> 0 us
  starting transfers between devices: 55.5 us -> 63.8 us
    ppermute x38 -> x51, waiting for transfers between devices: 149 us -> 87.8 us  [swap(): return lax.ppermute(value, axis, [(i, i ^ mask) for i in range(count)])]
    convert_element_type x0 -> x7, other arithmetic: none -> 28.2 us  [add_halves(): (left.astype(f32) + right.astype(f32)).astype(bf16)]
    pallas_call x49 -> x45, Pallas kernels: 506 us -> 488 us  [call(): pl.pallas_call(without_deps, out_shape=outs + [struct((8, 128), f32)] * M...]
    dot_general x3 -> x0, matrix products: 16.2 us -> none  [the longest x1 8.82 us: body(): jnp.einsum('td,jtc->jdc', line.pin(normed1), grads, preferred_element_typ...]
    squeeze x0 -> x5, other arithmetic: none -> 16.1 us  [the longest x3 10.2 us: last_step(): return [keep[0], swap(send, 'dp', n_dp, far)[0]]]
    reduce_scatter x2 -> x1, waiting for transfers between devices: 11.8 us -> 0.01 us  [spread(): lax.psum_scatter(value, 'dp', scatter_dimension=dimension, tiled=True)]
    ppermute x38 -> x51, starting transfers between devices: 40.1 us -> 48.6 us  [swap(): return lax.ppermute(value, axis, [(i, i ^ mask) for i in range(count)])]
  transfers between devices with their start and end apart: 47 -> 59, of which waited for: 16 -> 12; matrix products, arithmetic and copies ran while one was open for 5% -> 10% of each run, Pallas kernels for 64% -> 67%
where the time goes in v4:
time: 737 us; the launch traced here: 730 us
  Pallas kernels  488 us (66%)
  waiting for transfers between devices  87.9 us (12%)
  starting transfers between devices  63.8 us (9%)
  other arithmetic  52.8 us (7%)
  local copies, waits for them, and re-layouts  23.1 us (3%)
  between operations  14.4 us (2%)
    pallas_call x45, Pallas kernels, call(): pl.pallas_call(without_deps, out_shape=outs + [struct((8, 128), f32)] * M...  488 us
    ppermute x51, waiting for transfers between devices, swap(): return lax.ppermute(value, axis, [(i, i ^ mask) for i in range(count)])  87.8 us
    ppermute x51, starting transfers between devices, swap(): return lax.ppermute(value, axis, [(i, i ^ mask) for i in range(count)])  48.6 us
    convert_element_type x7, other arithmetic, add_halves(): (left.astype(f32) + right.astype(f32)).astype(bf16)  28.2 us
    all_to_all x3, starting transfers between devices, trade(): return lax.all_to_all(pieces, axis, 0, 0, tiled=True)  14.8 us
  transfers between devices with their start and end apart: 59, of which 12 were waited for; matrix products, arithmetic and copies ran while one was open for 10% of the time, Pallas kernels for 67%

profile of v4, /device:TPU:0, one launch (start us, length us, event | category | flops | bytes accessed | tf_op | source)
XLA Modules:
  0.0 730.1 jit_solution(6184218195142928535)
XLA Ops:
  32.2 13.6 %collective-permute-done.refs_5_ = bf16[1024,512]{1,0:T(8,128)(2,1)} collective-permute-done((bf16[1024,512]{1,0:T(8,128)(2,1)}, bf16[1024,512]{1,0:T(8,128)(2,1)}, u32[]{:S(2)}, u32[]{:S(2)}) %collective-permute-start) | collective-permute-done | bytes 1048608 | tf_op jit(solution)/shard_map/ppermute | solution.py:101
  67.0 16.0 %shard_map.274 = (bf16[1024,2048]{1,0:T(8,128)(2,1)}, bf16[1024,2048]{1,0:T(8,128)(2,1)}, f32[1024,1]{1,0:T(8,128)}, f32[1024,512]{1,0:T(8,128)}, f32[1024,512]{...) custom-call(s32[22]{0:T(128)} %stack.91.scalars, ...), custom_call_target="tpu_custom_call" | custom-call | flops 999999995904 | bytes 1 | tf_op jit(solution)/shard_map/pallas_call | solution.py:78
  82.9 11.8 %shard_map.275 = (bf16[512,512]{1,0:T(8,128)(2,1)}, bf16[512,512]{1,0:T(8,128)(2,1)}, f32[4,1024,1]{2,1,0:T(8,128)}, f32[8,128]{1,0:T(8,128)}, f32[8,128]{1,0:T(...) custom-call(s32[22]{0:T(128)} %stack.91.scalars, f32[8,128]{1,0:T(8,128)} %get-tuple-element.421.refs_0_, ...), custom_call_target="tpu_custom_call" | custom-call | flops 999999995904 | bytes 1 | tf_op jit(solution)/shard_map/pallas_call | solution.py:78
  98.9 6.6 shard_map.276
  105.4 6.1 shard_map.277
  111.5 6.2 collective-permute-done.10.refs_8_
  119.5 13.4 %shard_map.278 = (f32[1024,2048]{1,0:T(8,128)}, f32[8,128]{1,0:T(8,128)}, f32[8,128]{1,0:T(8,128)}, f32[8,128]{1,0:T(8,128)}, f32[8,128]{1,0:T(8,128)}) custom-call(s32[22]{0:T(128)} %stack.91.scalars, f32[8,128]{1,0:T(8,128)} %get-tuple-element.448.refs_0_, f32[8,128]{1,0:T(8,128)} %get-tuple-element.449.refs_1_, f32[8,128]{1,0:T(8,128)} %get-tuple-element.450.refs_2_, ...), custom_call_target="tpu_custom_call" | custom-call | flops 999999995904 | bytes 1 | tf_op jit(solution)/shard_map/pallas_call | solution.py:78
  136.3 14.0 %shard_map.279 = (f32[1024,2048]{1,0:T(8,128)}, bf16[1024,2048]{1,0:T(8,128)(2,1)}, bf16[1024,640]{1,0:T(8,128)(2,1)}, bf16[2048,1024]{1,0:T(8,128)(2,1)}, f32[1...) custom-call(s32[22]{0:T(128)} %stack.91.scalars, ...), custom_call_target="tpu_custom_call" | custom-call | flops 999999995904 | bytes 1 | tf_op jit(solution)/shard_map/pallas_call | solution.py:78
  154.6 6.3 shard_map.280
  160.9 14.1 %shard_map.281 = (bf16[2,1024,256]{2,1,0:T(8,128)(2,1)}, bf16[2,1024,512]{2,1,0:T(8,128)(2,1)}, f32[1024,16]{1,0:T(8,128)}, f32[8,128]{1,0:T(8,128)}, f32[8,128]...) custom-call(s32[22]{0:T(128)} %stack.91.scalars, f32[8,128]{1,0:T(8,128)} %get-tuple-element.475.refs_0_, ...), custom_call_target="tpu_custom_call" | custom-call | flops 999999995904 | bytes 1 | tf_op jit(solution)/shard_map/pallas_call | solution.py:78
  175.0 13.5 %shard_map.282 = (bf16[4,2,256,768]{3,2,1,0:T(8,128)(2,1)}, bf16[4,2,256,768]{3,2,1,0:T(8,128)(2,1)}, f32[8,128]{1,0:T(8,128)}, f32[8,128]{1,0:T(8,128)}, f32[8,128]{1,0:T(8,128)}, /*index=5*/f32[8,128]{1,0:T(8,128)}) custom-call(s32[22]{0:T(128)} %stack.91.scalars, f32[8,128]{1,0:T(8,128)} %get-tuple-element.482.refs_0_, ...), custom_call_target="tpu_custom_call" | custom-call | flops 999999995904 | bytes 1 | tf_op jit(solution)/shard_map/pallas_call | solution.py:78
  188.6 17.9 %shard_map.283 = (bf16[3,1024,256]{2,1,0:T(8,128)(2,1)}, bf16[3,1024,512]{2,1,0:T(8,128)(2,1)}, f32[1024,16]{1,0:T(8,128)}, f32[8,128]{1,0:T(8,128)}, f32[8,128]...) custom-call(s32[22]{0:T(128)} %stack.91.scalars, f32[8,128]{1,0:T(8,128)} %get-tuple-element.492.refs_0_, ...), custom_call_target="tpu_custom_call" | custom-call | flops 999999995904 | bytes 1 | tf_op jit(solution)/shard_map/pallas_call | solution.py:78
  216.5 17.1 %shard_map.284 = (bf16[4,3,256,768]{3,2,1,0:T(8,128)(2,1)}, bf16[4,3,256,768]{3,2,1,0:T(8,128)(2,1)}, f32[8,128]{1,0:T(8,128)}, f32[8,128]{1,0:T(8,128)}, f32[8,128]{1,0:T(8,128)}, /*index=5*/f32[8,128]{1,0:T(8,128)}) custom-call(s32[22]{0:T(128)} %stack.91.scalars, f32[8,128]{1,0:T(8,128)} %get-tuple-element.500.refs_0_, ...), custom_call_target="tpu_custom_call" | custom-call | flops 999999995904 | bytes 1 | tf_op jit(solution)/shard_map/pallas_call | solution.py:78
  233.9 18.0 %shard_map.285 = (bf16[3,1024,256]{2,1,0:T(8,128)(2,1)}, bf16[3,1024,512]{2,1,0:T(8,128)(2,1)}, f32[1024,16]{1,0:T(8,128)}, f32[8,128]{1,0:T(8,128)}, f32[8,128]...) custom-call(s32[22]{0:T(128)} %stack.91.scalars, f32[8,128]{1,0:T(8,128)} %get-tuple-element.510.refs_0_, ...), custom_call_target="tpu_custom_call" | custom-call | flops 999999995904 | bytes 1 | tf_op jit(solution)/shard_map/pallas_call | solution.py:78
  263.4 36.9 %shard_map.286 = (bf16[8,1024,256]{2,1,0:T(8,128)(2,1)}, bf16[8,1024,512]{2,1,0:T(8,128)(2,1)}, f32[1024,16]{1,0:T(8,128)}, f32[8,128]{1,0:T(8,128)}, f32[8,128]...) custom-call(s32[22]{0:T(128)} %stack.91.scalars, f32[8,128]{1,0:T(8,128)} %get-tuple-element.524.refs_0_, ...), custom_call_target="tpu_custom_call" | custom-call | flops 999999995904 | bytes 1 | tf_op jit(solution)/shard_map/pallas_call | solution.py:78
  300.3 16.7 %shard_map.287 = (bf16[4,3,256,768]{3,2,1,0:T(8,128)(2,1)}, bf16[4,3,256,768]{3,2,1,0:T(8,128)(2,1)}, f32[8,128]{1,0:T(8,128)}, f32[8,128]{1,0:T(8,128)}, f32[8,128]{1,0:T(8,128)}, /*index=5*/f32[8,128]{1,0:T(8,128)}) custom-call(s32[22]{0:T(128)} %stack.91.scalars, f32[8,128]{1,0:T(8,128)} %get-tuple-element.531.refs_0_, ...), custom_call_target="tpu_custom_call" | custom-call | flops 999999995904 | bytes 1 | tf_op jit(solution)/shard_map/pallas_call | solution.py:78
  317.3 6.0 shard_map.288
  337.8 46.7 %shard_map.290 = (bf16[4,256,2176]{2,1,0:T(8,128)(2,1)}, f32[8,128]{1,0:T(8,128)}, f32[8,128]{1,0:T(8,128)}, f32[8,128]{1,0:T(8,128)}, f32[8,128]{1,0:T(8,128)}) custom-call(s32[22]{0:T(128)} %stack.91.scalars, f32[8,128]{1,0:T(8,128)} %get-tuple-element.558.refs_0_, f32[8,128]{1,0:T(8,128)} %get-tuple-element.559.refs_1_, ...), custom_call_target="tpu_custom_call" | custom-call | flops 999999995904 | bytes 1 | tf_op jit(solution)/shard_map/pallas_call | solution.py:78
  389.9 6.1 shard_map.291
  396.1 15.1 %collective-permute-done.23 = bf16[2,3,256,768]{3,2,1,0:T(8,128)(2,1)} collective-permute-done((bf16[2,3,256,768]{3,2,1,0:T(8,128)(2,1)}, bf16[2,3,256,768]{3,2,1,0:T(8,128)(2,1)}, u32[]{:S(2)}, u32[]{:S(2)}) %collective-permute-start.23) | collective-permute-done | bytes 2359328 | tf_op jit(solution)/shard_map/ppermute | solution.py:101
  414.7 21.6 %shard_map.292 = (bf16[4,1024,256]{2,1,0:T(8,128)(2,1)}, bf16[4,1024,512]{2,1,0:T(8,128)(2,1)}, f32[1024,16]{1,0:T(8,128)}, f32[8,128]{1,0:T(8,128)}, f32[8,128]...) custom-call(s32[22]{0:T(128)} %stack.91.scalars, f32[8,128]{1,0:T(8,128)} %get-tuple-element.579.refs_0_, ...), custom_call_target="tpu_custom_call" | custom-call | flops 999999995904 | bytes 1 | tf_op jit(solution)/shard_map/pallas_call | solution.py:78
  436.4 23.2 %shard_map.293 = (bf16[4,2,256,768]{3,2,1,0:T(8,128)(2,1)}, bf16[4,2,256,768]{3,2,1,0:T(8,128)(2,1)}, f32[8,128]{1,0:T(8,128)}, f32[8,128]{1,0:T(8,128)}, f32[8,128]{1,0:T(8,128)}, /*index=5*/f32[8,128]{1,0:T(8,128)}) custom-call(s32[22]{0:T(128)} %stack.91.scalars, f32[8,128]{1,0:T(8,128)} %get-tuple-element.586.refs_0_, ...), custom_call_target="tpu_custom_call" | custom-call | flops 999999995904 | bytes 1 | tf_op jit(solution)/shard_map/pallas_call | solution.py:78
  460.2 7.4 %shard_map.294 = (bf16[256,2048]{1,0:T(8,128)(2,1)}, f32[1,2048]{1,0:T(1,128)}, f32[2048,16]{1,0:T(8,128)}, f32[8,128]{1,0:T(8,128)}, f32[8,128]{1,0:T(8,128)}, /*index=5*/f32[8,128]{1,0:T(8,128)}, f32[8,128]{1,0:T(8,128)}) custom-call(s32[22]{0:T(128)} %stack.91.scalars, f32[8,128]{1,0:T(8,128)} %get-tuple-element.597.refs_0_, ...), custom_call_target="tpu_custom_call" | custom-call | flops 999999995904 | bytes 1 | tf_op jit(solution)/shard_map/pallas_call | solution.py:78
  482.3 22.9 %shard_map.296 = (bf16[4,2,256,768]{3,2,1,0:T(8,128)(2,1)}, bf16[4,2,256,768]{3,2,1,0:T(8,128)(2,1)}, f32[8,128]{1,0:T(8,128)}, f32[8,128]{1,0:T(8,128)}, f32[8,128]{1,0:T(8,128)}, /*index=5*/f32[8,128]{1,0:T(8,128)}) custom-call(s32[22]{0:T(128)} %stack.91.scalars, f32[8,128]{1,0:T(8,128)} %get-tuple-element.618.refs_0_, ...), custom_call_target="tpu_custom_call" | custom-call | flops 999999995904 | bytes 1 | tf_op jit(solution)/shard_map/pallas_call | solution.py:78
  505.7 26.7 %shard_map.297 = (bf16[4,1024,512]{2,1,0:T(8,128)(2,1)}, f32[8,128]{1,0:T(8,128)}, f32[8,128]{1,0:T(8,128)}, f32[8,128]{1,0:T(8,128)}, f32[8,128]{1,0:T(8,128)}) custom-call(s32[22]{0:T(128)} %stack.91.scalars, f32[8,128]{1,0:T(8,128)} %get-tuple-element.624.refs_0_, f32[8,128]{1,0:T(8,128)} %get-tuple-element.625.refs_1_, ...), custom_call_target="tpu_custom_call" | custom-call | flops 999999995904 | bytes 1 | tf_op jit(solution)/shard_map/pallas_call | solution.py:78
  537.3 6.8 shard_map.298
  544.6 6.3 shard_map.299
  559.4 22.0 %shard_map.300 = (bf16[3,1024,512]{2,1,0:T(8,128)(2,1)}, f32[4,2,128]{2,1,0:T(2,128)}, f32[8,128]{1,0:T(8,128)}, f32[8,128]{1,0:T(8,128)}, f32[8,128]{1,0:T(8,128)}, /*index=5*/f32[8,128]{1,0:T(8,128)}) custom-call(s32[22]{0:T(128)} %stack.91.scalars, f32[8,128]{1,0:T(8,128)} %get-tuple-element.654.refs_0_, f32[8,128]{1,0:T(8,128)} %get-tuple-element.655.refs_1_, ...), custom_call_target="tpu_custom_call" | custom-call | flops 999999995904 | bytes 1 | tf_op jit(solution)/shard_map/pallas_call | solution.py:78
  586.0 11.6 %shard_map.301 = (bf16[3,2048,512]{2,1,0:T(8,128)(2,1)}, f32[8,128]{1,0:T(8,128)}, f32[8,128]{1,0:T(8,128)}, f32[8,128]{1,0:T(8,128)}, f32[8,128]{1,0:T(8,128)}) custom-call(s32[22]{0:T(128)} %stack.91.scalars, f32[8,128]{1,0:T(8,128)} %get-tuple-element.669.refs_0_, f32[8,128]{1,0:T(8,128)} %get-tuple-element.670.refs_1_, ...), custom_call_target="tpu_custom_call" | custom-call | flops 999999995904 | bytes 1 | tf_op jit(solution)/shard_map/pallas_call | solution.py:78
  602.5 14.2 %shard_map.303 = (bf16[4,1024,512]{2,1,0:T(8,128)(2,1)}, f32[1024,1]{1,0:T(8,128)}, f32[1,2048]{1,0:T(1,128)}, f32[8,128]{1,0:T(8,128)}, f32[8,128]{1,0:T(8,128)}, /*index=5*/f32[8,128]{1,0:T(8,128)}, f32[8,128]{1,0:T(8,128)}) custom-call(s32[22]{0:T(128)} %stack.91.scalars, f32[8,128]{1,0:T(8,128)} %get-tuple-element.684.refs_0_, ...), custom_call_target="tpu_custom_call" | custom-call | flops 999999995904 | bytes 1 | tf_op jit(solution)/shard_map/pallas_call | solution.py:78
  650.4 17.3 %collective-permute-done.43.refs_5_ = f32[19,2048]{1,0:T(8,128)} collective-permute-done((f32[19,2048]{1,0:T(8,128)}, f32[19,2048]{1,0:T(8,128)}, u32[]{:S(2)}, u32[]{:S(2)}) %collective-permute-start.43) | collective-permute-done | bytes 155680 | tf_op jit(solution)/shard_map/ppermute | solution.py:101
  675.0 16.3 %collective-permute-done.45.refs_5_ = f32[19,2048]{1,0:T(8,128)} collective-permute-done((f32[19,2048]{1,0:T(8,128)}, f32[19,2048]{1,0:T(8,128)}, u32[]{:S(2)}, u32[]{:S(2)}) %collective-permute-start.45) | collective-permute-done | bytes 155680 | tf_op jit(solution)/shard_map/ppermute | solution.py:101
  (212 shorter events, 217.3 us)
Async XLA Ops:
  7.2 112.4 %all-gather.12.cloned.1.call-start = ((), (), s32[]{:S(2)}) async-start(), calls=%async_computation.8 | async-start | bytes 9437184 | tf_op jit(solution)/shard_map/all_gather | solution.py:1042
  12.8 33.0 %collective-permute-start = (bf16[1024,512]{1,0:T(8,128)(2,1)}, bf16[1024,512]{1,0:T(8,128)(2,1)}, u32[]{:S(2)}, u32[]{:S(2)}) collective-permute-start(bf16[1024,512]{1,0:T(8,128)(2,1)} %refs_4_), channel_id=1, source_target_pairs={{0,1},{1,0},{2,3},{3,2},{4,5},{5,4},{6,7},{7,6},{8,9},{9,8},{10,11... | collective-permute-start | bytes 3145736 | tf_op jit(solution)/shard_map/ppermute | solution.py:101
  14.7 32.5 %collective-permute-start.1 = (bf16[1024,512]{1,0:T(8,128)(2,1)}, bf16[1024,512]{1,0:T(8,128)(2,1)}, u32[]{:S(2)}, u32[]{:S(2)}) collective-permute-start(bf16[1024,512]{1,0:T(8,128)(2,1)} %refs_4_), channel_id=1, source_target_pairs={{0,2},{1,3},{2,0},{3,1},{4,6},{5,7},{6,4},{7,5},{8,10},{9,11},{10,... | collective-permute-start | bytes 3145736 | tf_op jit(solution)/shard_map/ppermute | solution.py:101
  32.1 285.2 %all-gather.6.cloned.1.call-start = ((), (), s32[]{:S(2)}) async-start(), calls=%async_computation.4 | async-start | bytes 5242880 | tf_op jit(solution)/shard_map/all_gather | solution.py:1069
  64.1 30.6 %collective-permute-start.7 = (bf16[1024,512]{1,0:T(8,128)(2,1)}, bf16[1024,512]{1,0:T(8,128)(2,1)}, u32[]{:S(2)}, u32[]{:S(2)}) collective-permute-start(bf16[1024,512]{1,0:T(8,128)(2,1)} %refs_4_.1), channel_id=1, source_target_pairs={{0,1},{1,0},{2,3},{3,2},{4,5},{5,4},{6,7},{7,6},{8,9},{9,8},{10,11... | collective-permute-start | bytes 3145736 | tf_op jit(solution)/shard_map/ppermute | solution.py:101
  65.5 29.3 %collective-permute-start.8 = (bf16[1024,512]{1,0:T(8,128)(2,1)}, bf16[1024,512]{1,0:T(8,128)(2,1)}, u32[]{:S(2)}, u32[]{:S(2)}) collective-permute-start(bf16[1024,512]{1,0:T(8,128)(2,1)} %refs_4_.1), channel_id=1, source_target_pairs={{0,2},{1,3},{2,0},{3,1},{4,6},{5,7},{6,4},{7,5},{8,10},{9,11},{10,... | collective-permute-start | bytes 3145736 | tf_op jit(solution)/shard_map/ppermute | solution.py:101
  134.9 53.6 %collective-permute-start.21 = (bf16[1024,512]{1,0:T(8,128)(2,1)}, bf16[1024,512]{1,0:T(8,128)(2,1)}, u32[]{:S(2)}, u32[]{:S(2)}) collective-permute-start(bf16[1024,512]{1,0:T(8,128)(2,1)} %refs_4_.1), channel_id=1, source_target_pairs={{0,8},{4,12},{8,0},{12,4},{16,24},{20,28},{24,16},{28,20},{1,9},{5... | collective-permute-start | bytes 3145736 | tf_op jit(solution)/shard_map/ppermute | solution.py:101
  150.4 56.0 %collective-permute-start.26 = (bf16[1024,640]{1,0:T(8,128)(2,1)}, bf16[1024,640]{1,0:T(8,128)(2,1)}, u32[]{:S(2)}, u32[]{:S(2)}) collective-permute-start(bf16[1024,640]{1,0:T(8,128)(2,1)} %get-tuple-element.574), channel_id=1, source_target_pairs={{0,8},{4,12},{8,0},{12,4},{16,24},{20,28},{24,16},{28,20},{1,9},{5... | collective-permute-start | bytes 3932168 | tf_op jit(solution)/shard_map/ppermute | solution.py:101
  188.5 201.4 %all-gather.8.cloned.1.call-start = ((), (), s32[]{:S(2)}) async-start(), calls=%async_computation.5 | async-start | bytes 5242880 | tf_op jit(solution)/shard_map/all_gather | solution.py:1072
  215.3 37.1 %collective-permute-start.18 = (bf16[2,2,256,768]{3,2,1,0:T(8,128)(2,1)}, bf16[2,2,256,768]{3,2,1,0:T(8,128)(2,1)}, u32[]{:S(2)}, u32[]{:S(2)}) collective-permute-start(bf16[2,2,256,768]{3,2,1,0:T(8,128)(2,1)} %get-tuple-element.795.refs_4_), channel_id=1, source_target_pairs={{0,8},{4,12},{8,0},{12,4},{16,24},{20,28},{24,16},{28,20},{1,9},{5... | collective-permute-start | bytes 4718600 | tf_op jit(solution)/shard_map/ppermute | solution.py:101
  233.6 23.8 %collective-permute-start.17 = (bf16[4,3,256,768]{3,2,1,0:T(8,128)(2,1)}, bf16[4,3,256,768]{3,2,1,0:T(8,128)(2,1)}, u32[]{:S(2)}, u32[]{:S(2)}) collective-permute-start(bf16[4,3,256,768]{3,2,1,0:T(8,128)(2,1)} %get-tuple-element.509), channel_id=1, source_target_pairs={{0,4},{4,0},{8,12},{12,8},{16,20},{20,16},{24,28},{28,24},{1,5},{5... | collective-permute-start | bytes 14155784 | tf_op jit(solution)/shard_map/ppermute | solution.py:101
  255.5 67.8 %collective-permute-start.22 = (bf16[1,2,256,768]{3,2,1,0:T(8,128)(2,1)}, bf16[1,2,256,768]{3,2,1,0:T(8,128)(2,1)}, u32[]{:S(2)}, u32[]{:S(2)}) collective-permute-start(bf16[1,2,256,768]{3,2,1,0:T(8,128)(2,1)} %get-tuple-element.528.refs_4_), channel_id=1, source_target_pairs={{0,16},{4,20},{8,24},{12,28},{16,0},{20,4},{24,8},{28,12},{1,17},{... | collective-permute-start | bytes 2359304 | tf_op jit(solution)/shard_map/ppermute | solution.py:101
  257.4 42.9 %collective-permute-start.19 = (f32[8,128]{1,0:T(8,128)}, f32[8,128]{1,0:T(8,128)}, u32[]{:S(2)}, u32[]{:S(2)}) collective-permute-start(f32[8,128]{1,0:T(8,128)} %get-tuple-element.524.refs_0_), channel_id=1, source_target_pairs={{0,4},{4,0},{8,12},{12,8},{16,20},{20,16},{24,28},{28,24},{1,5},{5... | collective-permute-start | bytes 12296 | tf_op jit(solution)/shard_map/ppermute | solution.py:101
  261.8 70.8 %collective-permute-start.24 = (bf16[2,3,256,768]{3,2,1,0:T(8,128)(2,1)}, bf16[2,3,256,768]{3,2,1,0:T(8,128)(2,1)}, u32[]{:S(2)}, u32[]{:S(2)}) collective-permute-start(bf16[2,3,256,768]{3,2,1,0:T(8,128)(2,1)} %get-tuple-element.787.refs_5_), channel_id=1, source_target_pairs={{0,8},{4,12},{8,0},{12,4},{16,24},{20,28},{24,16},{28,20},{1,9},{5... | collective-permute-start | bytes 7077896 | tf_op jit(solution)/shard_map/ppermute | solution.py:101
  332.1 79.0 %collective-permute-start.23 = (bf16[2,3,256,768]{3,2,1,0:T(8,128)(2,1)}, bf16[2,3,256,768]{3,2,1,0:T(8,128)(2,1)}, u32[]{:S(2)}, u32[]{:S(2)}) collective-permute-start(bf16[2,3,256,768]{3,2,1,0:T(8,128)(2,1)} %get-tuple-element.562.refs_4_), channel_id=1, source_target_pairs={{0,8},{4,12},{8,0},{12,4},{16,24},{20,28},{24,16},{28,20},{1,9},{5... | collective-permute-start | bytes 7077896 | tf_op jit(solution)/shard_map/ppermute | solution.py:101
  336.1 141.6 %collective-permute-start.31 = (bf16[1,3,256,768]{3,2,1,0:T(8,128)(2,1)}, bf16[1,3,256,768]{3,2,1,0:T(8,128)(2,1)}, u32[]{:S(2)}, u32[]{:S(2)}) collective-permute-start(bf16[1,3,256,768]{3,2,1,0:T(8,128)(2,1)} %get-tuple-element.799.refs_5_), channel_id=1, source_target_pairs={{0,16},{4,20},{8,24},{12,28},{16,0},{20,4},{24,8},{28,12},{1,17},{... | collective-permute-start | bytes 3538952 | tf_op jit(solution)/shard_map/ppermute | solution.py:101
  384.6 75.5 %all-to-all-start = ((bf16[4,256,2176]{2,1,0:T(8,128)(2,1)}), bf16[4,256,2176]{2,1,0:T(8,128)(2,1)}, u32[]{:S(2)}, u32[]{:S(2)}) async-start(bf16[4,256,2176]{2,1,0:T(8,128)(2,1)} %get-tuple-element.601), calls=%async_computation | async-start | bytes 8912896 | tf_op jit(solution)/shard_map/all_to_all | solution.py:157
  389.6 147.6 %all-gather.10.cloned.1.call-start = ((), (), s32[]{:S(2)}) async-start(), calls=%async_computation.6 | async-start | bytes 5242880 | tf_op jit(solution)/shard_map/all_gather | solution.py:1152
  411.1 25.2 %collective-permute-start.28 = (f32[8,128]{1,0:T(8,128)}, f32[8,128]{1,0:T(8,128)}, u32[]{:S(2)}, u32[]{:S(2)}) collective-permute-start(f32[8,128]{1,0:T(8,128)} %get-tuple-element.579.refs_0_), channel_id=1, source_target_pairs={{0,4},{4,0},{8,12},{12,8},{16,20},{20,16},{24,28},{28,24},{1,5},{5... | collective-permute-start | bytes 12296 | tf_op jit(solution)/shard_map/ppermute | solution.py:101
  414.7 183.1 %collective-permute-start.37 = (bf16[1,3,256,768]{3,2,1,0:T(8,128)(2,1)}, bf16[1,3,256,768]{3,2,1,0:T(8,128)(2,1)}, u32[]{:S(2)}, u32[]{:S(2)}) collective-permute-start(bf16[1,3,256,768]{3,2,1,0:T(8,128)(2,1)} %get-tuple-element.797.refs_5_), channel_id=1, source_target_pairs={{0,16},{4,20},{8,24},{12,28},{16,0},{20,4},{24,8},{28,12},{1,17},{... | collective-permute-start | bytes 3538952 | tf_op jit(solution)/shard_map/ppermute | solution.py:101
  475.1 106.3 %collective-permute-start.30 = (bf16[2,2,256,768]{3,2,1,0:T(8,128)(2,1)}, bf16[2,2,256,768]{3,2,1,0:T(8,128)(2,1)}, u32[]{:S(2)}, u32[]{:S(2)}) collective-permute-start(bf16[2,2,256,768]{3,2,1,0:T(8,128)(2,1)} %get-tuple-element.792.refs_4_), channel_id=1, source_target_pairs={{0,16},{4,20},{8,24},{12,28},{16,0},{20,4},{24,8},{28,12},{1,17},{... | collective-permute-start | bytes 4718600 | tf_op jit(solution)/shard_map/ppermute | solution.py:101
  505.2 27.2 %collective-permute-start.33 = (bf16[4,2,256,768]{3,2,1,0:T(8,128)(2,1)}, bf16[4,2,256,768]{3,2,1,0:T(8,128)(2,1)}, u32[]{:S(2)}, u32[]{:S(2)}) collective-permute-start(bf16[4,2,256,768]{3,2,1,0:T(8,128)(2,1)} %get-tuple-element.623), channel_id=1, source_target_pairs={{0,4},{4,0},{8,12},{12,8},{16,20},{20,16},{24,28},{28,24},{1,5},{5... | collective-permute-start | bytes 9437192 | tf_op jit(solution)/shard_map/ppermute | solution.py:101
  536.8 103.9 %collective-permute-start.39 = (bf16[2,2,256,768]{3,2,1,0:T(8,128)(2,1)}, bf16[2,2,256,768]{3,2,1,0:T(8,128)(2,1)}, u32[]{:S(2)}, u32[]{:S(2)}) collective-permute-start(bf16[2,2,256,768]{3,2,1,0:T(8,128)(2,1)} %get-tuple-element.791.refs_4_), channel_id=1, source_target_pairs={{0,16},{4,20},{8,24},{12,28},{16,0},{20,4},{24,8},{28,12},{1,17},{... | collective-permute-start | bytes 4718600 | tf_op jit(solution)/shard_map/ppermute | solution.py:101
  550.9 70.9 %all-to-all-start.1 = ((bf16[4,1024,512]{2,1,0:T(8,128)(2,1)}), bf16[4,1024,512]{2,1,0:T(8,128)(2,1)}, u32[]{:S(2)}, u32[]{:S(2)}) async-start(bf16[4,1024,512]{2,1,0:T(8,128)(2,1)} %get-tuple-element.693), calls=%async_computation.1 | async-start | bytes 8388608 | tf_op jit(solution)/shard_map/all_to_all | solution.py:157
  555.9 164.9 %reduce-scatter.2.cloned.1.call-start = ((), (), s32[]{:S(2)}) async-start(), calls=%async_computation.7 | async-start | bytes 7077888 | tf_op jit(solution)/shard_map/reduce_scatter | solution.py:1162
  558.4 78.1 %collective-permute-start.40 = (bf16[2,1,512,256]{3,2,1,0:T(8,128)(2,1)}, bf16[2,1,512,256]{3,2,1,0:T(8,128)(2,1)}, u32[]{:S(2)}, u32[]{:S(2)}) collective-permute-start(bf16[2,1,512,256]{3,2,1,0:T(8,128)(2,1)} %get-tuple-element.807.refs_5_), channel_id=1, source_target_pairs={{0,8},{4,12},{8,0},{12,4},{16,24},{20,28},{24,16},{28,20},{1,9},{5... | collective-permute-start | bytes 1572872 | tf_op jit(solution)/shard_map/ppermute | solution.py:101
  584.4 85.7 %collective-permute-start.44 = (bf16[1,2,256,768]{3,2,1,0:T(8,128)(2,1)}, bf16[1,2,256,768]{3,2,1,0:T(8,128)(2,1)}, u32[]{:S(2)}, u32[]{:S(2)}) collective-permute-start(bf16[1,2,256,768]{3,2,1,0:T(8,128)(2,1)} %get-tuple-element.803.refs_4_), channel_id=1, source_target_pairs={{0,8},{4,12},{8,0},{12,4},{16,24},{20,28},{24,16},{28,20},{1,9},{5... | collective-permute-start | bytes 2359304 | tf_op jit(solution)/shard_map/ppermute | solution.py:101
  621.8 80.7 %all-to-all-start.2 = ((bf16[4,1024,512]{2,1,0:T(8,128)(2,1)}), bf16[4,1024,512]{2,1,0:T(8,128)(2,1)}, u32[]{:S(2)}, u32[]{:S(2)}) async-start(bf16[4,1024,512]{2,1,0:T(8,128)(2,1)} %get-tuple-element.755), calls=%async_computation.2 | async-start | bytes 8388608 | tf_op jit(solution)/shard_map/all_to_all | solution.py:157
  638.2 34.9 %collective-permute-start.49 = (bf16[1,1,512,256]{3,2,1,0:T(8,128)(2,1)}, bf16[1,1,512,256]{3,2,1,0:T(8,128)(2,1)}, u32[]{:S(2)}, u32[]{:S(2)}) collective-permute-start(bf16[1,1,512,256]{3,2,1,0:T(8,128)(2,1)} %add_convert_fusion.23.refs_4_), channel_id=1, source_target_pairs={{0,16},{4,20},{8,24},{12,28},{16,0},{20,4},{24,8},{28,12},{1,17},{... | collective-permute-start | bytes 786440 | tf_op jit(solution)/shard_map/ppermute | solution.py:101
  640.7 27.1 %collective-permute-start.43 = (f32[19,2048]{1,0:T(8,128)}, f32[19,2048]{1,0:T(8,128)}, u32[]{:S(2)}, u32[]{:S(2)}) collective-permute-start(f32[19,2048]{1,0:T(8,128)} %get-tuple-element.732.refs_4_), channel_id=1, source_target_pairs={{0,8},{4,12},{8,0},{12,4},{16,24},{20,28},{24,16},{28,20},{1,9},{5... | collective-permute-start | bytes 466952 | tf_op jit(solution)/shard_map/ppermute | solution.py:101
  640.9 52.9 %collective-permute-start.46 = (f32[8,128]{1,0:T(8,128)}, f32[8,128]{1,0:T(8,128)}, u32[]{:S(2)}, u32[]{:S(2)}) collective-permute-start(f32[8,128]{1,0:T(8,128)} %get-tuple-element.749.refs_4_), channel_id=1, source_target_pairs={{0,2},{1,3},{2,0},{3,1},{4,6},{5,7},{6,4},{7,5},{8,10},{9,11},{10,... | collective-permute-start | bytes 12296 | tf_op jit(solution)/shard_map/ppermute | solution.py:101
  645.8 70.9 %collective-permute-start.50 = (bf16[1,2,256,768]{3,2,1,0:T(8,128)(2,1)}, bf16[1,2,256,768]{3,2,1,0:T(8,128)(2,1)}, u32[]{:S(2)}, u32[]{:S(2)}) collective-permute-start(bf16[1,2,256,768]{3,2,1,0:T(8,128)(2,1)} %get-tuple-element.801.refs_5_), channel_id=1, source_target_pairs={{0,8},{4,12},{8,0},{12,4},{16,24},{20,28},{24,16},{28,20},{1,9},{5... | collective-permute-start | bytes 2359304 | tf_op jit(solution)/shard_map/ppermute | solution.py:101
  (49 other events, 573.0 us)
Sparse Core Ops, SparseCore 0:
  32.2 82.3 all-gather.11
  188.6 52.7 all-gather.5
  243.3 52.5 all-gather.7
  467.8 52.4 all-gather.9
  597.9 120.8 reduce-scatter.1

commit v5 on v4

--- a/solution.py
+++ b/solution.py
@@ -889,39 +889,26 @@
     )
 
 
-def flip_kernel(source, target):
-    target[...] = source[...].T
-
-
-def flip(scalars, value):
-    tokens, features = value.shape
-    return call(
-        lambda scalars, source, target: flip_kernel(source, target),
-        (tokens // TB,),
-        scalars,
-        [value],
-        [pl.BlockSpec((TB, features), lambda i, s: (i, 0))],
-        [struct((features, tokens), bf16)],
-        [pl.BlockSpec((features, TB), lambda i, s: (0, i))],
-    )[0]
-
-
-def head_weight_grads(scalars, flipped, grads):
-    features, tokens = flipped.shape
+def head_weight_grads(scalars, turned, grads, dp_count):
+    features, tokens = turned.shape
     count, _, local = grads.shape
-
-    def kernel(scalars, flipped, grad, out):
-        out[0] = dot(flipped[...], grad[0]).astype(bf16)
-
+    half, rows = dp_count // 2, features // dp_count
+
+    def kernel(scalars, turned, grad, keep_out, send_out):
+        product = dot(turned[...], grad[0]).astype(bf16).reshape(2 * half, rows, local)
+        keep_out[:, 0] = product[:half]
+        send_out[:, 0] = product[half:]
+
+    block = pl.BlockSpec((half, 1, rows, local), lambda i, s: (0, i, 0, 0))
     return call(
         kernel,
         (count,),
         scalars,
-        [flipped, grads],
+        [turned, grads],
         [whole_spec(), pl.BlockSpec((1, tokens, local), lambda i, s: (i, 0, 0))],
-        [struct((count, features, local), bf16)],
-        [pl.BlockSpec((1, features, local), lambda i, s: (i, 0, 0))],
-    )[0]
+        [struct((half, count, rows, local), bf16)] * 2,
+        [block] * 2,
+    )
 
 
 def output_weight_grads(scalars, top, bottom, grad, first, dp_count):
@@ -1004,6 +991,18 @@
         + [pl.BlockSpec((n_tp, TB, width), lambda i, s: (0, i, 0))],
         [struct((tokens, width), bf16)],
         [plain(width)],
+    )[0]
+
+
+def final_sum_kernel(scalars, left, right, out):
+    out[...] = left[...].astype(f32) + right[...].astype(f32)
+
+
+def final_sum(scalars, left, right):
+    count, rows, width = left.shape
+    block = pl.BlockSpec((1, rows, width), lambda i, s: (i, 0, 0))
+    return call(
+        final_sum_kernel, (count,), scalars, [left, right], [block] * 2, [struct(left.shape, f32)], [block]
     )[0]
 
 
@@ -1051,7 +1050,7 @@
     *attended, totals = attend(scalars, q_rot, k_rot, value, heads)
     attended, g_pieces = lax.optimization_barrier((tuple(attended), g_pieces))
     upstream, g_turned = whole_first(scalars, g_pieces, n_tp, n_dp, turned_base)
-    flipped = flip(scalars, normed1)
+    turned1 = turn(scalars, normed1, n_tp, n_dp)
     attended_pieces = gather_pieces(attended, "tensor", n_tp, pin=line.pin)
     stream = stream_first(scalars, attended_pieces[:early], x, w_all)
     g_mine = line.pin(g_mine)
@@ -1123,11 +1122,11 @@
     line.tick("dp", n_dp)
     turned_near = turn(scalars, normed2_near, n_tp, n_dp)
     line.take()
-    parts2 = last_step(take2)
-    line.tick("dp", n_dp)
     hidden_near, pair_near, _ = run_experts(
         scalars, normed2_near, upstream_near, gates_near, w_gate, w_up, w_down, lead, shared, shift
     )
+    line.tick("dp", n_dp)
+    parts2 = last_step(take2)
     line.take()
 
     def shared_sums(offset, count):
@@ -1158,9 +1157,6 @@
     result_parts = results(scalars, hiddens, w_down, n_tp)[0]
     take4 = shared_next(take4)
 
-    def spread(value, dimension):
-        return lax.psum_scatter(value, "dp", scatter_dimension=dimension, tiled=True).astype(f32)
-
     take5 = sum_step(*output_weight_grads(scalars, *attended, dattn, n_tp, n_dp), 1)
     line.tick("dp", n_dp)
     dattended = attended_grad(scalars, dattn, w_output)
@@ -1170,23 +1166,18 @@
     grads, dhead_gains = attend_back(
         scalars, q_rot, k_rot, value, dattended, totals, q_raw, k_raw, query_gain, key_gain, cosine, sine
     )
-    line.tick("dp", n_dp)
-    keep3, send3 = take3()
-    given3 = swap(send3, "dp", n_dp, near)
-    line.take()
-    grad_qkv = spread(head_weight_grads(scalars, flipped, grads), 1)
+    take6 = sum_step(*head_weight_grads(scalars, turned1, grads, n_dp), 1)
     line.tick("dp", n_dp)
     old = complete(parts2, old, 2)
     line.take()
+    take6 = sum_step(*take6(), lower[0])
     slices, row_dot, dgain1 = normed_grad(scalars, grads, w_query, w_key, w_value, x, factor1, gain1, n_tp)
     slices_arrived = trade(slices, "tensor")
 
-    mine = lambda array, dimension: lax.dynamic_slice_in_dim(
-        array, dp * (array.shape[dimension] // n_dp), array.shape[dimension] // n_dp, dimension
-    )
-    flat_heads = dhead_gains.reshape(1, -1)
-    flat_heads = jnp.pad(flat_heads, ((0, 0), (0, features - flat_heads.shape[1])))
+    own_heads = jnp.moveaxis(dhead_gains.reshape(heads, 2, n_dp, hd // n_dp), 2, 0).reshape(n_dp, -1)
+    flat_heads = jnp.pad(own_heads, ((0, 0), (0, features // n_dp - own_heads.shape[1]))).reshape(1, -1)
     small = jnp.concatenate([drouter.T, dgain2, dgain1, flat_heads], axis=0)
+    small = lax.psum_scatter(small, "dp", scatter_dimension=1, tiled=True)
     row_dot = row_dot.reshape(8, token_count // 8)
 
     def chain(value, axis, count):
@@ -1198,11 +1189,6 @@
             mask *= 2
         return value
 
-    def small_chain():
-        total = yield from chain(small, "dp", n_dp)
-        own = yield from chain(mine(total[: experts + 2], 1), "tensor", n_tp)
-        return total[experts + 2], own
-
     done = {}
 
     def advance(name, steps):
@@ -1212,34 +1198,41 @@
             except StopIteration as end:
                 done[name] = end.value
 
-    rows_chain, small_chain = chain(row_dot, "tensor", n_tp), small_chain()
+    def rest(take):
+        keep, send = take()
+        for mask in lower[1:]:
+            keep, send = sum_step(keep, send, mask)()
+        return keep, swap(send, "dp", n_dp, far)
+
+    rows_chain = chain(row_dot, "tensor", n_tp)
     advance("rows", rows_chain)
-    advance("small", small_chain)
     output = output_of(scalars, stream, result_arrived)
     advance("rows", rows_chain)
-    advance("small", small_chain)
-    keep5, send5 = take5()
-    for mask in lower[1:]:
-        keep5, send5 = sum_step(keep5, send5, mask)()
-    arrived5 = swap(send5, "dp", n_dp, far)
+    keep3, send3 = take3()
+    given3 = swap(send3, "dp", n_dp, near)
     keep4, send4 = take4()
     given4 = swap(send4, "dp", n_dp, near)
     old = finish(scalars, [keep3[0]], old, lead, shift, experts)
-    advance("small", small_chain)
-    old = finish(scalars, [given3[0]], old, lead, other_shift, experts)
-    advance("small", small_chain)
+    keep5, arrived5 = rest(take5)
+    keep6, arrived6 = rest(take6)
+    line.tick("dp", n_dp)
+    old = finish(scalars, [keep4[0]], old, lead + some, shift, experts)
+    line.take()
     while "rows" not in done:
         advance("rows", rows_chain)
     row_dot = done["rows"].reshape(token_count, 1)
+    head_gains = small[experts + 2, : own_heads.shape[1]].reshape(heads, 2, hd // n_dp)
+    sums_chain = chain(small[: experts + 2], "tensor", n_tp)
+    advance("sums", sums_chain)
     input_grad = final_grad(scalars, dattn, x, factor1, row_dot, gain1, slices_arrived)
-    advance("small", small_chain)
-    old = finish(scalars, [keep4[0]], old, lead + some, shift, experts)
-    while "small" not in done:
-        advance("small", small_chain)
+    advance("sums", sums_chain)
+    old = finish(scalars, [given3[0]], old, lead, other_shift, experts)
+    while "sums" not in done:
+        advance("sums", sums_chain)
+    small = done["sums"]
+    grad_output = final_sum(scalars, keep5[0], arrived5[0])[0]
     grad_gate, grad_up, grad_down = finish(scalars, [given4[0]], old, lead + some, other_shift, experts)
-    head_gains, small = done["small"]
-    head_gains = mine(head_gains[: dhead_gains.size].reshape(dhead_gains.shape), 2)
-    grad_output = keep5[0, 0].astype(f32) + line.pin(arrived5)[0, 0].astype(f32)
+    grad_qkv = final_sum(scalars, keep6[0], arrived6[0])
     return (
         output,
         input_grad,

time: 737 us -> 725 us (0.984)
  waiting for transfers between devices: 87.9 us -> 70.2 us
    ppermute x51, waiting for transfers between devices: 87.8 us -> 68.4 us  [swap(): return lax.ppermute(value, axis, [(i, i ^ mask) for i in range(count)])]
    pallas_call x45 -> x44, Pallas kernels: 488 us -> 487 us  [call(): pl.pallas_call(without_deps, out_shape=outs + [struct((8, 128), f32)] * M...]
  transfers between devices with their start and end apart: 59 -> 59, of which waited for: 12 -> 15; matrix products, arithmetic and copies ran while one was open for 10% -> 10% of each run, Pallas kernels for 67% -> 67%
where the time goes in v5:
time: 725 us; the launch traced here: 716 us
  Pallas kernels  487 us (67%)
  waiting for transfers between devices  70.2 us (10%)
  starting transfers between devices  63.7 us (9%)
  other arithmetic  57.4 us (8%)
  local copies, waits for them, and re-layouts  23.8 us (3%)
  between operations  14.4 us (2%)
    pallas_call x44, Pallas kernels, call(): pl.pallas_call(without_deps, out_shape=outs + [struct((8, 128), f32)] * M...  487 us
    ppermute x51, waiting for transfers between devices, swap(): return lax.ppermute(value, axis, [(i, i ^ mask) for i in range(count)])  68.4 us
    ppermute x51, starting transfers between devices, swap(): return lax.ppermute(value, axis, [(i, i ^ mask) for i in range(count)])  48.2 us
    convert_element_type x7, other arithmetic, add_halves(): (left.astype(f32) + right.astype(f32)).astype(bf16)  30.9 us
    all_to_all x3, starting transfers between devices, trade(): return lax.all_to_all(pieces, axis, 0, 0, tiled=True)  15.1 us
  transfers between devices with their start and end apart: 59, of which 15 were waited for; matrix products, arithmetic and copies ran while one was open for 10% of the time, Pallas kernels for 67%

profile of v5, /device:TPU:0, one launch (start us, length us, event | category | flops | bytes accessed | tf_op | source)
XLA Modules:
  0.0 716.4 jit_solution(3480461010960279147)
XLA Ops:
  32.2 13.6 %collective-permute-done.refs_5_ = bf16[1024,512]{1,0:T(8,128)(2,1)} collective-permute-done((bf16[1024,512]{1,0:T(8,128)(2,1)}, bf16[1024,512]{1,0:T(8,128)(2,1)}, u32[]{:S(2)}, u32[]{:S(2)}) %collective-permute-start) | collective-permute-done | bytes 1048608 | tf_op jit(solution)/shard_map/ppermute | solution.py:101
  67.0 16.0 %shard_map.274 = (bf16[1024,2048]{1,0:T(8,128)(2,1)}, bf16[1024,2048]{1,0:T(8,128)(2,1)}, f32[1024,1]{1,0:T(8,128)}, f32[1024,512]{1,0:T(8,128)}, f32[1024,512]{...) custom-call(s32[22]{0:T(128)} %stack.91.scalars, ...), custom_call_target="tpu_custom_call" | custom-call | flops 999999995904 | bytes 1 | tf_op jit(solution)/shard_map/pallas_call | solution.py:78
  82.9 11.8 %shard_map.275 = (bf16[512,512]{1,0:T(8,128)(2,1)}, bf16[512,512]{1,0:T(8,128)(2,1)}, f32[4,1024,1]{2,1,0:T(8,128)}, f32[8,128]{1,0:T(8,128)}, f32[8,128]{1,0:T(...) custom-call(s32[22]{0:T(128)} %stack.91.scalars, f32[8,128]{1,0:T(8,128)} %get-tuple-element.430.refs_0_, ...), custom_call_target="tpu_custom_call" | custom-call | flops 999999995904 | bytes 1 | tf_op jit(solution)/shard_map/pallas_call | solution.py:78
  98.9 6.6 shard_map.276
  105.4 6.1 shard_map.277
  111.5 6.2 collective-permute-done.10.refs_8_
  119.5 13.4 %shard_map.278 = (f32[1024,2048]{1,0:T(8,128)}, f32[8,128]{1,0:T(8,128)}, f32[8,128]{1,0:T(8,128)}, f32[8,128]{1,0:T(8,128)}, f32[8,128]{1,0:T(8,128)}) custom-call(s32[22]{0:T(128)} %stack.91.scalars, f32[8,128]{1,0:T(8,128)} %get-tuple-element.457.refs_0_, f32[8,128]{1,0:T(8,128)} %get-tuple-element.458.refs_1_, f32[8,128]{1,0:T(8,128)} %get-tuple-element.459.refs_2_, ...), custom_call_target="tpu_custom_call" | custom-call | flops 999999995904 | bytes 1 | tf_op jit(solution)/shard_map/pallas_call | solution.py:78
  136.4 14.0 %shard_map.279 = (f32[1024,2048]{1,0:T(8,128)}, bf16[1024,2048]{1,0:T(8,128)(2,1)}, bf16[1024,640]{1,0:T(8,128)(2,1)}, bf16[2048,1024]{1,0:T(8,128)(2,1)}, f32[1...) custom-call(s32[22]{0:T(128)} %stack.91.scalars, ...), custom_call_target="tpu_custom_call" | custom-call | flops 999999995904 | bytes 1 | tf_op jit(solution)/shard_map/pallas_call | solution.py:78
  154.6 6.3 shard_map.280
  160.9 14.1 %shard_map.281 = (bf16[2,1024,256]{2,1,0:T(8,128)(2,1)}, bf16[2,1024,512]{2,1,0:T(8,128)(2,1)}, f32[1024,16]{1,0:T(8,128)}, f32[8,128]{1,0:T(8,128)}, f32[8,128]...) custom-call(s32[22]{0:T(128)} %stack.91.scalars, f32[8,128]{1,0:T(8,128)} %get-tuple-element.484.refs_0_, ...), custom_call_target="tpu_custom_call" | custom-call | flops 999999995904 | bytes 1 | tf_op jit(solution)/shard_map/pallas_call | solution.py:78
  175.0 13.5 %shard_map.282 = (bf16[4,2,256,768]{3,2,1,0:T(8,128)(2,1)}, bf16[4,2,256,768]{3,2,1,0:T(8,128)(2,1)}, f32[8,128]{1,0:T(8,128)}, f32[8,128]{1,0:T(8,128)}, f32[8,128]{1,0:T(8,128)}, /*index=5*/f32[8,128]{1,0:T(8,128)}) custom-call(s32[22]{0:T(128)} %stack.91.scalars, f32[8,128]{1,0:T(8,128)} %get-tuple-element.491.refs_0_, ...), custom_call_target="tpu_custom_call" | custom-call | flops 999999995904 | bytes 1 | tf_op jit(solution)/shard_map/pallas_call | solution.py:78
  188.5 17.9 %shard_map.283 = (bf16[3,1024,256]{2,1,0:T(8,128)(2,1)}, bf16[3,1024,512]{2,1,0:T(8,128)(2,1)}, f32[1024,16]{1,0:T(8,128)}, f32[8,128]{1,0:T(8,128)}, f32[8,128]...) custom-call(s32[22]{0:T(128)} %stack.91.scalars, f32[8,128]{1,0:T(8,128)} %get-tuple-element.501.refs_0_, ...), custom_call_target="tpu_custom_call" | custom-call | flops 999999995904 | bytes 1 | tf_op jit(solution)/shard_map/pallas_call | solution.py:78
  216.4 17.2 %shard_map.284 = (bf16[4,3,256,768]{3,2,1,0:T(8,128)(2,1)}, bf16[4,3,256,768]{3,2,1,0:T(8,128)(2,1)}, f32[8,128]{1,0:T(8,128)}, f32[8,128]{1,0:T(8,128)}, f32[8,128]{1,0:T(8,128)}, /*index=5*/f32[8,128]{1,0:T(8,128)}) custom-call(s32[22]{0:T(128)} %stack.91.scalars, f32[8,128]{1,0:T(8,128)} %get-tuple-element.509.refs_0_, ...), custom_call_target="tpu_custom_call" | custom-call | flops 999999995904 | bytes 1 | tf_op jit(solution)/shard_map/pallas_call | solution.py:78
  233.9 18.1 %shard_map.285 = (bf16[3,1024,256]{2,1,0:T(8,128)(2,1)}, bf16[3,1024,512]{2,1,0:T(8,128)(2,1)}, f32[1024,16]{1,0:T(8,128)}, f32[8,128]{1,0:T(8,128)}, f32[8,128]...) custom-call(s32[22]{0:T(128)} %stack.91.scalars, f32[8,128]{1,0:T(8,128)} %get-tuple-element.519.refs_0_, ...), custom_call_target="tpu_custom_call" | custom-call | flops 999999995904 | bytes 1 | tf_op jit(solution)/shard_map/pallas_call | solution.py:78
  263.3 36.9 %shard_map.286 = (bf16[8,1024,256]{2,1,0:T(8,128)(2,1)}, bf16[8,1024,512]{2,1,0:T(8,128)(2,1)}, f32[1024,16]{1,0:T(8,128)}, f32[8,128]{1,0:T(8,128)}, f32[8,128]...) custom-call(s32[22]{0:T(128)} %stack.91.scalars, f32[8,128]{1,0:T(8,128)} %get-tuple-element.533.refs_0_, ...), custom_call_target="tpu_custom_call" | custom-call | flops 999999995904 | bytes 1 | tf_op jit(solution)/shard_map/pallas_call | solution.py:78
  300.3 16.7 %shard_map.287 = (bf16[4,3,256,768]{3,2,1,0:T(8,128)(2,1)}, bf16[4,3,256,768]{3,2,1,0:T(8,128)(2,1)}, f32[8,128]{1,0:T(8,128)}, f32[8,128]{1,0:T(8,128)}, f32[8,128]{1,0:T(8,128)}, /*index=5*/f32[8,128]{1,0:T(8,128)}) custom-call(s32[22]{0:T(128)} %stack.91.scalars, f32[8,128]{1,0:T(8,128)} %get-tuple-element.540.refs_0_, ...), custom_call_target="tpu_custom_call" | custom-call | flops 999999995904 | bytes 1 | tf_op jit(solution)/shard_map/pallas_call | solution.py:78
  317.2 6.0 shard_map.288
  337.7 46.7 %shard_map.290 = (bf16[4,256,2176]{2,1,0:T(8,128)(2,1)}, f32[8,128]{1,0:T(8,128)}, f32[8,128]{1,0:T(8,128)}, f32[8,128]{1,0:T(8,128)}, f32[8,128]{1,0:T(8,128)}) custom-call(s32[22]{0:T(128)} %stack.91.scalars, f32[8,128]{1,0:T(8,128)} %get-tuple-element.567.refs_0_, f32[8,128]{1,0:T(8,128)} %get-tuple-element.568.refs_1_, ...), custom_call_target="tpu_custom_call" | custom-call | flops 999999995904 | bytes 1 | tf_op jit(solution)/shard_map/pallas_call | solution.py:78
  389.9 6.0 shard_map.291
  395.8 21.7 %shard_map.292 = (bf16[4,1024,256]{2,1,0:T(8,128)(2,1)}, bf16[4,1024,512]{2,1,0:T(8,128)(2,1)}, f32[1024,16]{1,0:T(8,128)}, f32[8,128]{1,0:T(8,128)}, f32[8,128]...) custom-call(s32[22]{0:T(128)} %stack.91.scalars, f32[8,128]{1,0:T(8,128)} %get-tuple-element.584.refs_0_, ...), custom_call_target="tpu_custom_call" | custom-call | flops 999999995904 | bytes 1 | tf_op jit(solution)/shard_map/pallas_call | solution.py:78
  424.1 23.2 %shard_map.293 = (bf16[4,2,256,768]{3,2,1,0:T(8,128)(2,1)}, bf16[4,2,256,768]{3,2,1,0:T(8,128)(2,1)}, f32[8,128]{1,0:T(8,128)}, f32[8,128]{1,0:T(8,128)}, f32[8,128]{1,0:T(8,128)}, /*index=5*/f32[8,128]{1,0:T(8,128)}) custom-call(s32[22]{0:T(128)} %stack.91.scalars, f32[8,128]{1,0:T(8,128)} %get-tuple-element.592.refs_0_, ...), custom_call_target="tpu_custom_call" | custom-call | flops 999999995904 | bytes 1 | tf_op jit(solution)/shard_map/pallas_call | solution.py:78
  447.5 7.5 %shard_map.294 = (bf16[256,2048]{1,0:T(8,128)(2,1)}, f32[1,2048]{1,0:T(1,128)}, f32[2048,16]{1,0:T(8,128)}, f32[8,128]{1,0:T(8,128)}, f32[8,128]{1,0:T(8,128)}, /*index=5*/f32[8,128]{1,0:T(8,128)}, f32[8,128]{1,0:T(8,128)}) custom-call(s32[22]{0:T(128)} %stack.91.scalars, f32[8,128]{1,0:T(8,128)} %get-tuple-element.605.refs_0_, ...), custom_call_target="tpu_custom_call" | custom-call | flops 999999995904 | bytes 1 | tf_op jit(solution)/shard_map/pallas_call | solution.py:78
  468.5 22.9 %shard_map.296 = (bf16[4,2,256,768]{3,2,1,0:T(8,128)(2,1)}, bf16[4,2,256,768]{3,2,1,0:T(8,128)(2,1)}, f32[8,128]{1,0:T(8,128)}, f32[8,128]{1,0:T(8,128)}, f32[8,128]{1,0:T(8,128)}, /*index=5*/f32[8,128]{1,0:T(8,128)}) custom-call(s32[22]{0:T(128)} %stack.91.scalars, f32[8,128]{1,0:T(8,128)} %get-tuple-element.626.refs_0_, ...), custom_call_target="tpu_custom_call" | custom-call | flops 999999995904 | bytes 1 | tf_op jit(solution)/shard_map/pallas_call | solution.py:78
  491.3 26.8 %shard_map.297 = (bf16[4,1024,512]{2,1,0:T(8,128)(2,1)}, f32[8,128]{1,0:T(8,128)}, f32[8,128]{1,0:T(8,128)}, f32[8,128]{1,0:T(8,128)}, f32[8,128]{1,0:T(8,128)}) custom-call(s32[22]{0:T(128)} %stack.91.scalars, f32[8,128]{1,0:T(8,128)} %get-tuple-element.632.refs_0_, f32[8,128]{1,0:T(8,128)} %get-tuple-element.633.refs_1_, ...), custom_call_target="tpu_custom_call" | custom-call | flops 999999995904 | bytes 1 | tf_op jit(solution)/shard_map/pallas_call | solution.py:78
  524.5 6.8 shard_map.298
  531.9 6.3 shard_map.299
  547.2 21.9 %shard_map.300 = (bf16[3,1024,512]{2,1,0:T(8,128)(2,1)}, f32[4,2,128]{2,1,0:T(2,128)}, f32[8,128]{1,0:T(8,128)}, f32[8,128]{1,0:T(8,128)}, f32[8,128]{1,0:T(8,128)}, /*index=5*/f32[8,128]{1,0:T(8,128)}) custom-call(s32[22]{0:T(128)} %stack.91.scalars, f32[8,128]{1,0:T(8,128)} %get-tuple-element.662.refs_0_, f32[8,128]{1,0:T(8,128)} %get-tuple-element.663.refs_1_, ...), custom_call_target="tpu_custom_call" | custom-call | flops 999999995904 | bytes 1 | tf_op jit(solution)/shard_map/pallas_call | solution.py:78
  569.1 11.6 %shard_map.301 = (bf16[4,3,256,512]{3,2,1,0:T(8,128)(2,1)}, bf16[4,3,256,512]{3,2,1,0:T(8,128)(2,1)}, f32[8,128]{1,0:T(8,128)}, f32[8,128]{1,0:T(8,128)}, f32[8,128]{1,0:T(8,128)}, /*index=5*/f32[8,128]{1,0:T(8,128)}) custom-call(s32[22]{0:T(128)} %stack.91.scalars, f32[8,128]{1,0:T(8,128)} %get-tuple-element.673.refs_0_, ...), custom_call_target="tpu_custom_call" | custom-call | flops 999999995904 | bytes 1 | tf_op jit(solution)/shard_map/pallas_call | solution.py:78
  591.8 13.6 %shard_map.303 = (bf16[4,1024,512]{2,1,0:T(8,128)(2,1)}, f32[1024,1]{1,0:T(8,128)}, f32[1,2048]{1,0:T(1,128)}, f32[8,128]{1,0:T(8,128)}, f32[8,128]{1,0:T(8,128)}, /*index=5*/f32[8,128]{1,0:T(8,128)}, f32[8,128]{1,0:T(8,128)}) custom-call(s32[22]{0:T(128)} %stack.91.scalars, f32[8,128]{1,0:T(8,128)} %get-tuple-element.692.refs_0_, ...), custom_call_target="tpu_custom_call" | custom-call | flops 999999995904 | bytes 1 | tf_op jit(solution)/shard_map/pallas_call | solution.py:78
  642.0 10.3 %collective-permute-done.38 = bf16[2,3,256,512]{3,2,1,0:T(8,128)(2,1)} collective-permute-done((bf16[2,3,256,512]{3,2,1,0:T(8,128)(2,1)}, bf16[2,3,256,512]{3,2,1,0:T(8,128)(2,1)}, u32[]{:S(2)}, u32[]{:S(2)}) %collective-permute-start.38) | collective-permute-done | bytes 1572896 | tf_op jit(solution)/shard_map/ppermute | solution.py:101
  669.1 5.8 shard_map.309
  690.1 12.9 %collective-permute-done.50 = bf16[1,3,256,512]{3,2,1,0:T(8,128)(2,1)} collective-permute-done((bf16[1,3,256,512]{3,2,1,0:T(8,128)(2,1)}, bf16[1,3,256,512]{3,2,1,0:T(8,128)(2,1)}, u32[]{:S(2)}, u32[]{:S(2)}) %collective-permute-start.50) | collective-permute-done | bytes 786464 | tf_op jit(solution)/shard_map/ppermute | solution.py:101
  (220 shorter events, 224.0 us)
Async XLA Ops:
  7.2 112.4 %all-gather.12.cloned.1.call-start = ((), (), s32[]{:S(2)}) async-start(), calls=%async_computation.8 | async-start | bytes 9437184 | tf_op jit(solution)/shard_map/all_gather | solution.py:1041
  12.8 33.0 %collective-permute-start = (bf16[1024,512]{1,0:T(8,128)(2,1)}, bf16[1024,512]{1,0:T(8,128)(2,1)}, u32[]{:S(2)}, u32[]{:S(2)}) collective-permute-start(bf16[1024,512]{1,0:T(8,128)(2,1)} %refs_4_), channel_id=1, source_target_pairs={{0,1},{1,0},{2,3},{3,2},{4,5},{5,4},{6,7},{7,6},{8,9},{9,8},{10,11... | collective-permute-start | bytes 3145736 | tf_op jit(solution)/shard_map/ppermute | solution.py:101
  14.7 32.5 %collective-permute-start.1 = (bf16[1024,512]{1,0:T(8,128)(2,1)}, bf16[1024,512]{1,0:T(8,128)(2,1)}, u32[]{:S(2)}, u32[]{:S(2)}) collective-permute-start(bf16[1024,512]{1,0:T(8,128)(2,1)} %refs_4_), channel_id=1, source_target_pairs={{0,2},{1,3},{2,0},{3,1},{4,6},{5,7},{6,4},{7,5},{8,10},{9,11},{10,... | collective-permute-start | bytes 3145736 | tf_op jit(solution)/shard_map/ppermute | solution.py:101
  32.1 285.1 %all-gather.6.cloned.1.call-start = ((), (), s32[]{:S(2)}) async-start(), calls=%async_computation.4 | async-start | bytes 5242880 | tf_op jit(solution)/shard_map/all_gather | solution.py:1068
  64.1 30.7 %collective-permute-start.7 = (bf16[1024,512]{1,0:T(8,128)(2,1)}, bf16[1024,512]{1,0:T(8,128)(2,1)}, u32[]{:S(2)}, u32[]{:S(2)}) collective-permute-start(bf16[1024,512]{1,0:T(8,128)(2,1)} %refs_4_.1), channel_id=1, source_target_pairs={{0,1},{1,0},{2,3},{3,2},{4,5},{5,4},{6,7},{7,6},{8,9},{9,8},{10,11... | collective-permute-start | bytes 3145736 | tf_op jit(solution)/shard_map/ppermute | solution.py:101
  65.5 29.3 %collective-permute-start.8 = (bf16[1024,512]{1,0:T(8,128)(2,1)}, bf16[1024,512]{1,0:T(8,128)(2,1)}, u32[]{:S(2)}, u32[]{:S(2)}) collective-permute-start(bf16[1024,512]{1,0:T(8,128)(2,1)} %refs_4_.1), channel_id=1, source_target_pairs={{0,2},{1,3},{2,0},{3,1},{4,6},{5,7},{6,4},{7,5},{8,10},{9,11},{10,... | collective-permute-start | bytes 3145736 | tf_op jit(solution)/shard_map/ppermute | solution.py:101
  134.9 53.5 %collective-permute-start.21 = (bf16[1024,512]{1,0:T(8,128)(2,1)}, bf16[1024,512]{1,0:T(8,128)(2,1)}, u32[]{:S(2)}, u32[]{:S(2)}) collective-permute-start(bf16[1024,512]{1,0:T(8,128)(2,1)} %refs_4_.1), channel_id=1, source_target_pairs={{0,8},{4,12},{8,0},{12,4},{16,24},{20,28},{24,16},{28,20},{1,9},{5... | collective-permute-start | bytes 3145736 | tf_op jit(solution)/shard_map/ppermute | solution.py:101
  150.4 56.0 %collective-permute-start.26 = (bf16[1024,640]{1,0:T(8,128)(2,1)}, bf16[1024,640]{1,0:T(8,128)(2,1)}, u32[]{:S(2)}, u32[]{:S(2)}) collective-permute-start(bf16[1024,640]{1,0:T(8,128)(2,1)} %get-tuple-element.583), channel_id=1, source_target_pairs={{0,8},{4,12},{8,0},{12,4},{16,24},{20,28},{24,16},{28,20},{1,9},{5... | collective-permute-start | bytes 3932168 | tf_op jit(solution)/shard_map/ppermute | solution.py:101
  188.5 201.4 %all-gather.8.cloned.1.call-start = ((), (), s32[]{:S(2)}) async-start(), calls=%async_computation.5 | async-start | bytes 5242880 | tf_op jit(solution)/shard_map/all_gather | solution.py:1071
  215.2 37.1 %collective-permute-start.18 = (bf16[2,2,256,768]{3,2,1,0:T(8,128)(2,1)}, bf16[2,2,256,768]{3,2,1,0:T(8,128)(2,1)}, u32[]{:S(2)}, u32[]{:S(2)}) collective-permute-start(bf16[2,2,256,768]{3,2,1,0:T(8,128)(2,1)} %get-tuple-element.815.refs_4_), channel_id=1, source_target_pairs={{0,8},{4,12},{8,0},{12,4},{16,24},{20,28},{24,16},{28,20},{1,9},{5... | collective-permute-start | bytes 4718600 | tf_op jit(solution)/shard_map/ppermute | solution.py:101
  233.6 23.7 %collective-permute-start.17 = (bf16[4,3,256,768]{3,2,1,0:T(8,128)(2,1)}, bf16[4,3,256,768]{3,2,1,0:T(8,128)(2,1)}, u32[]{:S(2)}, u32[]{:S(2)}) collective-permute-start(bf16[4,3,256,768]{3,2,1,0:T(8,128)(2,1)} %get-tuple-element.518), channel_id=1, source_target_pairs={{0,4},{4,0},{8,12},{12,8},{16,20},{20,16},{24,28},{28,24},{1,5},{5... | collective-permute-start | bytes 14155784 | tf_op jit(solution)/shard_map/ppermute | solution.py:101
  255.4 67.9 %collective-permute-start.22 = (bf16[1,2,256,768]{3,2,1,0:T(8,128)(2,1)}, bf16[1,2,256,768]{3,2,1,0:T(8,128)(2,1)}, u32[]{:S(2)}, u32[]{:S(2)}) collective-permute-start(bf16[1,2,256,768]{3,2,1,0:T(8,128)(2,1)} %get-tuple-element.537.refs_4_), channel_id=1, source_target_pairs={{0,16},{4,20},{8,24},{12,28},{16,0},{20,4},{24,8},{28,12},{1,17},{... | collective-permute-start | bytes 2359304 | tf_op jit(solution)/shard_map/ppermute | solution.py:101
  257.3 42.9 %collective-permute-start.19 = (f32[8,128]{1,0:T(8,128)}, f32[8,128]{1,0:T(8,128)}, u32[]{:S(2)}, u32[]{:S(2)}) collective-permute-start(f32[8,128]{1,0:T(8,128)} %get-tuple-element.533.refs_0_), channel_id=1, source_target_pairs={{0,4},{4,0},{8,12},{12,8},{16,20},{20,16},{24,28},{28,24},{1,5},{5... | collective-permute-start | bytes 12296 | tf_op jit(solution)/shard_map/ppermute | solution.py:101
  261.7 70.8 %collective-permute-start.24 = (bf16[2,3,256,768]{3,2,1,0:T(8,128)(2,1)}, bf16[2,3,256,768]{3,2,1,0:T(8,128)(2,1)}, u32[]{:S(2)}, u32[]{:S(2)}) collective-permute-start(bf16[2,3,256,768]{3,2,1,0:T(8,128)(2,1)} %get-tuple-element.805.refs_5_), channel_id=1, source_target_pairs={{0,8},{4,12},{8,0},{12,4},{16,24},{20,28},{24,16},{28,20},{1,9},{5... | collective-permute-start | bytes 7077896 | tf_op jit(solution)/shard_map/ppermute | solution.py:101
  332.1 85.8 %collective-permute-start.23 = (bf16[2,3,256,768]{3,2,1,0:T(8,128)(2,1)}, bf16[2,3,256,768]{3,2,1,0:T(8,128)(2,1)}, u32[]{:S(2)}, u32[]{:S(2)}) collective-permute-start(bf16[2,3,256,768]{3,2,1,0:T(8,128)(2,1)} %get-tuple-element.571.refs_4_), channel_id=1, source_target_pairs={{0,8},{4,12},{8,0},{12,4},{16,24},{20,28},{24,16},{28,20},{1,9},{5... | collective-permute-start | bytes 7077896 | tf_op jit(solution)/shard_map/ppermute | solution.py:101
  336.1 127.8 %collective-permute-start.30 = (bf16[1,3,256,768]{3,2,1,0:T(8,128)(2,1)}, bf16[1,3,256,768]{3,2,1,0:T(8,128)(2,1)}, u32[]{:S(2)}, u32[]{:S(2)}) collective-permute-start(bf16[1,3,256,768]{3,2,1,0:T(8,128)(2,1)} %get-tuple-element.819.refs_5_), channel_id=1, source_target_pairs={{0,16},{4,20},{8,24},{12,28},{16,0},{20,4},{24,8},{28,12},{1,17},{... | collective-permute-start | bytes 3538952 | tf_op jit(solution)/shard_map/ppermute | solution.py:101
  384.6 62.9 %all-to-all-start = ((bf16[4,256,2176]{2,1,0:T(8,128)(2,1)}), bf16[4,256,2176]{2,1,0:T(8,128)(2,1)}, u32[]{:S(2)}, u32[]{:S(2)}) async-start(bf16[4,256,2176]{2,1,0:T(8,128)(2,1)} %get-tuple-element.609), calls=%async_computation | async-start | bytes 8912896 | tf_op jit(solution)/shard_map/all_to_all | solution.py:157
  389.6 135.0 %all-gather.10.cloned.1.call-start = ((), (), s32[]{:S(2)}) async-start(), calls=%async_computation.6 | async-start | bytes 5242880 | tf_op jit(solution)/shard_map/all_gather | solution.py:1151
  421.6 159.1 %collective-permute-start.36 = (bf16[1,3,256,768]{3,2,1,0:T(8,128)(2,1)}, bf16[1,3,256,768]{3,2,1,0:T(8,128)(2,1)}, u32[]{:S(2)}, u32[]{:S(2)}) collective-permute-start(bf16[1,3,256,768]{3,2,1,0:T(8,128)(2,1)} %get-tuple-element.817.refs_4_), channel_id=1, source_target_pairs={{0,16},{4,20},{8,24},{12,28},{16,0},{20,4},{24,8},{28,12},{1,17},{... | collective-permute-start | bytes 3538952 | tf_op jit(solution)/shard_map/ppermute | solution.py:101
  462.9 160.2 %collective-permute-start.41 = (bf16[2,2,256,768]{3,2,1,0:T(8,128)(2,1)}, bf16[2,2,256,768]{3,2,1,0:T(8,128)(2,1)}, u32[]{:S(2)}, u32[]{:S(2)}) collective-permute-start(bf16[2,2,256,768]{3,2,1,0:T(8,128)(2,1)} %get-tuple-element.809.refs_4_), channel_id=1, source_target_pairs={{0,16},{4,20},{8,24},{12,28},{16,0},{20,4},{24,8},{28,12},{1,17},{... | collective-permute-start | bytes 4718600 | tf_op jit(solution)/shard_map/ppermute | solution.py:101
  491.3 26.8 %collective-permute-start.32 = (bf16[4,2,256,768]{3,2,1,0:T(8,128)(2,1)}, bf16[4,2,256,768]{3,2,1,0:T(8,128)(2,1)}, u32[]{:S(2)}, u32[]{:S(2)}) collective-permute-start(bf16[4,2,256,768]{3,2,1,0:T(8,128)(2,1)} %get-tuple-element.631), channel_id=1, source_target_pairs={{0,4},{4,0},{8,12},{12,8},{16,20},{20,16},{24,28},{28,24},{1,5},{5... | collective-permute-start | bytes 9437192 | tf_op jit(solution)/shard_map/ppermute | solution.py:101
  522.5 105.3 %collective-permute-start.40 = (bf16[2,2,256,768]{3,2,1,0:T(8,128)(2,1)}, bf16[2,2,256,768]{3,2,1,0:T(8,128)(2,1)}, u32[]{:S(2)}, u32[]{:S(2)}) collective-permute-start(bf16[2,2,256,768]{3,2,1,0:T(8,128)(2,1)} %get-tuple-element.811.refs_4_), channel_id=1, source_target_pairs={{0,16},{4,20},{8,24},{12,28},{16,0},{20,4},{24,8},{28,12},{1,17},{... | collective-permute-start | bytes 4718600 | tf_op jit(solution)/shard_map/ppermute | solution.py:101
  538.2 72.5 %all-to-all-start.1 = ((bf16[4,1024,512]{2,1,0:T(8,128)(2,1)}), bf16[4,1024,512]{2,1,0:T(8,128)(2,1)}, u32[]{:S(2)}, u32[]{:S(2)}) async-start(bf16[4,1024,512]{2,1,0:T(8,128)(2,1)} %get-tuple-element.704), calls=%async_computation.1 | async-start | bytes 8388608 | tf_op jit(solution)/shard_map/all_to_all | solution.py:157
  543.1 97.5 %reduce-scatter.2.cloned.1.call-start = ((), (), s32[]{:S(2)}) async-start(), calls=%async_computation.7 | async-start | bytes 221184 | tf_op jit(solution)/shard_map/reduce_scatter | solution.py:1180
  545.6 88.5 %collective-permute-start.39 = (bf16[2,1,512,256]{3,2,1,0:T(8,128)(2,1)}, bf16[2,1,512,256]{3,2,1,0:T(8,128)(2,1)}, u32[]{:S(2)}, u32[]{:S(2)}) collective-permute-start(bf16[2,1,512,256]{3,2,1,0:T(8,128)(2,1)} %get-tuple-element.829.refs_5_), channel_id=1, source_target_pairs={{0,8},{4,12},{8,0},{12,4},{16,24},{20,28},{24,16},{28,20},{1,9},{5... | collective-permute-start | bytes 1572872 | tf_op jit(solution)/shard_map/ppermute | solution.py:101
  591.5 60.8 %collective-permute-start.38 = (bf16[2,3,256,512]{3,2,1,0:T(8,128)(2,1)}, bf16[2,3,256,512]{3,2,1,0:T(8,128)(2,1)}, u32[]{:S(2)}, u32[]{:S(2)}) collective-permute-start(bf16[2,3,256,512]{3,2,1,0:T(8,128)(2,1)} %get-tuple-element.813.refs_5_), channel_id=1, source_target_pairs={{0,8},{4,12},{8,0},{12,4},{16,24},{20,28},{24,16},{28,20},{1,9},{5... | collective-permute-start | bytes 4718600 | tf_op jit(solution)/shard_map/ppermute | solution.py:101
  610.6 58.5 %all-to-all-start.2 = ((bf16[4,1024,512]{2,1,0:T(8,128)(2,1)}), bf16[4,1024,512]{2,1,0:T(8,128)(2,1)}, u32[]{:S(2)}, u32[]{:S(2)}) async-start(bf16[4,1024,512]{2,1,0:T(8,128)(2,1)} %get-tuple-element.761), calls=%async_computation.2 | async-start | bytes 8388608 | tf_op jit(solution)/shard_map/all_to_all | solution.py:157
  626.1 51.4 %collective-permute-start.46 = (bf16[1,2,256,768]{3,2,1,0:T(8,128)(2,1)}, bf16[1,2,256,768]{3,2,1,0:T(8,128)(2,1)}, u32[]{:S(2)}, u32[]{:S(2)}) collective-permute-start(bf16[1,2,256,768]{3,2,1,0:T(8,128)(2,1)} %get-tuple-element.725.refs_4_), channel_id=1, source_target_pairs={{0,8},{4,12},{8,0},{12,4},{16,24},{20,28},{24,16},{28,20},{1,9},{5... | collective-permute-start | bytes 2359304 | tf_op jit(solution)/shard_map/ppermute | solution.py:101
  630.7 55.3 %collective-permute-start.49 = (bf16[1,2,256,768]{3,2,1,0:T(8,128)(2,1)}, bf16[1,2,256,768]{3,2,1,0:T(8,128)(2,1)}, u32[]{:S(2)}, u32[]{:S(2)}) collective-permute-start(bf16[1,2,256,768]{3,2,1,0:T(8,128)(2,1)} %get-tuple-element.823.refs_5_), channel_id=1, source_target_pairs={{0,8},{4,12},{8,0},{12,4},{16,24},{20,28},{24,16},{28,20},{1,9},{5... | collective-permute-start | bytes 2359304 | tf_op jit(solution)/shard_map/ppermute | solution.py:101
  634.1 29.1 %collective-permute-start.44 = (f32[8,128]{1,0:T(8,128)}, f32[8,128]{1,0:T(8,128)}, u32[]{:S(2)}, u32[]{:S(2)}) collective-permute-start(f32[8,128]{1,0:T(8,128)} %get-tuple-element.755.refs_5_), channel_id=1, source_target_pairs={{0,2},{1,3},{2,0},{3,1},{4,6},{5,7},{6,4},{7,5},{8,10},{9,11},{10,... | collective-permute-start | bytes 12296 | tf_op jit(solution)/shard_map/ppermute | solution.py:101
  638.1 45.1 %collective-permute-start.48 = (bf16[1,1,512,256]{3,2,1,0:T(8,128)(2,1)}, bf16[1,1,512,256]{3,2,1,0:T(8,128)(2,1)}, u32[]{:S(2)}, u32[]{:S(2)}) collective-permute-start(bf16[1,1,512,256]{3,2,1,0:T(8,128)(2,1)} %get-tuple-element.745.refs_4_), channel_id=1, source_target_pairs={{0,16},{4,20},{8,24},{12,28},{16,0},{20,4},{24,8},{28,12},{1,17},{... | collective-permute-start | bytes 786440 | tf_op jit(solution)/shard_map/ppermute | solution.py:101
  664.6 38.4 %collective-permute-start.50 = (bf16[1,3,256,512]{3,2,1,0:T(8,128)(2,1)}, bf16[1,3,256,512]{3,2,1,0:T(8,128)(2,1)}, u32[]{:S(2)}, u32[]{:S(2)}) collective-permute-start(bf16[1,3,256,512]{3,2,1,0:T(8,128)(2,1)} %get-tuple-element.821.refs_5_), channel_id=1, source_target_pairs={{0,16},{4,20},{8,24},{12,28},{16,0},{20,4},{24,8},{28,12},{1,17},{... | collective-permute-start | bytes 2359304 | tf_op jit(solution)/shard_map/ppermute | solution.py:101
  (51 other events, 573.4 us)
Sparse Core Ops, SparseCore 0:
  32.2 82.3 all-gather.11
  188.6 52.7 all-gather.5
  243.2 52.5 all-gather.7
  455.1 52.4 all-gather.9
  610.7 29.8 reduce-scatter.1

commit v6 on v5

--- a/solution.py
+++ b/solution.py
@@ -487,7 +487,9 @@
     pieces = read_pieces(refs[:n_in], halves)
     weights = refs[n_in : n_in + n_last]
     first, gain, router, kept = refs[n_in + n_last : n_in + n_last + 4]
-    stream_out, normed_out, mine_out, turned_out, factor_out, probs_out, gates_out = refs[n_in + n_last + 4 :]
+    stream_out, normed_out, mine_out, packed_out, turned_out, factor_out, probs_out, gates_out = refs[
+        n_in + n_last + 4 :
+    ]
     total = add_products(first[...], pieces, weights)
     width = total.shape[1] // n_tp
     stream_out[...] = total
@@ -495,14 +497,14 @@
     factor_out[...] = factor
     normed = (total * factor * gain[...]).astype(bf16)
     normed_out[...] = normed
-    mine_out[:, :width] = normed_out[:, pl.ds(pl.multiple_of(scalars[0] * width, width), width)]
+    mine_out[...] = normed_out[:, pl.ds(pl.multiple_of(scalars[0] * width, width), width)]
     logits = dot(normed, router[...])
     power = jnp.exp(logits - jnp.max(logits, axis=1, keepdims=True))
     probs = power / jnp.sum(power, axis=1, keepdims=True)
     probs_out[...] = probs
     gates = probs * kept[...]
     gates_out[...] = gates
-    mine_out[:, width:] = two_terms(gates, mine_out.shape[1] - width)
+    packed_out[...] = two_terms(gates, packed_out.shape[1])
     transpose_blocks(scalars, n_tp, normed_out, turned_out, dp_count)
 
 
@@ -523,7 +525,8 @@
         [
             struct((tokens, features), f32),
             struct((tokens, features), bf16),
-            struct((tokens, width + 128), bf16),
+            struct((tokens, width), bf16),
+            struct((tokens, 128), bf16),
             struct((features, tokens), bf16),
             struct((tokens, 1), f32),
             struct((tokens, experts), f32),
@@ -532,7 +535,8 @@
         [
             rows(features),
             rows(features),
-            rows(width + 128),
+            rows(width),
+            rows(128),
             pl.BlockSpec((features, TB), lambda i, s: (0, i)),
             rows(1),
             rows(experts),
@@ -552,7 +556,9 @@
 
     gate_val, up_val = dot(n_ref[...], wg[0]), dot(n_ref[...], wu[0])
     back = dot(g_ref[...], wd[0], NT)
-    gates = gates_ref[...]
+    gates, experts = gates_ref[...], dgate_out.shape[1]
+    if gates_ref.dtype == bf16:
+        gates = gates[:, :experts].astype(f32) + gates[:, experts : 2 * experts].astype(f32)
     here = lax.broadcasted_iota(jnp.int32, gates.shape, 1) == expert
     gate = jnp.sum(jnp.where(here, gates, 0.0), axis=1, keepdims=True)
     sigmoid = 1.0 / (1.0 + jnp.exp(-gate_val))
@@ -807,7 +813,7 @@
     soft = probs[...]
     dlogits = soft * (dprobs - jnp.sum(dprobs * soft, axis=1, keepdims=True))
     dlogits = dlogits.astype(bf16)
-    drouter_out[...] = dot(normed[...], dlogits, TN)
+    drouter_out[...] = dot(dlogits, normed[...], TN)
     total += dot(dlogits, router[...], NT)
     scale = factor[...]
     normal = stream[...] * scale
@@ -830,8 +836,8 @@
         [pl.BlockSpec(parts.shape, lambda i, s: (0, 0, 0))]
         + [mine(experts), mine(experts), mine(features), mine(features), mine(1), mine(features)]
         + [plain(1, features), plain(features, experts)],
-        [struct((rows, features), bf16), struct((1, features), f32), struct((features, experts), f32)],
-        [plain(rows, features), plain(1, features), plain(features, experts)],
+        [struct((rows, features), bf16), struct((1, features), f32), struct((experts, features), f32)],
+        [plain(rows, features), plain(1, features), plain(experts, features)],
     )
 
 
@@ -1056,7 +1062,7 @@
     g_mine = line.pin(g_mine)
     g_last = [swap(g_mine, "tensor", n_tp, r) for r in range(early, n_tp)]
     g_near = swap(g_mine, "dp", n_dp, near)
-    stream, normed2, normed2_mine, turned, factor2, probs, gates = stream_of(
+    stream, normed2, normed2_mine, packed, turned, factor2, probs, gates = stream_of(
         scalars, attended_pieces[early:], stream, w_all, gain2, w_router, kept, n_tp, n_dp
     )
     for r in range(early, n_tp):
@@ -1066,9 +1072,8 @@
     normed_near = swap(normed2_mine, "dp", n_dp, near)
     g_near, _ = lax.optimization_barrier((g_near, upstream))
     upstream_near = lax.all_gather(g_near, "tensor", axis=1, tiled=True)
-    gates_near = normed_near[:, width : width + experts].astype(f32)
-    gates_near += normed_near[:, width + experts : width + 2 * experts].astype(f32)
-    normed2_near = lax.all_gather(normed_near[:, :width], "tensor", axis=1, tiled=True)
+    gates_near = swap(packed, "dp", n_dp, near)
+    normed2_near = lax.all_gather(normed_near, "tensor", axis=1, tiled=True)
 
     hiddens, pairs, dgates = [], [], []
 
@@ -1176,7 +1181,7 @@
 
     own_heads = jnp.moveaxis(dhead_gains.reshape(heads, 2, n_dp, hd // n_dp), 2, 0).reshape(n_dp, -1)
     flat_heads = jnp.pad(own_heads, ((0, 0), (0, features // n_dp - own_heads.shape[1]))).reshape(1, -1)
-    small = jnp.concatenate([drouter.T, dgain2, dgain1, flat_heads], axis=0)
+    small = jnp.concatenate([drouter, dgain2, dgain1, flat_heads], axis=0)
     small = lax.psum_scatter(small, "dp", scatter_dimension=1, tiled=True)
     row_dot = row_dot.reshape(8, token_count // 8)
 

time: 725 us -> 723 us (level)
    ppermute x51 -> x52, waiting for transfers between devices: 68.4 us -> 72.9 us  [swap(): return lax.ppermute(value, axis, [(i, i ^ mask) for i in range(count)])]
    ppermute x51 -> x52, starting transfers between devices: 48.2 us -> 50.1 us  [swap(): return lax.ppermute(value, axis, [(i, i ^ mask) for i in range(count)])]
  transfers between devices with their start and end apart: 59 -> 60, of which waited for: 15 -> 14; matrix products, arithmetic and copies ran while one was open for 10% -> 10% of each run, Pallas kernels for 67% -> 67%
where the time goes in v6:
time: 723 us; the launch traced here: 717 us
  Pallas kernels  487 us (67%)
  waiting for transfers between devices  74.8 us (10%)
  starting transfers between devices  65.4 us (9%)
  other arithmetic  56.4 us (8%)
  local copies, waits for them, and re-layouts  19.2 us (3%)
  between operations  14.4 us (2%)
    pallas_call x44, Pallas kernels, call(): pl.pallas_call(without_deps, out_shape=outs + [struct((8, 128), f32)] * M...  487 us
    ppermute x52, waiting for transfers between devices, swap(): return lax.ppermute(value, axis, [(i, i ^ mask) for i in range(count)])  72.9 us
    ppermute x52, starting transfers between devices, swap(): return lax.ppermute(value, axis, [(i, i ^ mask) for i in range(count)])  50.1 us
    convert_element_type x7, other arithmetic, add_halves(): (left.astype(f32) + right.astype(f32)).astype(bf16)  31.9 us
    all_to_all x3, starting transfers between devices, trade(): return lax.all_to_all(pieces, axis, 0, 0, tiled=True)  15 us
  transfers between devices with their start and end apart: 60, of which 14 were waited for; matrix products, arithmetic and copies ran while one was open for 10% of the time, Pallas kernels for 67%

profile of v6, /device:TPU:0, one launch (start us, length us, event | category | flops | bytes accessed | tf_op | source)
XLA Modules:
  0.0 717.3 jit_solution(11489738403887819035)
XLA Ops:
  32.2 13.6 %collective-permute-done.refs_5_ = bf16[1024,512]{1,0:T(8,128)(2,1)} collective-permute-done((bf16[1024,512]{1,0:T(8,128)(2,1)}, bf16[1024,512]{1,0:T(8,128)(2,1)}, u32[]{:S(2)}, u32[]{:S(2)}) %collective-permute-start) | collective-permute-done | bytes 1048608 | tf_op jit(solution)/shard_map/ppermute | solution.py:101
  67.0 16.0 %shard_map.274 = (bf16[1024,2048]{1,0:T(8,128)(2,1)}, bf16[1024,2048]{1,0:T(8,128)(2,1)}, f32[1024,1]{1,0:T(8,128)}, f32[1024,512]{1,0:T(8,128)}, f32[1024,512]{...) custom-call(s32[22]{0:T(128)} %stack.91.scalars, ...), custom_call_target="tpu_custom_call" | custom-call | flops 999999995904 | bytes 1 | tf_op jit(solution)/shard_map/pallas_call | solution.py:78
  82.9 11.8 %shard_map.275 = (bf16[512,512]{1,0:T(8,128)(2,1)}, bf16[512,512]{1,0:T(8,128)(2,1)}, f32[4,1024,1]{2,1,0:T(8,128)}, f32[8,128]{1,0:T(8,128)}, f32[8,128]{1,0:T(...) custom-call(s32[22]{0:T(128)} %stack.91.scalars, f32[8,128]{1,0:T(8,128)} %get-tuple-element.431.refs_0_, ...), custom_call_target="tpu_custom_call" | custom-call | flops 999999995904 | bytes 1 | tf_op jit(solution)/shard_map/pallas_call | solution.py:78
  98.9 6.6 shard_map.276
  105.4 6.1 shard_map.277
  111.5 6.2 collective-permute-done.10.refs_8_
  119.5 13.4 %shard_map.278 = (f32[1024,2048]{1,0:T(8,128)}, f32[8,128]{1,0:T(8,128)}, f32[8,128]{1,0:T(8,128)}, f32[8,128]{1,0:T(8,128)}, f32[8,128]{1,0:T(8,128)}) custom-call(s32[22]{0:T(128)} %stack.91.scalars, f32[8,128]{1,0:T(8,128)} %get-tuple-element.458.refs_0_, f32[8,128]{1,0:T(8,128)} %get-tuple-element.459.refs_1_, f32[8,128]{1,0:T(8,128)} %get-tuple-element.460.refs_2_, ...), custom_call_target="tpu_custom_call" | custom-call | flops 999999995904 | bytes 1 | tf_op jit(solution)/shard_map/pallas_call | solution.py:78
  136.3 14.1 %shard_map.279 = (f32[1024,2048]{1,0:T(8,128)}, bf16[1024,2048]{1,0:T(8,128)(2,1)}, bf16[1024,512]{1,0:T(8,128)(2,1)}, bf16[1024,128]{1,0:T(8,128)(2,1)}, bf16[2...) custom-call(s32[22]{0:T(128)} %stack.91.scalars, ...), custom_call_target="tpu_custom_call" | custom-call | flops 999999995904 | bytes 1 | tf_op jit(solution)/shard_map/pallas_call | solution.py:78
  154.5 6.3 shard_map.280
  160.8 14.1 %shard_map.281 = (bf16[2,1024,256]{2,1,0:T(8,128)(2,1)}, bf16[2,1024,512]{2,1,0:T(8,128)(2,1)}, f32[1024,16]{1,0:T(8,128)}, f32[8,128]{1,0:T(8,128)}, f32[8,128]...) custom-call(s32[22]{0:T(128)} %stack.91.scalars, f32[8,128]{1,0:T(8,128)} %get-tuple-element.485.refs_0_, ...), custom_call_target="tpu_custom_call" | custom-call | flops 999999995904 | bytes 1 | tf_op jit(solution)/shard_map/pallas_call | solution.py:78
  174.9 13.5 %shard_map.282 = (bf16[4,2,256,768]{3,2,1,0:T(8,128)(2,1)}, bf16[4,2,256,768]{3,2,1,0:T(8,128)(2,1)}, f32[8,128]{1,0:T(8,128)}, f32[8,128]{1,0:T(8,128)}, f32[8,128]{1,0:T(8,128)}, /*index=5*/f32[8,128]{1,0:T(8,128)}) custom-call(s32[22]{0:T(128)} %stack.91.scalars, f32[8,128]{1,0:T(8,128)} %get-tuple-element.492.refs_0_, ...), custom_call_target="tpu_custom_call" | custom-call | flops 999999995904 | bytes 1 | tf_op jit(solution)/shard_map/pallas_call | solution.py:78
  188.5 18.1 %shard_map.283 = (bf16[3,1024,256]{2,1,0:T(8,128)(2,1)}, bf16[3,1024,512]{2,1,0:T(8,128)(2,1)}, f32[1024,16]{1,0:T(8,128)}, f32[8,128]{1,0:T(8,128)}, f32[8,128]...) custom-call(s32[22]{0:T(128)} %stack.91.scalars, f32[8,128]{1,0:T(8,128)} %get-tuple-element.502.refs_0_, ...), custom_call_target="tpu_custom_call" | custom-call | flops 999999995904 | bytes 1 | tf_op jit(solution)/shard_map/pallas_call | solution.py:78
  213.2 16.9 %shard_map.284 = (bf16[4,3,256,768]{3,2,1,0:T(8,128)(2,1)}, bf16[4,3,256,768]{3,2,1,0:T(8,128)(2,1)}, f32[8,128]{1,0:T(8,128)}, f32[8,128]{1,0:T(8,128)}, f32[8,128]{1,0:T(8,128)}, /*index=5*/f32[8,128]{1,0:T(8,128)}) custom-call(s32[22]{0:T(128)} %stack.91.scalars, f32[8,128]{1,0:T(8,128)} %get-tuple-element.510.refs_0_, ...), custom_call_target="tpu_custom_call" | custom-call | flops 999999995904 | bytes 1 | tf_op jit(solution)/shard_map/pallas_call | solution.py:78
  230.3 18.2 %shard_map.285 = (bf16[3,1024,256]{2,1,0:T(8,128)(2,1)}, bf16[3,1024,512]{2,1,0:T(8,128)(2,1)}, f32[1024,16]{1,0:T(8,128)}, f32[8,128]{1,0:T(8,128)}, f32[8,128]...) custom-call(s32[22]{0:T(128)} %stack.91.scalars, f32[8,128]{1,0:T(8,128)} %get-tuple-element.520.refs_0_, ...), custom_call_target="tpu_custom_call" | custom-call | flops 999999995904 | bytes 1 | tf_op jit(solution)/shard_map/pallas_call | solution.py:78
  260.2 36.9 %shard_map.286 = (bf16[8,1024,256]{2,1,0:T(8,128)(2,1)}, bf16[8,1024,512]{2,1,0:T(8,128)(2,1)}, f32[1024,16]{1,0:T(8,128)}, f32[8,128]{1,0:T(8,128)}, f32[8,128]...) custom-call(s32[22]{0:T(128)} %stack.91.scalars, f32[8,128]{1,0:T(8,128)} %get-tuple-element.534.refs_0_, ...), custom_call_target="tpu_custom_call" | custom-call | flops 999999995904 | bytes 1 | tf_op jit(solution)/shard_map/pallas_call | solution.py:78
  297.2 16.7 %shard_map.287 = (bf16[4,3,256,768]{3,2,1,0:T(8,128)(2,1)}, bf16[4,3,256,768]{3,2,1,0:T(8,128)(2,1)}, f32[8,128]{1,0:T(8,128)}, f32[8,128]{1,0:T(8,128)}, f32[8,128]{1,0:T(8,128)}, /*index=5*/f32[8,128]{1,0:T(8,128)}) custom-call(s32[22]{0:T(128)} %stack.91.scalars, f32[8,128]{1,0:T(8,128)} %get-tuple-element.541.refs_0_, ...), custom_call_target="tpu_custom_call" | custom-call | flops 999999995904 | bytes 1 | tf_op jit(solution)/shard_map/pallas_call | solution.py:78
  314.1 6.0 shard_map.288
  323.1 5.8 add_convert_fusion.1
  334.8 46.8 %shard_map.290 = (bf16[4,256,2176]{2,1,0:T(8,128)(2,1)}, f32[8,128]{1,0:T(8,128)}, f32[8,128]{1,0:T(8,128)}, f32[8,128]{1,0:T(8,128)}, f32[8,128]{1,0:T(8,128)}) custom-call(s32[22]{0:T(128)} %stack.91.scalars, f32[8,128]{1,0:T(8,128)} %get-tuple-element.568.refs_0_, f32[8,128]{1,0:T(8,128)} %get-tuple-element.569.refs_1_, ...), custom_call_target="tpu_custom_call" | custom-call | flops 999999995904 | bytes 1 | tf_op jit(solution)/shard_map/pallas_call | solution.py:78
  387.0 6.0 shard_map.291
  393.0 21.7 %shard_map.292 = (bf16[4,1024,256]{2,1,0:T(8,128)(2,1)}, bf16[4,1024,512]{2,1,0:T(8,128)(2,1)}, f32[1024,16]{1,0:T(8,128)}, f32[8,128]{1,0:T(8,128)}, f32[8,128]...) custom-call(s32[22]{0:T(128)} %stack.91.scalars, f32[8,128]{1,0:T(8,128)} %get-tuple-element.585.refs_0_, ...), custom_call_target="tpu_custom_call" | custom-call | flops 999999995904 | bytes 1 | tf_op jit(solution)/shard_map/pallas_call | solution.py:78
  421.0 23.2 %shard_map.293 = (bf16[4,2,256,768]{3,2,1,0:T(8,128)(2,1)}, bf16[4,2,256,768]{3,2,1,0:T(8,128)(2,1)}, f32[8,128]{1,0:T(8,128)}, f32[8,128]{1,0:T(8,128)}, f32[8,128]{1,0:T(8,128)}, /*index=5*/f32[8,128]{1,0:T(8,128)}) custom-call(s32[22]{0:T(128)} %stack.91.scalars, f32[8,128]{1,0:T(8,128)} %get-tuple-element.594.refs_0_, ...), custom_call_target="tpu_custom_call" | custom-call | flops 999999995904 | bytes 1 | tf_op jit(solution)/shard_map/pallas_call | solution.py:78
  444.3 7.2 %shard_map.294 = (bf16[256,2048]{1,0:T(8,128)(2,1)}, f32[1,2048]{1,0:T(1,128)}, f32[16,2048]{1,0:T(8,128)}, f32[8,128]{1,0:T(8,128)}, f32[8,128]{1,0:T(8,128)}, /*index=5*/f32[8,128]{1,0:T(8,128)}, f32[8,128]{1,0:T(8,128)}) custom-call(s32[22]{0:T(128)} %stack.91.scalars, f32[8,128]{1,0:T(8,128)} %get-tuple-element.607.refs_0_, ...), custom_call_target="tpu_custom_call" | custom-call | flops 999999995904 | bytes 1 | tf_op jit(solution)/shard_map/pallas_call | solution.py:78
  463.2 22.9 %shard_map.296 = (bf16[4,2,256,768]{3,2,1,0:T(8,128)(2,1)}, bf16[4,2,256,768]{3,2,1,0:T(8,128)(2,1)}, f32[8,128]{1,0:T(8,128)}, f32[8,128]{1,0:T(8,128)}, f32[8,128]{1,0:T(8,128)}, /*index=5*/f32[8,128]{1,0:T(8,128)}) custom-call(s32[22]{0:T(128)} %stack.91.scalars, f32[8,128]{1,0:T(8,128)} %get-tuple-element.628.refs_0_, ...), custom_call_target="tpu_custom_call" | custom-call | flops 999999995904 | bytes 1 | tf_op jit(solution)/shard_map/pallas_call | solution.py:78
  486.1 26.8 %shard_map.297 = (bf16[4,1024,512]{2,1,0:T(8,128)(2,1)}, f32[8,128]{1,0:T(8,128)}, f32[8,128]{1,0:T(8,128)}, f32[8,128]{1,0:T(8,128)}, f32[8,128]{1,0:T(8,128)}) custom-call(s32[22]{0:T(128)} %stack.91.scalars, f32[8,128]{1,0:T(8,128)} %get-tuple-element.634.refs_0_, f32[8,128]{1,0:T(8,128)} %get-tuple-element.635.refs_1_, ...), custom_call_target="tpu_custom_call" | custom-call | flops 999999995904 | bytes 1 | tf_op jit(solution)/shard_map/pallas_call | solution.py:78
  519.0 6.8 shard_map.298
  526.4 6.3 shard_map.299
  541.8 21.8 %shard_map.300 = (bf16[3,1024,512]{2,1,0:T(8,128)(2,1)}, f32[4,2,128]{2,1,0:T(2,128)}, f32[8,128]{1,0:T(8,128)}, f32[8,128]{1,0:T(8,128)}, f32[8,128]{1,0:T(8,128)}, /*index=5*/f32[8,128]{1,0:T(8,128)}) custom-call(s32[22]{0:T(128)} %stack.91.scalars, f32[8,128]{1,0:T(8,128)} %get-tuple-element.664.refs_0_, f32[8,128]{1,0:T(8,128)} %get-tuple-element.665.refs_1_, ...), custom_call_target="tpu_custom_call" | custom-call | flops 999999995904 | bytes 1 | tf_op jit(solution)/shard_map/pallas_call | solution.py:78
  563.7 11.6 %shard_map.301 = (bf16[4,3,256,512]{3,2,1,0:T(8,128)(2,1)}, bf16[4,3,256,512]{3,2,1,0:T(8,128)(2,1)}, f32[8,128]{1,0:T(8,128)}, f32[8,128]{1,0:T(8,128)}, f32[8,128]{1,0:T(8,128)}, /*index=5*/f32[8,128]{1,0:T(8,128)}) custom-call(s32[22]{0:T(128)} %stack.91.scalars, f32[8,128]{1,0:T(8,128)} %get-tuple-element.675.refs_0_, ...), custom_call_target="tpu_custom_call" | custom-call | flops 999999995904 | bytes 1 | tf_op jit(solution)/shard_map/pallas_call | solution.py:78
  586.3 13.6 %shard_map.303 = (bf16[4,1024,512]{2,1,0:T(8,128)(2,1)}, f32[1024,1]{1,0:T(8,128)}, f32[1,2048]{1,0:T(1,128)}, f32[8,128]{1,0:T(8,128)}, f32[8,128]{1,0:T(8,128)}, /*index=5*/f32[8,128]{1,0:T(8,128)}, f32[8,128]{1,0:T(8,128)}) custom-call(s32[22]{0:T(128)} %stack.91.scalars, f32[8,128]{1,0:T(8,128)} %get-tuple-element.694.refs_0_, ...), custom_call_target="tpu_custom_call" | custom-call | flops 999999995904 | bytes 1 | tf_op jit(solution)/shard_map/pallas_call | solution.py:78
  636.8 12.5 %collective-permute-done.39 = bf16[2,3,256,512]{3,2,1,0:T(8,128)(2,1)} collective-permute-done((bf16[2,3,256,512]{3,2,1,0:T(8,128)(2,1)}, bf16[2,3,256,512]{3,2,1,0:T(8,128)(2,1)}, u32[]{:S(2)}, u32[]{:S(2)}) %collective-permute-start.39) | collective-permute-done | bytes 1572896 | tf_op jit(solution)/shard_map/ppermute | solution.py:101
  680.4 19.4 %collective-permute-done.50 = bf16[1,2,256,768]{3,2,1,0:T(8,128)(2,1)} collective-permute-done((bf16[1,2,256,768]{3,2,1,0:T(8,128)(2,1)}, bf16[1,2,256,768]{3,2,1,0:T(8,128)(2,1)}, u32[]{:S(2)}, u32[]{:S(2)}) %collective-permute-start.50) | collective-permute-done | bytes 786464 | tf_op jit(solution)/shard_map/ppermute | solution.py:101
  (217 shorter events, 216.1 us)
Async XLA Ops:
  7.2 112.4 %all-gather.12.cloned.1.call-start = ((), (), s32[]{:S(2)}) async-start(), calls=%async_computation.8 | async-start | bytes 9437184 | tf_op jit(solution)/shard_map/all_gather | solution.py:1047
  12.8 33.0 %collective-permute-start = (bf16[1024,512]{1,0:T(8,128)(2,1)}, bf16[1024,512]{1,0:T(8,128)(2,1)}, u32[]{:S(2)}, u32[]{:S(2)}) collective-permute-start(bf16[1024,512]{1,0:T(8,128)(2,1)} %refs_4_), channel_id=1, source_target_pairs={{0,1},{1,0},{2,3},{3,2},{4,5},{5,4},{6,7},{7,6},{8,9},{9,8},{10,11... | collective-permute-start | bytes 3145736 | tf_op jit(solution)/shard_map/ppermute | solution.py:101
  14.7 32.5 %collective-permute-start.1 = (bf16[1024,512]{1,0:T(8,128)(2,1)}, bf16[1024,512]{1,0:T(8,128)(2,1)}, u32[]{:S(2)}, u32[]{:S(2)}) collective-permute-start(bf16[1024,512]{1,0:T(8,128)(2,1)} %refs_4_), channel_id=1, source_target_pairs={{0,2},{1,3},{2,0},{3,1},{4,6},{5,7},{6,4},{7,5},{8,10},{9,11},{10,... | collective-permute-start | bytes 3145736 | tf_op jit(solution)/shard_map/ppermute | solution.py:101
  32.1 282.0 %all-gather.6.cloned.1.call-start = ((), (), s32[]{:S(2)}) async-start(), calls=%async_computation.4 | async-start | bytes 5242880 | tf_op jit(solution)/shard_map/all_gather | solution.py:1074
  64.1 30.7 %collective-permute-start.7 = (bf16[1024,512]{1,0:T(8,128)(2,1)}, bf16[1024,512]{1,0:T(8,128)(2,1)}, u32[]{:S(2)}, u32[]{:S(2)}) collective-permute-start(bf16[1024,512]{1,0:T(8,128)(2,1)} %refs_4_.1), channel_id=1, source_target_pairs={{0,1},{1,0},{2,3},{3,2},{4,5},{5,4},{6,7},{7,6},{8,9},{9,8},{10,11... | collective-permute-start | bytes 3145736 | tf_op jit(solution)/shard_map/ppermute | solution.py:101
  65.5 29.3 %collective-permute-start.8 = (bf16[1024,512]{1,0:T(8,128)(2,1)}, bf16[1024,512]{1,0:T(8,128)(2,1)}, u32[]{:S(2)}, u32[]{:S(2)}) collective-permute-start(bf16[1024,512]{1,0:T(8,128)(2,1)} %refs_4_.1), channel_id=1, source_target_pairs={{0,2},{1,3},{2,0},{3,1},{4,6},{5,7},{6,4},{7,5},{8,10},{9,11},{10,... | collective-permute-start | bytes 3145736 | tf_op jit(solution)/shard_map/ppermute | solution.py:101
  134.9 53.5 %collective-permute-start.21 = (bf16[1024,512]{1,0:T(8,128)(2,1)}, bf16[1024,512]{1,0:T(8,128)(2,1)}, u32[]{:S(2)}, u32[]{:S(2)}) collective-permute-start(bf16[1024,512]{1,0:T(8,128)(2,1)} %refs_4_.1), channel_id=1, source_target_pairs={{0,8},{4,12},{8,0},{12,4},{16,24},{20,28},{24,16},{28,20},{1,9},{5... | collective-permute-start | bytes 3145736 | tf_op jit(solution)/shard_map/ppermute | solution.py:101
  150.4 56.2 %collective-permute-start.26 = (bf16[1024,512]{1,0:T(8,128)(2,1)}, bf16[1024,512]{1,0:T(8,128)(2,1)}, u32[]{:S(2)}, u32[]{:S(2)}) collective-permute-start(bf16[1024,512]{1,0:T(8,128)(2,1)} %get-tuple-element.584), channel_id=1, source_target_pairs={{0,8},{4,12},{8,0},{12,4},{16,24},{20,28},{24,16},{28,20},{1,9},{5... | collective-permute-start | bytes 3145736 | tf_op jit(solution)/shard_map/ppermute | solution.py:101
  151.1 242.0 %collective-permute-start.28 = (bf16[1024,128]{1,0:T(8,128)(2,1)}, bf16[1024,128]{1,0:T(8,128)(2,1)}, u32[]{:S(2)}, u32[]{:S(2)}) collective-permute-start(bf16[1024,128]{1,0:T(8,128)(2,1)} %get-tuple-element.589), channel_id=1, source_target_pairs={{0,8},{4,12},{8,0},{12,4},{16,24},{20,28},{24,16},{28,20},{1,9},{5... | collective-permute-start | bytes 786440 | tf_op jit(solution)/shard_map/ppermute | solution.py:101
  188.4 198.6 %all-gather.8.cloned.1.call-start = ((), (), s32[]{:S(2)}) async-start(), calls=%async_computation.5 | async-start | bytes 5242880 | tf_op jit(solution)/shard_map/all_gather | solution.py:1076
  211.9 37.1 %collective-permute-start.18 = (bf16[2,2,256,768]{3,2,1,0:T(8,128)(2,1)}, bf16[2,2,256,768]{3,2,1,0:T(8,128)(2,1)}, u32[]{:S(2)}, u32[]{:S(2)}) collective-permute-start(bf16[2,2,256,768]{3,2,1,0:T(8,128)(2,1)} %get-tuple-element.817.refs_4_), channel_id=1, source_target_pairs={{0,8},{4,12},{8,0},{12,4},{16,24},{20,28},{24,16},{28,20},{1,9},{5... | collective-permute-start | bytes 4718600 | tf_op jit(solution)/shard_map/ppermute | solution.py:101
  252.2 67.9 %collective-permute-start.22 = (bf16[1,2,256,768]{3,2,1,0:T(8,128)(2,1)}, bf16[1,2,256,768]{3,2,1,0:T(8,128)(2,1)}, u32[]{:S(2)}, u32[]{:S(2)}) collective-permute-start(bf16[1,2,256,768]{3,2,1,0:T(8,128)(2,1)} %get-tuple-element.538.refs_4_), channel_id=1, source_target_pairs={{0,16},{4,20},{8,24},{12,28},{16,0},{20,4},{24,8},{28,12},{1,17},{... | collective-permute-start | bytes 2359304 | tf_op jit(solution)/shard_map/ppermute | solution.py:101
  254.1 43.1 %collective-permute-start.19 = (f32[8,128]{1,0:T(8,128)}, f32[8,128]{1,0:T(8,128)}, u32[]{:S(2)}, u32[]{:S(2)}) collective-permute-start(f32[8,128]{1,0:T(8,128)} %get-tuple-element.534.refs_0_), channel_id=1, source_target_pairs={{0,4},{4,0},{8,12},{12,8},{16,20},{20,16},{24,28},{28,24},{1,5},{5... | collective-permute-start | bytes 12296 | tf_op jit(solution)/shard_map/ppermute | solution.py:101
  258.5 70.8 %collective-permute-start.24 = (bf16[2,3,256,768]{3,2,1,0:T(8,128)(2,1)}, bf16[2,3,256,768]{3,2,1,0:T(8,128)(2,1)}, u32[]{:S(2)}, u32[]{:S(2)}) collective-permute-start(bf16[2,3,256,768]{3,2,1,0:T(8,128)(2,1)} %get-tuple-element.807.refs_5_), channel_id=1, source_target_pairs={{0,8},{4,12},{8,0},{12,4},{16,24},{20,28},{24,16},{28,20},{1,9},{5... | collective-permute-start | bytes 7077896 | tf_op jit(solution)/shard_map/ppermute | solution.py:101
  329.0 86.2 %collective-permute-start.23 = (bf16[2,3,256,768]{3,2,1,0:T(8,128)(2,1)}, bf16[2,3,256,768]{3,2,1,0:T(8,128)(2,1)}, u32[]{:S(2)}, u32[]{:S(2)}) collective-permute-start(bf16[2,3,256,768]{3,2,1,0:T(8,128)(2,1)} %get-tuple-element.572.refs_4_), channel_id=1, source_target_pairs={{0,8},{4,12},{8,0},{12,4},{16,24},{20,28},{24,16},{28,20},{1,9},{5... | collective-permute-start | bytes 7077896 | tf_op jit(solution)/shard_map/ppermute | solution.py:101
  333.0 125.5 %collective-permute-start.31 = (bf16[1,3,256,768]{3,2,1,0:T(8,128)(2,1)}, bf16[1,3,256,768]{3,2,1,0:T(8,128)(2,1)}, u32[]{:S(2)}, u32[]{:S(2)}) collective-permute-start(bf16[1,3,256,768]{3,2,1,0:T(8,128)(2,1)} %get-tuple-element.821.refs_5_), channel_id=1, source_target_pairs={{0,16},{4,20},{8,24},{12,28},{16,0},{20,4},{24,8},{28,12},{1,17},{... | collective-permute-start | bytes 3538952 | tf_op jit(solution)/shard_map/ppermute | solution.py:101
  381.8 62.5 %all-to-all-start = ((bf16[4,256,2176]{2,1,0:T(8,128)(2,1)}), bf16[4,256,2176]{2,1,0:T(8,128)(2,1)}, u32[]{:S(2)}, u32[]{:S(2)}) async-start(bf16[4,256,2176]{2,1,0:T(8,128)(2,1)} %get-tuple-element.611), calls=%async_computation | async-start | bytes 8912896 | tf_op jit(solution)/shard_map/all_to_all | solution.py:157
  386.7 132.3 %all-gather.10.cloned.1.call-start = ((), (), s32[]{:S(2)}) async-start(), calls=%async_computation.6 | async-start | bytes 5242880 | tf_op jit(solution)/shard_map/all_gather | solution.py:1156
  418.7 156.6 %collective-permute-start.37 = (bf16[1,3,256,768]{3,2,1,0:T(8,128)(2,1)}, bf16[1,3,256,768]{3,2,1,0:T(8,128)(2,1)}, u32[]{:S(2)}, u32[]{:S(2)}) collective-permute-start(bf16[1,3,256,768]{3,2,1,0:T(8,128)(2,1)} %get-tuple-element.819.refs_4_), channel_id=1, source_target_pairs={{0,16},{4,20},{8,24},{12,28},{16,0},{20,4},{24,8},{28,12},{1,17},{... | collective-permute-start | bytes 3538952 | tf_op jit(solution)/shard_map/ppermute | solution.py:101
  457.3 160.3 %collective-permute-start.42 = (bf16[2,2,256,768]{3,2,1,0:T(8,128)(2,1)}, bf16[2,2,256,768]{3,2,1,0:T(8,128)(2,1)}, u32[]{:S(2)}, u32[]{:S(2)}) collective-permute-start(bf16[2,2,256,768]{3,2,1,0:T(8,128)(2,1)} %get-tuple-element.811.refs_4_), channel_id=1, source_target_pairs={{0,16},{4,20},{8,24},{12,28},{16,0},{20,4},{24,8},{28,12},{1,17},{... | collective-permute-start | bytes 4718600 | tf_op jit(solution)/shard_map/ppermute | solution.py:101
  486.1 26.8 %collective-permute-start.33 = (bf16[4,2,256,768]{3,2,1,0:T(8,128)(2,1)}, bf16[4,2,256,768]{3,2,1,0:T(8,128)(2,1)}, u32[]{:S(2)}, u32[]{:S(2)}) collective-permute-start(bf16[4,2,256,768]{3,2,1,0:T(8,128)(2,1)} %get-tuple-element.633), channel_id=1, source_target_pairs={{0,4},{4,0},{8,12},{12,8},{16,20},{20,16},{24,28},{28,24},{1,5},{5... | collective-permute-start | bytes 9437192 | tf_op jit(solution)/shard_map/ppermute | solution.py:101
  517.2 105.0 %collective-permute-start.41 = (bf16[2,2,256,768]{3,2,1,0:T(8,128)(2,1)}, bf16[2,2,256,768]{3,2,1,0:T(8,128)(2,1)}, u32[]{:S(2)}, u32[]{:S(2)}) collective-permute-start(bf16[2,2,256,768]{3,2,1,0:T(8,128)(2,1)} %get-tuple-element.813.refs_4_), channel_id=1, source_target_pairs={{0,16},{4,20},{8,24},{12,28},{16,0},{20,4},{24,8},{28,12},{1,17},{... | collective-permute-start | bytes 4718600 | tf_op jit(solution)/shard_map/ppermute | solution.py:101
  532.7 72.4 %all-to-all-start.1 = ((bf16[4,1024,512]{2,1,0:T(8,128)(2,1)}), bf16[4,1024,512]{2,1,0:T(8,128)(2,1)}, u32[]{:S(2)}, u32[]{:S(2)}) async-start(bf16[4,1024,512]{2,1,0:T(8,128)(2,1)} %get-tuple-element.706), calls=%async_computation.1 | async-start | bytes 8388608 | tf_op jit(solution)/shard_map/all_to_all | solution.py:157
  537.6 97.8 %reduce-scatter.2.cloned.1.call-start = ((), (), s32[]{:S(2)}) async-start(), calls=%async_computation.7 | async-start | bytes 221184 | tf_op jit(solution)/shard_map/reduce_scatter | solution.py:1185
  540.1 88.4 %collective-permute-start.40 = (bf16[2,1,512,256]{3,2,1,0:T(8,128)(2,1)}, bf16[2,1,512,256]{3,2,1,0:T(8,128)(2,1)}, u32[]{:S(2)}, u32[]{:S(2)}) collective-permute-start(bf16[2,1,512,256]{3,2,1,0:T(8,128)(2,1)} %get-tuple-element.831.refs_5_), channel_id=1, source_target_pairs={{0,8},{4,12},{8,0},{12,4},{16,24},{20,28},{24,16},{28,20},{1,9},{5... | collective-permute-start | bytes 1572872 | tf_op jit(solution)/shard_map/ppermute | solution.py:101
  586.0 63.4 %collective-permute-start.39 = (bf16[2,3,256,512]{3,2,1,0:T(8,128)(2,1)}, bf16[2,3,256,512]{3,2,1,0:T(8,128)(2,1)}, u32[]{:S(2)}, u32[]{:S(2)}) collective-permute-start(bf16[2,3,256,512]{3,2,1,0:T(8,128)(2,1)} %get-tuple-element.815.refs_5_), channel_id=1, source_target_pairs={{0,8},{4,12},{8,0},{12,4},{16,24},{20,28},{24,16},{28,20},{1,9},{5... | collective-permute-start | bytes 4718600 | tf_op jit(solution)/shard_map/ppermute | solution.py:101
  605.1 58.8 %all-to-all-start.2 = ((bf16[4,1024,512]{2,1,0:T(8,128)(2,1)}), bf16[4,1024,512]{2,1,0:T(8,128)(2,1)}, u32[]{:S(2)}, u32[]{:S(2)}) async-start(bf16[4,1024,512]{2,1,0:T(8,128)(2,1)} %get-tuple-element.763), calls=%async_computation.2 | async-start | bytes 8388608 | tf_op jit(solution)/shard_map/all_to_all | solution.py:157
  620.5 51.7 %collective-permute-start.47 = (bf16[1,2,256,768]{3,2,1,0:T(8,128)(2,1)}, bf16[1,2,256,768]{3,2,1,0:T(8,128)(2,1)}, u32[]{:S(2)}, u32[]{:S(2)}) collective-permute-start(bf16[1,2,256,768]{3,2,1,0:T(8,128)(2,1)} %get-tuple-element.727.refs_4_), channel_id=1, source_target_pairs={{0,8},{4,12},{8,0},{12,4},{16,24},{20,28},{24,16},{28,20},{1,9},{5... | collective-permute-start | bytes 2359304 | tf_op jit(solution)/shard_map/ppermute | solution.py:101
  625.2 74.6 %collective-permute-start.50 = (bf16[1,2,256,768]{3,2,1,0:T(8,128)(2,1)}, bf16[1,2,256,768]{3,2,1,0:T(8,128)(2,1)}, u32[]{:S(2)}, u32[]{:S(2)}) collective-permute-start(bf16[1,2,256,768]{3,2,1,0:T(8,128)(2,1)} %get-tuple-element.825.refs_5_), channel_id=1, source_target_pairs={{0,8},{4,12},{8,0},{12,4},{16,24},{20,28},{24,16},{28,20},{1,9},{5... | collective-permute-start | bytes 2359304 | tf_op jit(solution)/shard_map/ppermute | solution.py:101
  628.5 29.1 %collective-permute-start.45 = (f32[8,128]{1,0:T(8,128)}, f32[8,128]{1,0:T(8,128)}, u32[]{:S(2)}, u32[]{:S(2)}) collective-permute-start(f32[8,128]{1,0:T(8,128)} %get-tuple-element.757.refs_5_), channel_id=1, source_target_pairs={{0,2},{1,3},{2,0},{3,1},{4,6},{5,7},{6,4},{7,5},{8,10},{9,11},{10,... | collective-permute-start | bytes 12296 | tf_op jit(solution)/shard_map/ppermute | solution.py:101
  632.5 45.3 %collective-permute-start.49 = (bf16[1,1,512,256]{3,2,1,0:T(8,128)(2,1)}, bf16[1,1,512,256]{3,2,1,0:T(8,128)(2,1)}, u32[]{:S(2)}, u32[]{:S(2)}) collective-permute-start(bf16[1,1,512,256]{3,2,1,0:T(8,128)(2,1)} %get-tuple-element.747.refs_4_), channel_id=1, source_target_pairs={{0,16},{4,20},{8,24},{12,28},{16,0},{20,4},{24,8},{28,12},{1,17},{... | collective-permute-start | bytes 786440 | tf_op jit(solution)/shard_map/ppermute | solution.py:101
  659.1 44.9 %collective-permute-start.51 = (bf16[1,3,256,512]{3,2,1,0:T(8,128)(2,1)}, bf16[1,3,256,512]{3,2,1,0:T(8,128)(2,1)}, u32[]{:S(2)}, u32[]{:S(2)}) collective-permute-start(bf16[1,3,256,512]{3,2,1,0:T(8,128)(2,1)} %get-tuple-element.823.refs_5_), channel_id=1, source_target_pairs={{0,16},{4,20},{8,24},{12,28},{16,0},{20,4},{24,8},{28,12},{1,17},{... | collective-permute-start | bytes 2359304 | tf_op jit(solution)/shard_map/ppermute | solution.py:101
  (51 other events, 586.8 us)
Sparse Core Ops, SparseCore 0:
  32.2 82.3 all-gather.11
  188.6 52.7 all-gather.5
  243.2 52.5 all-gather.7
  451.6 52.5 all-gather.9
  605.2 30.1 reduce-scatter.1
